TPU v7x, 256 devices: a whole 4x4x8 slice. The times are simulated.
256 devices in a mesh: samp: 32 (over z_hi, y, core), site: 8 (over x, z_lo).
Axes of the slice: x: 4, y: 4, z: 8 (z_hi: 4, z_lo: 2; z = z_hi * 2 + z_lo), core: 2. Of those that a mesh axis runs over, the one named last changes fastest.
Arguments:
- values: bfloat16 [2048, 16384], P('samp', 'site'), may hold values from 0.099609375 to 2
- mask: int32 [2048, 16384], P('samp', 'site'), may hold values 0 or 1
- factor: float32 [2048, 128], P('samp'), may hold values from -9 to 9
Outputs:
- basis: float32 [2048, 128], P('samp')
- triangle: float32 [128, 128], replicated
All inputs are finite; a program needn't handle non-finite values. No bound on the sum of `mask` on one device may be relied on, other than what follows from the above.
Results may differ from a plain program's by a relative error of at most 0.0012.
Values may be sent and summed in bfloat16 or wider, within the bound.
No kernel may reach another device: no remote copies, remote signals or barrier semaphores. Data moves between devices by JAX's collectives and lax.ppermute only.
A program may use at most 64 MiB of HBM per device.

v0:
```python
import jax
import jax.numpy as jnp
from jax import lax
from jax.sharding import PartitionSpec as P


def correlate(counts, sum_row, sum_col, sq_row, sq_col, cross):
    numer = counts * cross - sum_row * sum_col
    var_row = counts * sq_row - sum_row * sum_row + counts + 1.0
    var_col = counts * sq_col - sum_col * sum_col + counts + 1.0
    return numer / jnp.sqrt(var_row * var_col)


def square_of(masked):
    wide = masked.astype(jnp.float32)
    return (wide * wide).astype(jnp.bfloat16)


def contract(lhs, rhs):
    return lax.dot_general(lhs, rhs, (((1,), (1,)), ((), ())), preferred_element_type=jnp.float32)


def pair_sums(held_rows, masked_rows, square_rows, column_masked):
    height = held_rows.shape[0]
    width = column_masked.shape[0]
    column_held = (column_masked != 0).astype(jnp.bfloat16)
    column_square = square_of(column_masked)
    stacked_rows = jnp.concatenate([held_rows, masked_rows, square_rows], axis=0)
    first_prod = contract(stacked_rows, column_held)
    second_prod = contract(held_rows, jnp.concatenate([column_masked, column_square], axis=0))
    cross = contract(masked_rows, column_masked)
    counts = first_prod[:height]
    sum_row = first_prod[height : 2 * height]
    sq_row = first_prod[2 * height :]
    sum_col = second_prod[:, :width]
    sq_col = second_prod[:, width:]
    return (counts, sum_row, sum_col, sq_row, sq_col, cross)


def orthogonal(triangle, image_rows):
    return lax.linalg.triangular_solve(
        triangle, image_rows, left_side=False, lower=True, transpose_a=True
    )


def local(values, mask, factor):
    height = values.shape[0]
    held_local = mask.astype(jnp.bfloat16)
    masked_local = jnp.where(mask == 1, values, jnp.zeros_like(values))
    square_local = square_of(masked_local)
    partial_sums = jnp.stack(
        pair_sums(
            held_local,
            masked_local,
            square_local,
            lax.all_gather(masked_local, "samp", axis=0, tiled=True),
        ),
        axis=0,
    )
    totals = lax.psum_scatter(partial_sums, "site", scatter_dimension=2, tiled=True)
    band = correlate(totals[0], totals[1], totals[2], totals[3], totals[4], totals[5])
    width = band.shape[1]
    factor_whole = lax.all_gather(factor, "samp", axis=0, tiled=True)
    factor_cols = lax.dynamic_slice_in_dim(factor_whole, lax.axis_index("site") * width, width, 0)
    image_part = jnp.dot(band, factor_cols, precision=lax.Precision.HIGHEST)
    total_samples = jnp.float32(height * lax.axis_size("samp"))
    image = lax.psum(image_part, "site")
    gram_local = jnp.dot(image.T, image, precision=lax.Precision.HIGHEST)
    gram = lax.psum(gram_local, "samp") / total_samples
    triangle = jnp.linalg.cholesky(gram)
    basis = orthogonal(triangle, image)
    return (basis, triangle)


def solution(mesh):
    return jax.shard_map(
        local,
        mesh=mesh,
        in_specs=(P("samp", "site"), P("samp", "site"), P("samp", None)),
        out_specs=(P("samp", None), P()),
        check_vma=False,
    )
```

profile of v0, /device:TPU:32, one launch (start us, length us, event | category | flops | bytes accessed | tf_op | source)
XLA Modules:
  0.0 537.1 jit_solution(1374483267469339377)
XLA Ops:
  7.2 0.0 all-gather.3.cloned.1.call-start
  7.2 1.9 multiply_convert_fusion.1
  9.1 0.0 all-gather.3.cloned.1.call-update
  9.2 0.0 all-gather.5.cloned.1.call-start
  9.2 0.7 all-gather.5.cloned.1.call-update
  9.9 0.0 reduce-scatter.2.cloned.1.call-start
  10.0 1.1 convert_element_type.16
  11.0 80.6 %all-gather.3.cloned.1.call-done = bf16[2048,2048]{1,0:T(8,128)(2,1)} async-done(((bf16[64,2048]{1,0:T(8,128)(2,1)}), bf16[2048,2048]{1,0:T(8,128)(2,1)}) %all-gather.3.cloned.1.call-update) | async-done | bytes 8388624 | tf_op jit(solution)/shard_map/all_gather | solution.py:56
  91.7 6.7 %fusion.4 = f32[192,2048]{1,0:T(8,128)S(1)} fusion(bf16[2048,2048]{1,0:T(8,128)(2,1)} %all-gather.3.cloned.1.call-done, bf16[64,2048]{1,0:T(8,128)(2,1)S(1)} %get-tuple-element.4, bf16[64,2048]{1,0:T(8,128)(2,1)} %get-tuple-element.5, bf16[64,2048]{1,0:T(8,128)(2,1)S(1)} %convert_element_type.16), kind=kOutput, calls=%fused_computation.5 | convolution fusion | flops 1617166336 | bytes 10747904 | tf_op jit(solution)/shard_map/dot_general | solution.py:20
  98.4 0.8 fusion.20
  99.2 0.0 slice-start
  99.2 9.8 %multiply_convert_fusion = bf16[2048,2048]{1,0:T(8,128)(2,1)} fusion(bf16[2048,2048]{1,0:T(8,128)(2,1)} %all-gather.3.cloned.1.call-done), kind=kLoop, calls=%fused_computation.4 | loop fusion | flops 12582912 | bytes 16777216 | tf_op jit(solution)/shard_map/convert_element_type | solution.py:16
  109.0 0.0 slice-start.1
  109.0 9.0 %fusion.6 = f32[64,4096]{1,0:T(8,128)S(1)} fusion(bf16[64,2048]{1,0:T(8,128)(2,1)S(1)} %convert_element_type.16, bf16[2048,2048]{1,0:T(8,128)(2,1)} %multiply_convert_fusion, bf16[2048,2048]{1,0:T(8,128)(2,1)} %all-gather.3.cloned.1.call-done), kind=kOutput, calls=%fused_computation.7 | convolution fusion | flops 1107296256 | bytes 18087936 | tf_op jit(solution)/shard_map/dot_general | solution.py:20
  118.0 0.0 copy-start
  118.0 0.8 fusion.19
  118.9 0.9 fusion.18
  119.7 0.8 fusion.17
  120.5 0.8 fusion.16
  121.4 0.0 slice-done
  121.4 0.0 slice-done.1
  121.4 0.0 copy-done
  121.4 3.5 fusion.10
  124.9 0.0 reduce-scatter.2.cloned.1.call-update
  124.9 0.0 all-reduce.2.cloned.1.call-start
  124.9 18.6 %all-gather.5.cloned.1.call-done = f32[2048,128]{1,0:T(8,128)} async-done(((f32[64,128]{1,0:T(8,128)}), f32[2048,128]{1,0:T(8,128)}) %all-gather.5.cloned.1.call-update) | async-done | bytes 1048592 | tf_op jit(solution)/shard_map/all_gather | solution.py:63
  143.5 74.3 %reduce-scatter.2.cloned.1.call-done = f32[6,64,256]{2,1,0:T(8,128)} async-done(((f32[6,64,2048]{2,1,0:T(8,128)}), f32[6,64,256]{2,1,0:T(8,128)}) %reduce-scatter.2.cloned.1.call-update) | async-done | bytes 393232 | tf_op jit(solution)/shard_map/reduce_scatter | solution.py:60
  217.8 1.3 fusion.21
  219.2 30.5 %psum.14 = f32[64,128]{1,0:T(8,128)S(1)} all-reduce(f32[64,128]{1,0:T(8,128)S(1)} %fusion.21), channel_id=1, replica_groups=mesh['samp'=32,'site'=8] {'site'}, use_global_device_ids=true, to_apply=%region_1.2 | all-reduce | flops 8192 | bytes 65536 | tf_op jit(solution)/shard_map/psum | solution.py:67
  249.7 0.9 fusion.56
  250.6 0.0 all-reduce.2.cloned.1.call-update
  250.7 253.8 %all-reduce.2.cloned.1.call-done = f32[128,128]{0,1:T(8,128)} async-done(((f32[128,128]{0,1:T(8,128)}), f32[128,128]{0,1:T(8,128)}) %all-reduce.2.cloned.1.call-update) | async-done | bytes 65552 | tf_op jit(solution)/shard_map/psum | solution.py:69
  504.5 0.8 broadcast_multiply_fusion
  505.3 0.1 copy.6
  505.4 0.9 fusion.41
  506.3 11.7 %cholesky.16 = f32[128,128]{1,0:T(8,128)S(1)} custom-call(f32[128,128]{1,0:T(8,128)S(1)} %fusion.41), custom_call_target="Cholesky" | custom-call | tf_op jit(solution)/shard_map/jit(cholesky)/cholesky | solution.py:70
  518.0 0.6 compare_reduce_fusion
  518.7 1.3 select_bitcast_fusion
  520.0 9.8 %custom-call.6 = f32[1,128,128]{1,2,0:T(8,128)S(1)} custom-call(f32[1,128,128]{2,1,0:T(8,128)S(1)} %get-tuple-element.2), custom_call_target="InvertDiagBlocksLowerTriangular" | custom-call | tf_op jit(solution)/shard_map/triangular_solve | solution.py:41
  529.8 0.8 fusion.39
  (2 shorter events, 0.0 us)
Async XLA Ops:
  7.2 84.5 %all-gather.3.cloned.1.call-start = ((), (), s32[]{:S(2)}) async-start(), calls=%async_computation.1 | async-start | bytes 8650752 | tf_op jit(solution)/shard_map/all_gather | solution.py:56
  9.2 134.3 %all-gather.5.cloned.1.call-start = ((), (), s32[]{:S(2)}) async-start(), calls=%async_computation.3 | async-start | bytes 1081344 | tf_op jit(solution)/shard_map/all_gather | solution.py:63
  9.9 207.9 %reduce-scatter.2.cloned.1.call-start = ((), (), s32[]{:S(2)}) async-start(), calls=%async_computation.2 | async-start | bytes 3538944 | tf_op jit(solution)/shard_map/reduce_scatter | solution.py:60
  99.2 22.2 %slice-start = ((s8[8388608]{0:T(1024)(128)(4,1)}), s8[4194304]{0:T(1024)(128)(4,1)S(1)}, s32[]{:S(2)}) async-start(s8[8388608]{0:T(1024)(128)(4,1)} %bitcast.100), calls=%async_computation.5 | async-start | bytes 8388608
  109.0 12.3 %slice-start.1 = ((s8[8388608]{0:T(1024)(128)(4,1)}), s8[4194304]{0:T(1024)(128)(4,1)S(1)}, s32[]{:S(2)}) async-start(s8[8388608]{0:T(1024)(128)(4,1)} %bitcast.100), calls=%async_computation.6 | async-start | bytes 8388608
  118.0 3.4 copy-start
  124.9 379.6 %all-reduce.2.cloned.1.call-start = ((), (), s32[]{:S(2)}) async-start(), calls=%async_computation.4 | async-start | bytes 131072 | tf_op jit(solution)/shard_map/psum | solution.py:69
Sparse Core Ops, SparseCore 0:
  10.6 81.0 all-gather.2
  94.2 49.2 all-gather.4
  146.0 71.7 reduce-scatter.1
  250.8 253.6 all-reduce.1
where the time goes:
time: 538 us; the launch traced here: 537 us
  waiting for transfers between devices  428 us (80%)
  other arithmetic  38 us (7%)
  blocking collectives  30.5 us (6%)
  matrix products  22.2 us (4%)
  between operations  13.8 us (3%)
    psum x1, waiting for transfers between devices, local(): gram = lax.psum(gram_local, 'samp') / total_samples  254 us
    all_gather x1, waiting for transfers between devices, local(): lax.all_gather(masked_local, 'samp', axis=0, tiled=True)  80.6 us
    reduce_scatter x1, waiting for transfers between devices, local(): lax.psum_scatter(partial_sums, 'site', scatter_dimension=2, tiled=True)  74.3 us
    psum x1, blocking collectives, local(): image = lax.psum(image_part, 'site')  30.5 us
    dot_general x3, matrix products, contract(): lax.dot_general(lhs, rhs, (((1,), (1,)), ((), ())), preferred_element_typ...  19.1 us
    all_gather x1, waiting for transfers between devices, local(): factor_whole = lax.all_gather(factor, 'samp', axis=0, tiled=True)  18.6 us
    another operation x3, other arithmetic, local(): triangle = jnp.linalg.cholesky(gram)  12.4 us
    convert_element_type x2, other arithmetic, square_of(): return (wide * wide).astype(jnp.bfloat16)  11.7 us
  transfers between devices with their start and end apart: 4, of which 4 were waited for; matrix products, arithmetic and copies ran while one was open for 6% of the time, Pallas kernels for 0%

commit v1 on v0

v1 whole, which is shorter than its diff:
```python
import functools

import jax
import jax.numpy as jnp
from jax import lax
from jax.experimental import pallas as pl
from jax.experimental.pallas import tpu as pltpu
from jax.sharding import PartitionSpec as P

DEPTHS = 4
BLOCKS = 8
SITE_PARTS = 8
PANEL = 8
ROUTES = ((2, 6, 1), (6, 1, 2), (1, 2, 6))
VMEM_LIMIT = 12 * 1024 * 1024
PAIR_VMEM_LIMIT = 22 * 1024 * 1024


def correlate(counts, sum_row, sum_col, sq_row, sq_col, cross):
    numer = counts * cross - sum_row * sum_col
    var_row = counts * sq_row - sum_row * sum_row + counts + 1.0
    var_col = counts * sq_col - sum_col * sum_col + counts + 1.0
    return numer / jnp.sqrt(var_row * var_col)


def square_of(masked):
    return masked * masked


def held_of(masked):
    return jnp.minimum(masked * 16, 1)


def contract(lhs, rhs):
    return lax.dot_general(lhs, rhs, (((1,), (1,)), ((), ())), preferred_element_type=jnp.float32)


def tree_sum(parts):
    parts = list(parts)
    while len(parts) > 1:
        parts = [parts[i] + parts[i + 1] for i in range(0, len(parts), 2)]
    return parts[0]


def kernel_call(body, out_shape, scratch=(), smem=0, cost=None, limit=VMEM_LIMIT):
    params = pltpu.CompilerParams(vmem_limit_bytes=limit)

    def call(*args):
        in_specs = [pl.BlockSpec(memory_space=pltpu.SMEM)] * smem
        in_specs += [pl.BlockSpec(memory_space=pltpu.VMEM)] * (len(args) - smem)
        return pl.pallas_call(
            body,
            out_shape=out_shape,
            in_specs=in_specs,
            out_specs=jax.tree.map(lambda _: pl.BlockSpec(memory_space=pltpu.VMEM), out_shape),
            scratch_shapes=list(scratch),
            compiler_params=params,
            cost_estimate=cost,
        )(*args)

    return call


ROW_PIECES = ((0, 1), (2, 3), (6, 7), (4,), (5,))
NEAR_BLOCKS = 3


def route_offsets(route, bit):
    first, second, third = ROUTES[route]
    return [(bit * first) ^ (two * second) ^ (three * third) for two in range(2) for three in range(2)]


def pair_body(bit, chunks, which, *refs):
    n_rows = len(ROW_PIECES)
    rows = refs[:n_rows]
    cols, outs = refs[n_rows:-7], refs[-7:-4]
    stack, masked, square, held = refs[-4:]
    height = stack.shape[1]
    sites = masked.shape[1]
    for ref, slots in zip(rows, ROW_PIECES):
        for at, slot in enumerate(slots):
            stack[slot] = ref[at * height : (at + 1) * height]
    begin = 0
    for ref in cols:
        block = ref[:, :sites]
        span = slice(begin, begin + block.shape[0])
        masked[span] = block
        square[span] = square_of(block)
        held[span] = held_of(block)
        begin += block.shape[0]
    blocks = [
        jnp.concatenate([stack[which[0] ^ k] for k in route_offsets(route, bit)], axis=0) for route in range(3)
    ]
    by_held = contract(jnp.concatenate([held_of(blocks[0]), blocks[0], square_of(blocks[1])], axis=0), held[...])
    by_masked = contract(jnp.concatenate([held_of(blocks[1]), blocks[2]], axis=0), masked[...])
    by_square = contract(held_of(blocks[2]), square[...])
    count = 4 * height
    sums = (
        (by_held[:count], by_held[count : 2 * count]),
        (by_masked[:count], by_held[2 * count :]),
        (by_square, by_masked[count:]),
    )
    for out, (first, second) in zip(outs, sums):
        at, parts = 0, []
        for chunk in chunks:
            if chunk == "near":
                at = 2 * height
                parts += [first[:, :at], second[:, :at]]
            parts.append(jnp.concatenate([first[:, at : at + height], second[:, at : at + height]], axis=1))
            at += height
        joined = parts[0] if len(parts) == 1 else jnp.concatenate(parts, axis=1)
        for k in range(4):
            out[k] = joined[k * height : (k + 1) * height]


def band_body(*refs):
    near, far, whole = refs[:3], refs[3:6], refs[6:15]
    pieces, own, out = refs[15:19], refs[19], refs[20]
    height = own.shape[0]
    edge = 2 * NEAR_BLOCKS * height
    totals = []
    for r in range(3):
        rest = tree_sum([ref[0] for ref in whole[3 * r : 3 * r + 2]]) + whole[3 * r + 2][0]
        front = near[r][0] + rest[:, :edge]
        back = far[r][0] + rest[:, edge:]
        for m in range(2):
            third = slice((4 + m) * height, (5 + m) * height)
            totals.append(
                jnp.concatenate(
                    [
                        front[:, 2 * m * height : 2 * (m + 1) * height],
                        jnp.concatenate([front[:, third], back[:, m * height : (m + 1) * height]], axis=1),
                    ],
                    axis=1,
                )
            )
    band = correlate(*totals)
    columns = own.shape[1]
    gathered = [piece[:, :columns].astype(jnp.float32) + piece[:, columns:].astype(jnp.float32) for piece in pieces]
    factor = jnp.concatenate([own[...]] + gathered, axis=0)
    out[...] = jnp.dot(band, factor, precision=lax.Precision.HIGHEST, preferred_element_type=jnp.float32)


def band_call(terms, pieces, own, shape):
    columns = own.shape[1]
    firsts = [pl.BlockSpec((1,) + term.shape[1:], lambda i: (0, 0, 0)) for term in terms]
    tails = [
        pl.BlockSpec((piece.shape[0], 2 * columns), lambda i, at=piece.shape[1] // (2 * columns) - 1: (0, at))
        for piece in pieces
    ]
    whole = pl.BlockSpec(own.shape, lambda i: (0, 0))
    return pl.pallas_call(
        band_body,
        grid=(1,),
        out_shape=shape,
        in_specs=firsts + tails + [whole],
        out_specs=whole,
        compiler_params=pltpu.CompilerParams(vmem_limit_bytes=VMEM_LIMIT),
    )(*terms, *pieces, own)


def gram_body(*refs):
    out = refs[-1]
    image = tree_sum([r[...] for r in refs[:-1]])
    gram = lax.dot_general(
        image, image, (((0,), (0,)), ((), ())), precision=lax.Precision.HIGHEST, preferred_element_type=jnp.float32
    )
    packed, diagonal = pack_gram(gram)
    half = packed.shape[0]
    out[:half] = packed
    out[half : half + PANEL] = diagonal
    out[half + PANEL :] = image


def pack_gram(gram):
    half = gram.shape[0] // 2
    rows = lax.broadcasted_iota(jnp.int32, (half, half), 0)
    cols = lax.broadcasted_iota(jnp.int32, (half, half), 1)
    first = jnp.where(cols < rows, gram[half:, half:], gram[:half, :half])
    lane = lax.broadcasted_iota(jnp.int32, (half, 2 * half), 1)
    row = lax.broadcasted_iota(jnp.int32, (half, 2 * half), 0)
    diagonal = jnp.sum(jnp.where(lane == row + half, gram[half:], 0.0), axis=0, keepdims=True)
    return jnp.concatenate([first, gram[:half, half:]], axis=1), jnp.broadcast_to(diagonal, (PANEL, 2 * half))


def unpack_gram(packed, diagonal):
    half = packed.shape[0]
    lane = lax.broadcasted_iota(jnp.int32, (half, 2 * half), 1)
    row = lax.broadcasted_iota(jnp.int32, (half, 2 * half), 0) + half
    turned = packed[:, :half].T
    turned = jnp.concatenate([turned, turned], axis=1)
    return packed, jnp.where(lane == row, diagonal, turned)


def factor_body(scale, *refs):
    grams, (image_ref, basis_ref, triangle_ref, work) = refs[:2], refs[2:]
    size = work.shape[0]
    half = size // 2
    total = tree_sum([gram[...] for gram in grams]) * scale
    top, bottom = unpack_gram(total[:half], total[half : half + 1])
    rows = lax.broadcasted_iota(jnp.int32, (size, size), 0)
    cols = lax.broadcasted_iota(jnp.int32, (size, size), 1)
    shape = (PANEL, size)
    lane = lax.broadcasted_iota(jnp.int32, shape, 1)
    line = lax.broadcasted_iota(jnp.int32, shape, 0)
    count = size // PANEL
    per_half = count // 2
    left_tiles = [
        (top if t < per_half else bottom)[(t % per_half) * PANEL : (t % per_half + 1) * PANEL] for t in range(count)
    ]
    right_tiles = [jnp.where(lane == line + t * PANEL, 1.0, 0.0) for t in range(count)]

    def spread_row(tile, i):
        return jnp.broadcast_to(tile[i : i + 1], shape)

    def spread_lane(row, at):
        return jnp.broadcast_to(row[:, at : at + 1], shape)

    def gather_rows(lines):
        tile = lines[0]
        for i in range(1, PANEL):
            tile = jnp.where(line == i, lines[i], tile)
        return tile

    left = [spread_row(left_tiles[0], i) for i in range(PANEL)]
    right = [spread_row(right_tiles[0], i) for i in range(PANEL)]
    for p in range(count):
        start, following = p * PANEL, (p + 1) * PANEL
        pivot = {(i, j): spread_lane(left[i], start + j) for i in range(PANEL) for j in range(i, PANEL)}
        if p + 1 < count:
            next_left = [spread_row(left_tiles[p + 1], i) for i in range(PANEL)]
            next_right = [spread_row(right_tiles[p + 1], i) for i in range(PANEL)]
        for k in range(PANEL):
            inverse = lax.rsqrt(pivot[k, k])
            left[k] = left[k] * inverse
            right[k] = right[k] * inverse
            upper = {j: pivot[k, j] * inverse for j in range(k + 1, PANEL)}
            for i in range(k + 1, PANEL):
                left[i] = left[i] - upper[i] * left[k]
                right[i] = right[i] - upper[i] * right[k]
                for j in range(i, PANEL):
                    pivot[i, j] = pivot[i, j] - upper[i] * upper[j]
            if p + 1 < count:
                for i in range(PANEL):
                    factor = spread_lane(left[k], following + i)
                    next_left[i] = next_left[i] - factor * left[k]
                    next_right[i] = next_right[i] - factor * right[k]
        left_panel, right_panel = gather_rows(left), gather_rows(right)
        work[start:following, :size] = left_panel
        work[start:following, size:] = right_panel
        if p + 2 < count:
            update = lax.dot_general(
                left_panel, jnp.concatenate([left_panel, right_panel], axis=1), (((0,), (0,)), ((), ())),
                precision=lax.Precision.HIGHEST, preferred_element_type=jnp.float32,
            )
            for t in range(p + 2, count):
                span = slice(t * PANEL, (t + 1) * PANEL)
                left_tiles[t] = left_tiles[t] - update[span, :size]
                right_tiles[t] = right_tiles[t] - update[span, size:]
        if p + 1 < count:
            left, right = next_left, next_right
    upper = jnp.where(cols >= rows, work[:, :size], 0.0)
    triangle_ref[...] = upper.T
    basis_ref[...] = lax.dot_general(
        image_ref[...], work[:, size:], (((1,), (1,)), ((), ())),
        precision=lax.Precision.HIGHEST, preferred_element_type=jnp.float32,
    )


def samp_perm(shift):
    return [(i, i ^ shift) for i in range(DEPTHS * BLOCKS)]


def site_perm(shift):
    return [(i, i ^ shift) for i in range(SITE_PARTS)]


def gather_line(block, near, other):
    half = block.shape[0] // 2
    one = lax.ppermute(block, "samp", samp_perm(near))
    three = lax.ppermute(block, "samp", samp_perm(other))
    top = lax.ppermute(one[:half], "samp", samp_perm(other))
    bottom = lax.ppermute(three[half:], "samp", samp_perm(near))
    return [block, one, three, top, bottom]


def spread(part, axis, shifts):
    perm = samp_perm if axis == "samp" else site_perm
    return [part] + [lax.ppermute(part, axis, perm(k)) for k in shifts]


def local(values, mask, factor):
    height, sites = values.shape
    columns = factor.shape[1]
    f32 = jnp.float32
    masked = jnp.where(mask == 1, values, jnp.zeros_like(values))
    rounded = lax.reduce_precision(factor, 8, 7)
    coarse, fine = rounded.astype(jnp.bfloat16), (factor - rounded).astype(jnp.bfloat16)
    tagged = jnp.concatenate([masked, coarse, fine], axis=1)
    both = jnp.concatenate([masked, lax.ppermute(masked, "samp", samp_perm(1))], axis=0)
    rows = gather_line(both, 2, 6)
    pieces = gather_line(tagged, BLOCKS, 3 * BLOCKS)[1:]
    near_cols, far_cols = [masked] + pieces[:2], pieces[2:]
    which = ((lax.axis_index("samp") % BLOCKS) ^ lax.axis_index("site")).astype(jnp.int32).reshape(1)

    def pairs(bit, chunks, cols, flops):
        lanes = {"near": 2 * NEAR_BLOCKS * height, "far": 2 * height}
        width = sum(col.shape[0] for col in cols)
        return kernel_call(
            functools.partial(pair_body, bit, chunks),
            [jax.ShapeDtypeStruct((4, height, sum(lanes[chunk] for chunk in chunks)), f32)] * 3,
            scratch=[pltpu.VMEM((BLOCKS, height, sites), jnp.bfloat16)] + [pltpu.VMEM((width, sites), jnp.bfloat16)] * 3,
            smem=1,
            limit=PAIR_VMEM_LIMIT,
            cost=pl.CostEstimate(flops=flops, bytes_accessed=100000, transcendentals=0),
        )(which, *rows, *cols)

    send_near = pairs(1, ("near",), near_cols, 1000000)
    came_near = [lax.ppermute(send_near[r], "site", site_perm(ROUTES[r][0])) for r in range(3)]
    far_cols[0], _ = lax.optimization_barrier((far_cols[0], send_near))
    send_far = pairs(1, ("far",), far_cols, 10000000000)
    came_far = [lax.ppermute(send_far[r], "site", site_perm(ROUTES[r][0])) for r in range(3)]
    far_kept, came_near, _ = lax.optimization_barrier((far_cols[1], came_near, send_far))
    keep = pairs(0, ("near", "far"), near_cols + [far_cols[0], far_kept], 10000000000)
    keep, came_far = lax.optimization_barrier((keep, came_far))

    def arrived(r, at):
        return jnp.concatenate([came_near[r][at], came_far[r][at]], axis=2)

    send = [keep[r][2:] + arrived(r, slice(2, 4)) for r in range(3)]
    came2 = [lax.ppermute(send[r], "site", site_perm(ROUTES[r][1])) for r in range(3)]
    send = [(keep[r][1:2] + came2[r][1:2]) + arrived(r, slice(1, 2)) for r in range(3)]
    came3 = [lax.ppermute(send[r], "site", site_perm(ROUTES[r][2])) for r in range(3)]
    terms = came_near + came_far + [t for r in range(3) for t in (keep[r], came2[r], came3[r])]
    part = band_call(terms, pieces, factor, jax.ShapeDtypeStruct((height, columns), f32))
    part = tree_sum(spread(part, "samp", [1]))
    packed = columns // 2 + PANEL
    message = kernel_call(gram_body, jax.ShapeDtypeStruct((packed + height, columns), f32))(*spread(part, "samp", [2, 4, 6]))
    is_gram = lax.broadcasted_iota(jnp.int32, message.shape, 0) < packed
    apart = which[0]
    came = spread(message, "site", [2, 4, 6])
    turn = apart >> 1
    picked = jnp.where(turn < 2, jnp.where(turn == 0, came[0], came[1]), jnp.where(turn == 2, came[2], came[3]))
    message = jnp.where(is_gram, tree_sum(came), picked)
    came = spread(message, "site", [1])
    message = jnp.where(is_gram, tree_sum(came), jnp.where((apart & 1) == 0, came[0], came[1]))
    gram, own_image = message[:packed], message[packed:]
    gram = tree_sum(spread(gram, "samp", [BLOCKS]))
    grams = spread(gram, "samp", [3 * BLOCKS])
    scale = 1.0 / (height * DEPTHS * BLOCKS)
    basis, triangle = kernel_call(
        functools.partial(factor_body, scale),
        [jax.ShapeDtypeStruct((height, columns), f32), jax.ShapeDtypeStruct((columns, columns), f32)],
        scratch=[pltpu.VMEM((columns, 2 * columns), f32)],
    )(*grams, own_image)
    return (basis, triangle)


def solution(mesh):
    return jax.shard_map(
        local,
        mesh=mesh,
        in_specs=(P("samp", "site"), P("samp", "site"), P("samp", None)),
        out_specs=(P("samp", None), P()),
        check_vma=False,
    )
```

time: 538 us -> 107 us (0.20)
  waiting for transfers between devices: 428 us -> 36.6 us
  starting transfers between devices: 0.16 us -> 51.3 us
  other arithmetic: 38 us -> 1.66 us
  blocking collectives: 30.5 us -> 0 us
  matrix products: 22.2 us -> 0 us
  between operations: 13.8 us -> 1.01 us
  Pallas kernels: 0 us -> 12.4 us
    psum x1 -> x0, waiting for transfers between devices: 254 us -> none  [local(): gram = lax.psum(gram_local, 'samp') / total_samples]
    all_gather x2 -> x0, waiting for transfers between devices: 99.2 us -> none  [the longest x1 80.6 us: local(): lax.all_gather(masked_local, 'samp', axis=0, tiled=True)]
    reduce_scatter x1 -> x0, waiting for transfers between devices: 74.3 us -> none  [local(): lax.psum_scatter(partial_sums, 'site', scatter_dimension=2, tiled=True)]
    ppermute x0 -> x31, starting transfers between devices: none -> 51.3 us  [the longest x10 12.6 us: spread(): return [part] + [lax.ppermute(part, axis, perm(k)) for k in shifts]]
    ppermute x0 -> x31, waiting for transfers between devices: none -> 36.6 us  [the longest x10 19.5 us: spread(): return [part] + [lax.ppermute(part, axis, perm(k)) for k in shifts]]
    psum x1 -> x0, blocking collectives: 30.5 us -> none  [local(): image = lax.psum(image_part, 'site')]
    another operation x5 -> x0, other arithmetic: 23.5 us -> none  [the longest x3 12.4 us: local(): triangle = jnp.linalg.cholesky(gram)]
    dot_general x5 -> x0, matrix products: 21.4 us -> none  [the longest x3 19.1 us: contract(): lax.dot_general(lhs, rhs, (((1,), (1,)), ((), ())), preferred_element_typ...]
  transfers between devices with their start and end apart: 4 -> 31, of which waited for: 4 -> 19; matrix products, arithmetic and copies ran while one was open for 6% -> 2% of each run, Pallas kernels for 0% -> 6%
where the time goes in v1:
time: 107 us
  starting transfers between devices  51.3 us (48%)
  waiting for transfers between devices  36.6 us (34%)
  Pallas kernels  12.4 us (12%)
  local copies, waits for them, and re-layouts  3.88 us (4%)
  other arithmetic  1.66 us (2%)
    ppermute x10, waiting for transfers between devices, spread(): return [part] + [lax.ppermute(part, axis, perm(k)) for k in shifts]  19.5 us
    ppermute x10, starting transfers between devices, spread(): return [part] + [lax.ppermute(part, axis, perm(k)) for k in shifts]  12.6 us
    pallas_call x5, Pallas kernels, call(): pl.pallas_call(body, out_shape=out_shape, in_specs=in_specs, out_specs=ja...  12.1 us
    ppermute x2, starting transfers between devices, gather_line(): top = lax.ppermute(one[:half], 'samp', samp_perm(other))  8.71 us
    ppermute x2, starting transfers between devices, gather_line(): three = lax.ppermute(block, 'samp', samp_perm(other))  5.76 us
    ppermute x3, starting transfers between devices, local(): lax.ppermute(send_near[r], 'site', site_perm(ROUTES[r][0]))  5.54 us
    ppermute x3, starting transfers between devices, local(): lax.ppermute(send_far[r], 'site', site_perm(ROUTES[r][0]))  5.21 us
    ppermute x2, starting transfers between devices, gather_line(): one = lax.ppermute(block, 'samp', samp_perm(near))  5.02 us
  transfers between devices with their start and end apart: 31, of which 19 were waited for; matrix products, arithmetic and copies ran while one was open for 2% of the time, Pallas kernels for 6%

profile of v1, /device:TPU:32, one launch (start us, length us, event | category | flops | bytes accessed | tf_op | source)
XLA Modules:
  0.0 106.8 jit_solution(7527524140323254515)
XLA Ops:
  0.6 1.2 %compare_select_fusion.refs_5_ = bf16[64,2048]{1,0:T(8,128)(2,1)S(1)} fusion(bf16[64,2048]{1,0:T(8,128)(2,1)} %param.3, s32[64,2048]{1,0:T(8,128)} %param.4), kind=kLoop, calls=%fused_computation.1 | loop fusion | flops 262144 | bytes 1048576 | tf_op jit(solution)/shard_map/jit(_where)/select_n | solution.py:296
  2.0 1.5 %collective-permute-done.2 = bf16[64,2048]{1,0:T(8,128)(2,1)S(1)} collective-permute-done((bf16[64,2048]{1,0:T(8,128)(2,1)S(1)}, bf16[64,2048]{1,0:T(8,128)(2,1)S(1)}, u32[]{:S(2)}, u32[]{:S(2)}) %collective-permute-start.2) | collective-permute-done | bytes 262176 | tf_op jit(solution)/shard_map/ppermute | solution.py:300
  3.5 1.7 %collective-permute-start.3 = (bf16[128,2048]{1,0:T(8,128)(2,1)S(1)}, bf16[128,2048]{1,0:T(8,128)(2,1)S(1)}, u32[]{:S(2)}, u32[]{:S(2)}) collective-permute-start(bf16[128,2048]{1,0:T(8,128)(2,1)S(1)} %pad_maximum_fusion.refs_0_), channel_id=1, source_target_pairs={{0,16},{8,24},{16,0},{24,8},{32,48},{40,56},{48,32},{56,40},{64,80... | collective-permute-start | bytes 1572872 | tf_op jit(solution)/shard_map/ppermute | solution.py:280
  5.2 2.2 %collective-permute-start.4 = (bf16[128,2048]{1,0:T(8,128)(2,1)S(1)}, bf16[128,2048]{1,0:T(8,128)(2,1)S(1)}, u32[]{:S(2)}, u32[]{:S(2)}) collective-permute-start(bf16[128,2048]{1,0:T(8,128)(2,1)S(1)} %pad_maximum_fusion.refs_0_), channel_id=1, source_target_pairs={{0,48},{8,56},{16,32},{24,40},{32,16},{40,24},{48,0},{56,8},{64,11... | collective-permute-start | bytes 1572872 | tf_op jit(solution)/shard_map/ppermute | solution.py:281
  7.4 3.4 %collective-permute-start.7 = (bf16[64,2304]{1,0:T(8,128)(2,1)S(1)}, bf16[64,2304]{1,0:T(8,128)(2,1)S(1)}, u32[]{:S(2)}, u32[]{:S(2)}) collective-permute-start(bf16[64,2304]{1,0:T(8,128)(2,1)S(1)} %pad_maximum_fusion.1), channel_id=1, source_target_pairs={{0,64},{8,72},{16,80},{24,88},{32,96},{40,104},{48,112},{56,120},{... | collective-permute-start | bytes 884744 | tf_op jit(solution)/shard_map/ppermute | solution.py:280
  10.7 3.6 %collective-permute-start = (bf16[64,2304]{1,0:T(8,128)(2,1)S(1)}, bf16[64,2304]{1,0:T(8,128)(2,1)S(1)}, u32[]{:S(2)}, u32[]{:S(2)}) collective-permute-start(bf16[64,2304]{1,0:T(8,128)(2,1)S(1)} %pad_maximum_fusion.1), channel_id=1, source_target_pairs={{0,192},{8,200},{16,208},{24,216},{32,224},{40,232},{48,240},{56,2... | collective-permute-start | bytes 884744 | tf_op jit(solution)/shard_map/ppermute | solution.py:281
  14.3 3.2 %collective-permute-done.3.refs_1_ = bf16[128,2048]{1,0:T(8,128)(2,1)S(1)} collective-permute-done((bf16[128,2048]{1,0:T(8,128)(2,1)S(1)}, bf16[128,2048]{1,0:T(8,128)(2,1)S(1)}, u32[]{:S(2)}, u32[]{:S(2)}) %collective-permute-start.3) | collective-permute-done | bytes 524320 | tf_op jit(solution)/shard_map/ppermute | solution.py:280
  17.6 3.1 %collective-permute-start.5 = (bf16[64,2048]{1,0:T(8,128)(2,1)S(1)}, bf16[64,2048]{1,0:T(8,128)(2,1)S(1)}, u32[]{:S(2)}, u32[]{:S(2)}) collective-permute-start(bf16[64,2048]{1,0:T(8,128)(2,1)S(1)} %slice.109), channel_id=1, source_target_pairs={{0,48},{8,56},{16,32},{24,40},{32,16},{40,24},{48,0},{56,8},{64,11... | collective-permute-start | bytes 786440 | tf_op jit(solution)/shard_map/ppermute | solution.py:282
  21.6 1.1 %collective-permute-done.7.refs_6_.refs_15_ = bf16[64,2304]{1,0:T(8,128)(2,1)S(1)} collective-permute-done((bf16[64,2304]{1,0:T(8,128)(2,1)S(1)}, bf16[64,2304]{1,0:T(8,128)(2,1)S(1)}, u32[]{:S(2)}, u32[]{:S(2)}) %collective-permute-start.7) | collective-permute-done | bytes 294944 | tf_op jit(solution)/shard_map/ppermute | solution.py:280
  23.3 5.6 %collective-permute-start.11 = (bf16[32,2304]{1,0:T(8,128)(2,1)}, bf16[32,2304]{1,0:T(8,128)(2,1)S(1)}, u32[]{:S(2)}, u32[]{:S(2)}) collective-permute-start(bf16[32,2304]{1,0:T(8,128)(2,1)} %slice.111), channel_id=1, source_target_pairs={{0,192},{8,200},{16,208},{24,216},{32,224},{40,232},{48,240},{56,2... | collective-permute-start | bytes 442376 | tf_op jit(solution)/shard_map/ppermute | solution.py:282
  29.6 0.9 collective-permute-start.1
  30.5 2.0 %shard_map.50 = (f32[4,64,384]{2,1,0:T(8,128)S(1)}, f32[4,64,384]{2,1,0:T(8,128)S(1)}, f32[4,64,384]{2,1,0:T(8,128)S(1)}) custom-call(s32[1]{0:T(128)} %bitcast.which, bf16[128,2048]{1,0:T(8,128)(2,1)S(1)} %pad_maximum_fusion.refs_0_, bf16[128,2048]{1,0:T(8,128)(2,1)S(1)} %collective-permute-done.3.refs_1_, ...), custom_call_target="tpu_custom_call" | custom-call | flops 1000000 | bytes 100000 | tf_op jit(solution)/shard_map/pallas_call | solution.py:51
  32.5 1.6 %collective-permute-start.8 = (f32[4,64,384]{2,1,0:T(8,128)S(1)}, f32[4,64,384]{2,1,0:T(8,128)S(1)}, u32[]{:S(2)}, u32[]{:S(2)}) collective-permute-start(f32[4,64,384]{2,1,0:T(8,128)S(1)} %get-tuple-element.22), channel_id=1, source_target_pairs={{0,2},{1,3},{2,0},{3,1},{4,6},{5,7},{6,4},{7,5},{8,10},{9,11},{10,... | collective-permute-start | bytes 1179656 | tf_op jit(solution)/shard_map/ppermute | solution.py:319
  34.1 2.1 %collective-permute-start.9 = (f32[4,64,384]{2,1,0:T(8,128)S(1)}, f32[4,64,384]{2,1,0:T(8,128)S(1)}, u32[]{:S(2)}, u32[]{:S(2)}) collective-permute-start(f32[4,64,384]{2,1,0:T(8,128)S(1)} %get-tuple-element.23), channel_id=1, source_target_pairs={{0,6},{1,7},{2,4},{3,5},{4,2},{5,3},{6,0},{7,1},{8,14},{9,15},{10,... | collective-permute-start | bytes 1179656 | tf_op jit(solution)/shard_map/ppermute | solution.py:319
  36.2 1.9 %collective-permute-start.10 = (f32[4,64,384]{2,1,0:T(8,128)S(1)}, f32[4,64,384]{2,1,0:T(8,128)S(1)}, u32[]{:S(2)}, u32[]{:S(2)}) collective-permute-start(f32[4,64,384]{2,1,0:T(8,128)S(1)} %get-tuple-element.24), channel_id=1, source_target_pairs={{0,1},{1,0},{2,3},{3,2},{4,5},{5,4},{6,7},{7,6},{8,9},{9,8},{10,11... | collective-permute-start | bytes 1179656 | tf_op jit(solution)/shard_map/ppermute | solution.py:319
  38.1 2.0 %shard_map.51 = (f32[4,64,128]{2,1,0:T(8,128)S(1)}, f32[4,64,128]{2,1,0:T(8,128)S(1)}, f32[4,64,128]{2,1,0:T(8,128)S(1)}) custom-call(s32[1]{0:T(128)} %bitcast.which, bf16[128,2048]{1,0:T(8,128)(2,1)S(1)} %pad_maximum_fusion.refs_0_, bf16[128,2048]{1,0:T(8,128)(2,1)S(1)} %collective-permute-done.3.refs_1_, ...), custom_call_target="tpu_custom_call" | custom-call | flops 10000000000 | bytes 100000 | tf_op jit(solution)/shard_map/pallas_call | solution.py:51
  40.0 2.0 %collective-permute-start.12 = (f32[4,64,128]{2,1,0:T(8,128)S(1)}, f32[4,64,128]{2,1,0:T(8,128)S(1)}, u32[]{:S(2)}, u32[]{:S(2)}) collective-permute-start(f32[4,64,128]{2,1,0:T(8,128)S(1)} %get-tuple-element.26), channel_id=1, source_target_pairs={{0,2},{1,3},{2,0},{3,1},{4,6},{5,7},{6,4},{7,5},{8,10},{9,11},{10,... | collective-permute-start | bytes 393224 | tf_op jit(solution)/shard_map/ppermute | solution.py:322
  42.0 2.6 %collective-permute-start.13 = (f32[4,64,128]{2,1,0:T(8,128)S(1)}, f32[4,64,128]{2,1,0:T(8,128)S(1)}, u32[]{:S(2)}, u32[]{:S(2)}) collective-permute-start(f32[4,64,128]{2,1,0:T(8,128)S(1)} %get-tuple-element.27), channel_id=1, source_target_pairs={{0,6},{1,7},{2,4},{3,5},{4,2},{5,3},{6,0},{7,1},{8,14},{9,15},{10,... | collective-permute-start | bytes 393224 | tf_op jit(solution)/shard_map/ppermute | solution.py:322
  45.8 0.8 collective-permute-done.10.refs_2_
  46.5 2.0 %shard_map.52 = (f32[4,64,512]{2,1,0:T(8,128)S(1)}, f32[4,64,512]{2,1,0:T(8,128)S(1)}, f32[4,64,512]{2,1,0:T(8,128)S(1)}) custom-call(s32[1]{0:T(128)} %bitcast.which, bf16[128,2048]{1,0:T(8,128)(2,1)S(1)} %pad_maximum_fusion.refs_0_, bf16[128,2048]{1,0:T(8,128)(2,1)S(1)} %collective-permute-done.3.refs_1_, ...), custom_call_target="tpu_custom_call" | custom-call | flops 10000000000 | bytes 100000 | tf_op jit(solution)/shard_map/pallas_call | solution.py:51
  48.6 1.0 collective-permute-done.14.refs_5_
  49.7 1.6 %collective-permute-start.15 = (f32[2,64,512]{2,1,0:T(8,128)S(1)}, f32[2,64,512]{2,1,0:T(8,128)S(1)}, u32[]{:S(2)}, u32[]{:S(2)}) collective-permute-start(f32[2,64,512]{2,1,0:T(8,128)S(1)} %maximum_add_fusion), channel_id=1, source_target_pairs={{0,6},{1,7},{2,4},{3,5},{4,2},{5,3},{6,0},{7,1},{8,14},{9,15},{10,... | collective-permute-start | bytes 786440 | tf_op jit(solution)/shard_map/ppermute | solution.py:331
  51.3 0.8 slice-done.4
  52.1 2.0 %collective-permute-start.17 = (f32[2,64,512]{2,1,0:T(8,128)S(1)}, f32[2,64,512]{2,1,0:T(8,128)S(1)}, u32[]{:S(2)}, u32[]{:S(2)}) collective-permute-start(f32[2,64,512]{2,1,0:T(8,128)S(1)} %maximum_add_fusion.1), channel_id=1, source_target_pairs={{0,1},{1,0},{2,3},{3,2},{4,5},{5,4},{6,7},{7,6},{8,9},{9,8},{10,11... | collective-permute-start | bytes 786440 | tf_op jit(solution)/shard_map/ppermute | solution.py:331
  54.1 0.8 slice-done.6
  55.4 1.9 %collective-permute-done.15.refs_7_ = f32[2,64,512]{2,1,0:T(8,128)S(1)} collective-permute-done((f32[2,64,512]{2,1,0:T(8,128)S(1)}, f32[2,64,512]{2,1,0:T(8,128)S(1)}, u32[]{:S(2)}, u32[]{:S(2)}) %collective-permute-start.15) | collective-permute-done | bytes 262176 | tf_op jit(solution)/shard_map/ppermute | solution.py:331
  57.4 0.8 collective-permute-start.16
  58.2 0.9 collective-permute-done.17.refs_10_
  59.1 1.0 collective-permute-start.18
  60.1 1.5 %collective-permute-done.19.refs_13_ = f32[2,64,512]{2,1,0:T(8,128)S(1)} collective-permute-done((f32[2,64,512]{2,1,0:T(8,128)S(1)}, f32[2,64,512]{2,1,0:T(8,128)S(1)}, u32[]{:S(2)}, u32[]{:S(2)}) %collective-permute-start.19) | collective-permute-done | bytes 262176 | tf_op jit(solution)/shard_map/ppermute | solution.py:331
  61.6 1.5 %collective-permute-start.20 = (f32[1,64,512]{2,1,0:T(8,128)S(1)}, f32[1,64,512]{2,1,0:T(8,128)S(1)}, u32[]{:S(2)}, u32[]{:S(2)}) collective-permute-start(f32[1,64,512]{2,1,0:T(8,128)S(1)} %fusion), channel_id=1, source_target_pairs={{0,6},{1,7},{2,4},{3,5},{4,2},{5,3},{6,0},{7,1},{8,14},{9,15},{10,... | collective-permute-start | bytes 393224 | tf_op jit(solution)/shard_map/ppermute | solution.py:333
  63.2 1.0 collective-permute-done.18.refs_11_
  64.2 3.7 %collective-permute-done.20.refs_14_ = f32[1,64,512]{2,1,0:T(8,128)S(1)} collective-permute-done((f32[1,64,512]{2,1,0:T(8,128)S(1)}, f32[1,64,512]{2,1,0:T(8,128)S(1)}, u32[]{:S(2)}, u32[]{:S(2)}) %collective-permute-start.20) | collective-permute-done | bytes 131104 | tf_op jit(solution)/shard_map/ppermute | solution.py:333
  68.4 1.2 %collective-permute-done.21 = f32[64,128]{1,0:T(8,128)S(1)} collective-permute-done((f32[64,128]{1,0:T(8,128)S(1)}, f32[64,128]{1,0:T(8,128)S(1)}, u32[]{:S(2)}, u32[]{:S(2)}) %collective-permute-start.21) | collective-permute-done | bytes 32800 | tf_op jit(solution)/shard_map/ppermute | solution.py:289
  69.6 2.0 %collective-permute-start.22 = (f32[64,128]{1,0:T(8,128)S(1)}, f32[64,128]{1,0:T(8,128)S(1)}, u32[]{:S(2)}, u32[]{:S(2)}) collective-permute-start(f32[64,128]{1,0:T(8,128)S(1)} %add.59.refs_0_), channel_id=1, source_target_pairs={{0,16},{8,24},{16,0},{24,8},{32,48},{40,56},{48,32},{56,40},{64,80... | collective-permute-start | bytes 98312 | tf_op jit(solution)/shard_map/ppermute | solution.py:289
  71.7 1.4 %collective-permute-start.23 = (f32[64,128]{1,0:T(8,128)S(1)}, f32[64,128]{1,0:T(8,128)S(1)}, u32[]{:S(2)}, u32[]{:S(2)}) collective-permute-start(f32[64,128]{1,0:T(8,128)S(1)} %add.59.refs_0_), channel_id=1, source_target_pairs={{0,32},{8,40},{16,48},{24,56},{32,0},{40,8},{48,16},{56,24},{64,96... | collective-permute-start | bytes 98312 | tf_op jit(solution)/shard_map/ppermute | solution.py:289
  73.1 1.4 %collective-permute-start.24 = (f32[64,128]{1,0:T(8,128)S(1)}, f32[64,128]{1,0:T(8,128)S(1)}, u32[]{:S(2)}, u32[]{:S(2)}) collective-permute-start(f32[64,128]{1,0:T(8,128)S(1)} %add.59.refs_0_), channel_id=1, source_target_pairs={{0,48},{8,56},{16,32},{24,40},{32,16},{40,24},{48,0},{56,8},{64,11... | collective-permute-start | bytes 98312 | tf_op jit(solution)/shard_map/ppermute | solution.py:289
  74.4 2.8 %collective-permute-done.23.refs_2_ = f32[64,128]{1,0:T(8,128)S(1)} collective-permute-done((f32[64,128]{1,0:T(8,128)S(1)}, f32[64,128]{1,0:T(8,128)S(1)}, u32[]{:S(2)}, u32[]{:S(2)}) %collective-permute-start.23) | collective-permute-done | bytes 32800 | tf_op jit(solution)/shard_map/ppermute | solution.py:289
  77.2 1.0 collective-permute-done.24.refs_3_
  78.6 1.8 %collective-permute-start.27 = (f32[136,128]{1,0:T(8,128)S(1)}, f32[136,128]{1,0:T(8,128)S(1)}, u32[]{:S(2)}, u32[]{:S(2)}) collective-permute-start(f32[136,128]{1,0:T(8,128)S(1)} %shard_map.54), channel_id=1, source_target_pairs={{0,6},{1,7},{2,4},{3,5},{4,2},{5,3},{6,0},{7,1},{8,14},{9,15},{10,... | collective-permute-start | bytes 208904 | tf_op jit(solution)/shard_map/ppermute | solution.py:289
  80.5 1.7 %collective-permute-start.25 = (f32[136,128]{1,0:T(8,128)S(1)}, f32[136,128]{1,0:T(8,128)S(1)}, u32[]{:S(2)}, u32[]{:S(2)}) collective-permute-start(f32[136,128]{1,0:T(8,128)S(1)} %shard_map.54), channel_id=1, source_target_pairs={{0,2},{1,3},{2,0},{3,1},{4,6},{5,7},{6,4},{7,5},{8,10},{9,11},{10,... | collective-permute-start | bytes 208904 | tf_op jit(solution)/shard_map/ppermute | solution.py:289
  82.1 2.4 %collective-permute-done.26 = f32[136,128]{1,0:T(8,128)S(1)} collective-permute-done((f32[136,128]{1,0:T(8,128)S(1)}, f32[136,128]{1,0:T(8,128)S(1)}, u32[]{:S(2)}, u32[]{:S(2)}) %collective-permute-start.26) | collective-permute-done | bytes 69664 | tf_op jit(solution)/shard_map/ppermute | solution.py:289
  85.6 4.3 %collective-permute-done.28 = f32[136,128]{1,0:T(8,128)S(1)} collective-permute-done((f32[136,128]{1,0:T(8,128)S(1)}, f32[136,128]{1,0:T(8,128)S(1)}, u32[]{:S(2)}, u32[]{:S(2)}) %collective-permute-start.28) | collective-permute-done | bytes 69664 | tf_op jit(solution)/shard_map/ppermute | solution.py:289
  90.0 1.0 collective-permute-start.29
  91.0 4.0 %collective-permute-done.29 = f32[72,128]{1,0:T(8,128)S(1)} collective-permute-done((f32[72,128]{1,0:T(8,128)S(1)}, f32[72,128]{1,0:T(8,128)S(1)}, u32[]{:S(2)}, u32[]{:S(2)}) %collective-permute-start.29) | collective-permute-done | bytes 36896 | tf_op jit(solution)/shard_map/ppermute | solution.py:289
  95.0 2.7 %collective-permute-start.30 = (f32[72,128]{1,0:T(8,128)S(1)}, f32[72,128]{1,0:T(8,128)S(1)}, u32[]{:S(2)}, u32[]{:S(2)}) collective-permute-start(f32[72,128]{1,0:T(8,128)S(1)} %slice_add_fusion.3.refs_0_), channel_id=1, source_target_pairs={{0,192},{8,200},{16,208},{24,216},{32,224},{40,232},{48,240},{56,2... | collective-permute-start | bytes 110600 | tf_op jit(solution)/shard_map/ppermute | solution.py:289
  97.6 3.4 %collective-permute-done.30.refs_1_ = f32[72,128]{1,0:T(8,128)S(1)} collective-permute-done((f32[72,128]{1,0:T(8,128)S(1)}, f32[72,128]{1,0:T(8,128)S(1)}, u32[]{:S(2)}, u32[]{:S(2)}) %collective-permute-start.30) | collective-permute-done | bytes 36896 | tf_op jit(solution)/shard_map/ppermute | solution.py:289
  101.0 5.8 %shard_map.55 = (f32[64,128]{1,0:T(8,128)}, f32[128,128]{1,0:T(8,128)}) custom-call(f32[72,128]{1,0:T(8,128)S(1)} %slice_add_fusion.3.refs_0_, f32[72,128]{1,0:T(8,128)S(1)} %collective-permute-done.30.refs_1_, f32[64,128]{1,0:T(8,128)S(1)} %slice.116.refs_2_), custom_call_target="tpu_custom_call" | custom-call | tf_op jit(solution)/shard_map/pallas_call | solution.py:51
  (87 shorter events, 6.3 us)
Async XLA Ops:
  1.8 1.6 %collective-permute-start.2 = (bf16[64,2048]{1,0:T(8,128)(2,1)S(1)}, bf16[64,2048]{1,0:T(8,128)(2,1)S(1)}, u32[]{:S(2)}, u32[]{:S(2)}) collective-permute-start(bf16[64,2048]{1,0:T(8,128)(2,1)S(1)} %compare_select_fusion.refs_5_), channel_id=1, source_target_pairs={{0,8},{8,0},{16,24},{24,16},{32,40},{40,32},{48,56},{56,48},{64,72... | collective-permute-start | bytes 786440 | tf_op jit(solution)/shard_map/ppermute | solution.py:300
  3.5 14.1 %collective-permute-start.3 = (bf16[128,2048]{1,0:T(8,128)(2,1)S(1)}, bf16[128,2048]{1,0:T(8,128)(2,1)S(1)}, u32[]{:S(2)}, u32[]{:S(2)}) collective-permute-start(bf16[128,2048]{1,0:T(8,128)(2,1)S(1)} %pad_maximum_fusion.refs_0_), channel_id=1, source_target_pairs={{0,16},{8,24},{16,0},{24,8},{32,48},{40,56},{48,32},{56,40},{64,80... | collective-permute-start | bytes 1572872 | tf_op jit(solution)/shard_map/ppermute | solution.py:280
  5.2 15.5 %collective-permute-start.4 = (bf16[128,2048]{1,0:T(8,128)(2,1)S(1)}, bf16[128,2048]{1,0:T(8,128)(2,1)S(1)}, u32[]{:S(2)}, u32[]{:S(2)}) collective-permute-start(bf16[128,2048]{1,0:T(8,128)(2,1)S(1)} %pad_maximum_fusion.refs_0_), channel_id=1, source_target_pairs={{0,48},{8,56},{16,32},{24,40},{32,16},{40,24},{48,0},{56,8},{64,11... | collective-permute-start | bytes 1572872 | tf_op jit(solution)/shard_map/ppermute | solution.py:281
  7.4 15.3 %collective-permute-start.7 = (bf16[64,2304]{1,0:T(8,128)(2,1)S(1)}, bf16[64,2304]{1,0:T(8,128)(2,1)S(1)}, u32[]{:S(2)}, u32[]{:S(2)}) collective-permute-start(bf16[64,2304]{1,0:T(8,128)(2,1)S(1)} %pad_maximum_fusion.1), channel_id=1, source_target_pairs={{0,64},{8,72},{16,80},{24,88},{32,96},{40,104},{48,112},{56,120},{... | collective-permute-start | bytes 884744 | tf_op jit(solution)/shard_map/ppermute | solution.py:280
  10.7 18.2 %collective-permute-start = (bf16[64,2304]{1,0:T(8,128)(2,1)S(1)}, bf16[64,2304]{1,0:T(8,128)(2,1)S(1)}, u32[]{:S(2)}, u32[]{:S(2)}) collective-permute-start(bf16[64,2304]{1,0:T(8,128)(2,1)S(1)} %pad_maximum_fusion.1), channel_id=1, source_target_pairs={{0,192},{8,200},{16,208},{24,216},{32,224},{40,232},{48,240},{56,2... | collective-permute-start | bytes 884744 | tf_op jit(solution)/shard_map/ppermute | solution.py:281
  17.6 12.9 %collective-permute-start.5 = (bf16[64,2048]{1,0:T(8,128)(2,1)S(1)}, bf16[64,2048]{1,0:T(8,128)(2,1)S(1)}, u32[]{:S(2)}, u32[]{:S(2)}) collective-permute-start(bf16[64,2048]{1,0:T(8,128)(2,1)S(1)} %slice.109), channel_id=1, source_target_pairs={{0,48},{8,56},{16,32},{24,40},{32,16},{40,24},{48,0},{56,8},{64,11... | collective-permute-start | bytes 786440 | tf_op jit(solution)/shard_map/ppermute | solution.py:282
  21.4 9.1 %collective-permute-start.6 = (bf16[64,2048]{1,0:T(8,128)(2,1)}, bf16[64,2048]{1,0:T(8,128)(2,1)S(1)}, u32[]{:S(2)}, u32[]{:S(2)}) collective-permute-start(bf16[64,2048]{1,0:T(8,128)(2,1)} %slice.110), channel_id=1, source_target_pairs={{0,16},{8,24},{16,0},{24,8},{32,48},{40,56},{48,32},{56,40},{64,80... | collective-permute-start | bytes 786440 | tf_op jit(solution)/shard_map/ppermute | solution.py:283
  23.3 14.7 %collective-permute-start.11 = (bf16[32,2304]{1,0:T(8,128)(2,1)}, bf16[32,2304]{1,0:T(8,128)(2,1)S(1)}, u32[]{:S(2)}, u32[]{:S(2)}) collective-permute-start(bf16[32,2304]{1,0:T(8,128)(2,1)} %slice.111), channel_id=1, source_target_pairs={{0,192},{8,200},{16,208},{24,216},{32,224},{40,232},{48,240},{56,2... | collective-permute-start | bytes 442376 | tf_op jit(solution)/shard_map/ppermute | solution.py:282
  29.6 8.4 %collective-permute-start.1 = (bf16[32,2304]{1,0:T(8,128)(2,1)}, bf16[32,2304]{1,0:T(8,128)(2,1)S(1)}, u32[]{:S(2)}, u32[]{:S(2)}) collective-permute-start(bf16[32,2304]{1,0:T(8,128)(2,1)} %slice.108), channel_id=1, source_target_pairs={{0,64},{8,72},{16,80},{24,88},{32,96},{40,104},{48,112},{56,120},{... | collective-permute-start | bytes 442376 | tf_op jit(solution)/shard_map/ppermute | solution.py:283
  32.5 12.1 %collective-permute-start.8 = (f32[4,64,384]{2,1,0:T(8,128)S(1)}, f32[4,64,384]{2,1,0:T(8,128)S(1)}, u32[]{:S(2)}, u32[]{:S(2)}) collective-permute-start(f32[4,64,384]{2,1,0:T(8,128)S(1)} %get-tuple-element.22), channel_id=1, source_target_pairs={{0,2},{1,3},{2,0},{3,1},{4,6},{5,7},{6,4},{7,5},{8,10},{9,11},{10,... | collective-permute-start | bytes 1179656 | tf_op jit(solution)/shard_map/ppermute | solution.py:319
  34.1 11.7 %collective-permute-start.9 = (f32[4,64,384]{2,1,0:T(8,128)S(1)}, f32[4,64,384]{2,1,0:T(8,128)S(1)}, u32[]{:S(2)}, u32[]{:S(2)}) collective-permute-start(f32[4,64,384]{2,1,0:T(8,128)S(1)} %get-tuple-element.23), channel_id=1, source_target_pairs={{0,6},{1,7},{2,4},{3,5},{4,2},{5,3},{6,0},{7,1},{8,14},{9,15},{10,... | collective-permute-start | bytes 1179656 | tf_op jit(solution)/shard_map/ppermute | solution.py:319
  36.2 10.3 %collective-permute-start.10 = (f32[4,64,384]{2,1,0:T(8,128)S(1)}, f32[4,64,384]{2,1,0:T(8,128)S(1)}, u32[]{:S(2)}, u32[]{:S(2)}) collective-permute-start(f32[4,64,384]{2,1,0:T(8,128)S(1)} %get-tuple-element.24), channel_id=1, source_target_pairs={{0,1},{1,0},{2,3},{3,2},{4,5},{5,4},{6,7},{7,6},{8,9},{9,8},{10,11... | collective-permute-start | bytes 1179656 | tf_op jit(solution)/shard_map/ppermute | solution.py:319
  40.0 8.5 %collective-permute-start.12 = (f32[4,64,128]{2,1,0:T(8,128)S(1)}, f32[4,64,128]{2,1,0:T(8,128)S(1)}, u32[]{:S(2)}, u32[]{:S(2)}) collective-permute-start(f32[4,64,128]{2,1,0:T(8,128)S(1)} %get-tuple-element.26), channel_id=1, source_target_pairs={{0,2},{1,3},{2,0},{3,1},{4,6},{5,7},{6,4},{7,5},{8,10},{9,11},{10,... | collective-permute-start | bytes 393224 | tf_op jit(solution)/shard_map/ppermute | solution.py:322
  42.0 6.6 %collective-permute-start.13 = (f32[4,64,128]{2,1,0:T(8,128)S(1)}, f32[4,64,128]{2,1,0:T(8,128)S(1)}, u32[]{:S(2)}, u32[]{:S(2)}) collective-permute-start(f32[4,64,128]{2,1,0:T(8,128)S(1)} %get-tuple-element.27), channel_id=1, source_target_pairs={{0,6},{1,7},{2,4},{3,5},{4,2},{5,3},{6,0},{7,1},{8,14},{9,15},{10,... | collective-permute-start | bytes 393224 | tf_op jit(solution)/shard_map/ppermute | solution.py:322
  44.6 10.4 %copy-start = (f32[4,64,384]{2,1,0:T(8,128)}, f32[4,64,384]{2,1,0:T(8,128)S(1)}, u32[]{:S(2)}) copy-start(f32[4,64,384]{2,1,0:T(8,128)S(1)} %collective-permute-done.8.refs_0_) | copy-start | bytes 1179652
  44.6 5.0 %collective-permute-start.14 = (f32[4,64,128]{2,1,0:T(8,128)S(1)}, f32[4,64,128]{2,1,0:T(8,128)S(1)}, u32[]{:S(2)}, u32[]{:S(2)}) collective-permute-start(f32[4,64,128]{2,1,0:T(8,128)S(1)} %get-tuple-element.28), channel_id=1, source_target_pairs={{0,1},{1,0},{2,3},{3,2},{4,5},{5,4},{6,7},{7,6},{8,9},{9,8},{10,11... | collective-permute-start | bytes 393224 | tf_op jit(solution)/shard_map/ppermute | solution.py:322
  45.8 9.2 %copy-start.2 = (f32[4,64,384]{2,1,0:T(8,128)}, f32[4,64,384]{2,1,0:T(8,128)S(1)}, u32[]{:S(2)}) copy-start(f32[4,64,384]{2,1,0:T(8,128)S(1)} %collective-permute-done.9.refs_1_) | copy-start | bytes 1179652
  46.5 8.5 %copy-start.4 = (f32[4,64,384]{2,1,0:T(8,128)}, f32[4,64,384]{2,1,0:T(8,128)S(1)}, u32[]{:S(2)}) copy-start(f32[4,64,384]{2,1,0:T(8,128)S(1)} %collective-permute-done.10.refs_2_) | copy-start | bytes 1179652
  48.5 6.5 %copy-start.6 = (f32[4,64,128]{2,1,0:T(8,128)}, f32[4,64,128]{2,1,0:T(8,128)S(1)}, u32[]{:S(2)}) copy-start(f32[4,64,128]{2,1,0:T(8,128)S(1)} %collective-permute-done.12.refs_3_) | copy-start | bytes 393220
  48.6 2.7 %copy-start.8 = (f32[4,64,128]{2,1,0:T(8,128)}, f32[4,64,128]{2,1,0:T(8,128)S(1)}, u32[]{:S(2)}) copy-start(f32[4,64,128]{2,1,0:T(8,128)S(1)} %collective-permute-done.13.refs_4_) | copy-start | bytes 393220
  49.6 4.5 %copy-start.10 = (f32[4,64,128]{2,1,0:T(8,128)}, f32[4,64,128]{2,1,0:T(8,128)S(1)}, u32[]{:S(2)}) copy-start(f32[4,64,128]{2,1,0:T(8,128)S(1)} %collective-permute-done.14.refs_5_) | copy-start | bytes 393220
  49.7 7.7 %collective-permute-start.15 = (f32[2,64,512]{2,1,0:T(8,128)S(1)}, f32[2,64,512]{2,1,0:T(8,128)S(1)}, u32[]{:S(2)}, u32[]{:S(2)}) collective-permute-start(f32[2,64,512]{2,1,0:T(8,128)S(1)} %maximum_add_fusion), channel_id=1, source_target_pairs={{0,6},{1,7},{2,4},{3,5},{4,2},{5,3},{6,0},{7,1},{8,14},{9,15},{10,... | collective-permute-start | bytes 786440 | tf_op jit(solution)/shard_map/ppermute | solution.py:331
  52.1 7.0 %collective-permute-start.17 = (f32[2,64,512]{2,1,0:T(8,128)S(1)}, f32[2,64,512]{2,1,0:T(8,128)S(1)}, u32[]{:S(2)}, u32[]{:S(2)}) collective-permute-start(f32[2,64,512]{2,1,0:T(8,128)S(1)} %maximum_add_fusion.1), channel_id=1, source_target_pairs={{0,1},{1,0},{2,3},{3,2},{4,5},{5,4},{6,7},{7,6},{8,9},{9,8},{10,11... | collective-permute-start | bytes 786440 | tf_op jit(solution)/shard_map/ppermute | solution.py:331
  55.0 12.9 %copy-start.11 = (f32[4,64,128]{2,1,0:T(8,128)S(1)}, f32[4,64,128]{2,1,0:T(8,128)}, u32[]{:S(2)}) copy-start(f32[4,64,128]{2,1,0:T(8,128)} %copy-done.10) | copy-start | bytes 393220
  55.0 12.9 %copy-start.9 = (f32[4,64,128]{2,1,0:T(8,128)S(1)}, f32[4,64,128]{2,1,0:T(8,128)}, u32[]{:S(2)}) copy-start(f32[4,64,128]{2,1,0:T(8,128)} %copy-done.8) | copy-start | bytes 393220
  55.0 2.3 %slice-start = ((f32[4,64,384]{2,1,0:T(8,128)}), f32[1,64,384]{2,1,0:T(8,128)S(1)}, s32[]{:S(2)}) async-start(f32[4,64,384]{2,1,0:T(8,128)} %copy-done), calls=%async_computation | async-start | bytes 196608 | tf_op jit(solution)/shard_map/slice | solution.py:328
  55.1 4.0 %slice-start.1 = ((f32[4,64,384]{2,1,0:T(8,128)}), f32[1,64,384]{2,1,0:T(8,128)S(1)}, s32[]{:S(2)}) async-start(f32[4,64,384]{2,1,0:T(8,128)} %copy-done.2), calls=%async_computation.1 | async-start | bytes 196608 | tf_op jit(solution)/shard_map/slice | solution.py:328
  55.1 4.0 %slice-start.5 = ((f32[4,64,128]{2,1,0:T(8,128)}), f32[1,64,128]{2,1,0:T(8,128)S(1)}, s32[]{:S(2)}) async-start(f32[4,64,128]{2,1,0:T(8,128)} %copy-done.8), calls=%async_computation.5 | async-start | bytes 65536 | tf_op jit(solution)/shard_map/slice | solution.py:328
  55.1 6.5 %collective-permute-start.19 = (f32[2,64,512]{2,1,0:T(8,128)S(1)}, f32[2,64,512]{2,1,0:T(8,128)S(1)}, u32[]{:S(2)}, u32[]{:S(2)}) collective-permute-start(f32[2,64,512]{2,1,0:T(8,128)S(1)} %maximum_add_fusion.2), channel_id=1, source_target_pairs={{0,2},{1,3},{2,0},{3,1},{4,6},{5,7},{6,4},{7,5},{8,10},{9,11},{10,... | collective-permute-start | bytes 786440 | tf_op jit(solution)/shard_map/ppermute | solution.py:331
  57.3 10.6 %copy-start.5 = (f32[4,64,384]{2,1,0:T(8,128)S(1)}, f32[4,64,384]{2,1,0:T(8,128)}, u32[]{:S(2)}) copy-start(f32[4,64,384]{2,1,0:T(8,128)} %copy-done.4) | copy-start | bytes 1179652
  57.4 4.2 %slice-start.2 = ((f32[4,64,384]{2,1,0:T(8,128)}), f32[1,64,384]{2,1,0:T(8,128)S(1)}, s32[]{:S(2)}) async-start(f32[4,64,384]{2,1,0:T(8,128)} %copy-done.4), calls=%async_computation.2 | async-start | bytes 196608 | tf_op jit(solution)/shard_map/slice | solution.py:328
  57.4 4.2 %slice-start.7 = ((f32[4,64,128]{2,1,0:T(8,128)}), f32[1,64,128]{2,1,0:T(8,128)S(1)}, s32[]{:S(2)}) async-start(f32[4,64,128]{2,1,0:T(8,128)} %copy-done.10), calls=%async_computation.7 | async-start | bytes 65536 | tf_op jit(solution)/shard_map/slice | solution.py:328
  57.4 5.8 %collective-permute-start.16 = (f32[1,64,512]{2,1,0:T(8,128)S(1)}, f32[1,64,512]{2,1,0:T(8,128)S(1)}, u32[]{:S(2)}, u32[]{:S(2)}) collective-permute-start(f32[1,64,512]{2,1,0:T(8,128)S(1)} %fusion.2), channel_id=1, source_target_pairs={{0,1},{1,0},{2,3},{3,2},{4,5},{5,4},{6,7},{7,6},{8,9},{9,8},{10,11... | collective-permute-start | bytes 393224 | tf_op jit(solution)/shard_map/ppermute | solution.py:333
  59.1 8.8 %copy-start.3 = (f32[4,64,384]{2,1,0:T(8,128)S(1)}, f32[4,64,384]{2,1,0:T(8,128)}, u32[]{:S(2)}) copy-start(f32[4,64,384]{2,1,0:T(8,128)} %copy-done.2) | copy-start | bytes 1179652
  59.1 8.8 %copy-start.1 = (f32[4,64,384]{2,1,0:T(8,128)S(1)}, f32[4,64,384]{2,1,0:T(8,128)}, u32[]{:S(2)}) copy-start(f32[4,64,384]{2,1,0:T(8,128)} %copy-done) | copy-start | bytes 1179652
  59.1 8.8 %copy-start.7 = (f32[4,64,128]{2,1,0:T(8,128)S(1)}, f32[4,64,128]{2,1,0:T(8,128)}, u32[]{:S(2)}) copy-start(f32[4,64,128]{2,1,0:T(8,128)} %copy-done.6) | copy-start | bytes 393220
  59.1 5.1 %collective-permute-start.18 = (f32[1,64,512]{2,1,0:T(8,128)S(1)}, f32[1,64,512]{2,1,0:T(8,128)S(1)}, u32[]{:S(2)}, u32[]{:S(2)}) collective-permute-start(f32[1,64,512]{2,1,0:T(8,128)S(1)} %fusion.1), channel_id=1, source_target_pairs={{0,2},{1,3},{2,0},{3,1},{4,6},{5,7},{6,4},{7,5},{8,10},{9,11},{10,... | collective-permute-start | bytes 393224 | tf_op jit(solution)/shard_map/ppermute | solution.py:333
  61.6 6.3 %collective-permute-start.20 = (f32[1,64,512]{2,1,0:T(8,128)S(1)}, f32[1,64,512]{2,1,0:T(8,128)S(1)}, u32[]{:S(2)}, u32[]{:S(2)}) collective-permute-start(f32[1,64,512]{2,1,0:T(8,128)S(1)} %fusion), channel_id=1, source_target_pairs={{0,6},{1,7},{2,4},{3,5},{4,2},{5,3},{6,0},{7,1},{8,14},{9,15},{10,... | collective-permute-start | bytes 393224 | tf_op jit(solution)/shard_map/ppermute | solution.py:333
  68.3 1.3 %collective-permute-start.21 = (f32[64,128]{1,0:T(8,128)S(1)}, f32[64,128]{1,0:T(8,128)S(1)}, u32[]{:S(2)}, u32[]{:S(2)}) collective-permute-start(f32[64,128]{1,0:T(8,128)S(1)} %shard_map.53), channel_id=1, source_target_pairs={{0,8},{8,0},{16,24},{24,16},{32,40},{40,32},{48,56},{56,48},{64,72... | collective-permute-start | bytes 98312 | tf_op jit(solution)/shard_map/ppermute | solution.py:289
  69.6 4.8 %collective-permute-start.22 = (f32[64,128]{1,0:T(8,128)S(1)}, f32[64,128]{1,0:T(8,128)S(1)}, u32[]{:S(2)}, u32[]{:S(2)}) collective-permute-start(f32[64,128]{1,0:T(8,128)S(1)} %add.59.refs_0_), channel_id=1, source_target_pairs={{0,16},{8,24},{16,0},{24,8},{32,48},{40,56},{48,32},{56,40},{64,80... | collective-permute-start | bytes 98312 | tf_op jit(solution)/shard_map/ppermute | solution.py:289
  71.7 5.5 %collective-permute-start.23 = (f32[64,128]{1,0:T(8,128)S(1)}, f32[64,128]{1,0:T(8,128)S(1)}, u32[]{:S(2)}, u32[]{:S(2)}) collective-permute-start(f32[64,128]{1,0:T(8,128)S(1)} %add.59.refs_0_), channel_id=1, source_target_pairs={{0,32},{8,40},{16,48},{24,56},{32,0},{40,8},{48,16},{56,24},{64,96... | collective-permute-start | bytes 98312 | tf_op jit(solution)/shard_map/ppermute | solution.py:289
  73.1 5.1 %collective-permute-start.24 = (f32[64,128]{1,0:T(8,128)S(1)}, f32[64,128]{1,0:T(8,128)S(1)}, u32[]{:S(2)}, u32[]{:S(2)}) collective-permute-start(f32[64,128]{1,0:T(8,128)S(1)} %add.59.refs_0_), channel_id=1, source_target_pairs={{0,48},{8,56},{16,32},{24,40},{32,16},{40,24},{48,0},{56,8},{64,11... | collective-permute-start | bytes 98312 | tf_op jit(solution)/shard_map/ppermute | solution.py:289
  78.5 6.0 %collective-permute-start.26 = (f32[136,128]{1,0:T(8,128)S(1)}, f32[136,128]{1,0:T(8,128)S(1)}, u32[]{:S(2)}, u32[]{:S(2)}) collective-permute-start(f32[136,128]{1,0:T(8,128)S(1)} %shard_map.54), channel_id=1, source_target_pairs={{0,4},{1,5},{2,6},{3,7},{4,0},{5,1},{6,2},{7,3},{8,12},{9,13},{10,... | collective-permute-start | bytes 208904 | tf_op jit(solution)/shard_map/ppermute | solution.py:289
  78.6 6.4 %collective-permute-start.27 = (f32[136,128]{1,0:T(8,128)S(1)}, f32[136,128]{1,0:T(8,128)S(1)}, u32[]{:S(2)}, u32[]{:S(2)}) collective-permute-start(f32[136,128]{1,0:T(8,128)S(1)} %shard_map.54), channel_id=1, source_target_pairs={{0,6},{1,7},{2,4},{3,5},{4,2},{5,3},{6,0},{7,1},{8,14},{9,15},{10,... | collective-permute-start | bytes 208904 | tf_op jit(solution)/shard_map/ppermute | solution.py:289
  80.5 4.5 %collective-permute-start.25 = (f32[136,128]{1,0:T(8,128)S(1)}, f32[136,128]{1,0:T(8,128)S(1)}, u32[]{:S(2)}, u32[]{:S(2)}) collective-permute-start(f32[136,128]{1,0:T(8,128)S(1)} %shard_map.54), channel_id=1, source_target_pairs={{0,2},{1,3},{2,0},{3,1},{4,6},{5,7},{6,4},{7,5},{8,10},{9,11},{10,... | collective-permute-start | bytes 208904 | tf_op jit(solution)/shard_map/ppermute | solution.py:289
  85.1 4.8 %collective-permute-start.28 = (f32[136,128]{1,0:T(8,128)S(1)}, f32[136,128]{1,0:T(8,128)S(1)}, u32[]{:S(2)}, u32[]{:S(2)}) collective-permute-start(f32[136,128]{1,0:T(8,128)S(1)} %select_select_fusion.1), channel_id=1, source_target_pairs={{0,1},{1,0},{2,3},{3,2},{4,5},{5,4},{6,7},{7,6},{8,9},{9,8},{10,11... | collective-permute-start | bytes 208904 | tf_op jit(solution)/shard_map/ppermute | solution.py:289
  90.0 4.9 %collective-permute-start.29 = (f32[72,128]{1,0:T(8,128)S(1)}, f32[72,128]{1,0:T(8,128)S(1)}, u32[]{:S(2)}, u32[]{:S(2)}) collective-permute-start(f32[72,128]{1,0:T(8,128)S(1)} %slice.115), channel_id=1, source_target_pairs={{0,64},{8,72},{16,80},{24,88},{32,96},{40,104},{48,112},{56,120},{... | collective-permute-start | bytes 110600 | tf_op jit(solution)/shard_map/ppermute | solution.py:289
  95.0 6.1 %collective-permute-start.30 = (f32[72,128]{1,0:T(8,128)S(1)}, f32[72,128]{1,0:T(8,128)S(1)}, u32[]{:S(2)}, u32[]{:S(2)}) collective-permute-start(f32[72,128]{1,0:T(8,128)S(1)} %slice_add_fusion.3.refs_0_), channel_id=1, source_target_pairs={{0,192},{8,200},{16,208},{24,216},{32,224},{40,232},{48,240},{56,2... | collective-permute-start | bytes 110600 | tf_op jit(solution)/shard_map/ppermute | solution.py:289
  (4 other events, 5.3 us)

commit v2 on v1

--- a/solution.py
+++ b/solution.py
@@ -113,16 +113,27 @@
             out[k] = joined[k * height : (k + 1) * height]
 
 
+def fold_body(keep, near, far, send, later, last):
+    edge = near.shape[2]
+    for out, begin in ((send, 2), (later, 1), (last, 0)):
+        span = slice(begin, begin + out.shape[0])
+        out[:, :, :edge] = keep[span, :, :edge] + near[span]
+        out[:, :, edge:] = keep[span, :, edge:] + far[span]
+
+
+def fold(keep, near, far):
+    shapes = [jax.ShapeDtypeStruct((count,) + keep.shape[1:], jnp.float32) for count in (2, 1, 1)]
+    return kernel_call(fold_body, shapes)(keep, near, far)
+
+
 def band_body(*refs):
-    near, far, whole = refs[:3], refs[3:6], refs[6:15]
-    pieces, own, out = refs[15:19], refs[19], refs[20]
+    whole, pieces, own, out = refs[:9], refs[9:13], refs[13], refs[14]
     height = own.shape[0]
     edge = 2 * NEAR_BLOCKS * height
     totals = []
     for r in range(3):
-        rest = tree_sum([ref[0] for ref in whole[3 * r : 3 * r + 2]]) + whole[3 * r + 2][0]
-        front = near[r][0] + rest[:, :edge]
-        back = far[r][0] + rest[:, edge:]
+        rest = (whole[3 * r][0] + whole[3 * r + 1][0]) + whole[3 * r + 2][0]
+        front, back = rest[:, :edge], rest[:, edge:]
         for m in range(2):
             third = slice((4 + m) * height, (5 + m) * height)
             totals.append(
@@ -275,12 +286,27 @@
     return [(i, i ^ shift) for i in range(SITE_PARTS)]
 
 
+def half_body(whole, out):
+    out[...] = whole[...]
+
+
+def half_of(block, part):
+    shape = (block.shape[0] // 2, block.shape[1])
+    return pl.pallas_call(
+        half_body,
+        grid=(1,),
+        out_shape=jax.ShapeDtypeStruct(shape, block.dtype),
+        in_specs=[pl.BlockSpec(shape, lambda i: (part, 0))],
+        out_specs=pl.BlockSpec(shape, lambda i: (0, 0)),
+        compiler_params=pltpu.CompilerParams(vmem_limit_bytes=VMEM_LIMIT),
+    )(block)
+
+
 def gather_line(block, near, other):
-    half = block.shape[0] // 2
     one = lax.ppermute(block, "samp", samp_perm(near))
     three = lax.ppermute(block, "samp", samp_perm(other))
-    top = lax.ppermute(one[:half], "samp", samp_perm(other))
-    bottom = lax.ppermute(three[half:], "samp", samp_perm(near))
+    top = lax.ppermute(half_of(one, 0), "samp", samp_perm(other))
+    bottom = lax.ppermute(half_of(three, 1), "samp", samp_perm(near))
     return [block, one, three, top, bottom]
 
 
@@ -323,15 +349,11 @@
     far_kept, came_near, _ = lax.optimization_barrier((far_cols[1], came_near, send_far))
     keep = pairs(0, ("near", "far"), near_cols + [far_cols[0], far_kept], 10000000000)
     keep, came_far = lax.optimization_barrier((keep, came_far))
-
-    def arrived(r, at):
-        return jnp.concatenate([came_near[r][at], came_far[r][at]], axis=2)
-
-    send = [keep[r][2:] + arrived(r, slice(2, 4)) for r in range(3)]
-    came2 = [lax.ppermute(send[r], "site", site_perm(ROUTES[r][1])) for r in range(3)]
-    send = [(keep[r][1:2] + came2[r][1:2]) + arrived(r, slice(1, 2)) for r in range(3)]
+    folded = [fold(keep[r], came_near[r], came_far[r]) for r in range(3)]
+    came2 = [lax.ppermute(folded[r][0], "site", site_perm(ROUTES[r][1])) for r in range(3)]
+    send = [folded[r][1] + came2[r][1:] for r in range(3)]
     came3 = [lax.ppermute(send[r], "site", site_perm(ROUTES[r][2])) for r in range(3)]
-    terms = came_near + came_far + [t for r in range(3) for t in (keep[r], came2[r], came3[r])]
+    terms = [t for r in range(3) for t in (folded[r][2], came2[r], came3[r])]
     part = band_call(terms, pieces, factor, jax.ShapeDtypeStruct((height, columns), f32))
     part = tree_sum(spread(part, "samp", [1]))
     packed = columns // 2 + PANEL

time: 107 us -> 108 us (level)
  starting transfers between devices: 51.3 us -> 56.9 us
  waiting for transfers between devices: 36.6 us -> 31.3 us
  Pallas kernels: 12.4 us -> 16.7 us
  local copies, waits for them, and re-layouts: 3.88 us -> 0.01 us
    ppermute x10, starting transfers between devices: 12.6 us -> 19.2 us  [spread(): return [part] + [lax.ppermute(part, axis, perm(k)) for k in shifts]]
    ppermute x10, waiting for transfers between devices: 19.5 us -> 14.8 us  [spread(): return [part] + [lax.ppermute(part, axis, perm(k)) for k in shifts]]
    slice x24 -> x0, local copies, waits for them, and re-layouts: 3.82 us -> none  [the longest x20 1.72 us: arrived(): return jnp.concatenate([came_near[r][at], came_far[r][at]], axis=2)]
    pallas_call x5 -> x8, Pallas kernels: 12.1 us -> 14.2 us  [call(): pl.pallas_call(body, out_shape=out_shape, in_specs=in_specs, out_specs=ja...]
    pallas_call x0 -> x4, Pallas kernels: none -> 1.38 us  [half_of(): pl.pallas_call(half_body, grid=(1,), out_shape=jax.ShapeDtypeStruct(shape...]
  transfers between devices with their start and end apart: 31 -> 31, of which waited for: 19 -> 17; matrix products, arithmetic and copies ran while one was open for 2% -> 0% of each run, Pallas kernels for 6% -> 9%
where the time goes in v2:
time: 108 us; the launch traced here: 107 us
  starting transfers between devices  56.9 us (53%)
  waiting for transfers between devices  31.3 us (29%)
  Pallas kernels  16.7 us (15%)
  other arithmetic  1.53 us (1%)
    ppermute x10, starting transfers between devices, spread(): return [part] + [lax.ppermute(part, axis, perm(k)) for k in shifts]  19.2 us
    ppermute x10, waiting for transfers between devices, spread(): return [part] + [lax.ppermute(part, axis, perm(k)) for k in shifts]  14.8 us
    pallas_call x8, Pallas kernels, call(): pl.pallas_call(body, out_shape=out_shape, in_specs=in_specs, out_specs=ja...  14.2 us
    ppermute x2, starting transfers between devices, gather_line(): top = lax.ppermute(half_of(one, 0), 'samp', samp_perm(other))  8.71 us
    ppermute x2, starting transfers between devices, gather_line(): three = lax.ppermute(block, 'samp', samp_perm(other))  5.76 us
    ppermute x3, starting transfers between devices, local(): lax.ppermute(send_far[r], 'site', site_perm(ROUTES[r][0]))  5.26 us
    ppermute x2, starting transfers between devices, gather_line(): one = lax.ppermute(block, 'samp', samp_perm(near))  5.02 us
    ppermute x2, waiting for transfers between devices, gather_line(): one = lax.ppermute(block, 'samp', samp_perm(near))  4.96 us
  transfers between devices with their start and end apart: 31, of which 17 were waited for; matrix products, arithmetic and copies ran while one was open for 0% of the time, Pallas kernels for 9%

profile of v2, /device:TPU:32, one launch (start us, length us, event | category | flops | bytes accessed | tf_op | source)
XLA Modules:
  0.0 107.3 jit_solution(12787302208209909837)
XLA Ops:
  0.6 1.2 %compare_select_fusion.refs_5_ = bf16[64,2048]{1,0:T(8,128)(2,1)S(1)} fusion(bf16[64,2048]{1,0:T(8,128)(2,1)} %param.3, s32[64,2048]{1,0:T(8,128)} %param.4), kind=kLoop, calls=%fused_computation.1 | loop fusion | flops 262144 | bytes 1048576 | tf_op jit(solution)/shard_map/jit(_where)/select_n | solution.py:322
  2.0 1.5 %collective-permute-done = bf16[64,2048]{1,0:T(8,128)(2,1)S(1)} collective-permute-done((bf16[64,2048]{1,0:T(8,128)(2,1)S(1)}, bf16[64,2048]{1,0:T(8,128)(2,1)S(1)}, u32[]{:S(2)}, u32[]{:S(2)}) %collective-permute-start) | collective-permute-done | bytes 262176 | tf_op jit(solution)/shard_map/ppermute | solution.py:326
  3.5 1.7 %collective-permute-start.1 = (bf16[128,2048]{1,0:T(8,128)(2,1)S(1)}, bf16[128,2048]{1,0:T(8,128)(2,1)S(1)}, u32[]{:S(2)}, u32[]{:S(2)}) collective-permute-start(bf16[128,2048]{1,0:T(8,128)(2,1)S(1)} %pad_maximum_fusion.refs_0_), channel_id=1, source_target_pairs={{0,16},{8,24},{16,0},{24,8},{32,48},{40,56},{48,32},{56,40},{64,80... | collective-permute-start | bytes 1572872 | tf_op jit(solution)/shard_map/ppermute | solution.py:306
  5.2 2.2 %collective-permute-start.2 = (bf16[128,2048]{1,0:T(8,128)(2,1)S(1)}, bf16[128,2048]{1,0:T(8,128)(2,1)S(1)}, u32[]{:S(2)}, u32[]{:S(2)}) collective-permute-start(bf16[128,2048]{1,0:T(8,128)(2,1)S(1)} %pad_maximum_fusion.refs_0_), channel_id=1, source_target_pairs={{0,48},{8,56},{16,32},{24,40},{32,16},{40,24},{48,0},{56,8},{64,11... | collective-permute-start | bytes 1572872 | tf_op jit(solution)/shard_map/ppermute | solution.py:307
  7.4 3.4 %collective-permute-start.5 = (bf16[64,2304]{1,0:T(8,128)(2,1)S(1)}, bf16[64,2304]{1,0:T(8,128)(2,1)S(1)}, u32[]{:S(2)}, u32[]{:S(2)}) collective-permute-start(bf16[64,2304]{1,0:T(8,128)(2,1)S(1)} %pad_maximum_fusion.1), channel_id=1, source_target_pairs={{0,64},{8,72},{16,80},{24,88},{32,96},{40,104},{48,112},{56,120},{... | collective-permute-start | bytes 884744 | tf_op jit(solution)/shard_map/ppermute | solution.py:306
  10.7 3.6 %collective-permute-start.6 = (bf16[64,2304]{1,0:T(8,128)(2,1)S(1)}, bf16[64,2304]{1,0:T(8,128)(2,1)S(1)}, u32[]{:S(2)}, u32[]{:S(2)}) collective-permute-start(bf16[64,2304]{1,0:T(8,128)(2,1)S(1)} %pad_maximum_fusion.1), channel_id=1, source_target_pairs={{0,192},{8,200},{16,208},{24,216},{32,224},{40,232},{48,240},{56,2... | collective-permute-start | bytes 884744 | tf_op jit(solution)/shard_map/ppermute | solution.py:307
  14.3 3.2 %collective-permute-done.1.whole.refs_1_ = bf16[128,2048]{1,0:T(8,128)(2,1)S(1)} collective-permute-done((bf16[128,2048]{1,0:T(8,128)(2,1)S(1)}, bf16[128,2048]{1,0:T(8,128)(2,1)S(1)}, u32[]{:S(2)}, u32[]{:S(2)}) %collective-permute-start.1) | collective-permute-done | bytes 524320 | tf_op jit(solution)/shard_map/ppermute | solution.py:306
  17.6 3.1 %collective-permute-start.3 = (bf16[64,2048]{1,0:T(8,128)(2,1)S(1)}, bf16[64,2048]{1,0:T(8,128)(2,1)S(1)}, u32[]{:S(2)}, u32[]{:S(2)}) collective-permute-start(bf16[64,2048]{1,0:T(8,128)(2,1)S(1)} %shard_map.50), channel_id=1, source_target_pairs={{0,48},{8,56},{16,32},{24,40},{32,16},{40,24},{48,0},{56,8},{64,11... | collective-permute-start | bytes 786440 | tf_op jit(solution)/shard_map/ppermute | solution.py:308
  20.9 1.7 %collective-permute-done.5.whole.refs_6_.refs_9_ = bf16[64,2304]{1,0:T(8,128)(2,1)S(1)} collective-permute-done((bf16[64,2304]{1,0:T(8,128)(2,1)S(1)}, bf16[64,2304]{1,0:T(8,128)(2,1)S(1)}, u32[]{:S(2)}, u32[]{:S(2)}) %collective-permute-start.5) | collective-permute-done | bytes 294944 | tf_op jit(solution)/shard_map/ppermute | solution.py:306
  22.7 0.7 shard_map.52
  23.3 5.6 %collective-permute-start.7 = (bf16[32,2304]{1,0:T(8,128)(2,1)}, bf16[32,2304]{1,0:T(8,128)(2,1)}, u32[]{:S(2)}, u32[]{:S(2)}) collective-permute-start(bf16[32,2304]{1,0:T(8,128)(2,1)} %shard_map.52), channel_id=1, source_target_pairs={{0,192},{8,200},{16,208},{24,216},{32,224},{40,232},{48,240},{56,2... | collective-permute-start | bytes 442376 | tf_op jit(solution)/shard_map/ppermute | solution.py:308
  29.6 0.9 collective-permute-start.8
  30.5 2.0 %shard_map.53 = (f32[4,64,384]{2,1,0:T(8,128)S(1)}, f32[4,64,384]{2,1,0:T(8,128)S(1)}, f32[4,64,384]{2,1,0:T(8,128)S(1)}) custom-call(s32[1]{0:T(128)} %bitcast.which, bf16[128,2048]{1,0:T(8,128)(2,1)S(1)} %pad_maximum_fusion.refs_0_, bf16[128,2048]{1,0:T(8,128)(2,1)S(1)} %collective-permute-done.1.whole.refs_1_, ...), custom_call_target="tpu_custom_call" | custom-call | flops 1000000 | bytes 100000 | tf_op jit(solution)/shard_map/pallas_call | solution.py:51
  32.5 2.8 %collective-permute-start.10 = (f32[4,64,384]{2,1,0:T(8,128)S(1)}, f32[4,64,384]{2,1,0:T(8,128)S(1)}, u32[]{:S(2)}, u32[]{:S(2)}) collective-permute-start(f32[4,64,384]{2,1,0:T(8,128)S(1)} %get-tuple-element.32), channel_id=1, source_target_pairs={{0,6},{1,7},{2,4},{3,5},{4,2},{5,3},{6,0},{7,1},{8,14},{9,15},{10,... | collective-permute-start | bytes 1179656 | tf_op jit(solution)/shard_map/ppermute | solution.py:345
  35.3 1.9 %collective-permute-start.11 = (f32[4,64,384]{2,1,0:T(8,128)S(1)}, f32[4,64,384]{2,1,0:T(8,128)S(1)}, u32[]{:S(2)}, u32[]{:S(2)}) collective-permute-start(f32[4,64,384]{2,1,0:T(8,128)S(1)} %get-tuple-element.33), channel_id=1, source_target_pairs={{0,1},{1,0},{2,3},{3,2},{4,5},{5,4},{6,7},{7,6},{8,9},{9,8},{10,11... | collective-permute-start | bytes 1179656 | tf_op jit(solution)/shard_map/ppermute | solution.py:345
  37.4 0.7 collective-permute-done.8.refs_6_.refs_9_.refs_12_
  38.2 2.9 %shard_map.55 = (f32[4,64,128]{2,1,0:T(8,128)S(1)}, f32[4,64,128]{2,1,0:T(8,128)S(1)}, f32[4,64,128]{2,1,0:T(8,128)S(1)}) custom-call(s32[1]{0:T(128)} %bitcast.which, bf16[128,2048]{1,0:T(8,128)(2,1)S(1)} %pad_maximum_fusion.refs_0_, bf16[128,2048]{1,0:T(8,128)(2,1)S(1)} %collective-permute-done.1.whole.refs_1_, ...), custom_call_target="tpu_custom_call" | custom-call | flops 10000000000 | bytes 100000 | tf_op jit(solution)/shard_map/pallas_call | solution.py:51
  41.1 2.4 %collective-permute-start.12 = (f32[4,64,128]{2,1,0:T(8,128)S(1)}, f32[4,64,128]{2,1,0:T(8,128)S(1)}, u32[]{:S(2)}, u32[]{:S(2)}) collective-permute-start(f32[4,64,128]{2,1,0:T(8,128)S(1)} %get-tuple-element.35), channel_id=1, source_target_pairs={{0,2},{1,3},{2,0},{3,1},{4,6},{5,7},{6,4},{7,5},{8,10},{9,11},{10,... | collective-permute-start | bytes 393224 | tf_op jit(solution)/shard_map/ppermute | solution.py:348
  43.6 2.1 %collective-permute-start.13 = (f32[4,64,128]{2,1,0:T(8,128)S(1)}, f32[4,64,128]{2,1,0:T(8,128)S(1)}, u32[]{:S(2)}, u32[]{:S(2)}) collective-permute-start(f32[4,64,128]{2,1,0:T(8,128)S(1)} %get-tuple-element.36), channel_id=1, source_target_pairs={{0,6},{1,7},{2,4},{3,5},{4,2},{5,3},{6,0},{7,1},{8,14},{9,15},{10,... | collective-permute-start | bytes 393224 | tf_op jit(solution)/shard_map/ppermute | solution.py:348
  45.7 0.7 collective-permute-start.14
  46.4 1.0 collective-permute-done.9.near
  47.4 3.0 %shard_map.56 = (f32[4,64,512]{2,1,0:T(8,128)S(1)}, f32[4,64,512]{2,1,0:T(8,128)S(1)}, f32[4,64,512]{2,1,0:T(8,128)S(1)}) custom-call(s32[1]{0:T(128)} %bitcast.which, bf16[128,2048]{1,0:T(8,128)(2,1)S(1)} %pad_maximum_fusion.refs_0_, bf16[128,2048]{1,0:T(8,128)(2,1)S(1)} %collective-permute-done.1.whole.refs_1_, ...), custom_call_target="tpu_custom_call" | custom-call | flops 10000000000 | bytes 100000 | tf_op jit(solution)/shard_map/pallas_call | solution.py:51
  50.4 0.7 collective-permute-done.14.far
  52.3 2.3 %collective-permute-start.15 = (f32[2,64,512]{2,1,0:T(8,128)S(1)}, f32[2,64,512]{2,1,0:T(8,128)S(1)}, u32[]{:S(2)}, u32[]{:S(2)}) collective-permute-start(f32[2,64,512]{2,1,0:T(8,128)S(1)} %get-tuple-element.46), channel_id=1, source_target_pairs={{0,6},{1,7},{2,4},{3,5},{4,2},{5,3},{6,0},{7,1},{8,14},{9,15},{10,... | collective-permute-start | bytes 786440 | tf_op jit(solution)/shard_map/ppermute | solution.py:353
  54.7 3.7 %collective-permute-done.19.refs_7_ = f32[2,64,512]{2,1,0:T(8,128)S(1)} collective-permute-done((f32[2,64,512]{2,1,0:T(8,128)S(1)}, f32[2,64,512]{2,1,0:T(8,128)S(1)}, u32[]{:S(2)}, u32[]{:S(2)}) %collective-permute-start.19) | collective-permute-done | bytes 262176 | tf_op jit(solution)/shard_map/ppermute | solution.py:353
  58.4 1.1 %collective-permute-start.20 = (f32[1,64,512]{2,1,0:T(8,128)S(1)}, f32[1,64,512]{2,1,0:T(8,128)S(1)}, u32[]{:S(2)}, u32[]{:S(2)}) collective-permute-start(f32[1,64,512]{2,1,0:T(8,128)S(1)} %slice_add_fusion), channel_id=1, source_target_pairs={{0,6},{1,7},{2,4},{3,5},{4,2},{5,3},{6,0},{7,1},{8,14},{9,15},{10,... | collective-permute-start | bytes 393224 | tf_op jit(solution)/shard_map/ppermute | solution.py:355
  59.6 1.2 %collective-permute-start.18 = (f32[1,64,512]{2,1,0:T(8,128)S(1)}, f32[1,64,512]{2,1,0:T(8,128)S(1)}, u32[]{:S(2)}, u32[]{:S(2)}) collective-permute-start(f32[1,64,512]{2,1,0:T(8,128)S(1)} %slice_add_fusion.1), channel_id=1, source_target_pairs={{0,2},{1,3},{2,0},{3,1},{4,6},{5,7},{6,4},{7,5},{8,10},{9,11},{10,... | collective-permute-start | bytes 393224 | tf_op jit(solution)/shard_map/ppermute | solution.py:355
  60.8 1.2 %collective-permute-start.16 = (f32[1,64,512]{2,1,0:T(8,128)S(1)}, f32[1,64,512]{2,1,0:T(8,128)S(1)}, u32[]{:S(2)}, u32[]{:S(2)}) collective-permute-start(f32[1,64,512]{2,1,0:T(8,128)S(1)} %slice_add_fusion.2), channel_id=1, source_target_pairs={{0,1},{1,0},{2,3},{3,2},{4,5},{5,4},{6,7},{7,6},{8,9},{9,8},{10,11... | collective-permute-start | bytes 393224 | tf_op jit(solution)/shard_map/ppermute | solution.py:355
  62.0 2.7 %collective-permute-done.20.refs_8_ = f32[1,64,512]{2,1,0:T(8,128)S(1)} collective-permute-done((f32[1,64,512]{2,1,0:T(8,128)S(1)}, f32[1,64,512]{2,1,0:T(8,128)S(1)}, u32[]{:S(2)}, u32[]{:S(2)}) %collective-permute-start.20) | collective-permute-done | bytes 131104 | tf_op jit(solution)/shard_map/ppermute | solution.py:355
  64.7 1.1 %collective-permute-done.16.refs_2_ = f32[1,64,512]{2,1,0:T(8,128)S(1)} collective-permute-done((f32[1,64,512]{2,1,0:T(8,128)S(1)}, f32[1,64,512]{2,1,0:T(8,128)S(1)}, u32[]{:S(2)}, u32[]{:S(2)}) %collective-permute-start.16) | collective-permute-done | bytes 131104 | tf_op jit(solution)/shard_map/ppermute | solution.py:355
  65.8 1.1 %shard_map.60 = f32[64,128]{1,0:T(8,128)S(1)} custom-call(f32[1,64,512]{2,1,0:T(8,128)S(1)} %get-tuple-element.45.refs_0_, f32[2,64,512]{2,1,0:T(8,128)S(1)} %collective-permute-done.15.refs_1_, f32[1,64,512]{2,1,0:T(8,128)S(1)} %collective-permute-done.16.refs_2_, f32[1,64,512]{2,1,0:T(8,128)S(1)} %get-tuple-element.51.refs_3_, ...), custom_call_target="tpu_custom_call" | custom-call | tf_op jit(solution)/shard_map/pallas_call | solution.py:163
  67.0 1.2 %collective-permute-done.21 = f32[64,128]{1,0:T(8,128)S(1)} collective-permute-done((f32[64,128]{1,0:T(8,128)S(1)}, f32[64,128]{1,0:T(8,128)S(1)}, u32[]{:S(2)}, u32[]{:S(2)}) %collective-permute-start.21) | collective-permute-done | bytes 32800 | tf_op jit(solution)/shard_map/ppermute | solution.py:315
  68.5 2.3 %collective-permute-start.23 = (f32[64,128]{1,0:T(8,128)S(1)}, f32[64,128]{1,0:T(8,128)S(1)}, u32[]{:S(2)}, u32[]{:S(2)}) collective-permute-start(f32[64,128]{1,0:T(8,128)S(1)} %add.35.refs_0_), channel_id=1, source_target_pairs={{0,32},{8,40},{16,48},{24,56},{32,0},{40,8},{48,16},{56,24},{64,96... | collective-permute-start | bytes 98312 | tf_op jit(solution)/shard_map/ppermute | solution.py:315
  70.7 2.2 %collective-permute-start.24 = (f32[64,128]{1,0:T(8,128)S(1)}, f32[64,128]{1,0:T(8,128)S(1)}, u32[]{:S(2)}, u32[]{:S(2)}) collective-permute-start(f32[64,128]{1,0:T(8,128)S(1)} %add.35.refs_0_), channel_id=1, source_target_pairs={{0,48},{8,56},{16,32},{24,40},{32,16},{40,24},{48,0},{56,8},{64,11... | collective-permute-start | bytes 98312 | tf_op jit(solution)/shard_map/ppermute | solution.py:315
  72.9 1.0 collective-permute-done.23.refs_2_
  73.9 2.0 %collective-permute-done.24.refs_3_ = f32[64,128]{1,0:T(8,128)S(1)} collective-permute-done((f32[64,128]{1,0:T(8,128)S(1)}, f32[64,128]{1,0:T(8,128)S(1)}, u32[]{:S(2)}, u32[]{:S(2)}) %collective-permute-start.24) | collective-permute-done | bytes 32800 | tf_op jit(solution)/shard_map/ppermute | solution.py:315
  76.2 1.2 %collective-permute-start.25 = (f32[136,128]{1,0:T(8,128)S(1)}, f32[136,128]{1,0:T(8,128)S(1)}, u32[]{:S(2)}, u32[]{:S(2)}) collective-permute-start(f32[136,128]{1,0:T(8,128)S(1)} %shard_map.61), channel_id=1, source_target_pairs={{0,2},{1,3},{2,0},{3,1},{4,6},{5,7},{6,4},{7,5},{8,10},{9,11},{10,... | collective-permute-start | bytes 208904 | tf_op jit(solution)/shard_map/ppermute | solution.py:315
  77.4 2.1 %collective-permute-start.26 = (f32[136,128]{1,0:T(8,128)S(1)}, f32[136,128]{1,0:T(8,128)S(1)}, u32[]{:S(2)}, u32[]{:S(2)}) collective-permute-start(f32[136,128]{1,0:T(8,128)S(1)} %shard_map.61), channel_id=1, source_target_pairs={{0,4},{1,5},{2,6},{3,7},{4,0},{5,1},{6,2},{7,3},{8,12},{9,13},{10,... | collective-permute-start | bytes 208904 | tf_op jit(solution)/shard_map/ppermute | solution.py:315
  79.5 1.5 %collective-permute-start.27 = (f32[136,128]{1,0:T(8,128)S(1)}, f32[136,128]{1,0:T(8,128)S(1)}, u32[]{:S(2)}, u32[]{:S(2)}) collective-permute-start(f32[136,128]{1,0:T(8,128)S(1)} %shard_map.61), channel_id=1, source_target_pairs={{0,6},{1,7},{2,4},{3,5},{4,2},{5,3},{6,0},{7,1},{8,14},{9,15},{10,... | collective-permute-start | bytes 208904 | tf_op jit(solution)/shard_map/ppermute | solution.py:315
  81.0 2.2 %collective-permute-done.26 = f32[136,128]{1,0:T(8,128)S(1)} collective-permute-done((f32[136,128]{1,0:T(8,128)S(1)}, f32[136,128]{1,0:T(8,128)S(1)}, u32[]{:S(2)}, u32[]{:S(2)}) %collective-permute-start.26) | collective-permute-done | bytes 69664 | tf_op jit(solution)/shard_map/ppermute | solution.py:315
  83.2 1.8 %collective-permute-done.27 = f32[136,128]{1,0:T(8,128)S(1)} collective-permute-done((f32[136,128]{1,0:T(8,128)S(1)}, f32[136,128]{1,0:T(8,128)S(1)}, u32[]{:S(2)}, u32[]{:S(2)}) %collective-permute-start.27) | collective-permute-done | bytes 69664 | tf_op jit(solution)/shard_map/ppermute | solution.py:315
  85.1 1.8 %collective-permute-start.28 = (f32[136,128]{1,0:T(8,128)S(1)}, f32[136,128]{1,0:T(8,128)S(1)}, u32[]{:S(2)}, u32[]{:S(2)}) collective-permute-start(f32[136,128]{1,0:T(8,128)S(1)} %select_select_fusion.1), channel_id=1, source_target_pairs={{0,1},{1,0},{2,3},{3,2},{4,5},{5,4},{6,7},{7,6},{8,9},{9,8},{10,11... | collective-permute-start | bytes 208904 | tf_op jit(solution)/shard_map/ppermute | solution.py:315
  87.0 2.8 %collective-permute-done.28 = f32[136,128]{1,0:T(8,128)S(1)} collective-permute-done((f32[136,128]{1,0:T(8,128)S(1)}, f32[136,128]{1,0:T(8,128)S(1)}, u32[]{:S(2)}, u32[]{:S(2)}) %collective-permute-start.28) | collective-permute-done | bytes 69664 | tf_op jit(solution)/shard_map/ppermute | solution.py:315
  89.8 3.2 %collective-permute-start.29 = (f32[72,128]{1,0:T(8,128)S(1)}, f32[72,128]{1,0:T(8,128)S(1)}, u32[]{:S(2)}, u32[]{:S(2)}) collective-permute-start(f32[72,128]{1,0:T(8,128)S(1)} %slice.23), channel_id=1, source_target_pairs={{0,64},{8,72},{16,80},{24,88},{32,96},{40,104},{48,112},{56,120},{... | collective-permute-start | bytes 110600 | tf_op jit(solution)/shard_map/ppermute | solution.py:315
  93.0 1.9 %collective-permute-done.29 = f32[72,128]{1,0:T(8,128)S(1)} collective-permute-done((f32[72,128]{1,0:T(8,128)S(1)}, f32[72,128]{1,0:T(8,128)S(1)}, u32[]{:S(2)}, u32[]{:S(2)}) %collective-permute-start.29) | collective-permute-done | bytes 36896 | tf_op jit(solution)/shard_map/ppermute | solution.py:315
  95.0 4.5 %collective-permute-start.30 = (f32[72,128]{1,0:T(8,128)S(1)}, f32[72,128]{1,0:T(8,128)S(1)}, u32[]{:S(2)}, u32[]{:S(2)}) collective-permute-start(f32[72,128]{1,0:T(8,128)S(1)} %slice_add_fusion.3.refs_0_), channel_id=1, source_target_pairs={{0,192},{8,200},{16,208},{24,216},{32,224},{40,232},{48,240},{56,2... | collective-permute-start | bytes 110600 | tf_op jit(solution)/shard_map/ppermute | solution.py:315
  99.5 1.9 %collective-permute-done.30.refs_1_ = f32[72,128]{1,0:T(8,128)S(1)} collective-permute-done((f32[72,128]{1,0:T(8,128)S(1)}, f32[72,128]{1,0:T(8,128)S(1)}, u32[]{:S(2)}, u32[]{:S(2)}) %collective-permute-start.30) | collective-permute-done | bytes 36896 | tf_op jit(solution)/shard_map/ppermute | solution.py:315
  101.5 5.8 %shard_map.62 = (f32[64,128]{1,0:T(8,128)}, f32[128,128]{1,0:T(8,128)}) custom-call(f32[72,128]{1,0:T(8,128)S(1)} %slice_add_fusion.3.refs_0_, f32[72,128]{1,0:T(8,128)S(1)} %collective-permute-done.30.refs_1_, f32[64,128]{1,0:T(8,128)S(1)} %slice.24.refs_2_), custom_call_target="tpu_custom_call" | custom-call | tf_op jit(solution)/shard_map/pallas_call | solution.py:51
  (43 shorter events, 3.5 us)
Async XLA Ops:
  0.6 1.3 %copy-start = (f32[64,128]{1,0:T(8,128)S(1)}, f32[64,128]{1,0:T(8,128)}, u32[]{:S(2)}) copy-start(f32[64,128]{1,0:T(8,128)} %refs_13_.1) | copy-start | bytes 98308
  1.8 1.6 %collective-permute-start = (bf16[64,2048]{1,0:T(8,128)(2,1)S(1)}, bf16[64,2048]{1,0:T(8,128)(2,1)S(1)}, u32[]{:S(2)}, u32[]{:S(2)}) collective-permute-start(bf16[64,2048]{1,0:T(8,128)(2,1)S(1)} %compare_select_fusion.refs_5_), channel_id=1, source_target_pairs={{0,8},{8,0},{16,24},{24,16},{32,40},{40,32},{48,56},{56,48},{64,72... | collective-permute-start | bytes 786440 | tf_op jit(solution)/shard_map/ppermute | solution.py:326
  3.5 14.1 %collective-permute-start.1 = (bf16[128,2048]{1,0:T(8,128)(2,1)S(1)}, bf16[128,2048]{1,0:T(8,128)(2,1)S(1)}, u32[]{:S(2)}, u32[]{:S(2)}) collective-permute-start(bf16[128,2048]{1,0:T(8,128)(2,1)S(1)} %pad_maximum_fusion.refs_0_), channel_id=1, source_target_pairs={{0,16},{8,24},{16,0},{24,8},{32,48},{40,56},{48,32},{56,40},{64,80... | collective-permute-start | bytes 1572872 | tf_op jit(solution)/shard_map/ppermute | solution.py:306
  5.2 15.5 %collective-permute-start.2 = (bf16[128,2048]{1,0:T(8,128)(2,1)S(1)}, bf16[128,2048]{1,0:T(8,128)(2,1)S(1)}, u32[]{:S(2)}, u32[]{:S(2)}) collective-permute-start(bf16[128,2048]{1,0:T(8,128)(2,1)S(1)} %pad_maximum_fusion.refs_0_), channel_id=1, source_target_pairs={{0,48},{8,56},{16,32},{24,40},{32,16},{40,24},{48,0},{56,8},{64,11... | collective-permute-start | bytes 1572872 | tf_op jit(solution)/shard_map/ppermute | solution.py:307
  7.4 15.3 %collective-permute-start.5 = (bf16[64,2304]{1,0:T(8,128)(2,1)S(1)}, bf16[64,2304]{1,0:T(8,128)(2,1)S(1)}, u32[]{:S(2)}, u32[]{:S(2)}) collective-permute-start(bf16[64,2304]{1,0:T(8,128)(2,1)S(1)} %pad_maximum_fusion.1), channel_id=1, source_target_pairs={{0,64},{8,72},{16,80},{24,88},{32,96},{40,104},{48,112},{56,120},{... | collective-permute-start | bytes 884744 | tf_op jit(solution)/shard_map/ppermute | solution.py:306
  10.7 18.2 %collective-permute-start.6 = (bf16[64,2304]{1,0:T(8,128)(2,1)S(1)}, bf16[64,2304]{1,0:T(8,128)(2,1)S(1)}, u32[]{:S(2)}, u32[]{:S(2)}) collective-permute-start(bf16[64,2304]{1,0:T(8,128)(2,1)S(1)} %pad_maximum_fusion.1), channel_id=1, source_target_pairs={{0,192},{8,200},{16,208},{24,216},{32,224},{40,232},{48,240},{56,2... | collective-permute-start | bytes 884744 | tf_op jit(solution)/shard_map/ppermute | solution.py:307
  17.6 12.9 %collective-permute-start.3 = (bf16[64,2048]{1,0:T(8,128)(2,1)S(1)}, bf16[64,2048]{1,0:T(8,128)(2,1)S(1)}, u32[]{:S(2)}, u32[]{:S(2)}) collective-permute-start(bf16[64,2048]{1,0:T(8,128)(2,1)S(1)} %shard_map.50), channel_id=1, source_target_pairs={{0,48},{8,56},{16,32},{24,40},{32,16},{40,24},{48,0},{56,8},{64,11... | collective-permute-start | bytes 786440 | tf_op jit(solution)/shard_map/ppermute | solution.py:308
  20.7 9.8 %collective-permute-start.4 = (bf16[64,2048]{1,0:T(8,128)(2,1)S(1)}, bf16[64,2048]{1,0:T(8,128)(2,1)S(1)}, u32[]{:S(2)}, u32[]{:S(2)}) collective-permute-start(bf16[64,2048]{1,0:T(8,128)(2,1)S(1)} %shard_map.51), channel_id=1, source_target_pairs={{0,16},{8,24},{16,0},{24,8},{32,48},{40,56},{48,32},{56,40},{64,80... | collective-permute-start | bytes 786440 | tf_op jit(solution)/shard_map/ppermute | solution.py:309
  23.3 14.1 %collective-permute-start.7 = (bf16[32,2304]{1,0:T(8,128)(2,1)}, bf16[32,2304]{1,0:T(8,128)(2,1)}, u32[]{:S(2)}, u32[]{:S(2)}) collective-permute-start(bf16[32,2304]{1,0:T(8,128)(2,1)} %shard_map.52), channel_id=1, source_target_pairs={{0,192},{8,200},{16,208},{24,216},{32,224},{40,232},{48,240},{56,2... | collective-permute-start | bytes 442376 | tf_op jit(solution)/shard_map/ppermute | solution.py:308
  29.6 8.6 %collective-permute-start.8 = (bf16[32,2304]{1,0:T(8,128)(2,1)}, bf16[32,2304]{1,0:T(8,128)(2,1)}, u32[]{:S(2)}, u32[]{:S(2)}) collective-permute-start(bf16[32,2304]{1,0:T(8,128)(2,1)} %shard_map.54), channel_id=1, source_target_pairs={{0,64},{8,72},{16,80},{24,88},{32,96},{40,104},{48,112},{56,120},{... | collective-permute-start | bytes 442376 | tf_op jit(solution)/shard_map/ppermute | solution.py:309
  32.5 13.2 %collective-permute-start.10 = (f32[4,64,384]{2,1,0:T(8,128)S(1)}, f32[4,64,384]{2,1,0:T(8,128)S(1)}, u32[]{:S(2)}, u32[]{:S(2)}) collective-permute-start(f32[4,64,384]{2,1,0:T(8,128)S(1)} %get-tuple-element.32), channel_id=1, source_target_pairs={{0,6},{1,7},{2,4},{3,5},{4,2},{5,3},{6,0},{7,1},{8,14},{9,15},{10,... | collective-permute-start | bytes 1179656 | tf_op jit(solution)/shard_map/ppermute | solution.py:345
  35.3 11.1 %collective-permute-start.11 = (f32[4,64,384]{2,1,0:T(8,128)S(1)}, f32[4,64,384]{2,1,0:T(8,128)S(1)}, u32[]{:S(2)}, u32[]{:S(2)}) collective-permute-start(f32[4,64,384]{2,1,0:T(8,128)S(1)} %get-tuple-element.33), channel_id=1, source_target_pairs={{0,1},{1,0},{2,3},{3,2},{4,5},{5,4},{6,7},{7,6},{8,9},{9,8},{10,11... | collective-permute-start | bytes 1179656 | tf_op jit(solution)/shard_map/ppermute | solution.py:345
  37.2 10.2 %collective-permute-start.9 = (f32[4,64,384]{2,1,0:T(8,128)S(1)}, f32[4,64,384]{2,1,0:T(8,128)S(1)}, u32[]{:S(2)}, u32[]{:S(2)}) collective-permute-start(f32[4,64,384]{2,1,0:T(8,128)S(1)} %get-tuple-element.31), channel_id=1, source_target_pairs={{0,2},{1,3},{2,0},{3,1},{4,6},{5,7},{6,4},{7,5},{8,10},{9,11},{10,... | collective-permute-start | bytes 1179656 | tf_op jit(solution)/shard_map/ppermute | solution.py:345
  41.1 9.3 %collective-permute-start.12 = (f32[4,64,128]{2,1,0:T(8,128)S(1)}, f32[4,64,128]{2,1,0:T(8,128)S(1)}, u32[]{:S(2)}, u32[]{:S(2)}) collective-permute-start(f32[4,64,128]{2,1,0:T(8,128)S(1)} %get-tuple-element.35), channel_id=1, source_target_pairs={{0,2},{1,3},{2,0},{3,1},{4,6},{5,7},{6,4},{7,5},{8,10},{9,11},{10,... | collective-permute-start | bytes 393224 | tf_op jit(solution)/shard_map/ppermute | solution.py:348
  43.6 6.8 %collective-permute-start.13 = (f32[4,64,128]{2,1,0:T(8,128)S(1)}, f32[4,64,128]{2,1,0:T(8,128)S(1)}, u32[]{:S(2)}, u32[]{:S(2)}) collective-permute-start(f32[4,64,128]{2,1,0:T(8,128)S(1)} %get-tuple-element.36), channel_id=1, source_target_pairs={{0,6},{1,7},{2,4},{3,5},{4,2},{5,3},{6,0},{7,1},{8,14},{9,15},{10,... | collective-permute-start | bytes 393224 | tf_op jit(solution)/shard_map/ppermute | solution.py:348
  45.7 5.5 %collective-permute-start.14 = (f32[4,64,128]{2,1,0:T(8,128)S(1)}, f32[4,64,128]{2,1,0:T(8,128)S(1)}, u32[]{:S(2)}, u32[]{:S(2)}) collective-permute-start(f32[4,64,128]{2,1,0:T(8,128)S(1)} %get-tuple-element.37), channel_id=1, source_target_pairs={{0,1},{1,0},{2,3},{3,2},{4,5},{5,4},{6,7},{7,6},{8,9},{9,8},{10,11... | collective-permute-start | bytes 393224 | tf_op jit(solution)/shard_map/ppermute | solution.py:348
  51.2 7.2 %collective-permute-start.19 = (f32[2,64,512]{2,1,0:T(8,128)S(1)}, f32[2,64,512]{2,1,0:T(8,128)S(1)}, u32[]{:S(2)}, u32[]{:S(2)}) collective-permute-start(f32[2,64,512]{2,1,0:T(8,128)S(1)} %get-tuple-element.58), channel_id=1, source_target_pairs={{0,2},{1,3},{2,0},{3,1},{4,6},{5,7},{6,4},{7,5},{8,10},{9,11},{10,... | collective-permute-start | bytes 786440 | tf_op jit(solution)/shard_map/ppermute | solution.py:353
  52.0 7.6 %collective-permute-start.17 = (f32[2,64,512]{2,1,0:T(8,128)S(1)}, f32[2,64,512]{2,1,0:T(8,128)S(1)}, u32[]{:S(2)}, u32[]{:S(2)}) collective-permute-start(f32[2,64,512]{2,1,0:T(8,128)S(1)} %get-tuple-element.52), channel_id=1, source_target_pairs={{0,1},{1,0},{2,3},{3,2},{4,5},{5,4},{6,7},{7,6},{8,9},{9,8},{10,11... | collective-permute-start | bytes 786440 | tf_op jit(solution)/shard_map/ppermute | solution.py:353
  52.3 8.4 %collective-permute-start.15 = (f32[2,64,512]{2,1,0:T(8,128)S(1)}, f32[2,64,512]{2,1,0:T(8,128)S(1)}, u32[]{:S(2)}, u32[]{:S(2)}) collective-permute-start(f32[2,64,512]{2,1,0:T(8,128)S(1)} %get-tuple-element.46), channel_id=1, source_target_pairs={{0,6},{1,7},{2,4},{3,5},{4,2},{5,3},{6,0},{7,1},{8,14},{9,15},{10,... | collective-permute-start | bytes 786440 | tf_op jit(solution)/shard_map/ppermute | solution.py:353
  58.4 6.3 %collective-permute-start.20 = (f32[1,64,512]{2,1,0:T(8,128)S(1)}, f32[1,64,512]{2,1,0:T(8,128)S(1)}, u32[]{:S(2)}, u32[]{:S(2)}) collective-permute-start(f32[1,64,512]{2,1,0:T(8,128)S(1)} %slice_add_fusion), channel_id=1, source_target_pairs={{0,6},{1,7},{2,4},{3,5},{4,2},{5,3},{6,0},{7,1},{8,14},{9,15},{10,... | collective-permute-start | bytes 393224 | tf_op jit(solution)/shard_map/ppermute | solution.py:355
  59.6 5.1 %collective-permute-start.18 = (f32[1,64,512]{2,1,0:T(8,128)S(1)}, f32[1,64,512]{2,1,0:T(8,128)S(1)}, u32[]{:S(2)}, u32[]{:S(2)}) collective-permute-start(f32[1,64,512]{2,1,0:T(8,128)S(1)} %slice_add_fusion.1), channel_id=1, source_target_pairs={{0,2},{1,3},{2,0},{3,1},{4,6},{5,7},{6,4},{7,5},{8,10},{9,11},{10,... | collective-permute-start | bytes 393224 | tf_op jit(solution)/shard_map/ppermute | solution.py:355
  60.8 5.1 %collective-permute-start.16 = (f32[1,64,512]{2,1,0:T(8,128)S(1)}, f32[1,64,512]{2,1,0:T(8,128)S(1)}, u32[]{:S(2)}, u32[]{:S(2)}) collective-permute-start(f32[1,64,512]{2,1,0:T(8,128)S(1)} %slice_add_fusion.2), channel_id=1, source_target_pairs={{0,1},{1,0},{2,3},{3,2},{4,5},{5,4},{6,7},{7,6},{8,9},{9,8},{10,11... | collective-permute-start | bytes 393224 | tf_op jit(solution)/shard_map/ppermute | solution.py:355
  66.9 1.3 %collective-permute-start.21 = (f32[64,128]{1,0:T(8,128)S(1)}, f32[64,128]{1,0:T(8,128)S(1)}, u32[]{:S(2)}, u32[]{:S(2)}) collective-permute-start(f32[64,128]{1,0:T(8,128)S(1)} %shard_map.60), channel_id=1, source_target_pairs={{0,8},{8,0},{16,24},{24,16},{32,40},{40,32},{48,56},{56,48},{64,72... | collective-permute-start | bytes 98312 | tf_op jit(solution)/shard_map/ppermute | solution.py:315
  68.2 4.7 %collective-permute-start.22 = (f32[64,128]{1,0:T(8,128)S(1)}, f32[64,128]{1,0:T(8,128)S(1)}, u32[]{:S(2)}, u32[]{:S(2)}) collective-permute-start(f32[64,128]{1,0:T(8,128)S(1)} %add.35.refs_0_), channel_id=1, source_target_pairs={{0,16},{8,24},{16,0},{24,8},{32,48},{40,56},{48,32},{56,40},{64,80... | collective-permute-start | bytes 98312 | tf_op jit(solution)/shard_map/ppermute | solution.py:315
  68.5 5.4 %collective-permute-start.23 = (f32[64,128]{1,0:T(8,128)S(1)}, f32[64,128]{1,0:T(8,128)S(1)}, u32[]{:S(2)}, u32[]{:S(2)}) collective-permute-start(f32[64,128]{1,0:T(8,128)S(1)} %add.35.refs_0_), channel_id=1, source_target_pairs={{0,32},{8,40},{16,48},{24,56},{32,0},{40,8},{48,16},{56,24},{64,96... | collective-permute-start | bytes 98312 | tf_op jit(solution)/shard_map/ppermute | solution.py:315
  70.7 5.1 %collective-permute-start.24 = (f32[64,128]{1,0:T(8,128)S(1)}, f32[64,128]{1,0:T(8,128)S(1)}, u32[]{:S(2)}, u32[]{:S(2)}) collective-permute-start(f32[64,128]{1,0:T(8,128)S(1)} %add.35.refs_0_), channel_id=1, source_target_pairs={{0,48},{8,56},{16,32},{24,40},{32,16},{40,24},{48,0},{56,8},{64,11... | collective-permute-start | bytes 98312 | tf_op jit(solution)/shard_map/ppermute | solution.py:315
  76.2 4.8 %collective-permute-start.25 = (f32[136,128]{1,0:T(8,128)S(1)}, f32[136,128]{1,0:T(8,128)S(1)}, u32[]{:S(2)}, u32[]{:S(2)}) collective-permute-start(f32[136,128]{1,0:T(8,128)S(1)} %shard_map.61), channel_id=1, source_target_pairs={{0,2},{1,3},{2,0},{3,1},{4,6},{5,7},{6,4},{7,5},{8,10},{9,11},{10,... | collective-permute-start | bytes 208904 | tf_op jit(solution)/shard_map/ppermute | solution.py:315
  77.4 5.8 %collective-permute-start.26 = (f32[136,128]{1,0:T(8,128)S(1)}, f32[136,128]{1,0:T(8,128)S(1)}, u32[]{:S(2)}, u32[]{:S(2)}) collective-permute-start(f32[136,128]{1,0:T(8,128)S(1)} %shard_map.61), channel_id=1, source_target_pairs={{0,4},{1,5},{2,6},{3,7},{4,0},{5,1},{6,2},{7,3},{8,12},{9,13},{10,... | collective-permute-start | bytes 208904 | tf_op jit(solution)/shard_map/ppermute | solution.py:315
  79.5 5.5 %collective-permute-start.27 = (f32[136,128]{1,0:T(8,128)S(1)}, f32[136,128]{1,0:T(8,128)S(1)}, u32[]{:S(2)}, u32[]{:S(2)}) collective-permute-start(f32[136,128]{1,0:T(8,128)S(1)} %shard_map.61), channel_id=1, source_target_pairs={{0,6},{1,7},{2,4},{3,5},{4,2},{5,3},{6,0},{7,1},{8,14},{9,15},{10,... | collective-permute-start | bytes 208904 | tf_op jit(solution)/shard_map/ppermute | solution.py:315
  85.1 4.6 %collective-permute-start.28 = (f32[136,128]{1,0:T(8,128)S(1)}, f32[136,128]{1,0:T(8,128)S(1)}, u32[]{:S(2)}, u32[]{:S(2)}) collective-permute-start(f32[136,128]{1,0:T(8,128)S(1)} %select_select_fusion.1), channel_id=1, source_target_pairs={{0,1},{1,0},{2,3},{3,2},{4,5},{5,4},{6,7},{7,6},{8,9},{9,8},{10,11... | collective-permute-start | bytes 208904 | tf_op jit(solution)/shard_map/ppermute | solution.py:315
  89.8 5.2 %collective-permute-start.29 = (f32[72,128]{1,0:T(8,128)S(1)}, f32[72,128]{1,0:T(8,128)S(1)}, u32[]{:S(2)}, u32[]{:S(2)}) collective-permute-start(f32[72,128]{1,0:T(8,128)S(1)} %slice.23), channel_id=1, source_target_pairs={{0,64},{8,72},{16,80},{24,88},{32,96},{40,104},{48,112},{56,120},{... | collective-permute-start | bytes 110600 | tf_op jit(solution)/shard_map/ppermute | solution.py:315
  95.0 6.5 %collective-permute-start.30 = (f32[72,128]{1,0:T(8,128)S(1)}, f32[72,128]{1,0:T(8,128)S(1)}, u32[]{:S(2)}, u32[]{:S(2)}) collective-permute-start(f32[72,128]{1,0:T(8,128)S(1)} %slice_add_fusion.3.refs_0_), channel_id=1, source_target_pairs={{0,192},{8,200},{16,208},{24,216},{32,224},{40,232},{48,240},{56,2... | collective-permute-start | bytes 110600 | tf_op jit(solution)/shard_map/ppermute | solution.py:315

commit v3 on v2

--- a/solution.py
+++ b/solution.py
@@ -61,7 +61,7 @@
     return call
 
 
-ROW_PIECES = ((0, 1), (2, 3), (6, 7), (4,), (5,))
+ROW_PIECES = ((0,), (2, 6), (4,), (1,), (3, 7), (5,))
 NEAR_BLOCKS = 3
 
 
@@ -73,7 +73,8 @@
 def pair_body(bit, chunks, which, *refs):
     n_rows = len(ROW_PIECES)
     rows = refs[:n_rows]
-    cols, outs = refs[n_rows:-7], refs[-7:-4]
+    whole = len(chunks) == 2
+    cols, outs = refs[n_rows : -7 - whole], refs[-7 - whole : -4 - whole]
     stack, masked, square, held = refs[-4:]
     height = stack.shape[1]
     sites = masked.shape[1]
@@ -87,6 +88,10 @@
         masked[span] = block
         square[span] = square_of(block)
         held[span] = held_of(block)
+        if whole and begin > 0:
+            columns = (ref.shape[1] - sites) // 2
+            gathered = ref[:, sites : sites + columns].astype(jnp.float32) + ref[:, sites + columns :].astype(jnp.float32)
+            refs[-5][begin - height : begin - height + block.shape[0]] = gathered
         begin += block.shape[0]
     blocks = [
         jnp.concatenate([stack[which[0] ^ k] for k in route_offsets(route, bit)], axis=0) for route in range(3)
@@ -127,7 +132,7 @@
 
 
 def band_body(*refs):
-    whole, pieces, own, out = refs[:9], refs[9:13], refs[13], refs[14]
+    whole, gathered, own, out = refs[:9], refs[9], refs[10], refs[11]
     height = own.shape[0]
     edge = 2 * NEAR_BLOCKS * height
     totals = []
@@ -146,28 +151,8 @@
                 )
             )
     band = correlate(*totals)
-    columns = own.shape[1]
-    gathered = [piece[:, :columns].astype(jnp.float32) + piece[:, columns:].astype(jnp.float32) for piece in pieces]
-    factor = jnp.concatenate([own[...]] + gathered, axis=0)
+    factor = jnp.concatenate([own[...], gathered[...]], axis=0)
     out[...] = jnp.dot(band, factor, precision=lax.Precision.HIGHEST, preferred_element_type=jnp.float32)
-
-
-def band_call(terms, pieces, own, shape):
-    columns = own.shape[1]
-    firsts = [pl.BlockSpec((1,) + term.shape[1:], lambda i: (0, 0, 0)) for term in terms]
-    tails = [
-        pl.BlockSpec((piece.shape[0], 2 * columns), lambda i, at=piece.shape[1] // (2 * columns) - 1: (0, at))
-        for piece in pieces
-    ]
-    whole = pl.BlockSpec(own.shape, lambda i: (0, 0))
-    return pl.pallas_call(
-        band_body,
-        grid=(1,),
-        out_shape=shape,
-        in_specs=firsts + tails + [whole],
-        out_specs=whole,
-        compiler_params=pltpu.CompilerParams(vmem_limit_bytes=VMEM_LIMIT),
-    )(*terms, *pieces, own)
 
 
 def gram_body(*refs):
@@ -286,27 +271,21 @@
     return [(i, i ^ shift) for i in range(SITE_PARTS)]
 
 
-def half_body(whole, out):
-    out[...] = whole[...]
+def half_body(part, whole, out):
+    count = out.shape[0]
+    out[...] = whole[part * count : (part + 1) * count]
 
 
 def half_of(block, part):
-    shape = (block.shape[0] // 2, block.shape[1])
-    return pl.pallas_call(
-        half_body,
-        grid=(1,),
-        out_shape=jax.ShapeDtypeStruct(shape, block.dtype),
-        in_specs=[pl.BlockSpec(shape, lambda i: (part, 0))],
-        out_specs=pl.BlockSpec(shape, lambda i: (0, 0)),
-        compiler_params=pltpu.CompilerParams(vmem_limit_bytes=VMEM_LIMIT),
-    )(block)
-
-
-def gather_line(block, near, other):
+    shape = jax.ShapeDtypeStruct((block.shape[0] // 2, block.shape[1]), block.dtype)
+    return kernel_call(functools.partial(half_body, part), shape)(block)
+
+
+def gather_line(block, near, other, cut):
     one = lax.ppermute(block, "samp", samp_perm(near))
     three = lax.ppermute(block, "samp", samp_perm(other))
-    top = lax.ppermute(half_of(one, 0), "samp", samp_perm(other))
-    bottom = lax.ppermute(half_of(three, 1), "samp", samp_perm(near))
+    top = lax.ppermute(cut(one, 0), "samp", samp_perm(other))
+    bottom = lax.ppermute(cut(three, 1), "samp", samp_perm(near))
     return [block, one, three, top, bottom]
 
 
@@ -323,18 +302,20 @@
     rounded = lax.reduce_precision(factor, 8, 7)
     coarse, fine = rounded.astype(jnp.bfloat16), (factor - rounded).astype(jnp.bfloat16)
     tagged = jnp.concatenate([masked, coarse, fine], axis=1)
-    both = jnp.concatenate([masked, lax.ppermute(masked, "samp", samp_perm(1))], axis=0)
-    rows = gather_line(both, 2, 6)
-    pieces = gather_line(tagged, BLOCKS, 3 * BLOCKS)[1:]
+    mine = gather_line(masked, 2, 6, half_of)
+    middle = jnp.concatenate(mine[1:3], axis=0)
+    end = jnp.concatenate(mine[3:], axis=0)
+    rows = [masked, middle, end] + [lax.ppermute(part, "samp", samp_perm(1)) for part in (masked, middle, end)]
+    pieces = gather_line(tagged, BLOCKS, 3 * BLOCKS, lambda block, part: jnp.split(block, 2)[part])[1:]
     near_cols, far_cols = [masked] + pieces[:2], pieces[2:]
     which = ((lax.axis_index("samp") % BLOCKS) ^ lax.axis_index("site")).astype(jnp.int32).reshape(1)
 
-    def pairs(bit, chunks, cols, flops):
+    def pairs(bit, chunks, cols, flops, extra=()):
         lanes = {"near": 2 * NEAR_BLOCKS * height, "far": 2 * height}
         width = sum(col.shape[0] for col in cols)
         return kernel_call(
             functools.partial(pair_body, bit, chunks),
-            [jax.ShapeDtypeStruct((4, height, sum(lanes[chunk] for chunk in chunks)), f32)] * 3,
+            [jax.ShapeDtypeStruct((4, height, sum(lanes[chunk] for chunk in chunks)), f32)] * 3 + list(extra),
             scratch=[pltpu.VMEM((BLOCKS, height, sites), jnp.bfloat16)] + [pltpu.VMEM((width, sites), jnp.bfloat16)] * 3,
             smem=1,
             limit=PAIR_VMEM_LIMIT,
@@ -347,14 +328,15 @@
     send_far = pairs(1, ("far",), far_cols, 10000000000)
     came_far = [lax.ppermute(send_far[r], "site", site_perm(ROUTES[r][0])) for r in range(3)]
     far_kept, came_near, _ = lax.optimization_barrier((far_cols[1], came_near, send_far))
-    keep = pairs(0, ("near", "far"), near_cols + [far_cols[0], far_kept], 10000000000)
+    gathered_shape = jax.ShapeDtypeStruct(((DEPTHS - 1) * height, columns), f32)
+    *keep, gathered = pairs(0, ("near", "far"), near_cols + [far_cols[0], far_kept], 10000000000, [gathered_shape])
     keep, came_far = lax.optimization_barrier((keep, came_far))
     folded = [fold(keep[r], came_near[r], came_far[r]) for r in range(3)]
     came2 = [lax.ppermute(folded[r][0], "site", site_perm(ROUTES[r][1])) for r in range(3)]
     send = [folded[r][1] + came2[r][1:] for r in range(3)]
     came3 = [lax.ppermute(send[r], "site", site_perm(ROUTES[r][2])) for r in range(3)]
     terms = [t for r in range(3) for t in (folded[r][2], came2[r], came3[r])]
-    part = band_call(terms, pieces, factor, jax.ShapeDtypeStruct((height, columns), f32))
+    part = kernel_call(band_body, jax.ShapeDtypeStruct((height, columns), f32))(*terms, gathered, factor)
     part = tree_sum(spread(part, "samp", [1]))
     packed = columns // 2 + PANEL
     message = kernel_call(gram_body, jax.ShapeDtypeStruct((packed + height, columns), f32))(*spread(part, "samp", [2, 4, 6]))

time: 108 us -> 103 us (0.954); the launches traced: 107 us -> 103 us
  waiting for transfers between devices: 31.3 us -> 36.8 us
  starting transfers between devices: 56.9 us -> 51.5 us
  Pallas kernels: 16.7 us -> 12.6 us
    ppermute x10, waiting for transfers between devices: 14.8 us -> 21.6 us  [spread(): return [part] + [lax.ppermute(part, axis, perm(k)) for k in shifts]]
    ppermute x10, starting transfers between devices: 19.2 us -> 12.9 us  [spread(): return [part] + [lax.ppermute(part, axis, perm(k)) for k in shifts]]
    ppermute x2, waiting for transfers between devices: 4.96 us -> 0.17 us  [gather_line(): one = lax.ppermute(block, 'samp', samp_perm(near))]
    ppermute x5 -> x7, waiting for transfers between devices: 2.25 us -> 5.91 us  [the longest x2 5.89 us: gather_line(): top = lax.ppermute(cut(one, 0), 'samp', samp_perm(other))]
    pallas_call x5 -> x0, Pallas kernels: 2.46 us -> none  [the longest x4 1.38 us: half_of(): pl.pallas_call(half_body, grid=(1,), out_shape=jax.ShapeDtypeStruct(shape...]
    ppermute x3, starting transfers between devices: 3.3 us -> 5.22 us  [local(): lax.ppermute(folded[r][0], 'site', site_perm(ROUTES[r][1]))]
    pallas_call x8 -> x11, Pallas kernels: 14.2 us -> 12.6 us  [call(): pl.pallas_call(body, out_shape=out_shape, in_specs=in_specs, out_specs=ja...]
    ppermute x5 -> x7, starting transfers between devices: 9.94 us -> 8.53 us  [the longest x2 6.84 us: gather_line(): top = lax.ppermute(cut(one, 0), 'samp', samp_perm(other))]
  transfers between devices with their start and end apart: 31 -> 33, of which waited for: 17 -> 18; matrix products, arithmetic and copies ran while one was open for 0% -> 0% of each run, Pallas kernels for 9% -> 6%
where the time goes in v3:
time: 103 us
  starting transfers between devices  51.5 us (50%)
  waiting for transfers between devices  36.8 us (36%)
  Pallas kernels  12.6 us (12%)
  other arithmetic  1.49 us (1%)
    ppermute x10, waiting for transfers between devices, spread(): return [part] + [lax.ppermute(part, axis, perm(k)) for k in shifts]  21.6 us
    ppermute x10, starting transfers between devices, spread(): return [part] + [lax.ppermute(part, axis, perm(k)) for k in shifts]  12.9 us
    pallas_call x11, Pallas kernels, call(): pl.pallas_call(body, out_shape=out_shape, in_specs=in_specs, out_specs=ja...  12.6 us
    ppermute x2, starting transfers between devices, gather_line(): top = lax.ppermute(cut(one, 0), 'samp', samp_perm(other))  6.84 us
    ppermute x2, waiting for transfers between devices, gather_line(): top = lax.ppermute(cut(one, 0), 'samp', samp_perm(other))  5.89 us
    ppermute x2, starting transfers between devices, gather_line(): three = lax.ppermute(block, 'samp', samp_perm(other))  5.76 us
    ppermute x3, starting transfers between devices, local(): lax.ppermute(send_near[r], 'site', site_perm(ROUTES[r][0]))  5.54 us
    ppermute x3, starting transfers between devices, local(): lax.ppermute(folded[r][0], 'site', site_perm(ROUTES[r][1]))  5.22 us
  transfers between devices with their start and end apart: 33, of which 18 were waited for; matrix products, arithmetic and copies ran while one was open for 0% of the time, Pallas kernels for 6%

profile of v3, /device:TPU:32, one launch (start us, length us, event | category | flops | bytes accessed | tf_op | source)
XLA Modules:
  0.0 103.4 jit_solution(17725599677222641902)
XLA Ops:
  0.6 1.2 %compare_select_fusion.refs_0_.refs_6_ = bf16[64,2048]{1,0:T(8,128)(2,1)S(1)} fusion(bf16[64,2048]{1,0:T(8,128)(2,1)} %param.3, s32[64,2048]{1,0:T(8,128)} %param.4), kind=kLoop, calls=%fused_computation | loop fusion | flops 262144 | bytes 1048576 | tf_op jit(solution)/shard_map/jit(_where)/select_n | solution.py:301
  1.8 1.7 %collective-permute-start = (bf16[64,2048]{1,0:T(8,128)(2,1)S(1)}, bf16[64,2048]{1,0:T(8,128)(2,1)S(1)}, u32[]{:S(2)}, u32[]{:S(2)}) collective-permute-start(bf16[64,2048]{1,0:T(8,128)(2,1)S(1)} %compare_select_fusion.refs_0_.refs_6_), channel_id=1, source_target_pairs={{0,16},{8,24},{16,0},{24,8},{32,48},{40,56},{48,32},{56,40},{64,80... | collective-permute-start | bytes 786440 | tf_op jit(solution)/shard_map/ppermute | solution.py:285
  3.5 2.2 %collective-permute-start.1 = (bf16[64,2048]{1,0:T(8,128)(2,1)S(1)}, bf16[64,2048]{1,0:T(8,128)(2,1)S(1)}, u32[]{:S(2)}, u32[]{:S(2)}) collective-permute-start(bf16[64,2048]{1,0:T(8,128)(2,1)S(1)} %compare_select_fusion.refs_0_.refs_6_), channel_id=1, source_target_pairs={{0,48},{8,56},{16,32},{24,40},{32,16},{40,24},{48,0},{56,8},{64,11... | collective-permute-start | bytes 786440 | tf_op jit(solution)/shard_map/ppermute | solution.py:286
  5.7 3.4 %collective-permute-start.7 = (bf16[64,2304]{1,0:T(8,128)(2,1)S(1)}, bf16[64,2304]{1,0:T(8,128)(2,1)S(1)}, u32[]{:S(2)}, u32[]{:S(2)}) collective-permute-start(bf16[64,2304]{1,0:T(8,128)(2,1)S(1)} %pad_maximum_fusion), channel_id=1, source_target_pairs={{0,64},{8,72},{16,80},{24,88},{32,96},{40,104},{48,112},{56,120},{... | collective-permute-start | bytes 884744 | tf_op jit(solution)/shard_map/ppermute | solution.py:285
  9.1 3.6 %collective-permute-start.8 = (bf16[64,2304]{1,0:T(8,128)(2,1)S(1)}, bf16[64,2304]{1,0:T(8,128)(2,1)S(1)}, u32[]{:S(2)}, u32[]{:S(2)}) collective-permute-start(bf16[64,2304]{1,0:T(8,128)(2,1)S(1)} %pad_maximum_fusion), channel_id=1, source_target_pairs={{0,192},{8,200},{16,208},{24,216},{32,224},{40,232},{48,240},{56,2... | collective-permute-start | bytes 884744 | tf_op jit(solution)/shard_map/ppermute | solution.py:286
  12.7 1.1 %collective-permute-start.2 = (bf16[32,2048]{1,0:T(8,128)(2,1)S(1)}, bf16[32,2048]{1,0:T(8,128)(2,1)S(1)}, u32[]{:S(2)}, u32[]{:S(2)}) collective-permute-start(bf16[32,2048]{1,0:T(8,128)(2,1)S(1)} %shard_map.50), channel_id=1, source_target_pairs={{0,48},{8,56},{16,32},{24,40},{32,16},{40,24},{48,0},{56,8},{64,11... | collective-permute-start | bytes 393224 | tf_op jit(solution)/shard_map/ppermute | solution.py:287
  14.0 5.9 %collective-permute-done.2 = bf16[32,2048]{1,0:T(8,128)(2,1)S(1)} collective-permute-done((bf16[32,2048]{1,0:T(8,128)(2,1)S(1)}, bf16[32,2048]{1,0:T(8,128)(2,1)S(1)}, u32[]{:S(2)}, u32[]{:S(2)}) %collective-permute-start.2) | collective-permute-done | bytes 131104 | tf_op jit(solution)/shard_map/ppermute | solution.py:287
  19.9 0.6 collective-permute-start.6
  20.7 5.7 %collective-permute-start.9 = (bf16[32,2304]{1,0:T(8,128)(2,1)S(1)}, bf16[32,2304]{1,0:T(8,128)(2,1)S(1)}, u32[]{:S(2)}, u32[]{:S(2)}) collective-permute-start(bf16[32,2304]{1,0:T(8,128)(2,1)S(1)} %split.8), channel_id=1, source_target_pairs={{0,192},{8,200},{16,208},{24,216},{32,224},{40,232},{48,240},{56,2... | collective-permute-start | bytes 442376 | tf_op jit(solution)/shard_map/ppermute | solution.py:287
  26.4 1.0 collective-permute-start.10
  27.4 2.0 %shard_map.52 = (f32[4,64,384]{2,1,0:T(8,128)S(1)}, f32[4,64,384]{2,1,0:T(8,128)S(1)}, f32[4,64,384]{2,1,0:T(8,128)S(1)}) custom-call(s32[1]{0:T(128)} %bitcast.which, bf16[64,2048]{1,0:T(8,128)(2,1)S(1)} %compare_select_fusion.refs_0_.refs_6_, bf16[128,2048]{1,0:T(8,128)(2,1)S(1)} %constant_dynamic-update-slice_fusion.refs_1_, ...), custom_call_target="tpu_custom_call" | custom-call | flops 1000000 | bytes 100000 | tf_op jit(solution)/shard_map/pallas_call | solution.py:51
  29.4 1.6 %collective-permute-start.11 = (f32[4,64,384]{2,1,0:T(8,128)S(1)}, f32[4,64,384]{2,1,0:T(8,128)S(1)}, u32[]{:S(2)}, u32[]{:S(2)}) collective-permute-start(f32[4,64,384]{2,1,0:T(8,128)S(1)} %get-tuple-element.32), channel_id=1, source_target_pairs={{0,2},{1,3},{2,0},{3,1},{4,6},{5,7},{6,4},{7,5},{8,10},{9,11},{10,... | collective-permute-start | bytes 1179656 | tf_op jit(solution)/shard_map/ppermute | solution.py:326
  31.0 2.1 %collective-permute-start.12 = (f32[4,64,384]{2,1,0:T(8,128)S(1)}, f32[4,64,384]{2,1,0:T(8,128)S(1)}, u32[]{:S(2)}, u32[]{:S(2)}) collective-permute-start(f32[4,64,384]{2,1,0:T(8,128)S(1)} %get-tuple-element.33), channel_id=1, source_target_pairs={{0,6},{1,7},{2,4},{3,5},{4,2},{5,3},{6,0},{7,1},{8,14},{9,15},{10,... | collective-permute-start | bytes 1179656 | tf_op jit(solution)/shard_map/ppermute | solution.py:326
  33.1 1.9 %collective-permute-start.13 = (f32[4,64,384]{2,1,0:T(8,128)S(1)}, f32[4,64,384]{2,1,0:T(8,128)S(1)}, u32[]{:S(2)}, u32[]{:S(2)}) collective-permute-start(f32[4,64,384]{2,1,0:T(8,128)S(1)} %get-tuple-element.34), channel_id=1, source_target_pairs={{0,1},{1,0},{2,3},{3,2},{4,5},{5,4},{6,7},{7,6},{8,9},{9,8},{10,11... | collective-permute-start | bytes 1179656 | tf_op jit(solution)/shard_map/ppermute | solution.py:326
  35.0 2.0 %shard_map.53 = (f32[4,64,128]{2,1,0:T(8,128)S(1)}, f32[4,64,128]{2,1,0:T(8,128)S(1)}, f32[4,64,128]{2,1,0:T(8,128)S(1)}) custom-call(s32[1]{0:T(128)} %bitcast.which, bf16[64,2048]{1,0:T(8,128)(2,1)S(1)} %compare_select_fusion.refs_0_.refs_6_, bf16[128,2048]{1,0:T(8,128)(2,1)S(1)} %constant_dynamic-update-slice_fusion.refs_1_, ...), custom_call_target="tpu_custom_call" | custom-call | flops 10000000000 | bytes 100000 | tf_op jit(solution)/shard_map/pallas_call | solution.py:51
  36.9 1.5 %collective-permute-start.14 = (f32[4,64,128]{2,1,0:T(8,128)S(1)}, f32[4,64,128]{2,1,0:T(8,128)S(1)}, u32[]{:S(2)}, u32[]{:S(2)}) collective-permute-start(f32[4,64,128]{2,1,0:T(8,128)S(1)} %get-tuple-element.36), channel_id=1, source_target_pairs={{0,2},{1,3},{2,0},{3,1},{4,6},{5,7},{6,4},{7,5},{8,10},{9,11},{10,... | collective-permute-start | bytes 393224 | tf_op jit(solution)/shard_map/ppermute | solution.py:329
  38.5 2.3 %collective-permute-start.15 = (f32[4,64,128]{2,1,0:T(8,128)S(1)}, f32[4,64,128]{2,1,0:T(8,128)S(1)}, u32[]{:S(2)}, u32[]{:S(2)}) collective-permute-start(f32[4,64,128]{2,1,0:T(8,128)S(1)} %get-tuple-element.37), channel_id=1, source_target_pairs={{0,6},{1,7},{2,4},{3,5},{4,2},{5,3},{6,0},{7,1},{8,14},{9,15},{10,... | collective-permute-start | bytes 393224 | tf_op jit(solution)/shard_map/ppermute | solution.py:329
  40.8 1.4 %collective-permute-start.16 = (f32[4,64,128]{2,1,0:T(8,128)S(1)}, f32[4,64,128]{2,1,0:T(8,128)S(1)}, u32[]{:S(2)}, u32[]{:S(2)}) collective-permute-start(f32[4,64,128]{2,1,0:T(8,128)S(1)} %get-tuple-element.38), channel_id=1, source_target_pairs={{0,1},{1,0},{2,3},{3,2},{4,5},{5,4},{6,7},{7,6},{8,9},{9,8},{10,11... | collective-permute-start | bytes 393224 | tf_op jit(solution)/shard_map/ppermute | solution.py:329
  42.1 0.6 collective-permute-done.12.near
  42.7 0.8 collective-permute-done.13.near
  43.5 2.0 %shard_map.54 = (f32[4,64,512]{2,1,0:T(8,128)S(1)}, f32[4,64,512]{2,1,0:T(8,128)S(1)}, f32[4,64,512]{2,1,0:T(8,128)S(1)}, f32[192,128]{1,0:T(8,128)S(1)}) custom-call(s32[1]{0:T(128)} %bitcast.which, bf16[64,2048]{1,0:T(8,128)(2,1)S(1)} %compare_select_fusion.refs_0_.refs_6_, bf16[128,2048]{1,0:T(8,128)(2,1)S(1)} %constant_dynamic-update-slice_fusion.refs_1_, ...), custom_call_target="tpu_custom_call" | custom-call | flops 10000000000 | bytes 100000 | tf_op jit(solution)/shard_map/pallas_call | solution.py:51
  45.8 1.4 %collective-permute-start.21 = (f32[2,64,512]{2,1,0:T(8,128)S(1)}, f32[2,64,512]{2,1,0:T(8,128)S(1)}, u32[]{:S(2)}, u32[]{:S(2)}) collective-permute-start(f32[2,64,512]{2,1,0:T(8,128)S(1)} %get-tuple-element.59), channel_id=1, source_target_pairs={{0,2},{1,3},{2,0},{3,1},{4,6},{5,7},{6,4},{7,5},{8,10},{9,11},{10,... | collective-permute-start | bytes 786440 | tf_op jit(solution)/shard_map/ppermute | solution.py:335
  47.3 1.8 %collective-permute-start.19 = (f32[2,64,512]{2,1,0:T(8,128)S(1)}, f32[2,64,512]{2,1,0:T(8,128)S(1)}, u32[]{:S(2)}, u32[]{:S(2)}) collective-permute-start(f32[2,64,512]{2,1,0:T(8,128)S(1)} %get-tuple-element.53), channel_id=1, source_target_pairs={{0,1},{1,0},{2,3},{3,2},{4,5},{5,4},{6,7},{7,6},{8,9},{9,8},{10,11... | collective-permute-start | bytes 786440 | tf_op jit(solution)/shard_map/ppermute | solution.py:335
  49.1 2.0 %collective-permute-start.17 = (f32[2,64,512]{2,1,0:T(8,128)S(1)}, f32[2,64,512]{2,1,0:T(8,128)S(1)}, u32[]{:S(2)}, u32[]{:S(2)}) collective-permute-start(f32[2,64,512]{2,1,0:T(8,128)S(1)} %get-tuple-element.47), channel_id=1, source_target_pairs={{0,6},{1,7},{2,4},{3,5},{4,2},{5,3},{6,0},{7,1},{8,14},{9,15},{10,... | collective-permute-start | bytes 786440 | tf_op jit(solution)/shard_map/ppermute | solution.py:335
  51.1 1.1 %collective-permute-done.21.refs_7_ = f32[2,64,512]{2,1,0:T(8,128)S(1)} collective-permute-done((f32[2,64,512]{2,1,0:T(8,128)S(1)}, f32[2,64,512]{2,1,0:T(8,128)S(1)}, u32[]{:S(2)}, u32[]{:S(2)}) %collective-permute-start.21) | collective-permute-done | bytes 262176 | tf_op jit(solution)/shard_map/ppermute | solution.py:335
  52.3 2.7 %collective-permute-start.22 = (f32[1,64,512]{2,1,0:T(8,128)S(1)}, f32[1,64,512]{2,1,0:T(8,128)S(1)}, u32[]{:S(2)}, u32[]{:S(2)}) collective-permute-start(f32[1,64,512]{2,1,0:T(8,128)S(1)} %slice_add_fusion), channel_id=1, source_target_pairs={{0,6},{1,7},{2,4},{3,5},{4,2},{5,3},{6,0},{7,1},{8,14},{9,15},{10,... | collective-permute-start | bytes 393224 | tf_op jit(solution)/shard_map/ppermute | solution.py:337
  55.1 1.9 %collective-permute-done.17.refs_1_ = f32[2,64,512]{2,1,0:T(8,128)S(1)} collective-permute-done((f32[2,64,512]{2,1,0:T(8,128)S(1)}, f32[2,64,512]{2,1,0:T(8,128)S(1)}, u32[]{:S(2)}, u32[]{:S(2)}) %collective-permute-start.17) | collective-permute-done | bytes 262176 | tf_op jit(solution)/shard_map/ppermute | solution.py:335
  57.0 0.5 collective-permute-start.18
  57.5 1.0 collective-permute-done.22.refs_8_
  58.6 1.5 %collective-permute-done.20.refs_5_ = f32[1,64,512]{2,1,0:T(8,128)S(1)} collective-permute-done((f32[1,64,512]{2,1,0:T(8,128)S(1)}, f32[1,64,512]{2,1,0:T(8,128)S(1)}, u32[]{:S(2)}, u32[]{:S(2)}) %collective-permute-start.20) | collective-permute-done | bytes 131104 | tf_op jit(solution)/shard_map/ppermute | solution.py:337
  60.0 2.0 %collective-permute-done.18.refs_2_ = f32[1,64,512]{2,1,0:T(8,128)S(1)} collective-permute-done((f32[1,64,512]{2,1,0:T(8,128)S(1)}, f32[1,64,512]{2,1,0:T(8,128)S(1)}, u32[]{:S(2)}, u32[]{:S(2)}) %collective-permute-start.18) | collective-permute-done | bytes 131104 | tf_op jit(solution)/shard_map/ppermute | solution.py:337
  62.5 1.2 %collective-permute-done.23 = f32[64,128]{1,0:T(8,128)S(1)} collective-permute-done((f32[64,128]{1,0:T(8,128)S(1)}, f32[64,128]{1,0:T(8,128)S(1)}, u32[]{:S(2)}, u32[]{:S(2)}) %collective-permute-start.23) | collective-permute-done | bytes 32800 | tf_op jit(solution)/shard_map/ppermute | solution.py:294
  63.7 0.5 collective-permute-start.24
  64.2 3.0 %collective-permute-start.25 = (f32[64,128]{1,0:T(8,128)S(1)}, f32[64,128]{1,0:T(8,128)S(1)}, u32[]{:S(2)}, u32[]{:S(2)}) collective-permute-start(f32[64,128]{1,0:T(8,128)S(1)} %add.35.refs_0_), channel_id=1, source_target_pairs={{0,32},{8,40},{16,48},{24,56},{32,0},{40,8},{48,16},{56,24},{64,96... | collective-permute-start | bytes 98312 | tf_op jit(solution)/shard_map/ppermute | solution.py:294
  67.3 1.1 %collective-permute-start.26 = (f32[64,128]{1,0:T(8,128)S(1)}, f32[64,128]{1,0:T(8,128)S(1)}, u32[]{:S(2)}, u32[]{:S(2)}) collective-permute-start(f32[64,128]{1,0:T(8,128)S(1)} %add.35.refs_0_), channel_id=1, source_target_pairs={{0,48},{8,56},{16,32},{24,40},{32,16},{40,24},{48,0},{56,8},{64,11... | collective-permute-start | bytes 98312 | tf_op jit(solution)/shard_map/ppermute | solution.py:294
  68.4 1.3 %collective-permute-done.25.refs_2_ = f32[64,128]{1,0:T(8,128)S(1)} collective-permute-done((f32[64,128]{1,0:T(8,128)S(1)}, f32[64,128]{1,0:T(8,128)S(1)}, u32[]{:S(2)}, u32[]{:S(2)}) %collective-permute-start.25) | collective-permute-done | bytes 32800 | tf_op jit(solution)/shard_map/ppermute | solution.py:294
  69.7 2.7 %collective-permute-done.26.refs_3_ = f32[64,128]{1,0:T(8,128)S(1)} collective-permute-done((f32[64,128]{1,0:T(8,128)S(1)}, f32[64,128]{1,0:T(8,128)S(1)}, u32[]{:S(2)}, u32[]{:S(2)}) %collective-permute-start.26) | collective-permute-done | bytes 32800 | tf_op jit(solution)/shard_map/ppermute | solution.py:294
  72.9 3.1 %collective-permute-start.28 = (f32[136,128]{1,0:T(8,128)S(1)}, f32[136,128]{1,0:T(8,128)S(1)}, u32[]{:S(2)}, u32[]{:S(2)}) collective-permute-start(f32[136,128]{1,0:T(8,128)S(1)} %shard_map.59), channel_id=1, source_target_pairs={{0,4},{1,5},{2,6},{3,7},{4,0},{5,1},{6,2},{7,3},{8,12},{9,13},{10,... | collective-permute-start | bytes 208904 | tf_op jit(solution)/shard_map/ppermute | solution.py:294
  76.0 1.5 %collective-permute-start.29 = (f32[136,128]{1,0:T(8,128)S(1)}, f32[136,128]{1,0:T(8,128)S(1)}, u32[]{:S(2)}, u32[]{:S(2)}) collective-permute-start(f32[136,128]{1,0:T(8,128)S(1)} %shard_map.59), channel_id=1, source_target_pairs={{0,6},{1,7},{2,4},{3,5},{4,2},{5,3},{6,0},{7,1},{8,14},{9,15},{10,... | collective-permute-start | bytes 208904 | tf_op jit(solution)/shard_map/ppermute | solution.py:294
  77.6 1.6 %collective-permute-done.28 = f32[136,128]{1,0:T(8,128)S(1)} collective-permute-done((f32[136,128]{1,0:T(8,128)S(1)}, f32[136,128]{1,0:T(8,128)S(1)}, u32[]{:S(2)}, u32[]{:S(2)}) %collective-permute-start.28) | collective-permute-done | bytes 69664 | tf_op jit(solution)/shard_map/ppermute | solution.py:294
  79.2 2.4 %collective-permute-done.29 = f32[136,128]{1,0:T(8,128)S(1)} collective-permute-done((f32[136,128]{1,0:T(8,128)S(1)}, f32[136,128]{1,0:T(8,128)S(1)}, u32[]{:S(2)}, u32[]{:S(2)}) %collective-permute-start.29) | collective-permute-done | bytes 69664 | tf_op jit(solution)/shard_map/ppermute | solution.py:294
  81.6 1.4 %collective-permute-start.30 = (f32[136,128]{1,0:T(8,128)S(1)}, f32[136,128]{1,0:T(8,128)S(1)}, u32[]{:S(2)}, u32[]{:S(2)}) collective-permute-start(f32[136,128]{1,0:T(8,128)S(1)} %select_select_fusion.1), channel_id=1, source_target_pairs={{0,1},{1,0},{2,3},{3,2},{4,5},{5,4},{6,7},{7,6},{8,9},{9,8},{10,11... | collective-permute-start | bytes 208904 | tf_op jit(solution)/shard_map/ppermute | solution.py:294
  83.0 3.4 %collective-permute-done.30 = f32[136,128]{1,0:T(8,128)S(1)} collective-permute-done((f32[136,128]{1,0:T(8,128)S(1)}, f32[136,128]{1,0:T(8,128)S(1)}, u32[]{:S(2)}, u32[]{:S(2)}) %collective-permute-start.30) | collective-permute-done | bytes 69664 | tf_op jit(solution)/shard_map/ppermute | solution.py:294
  86.5 1.0 %collective-permute-start.31 = (f32[72,128]{1,0:T(8,128)S(1)}, f32[72,128]{1,0:T(8,128)S(1)}, u32[]{:S(2)}, u32[]{:S(2)}) collective-permute-start(f32[72,128]{1,0:T(8,128)S(1)} %slice.23), channel_id=1, source_target_pairs={{0,64},{8,72},{16,80},{24,88},{32,96},{40,104},{48,112},{56,120},{... | collective-permute-start | bytes 110600 | tf_op jit(solution)/shard_map/ppermute | solution.py:294
  87.6 3.9 %collective-permute-done.31 = f32[72,128]{1,0:T(8,128)S(1)} collective-permute-done((f32[72,128]{1,0:T(8,128)S(1)}, f32[72,128]{1,0:T(8,128)S(1)}, u32[]{:S(2)}, u32[]{:S(2)}) %collective-permute-start.31) | collective-permute-done | bytes 36896 | tf_op jit(solution)/shard_map/ppermute | solution.py:294
  91.5 0.9 collective-permute-start.32
  92.4 5.2 %collective-permute-done.32.refs_1_ = f32[72,128]{1,0:T(8,128)S(1)} collective-permute-done((f32[72,128]{1,0:T(8,128)S(1)}, f32[72,128]{1,0:T(8,128)S(1)}, u32[]{:S(2)}, u32[]{:S(2)}) %collective-permute-start.32) | collective-permute-done | bytes 36896 | tf_op jit(solution)/shard_map/ppermute | solution.py:294
  97.6 5.8 %shard_map.60 = (f32[64,128]{1,0:T(8,128)}, f32[128,128]{1,0:T(8,128)}) custom-call(f32[72,128]{1,0:T(8,128)S(1)} %slice_add_fusion.3.refs_0_, f32[72,128]{1,0:T(8,128)S(1)} %collective-permute-done.32.refs_1_, f32[64,128]{1,0:T(8,128)S(1)} %slice.24.refs_2_), custom_call_target="tpu_custom_call" | custom-call | tf_op jit(solution)/shard_map/pallas_call | solution.py:51
  (50 shorter events, 2.1 us)
Async XLA Ops:
  0.6 5.1 %copy-start = (f32[64,128]{1,0:T(8,128)S(1)}, f32[64,128]{1,0:T(8,128)}, u32[]{:S(2)}) copy-start(f32[64,128]{1,0:T(8,128)} %refs_10_.1) | copy-start | bytes 98308
  1.8 10.8 %collective-permute-start = (bf16[64,2048]{1,0:T(8,128)(2,1)S(1)}, bf16[64,2048]{1,0:T(8,128)(2,1)S(1)}, u32[]{:S(2)}, u32[]{:S(2)}) collective-permute-start(bf16[64,2048]{1,0:T(8,128)(2,1)S(1)} %compare_select_fusion.refs_0_.refs_6_), channel_id=1, source_target_pairs={{0,16},{8,24},{16,0},{24,8},{32,48},{40,56},{48,32},{56,40},{64,80... | collective-permute-start | bytes 786440 | tf_op jit(solution)/shard_map/ppermute | solution.py:285
  3.5 10.3 %collective-permute-start.1 = (bf16[64,2048]{1,0:T(8,128)(2,1)S(1)}, bf16[64,2048]{1,0:T(8,128)(2,1)S(1)}, u32[]{:S(2)}, u32[]{:S(2)}) collective-permute-start(bf16[64,2048]{1,0:T(8,128)(2,1)S(1)} %compare_select_fusion.refs_0_.refs_6_), channel_id=1, source_target_pairs={{0,48},{8,56},{16,32},{24,40},{32,16},{40,24},{48,0},{56,8},{64,11... | collective-permute-start | bytes 786440 | tf_op jit(solution)/shard_map/ppermute | solution.py:286
  5.7 15.0 %collective-permute-start.7 = (bf16[64,2304]{1,0:T(8,128)(2,1)S(1)}, bf16[64,2304]{1,0:T(8,128)(2,1)S(1)}, u32[]{:S(2)}, u32[]{:S(2)}) collective-permute-start(bf16[64,2304]{1,0:T(8,128)(2,1)S(1)} %pad_maximum_fusion), channel_id=1, source_target_pairs={{0,64},{8,72},{16,80},{24,88},{32,96},{40,104},{48,112},{56,120},{... | collective-permute-start | bytes 884744 | tf_op jit(solution)/shard_map/ppermute | solution.py:285
  9.1 17.3 %collective-permute-start.8 = (bf16[64,2304]{1,0:T(8,128)(2,1)S(1)}, bf16[64,2304]{1,0:T(8,128)(2,1)S(1)}, u32[]{:S(2)}, u32[]{:S(2)}) collective-permute-start(bf16[64,2304]{1,0:T(8,128)(2,1)S(1)} %pad_maximum_fusion), channel_id=1, source_target_pairs={{0,192},{8,200},{16,208},{24,216},{32,224},{40,232},{48,240},{56,2... | collective-permute-start | bytes 884744 | tf_op jit(solution)/shard_map/ppermute | solution.py:286
  12.7 14.8 %collective-permute-start.4 = (bf16[64,2048]{1,0:T(8,128)(2,1)S(1)}, bf16[64,2048]{1,0:T(8,128)(2,1)S(1)}, u32[]{:S(2)}, u32[]{:S(2)}) collective-permute-start(bf16[64,2048]{1,0:T(8,128)(2,1)S(1)} %compare_select_fusion.refs_0_.refs_6_), channel_id=1, source_target_pairs={{0,8},{8,0},{16,24},{24,16},{32,40},{40,32},{48,56},{56,48},{64,72... | collective-permute-start | bytes 786440 | tf_op jit(solution)/shard_map/ppermute | solution.py:308
  12.7 7.2 %collective-permute-start.2 = (bf16[32,2048]{1,0:T(8,128)(2,1)S(1)}, bf16[32,2048]{1,0:T(8,128)(2,1)S(1)}, u32[]{:S(2)}, u32[]{:S(2)}) collective-permute-start(bf16[32,2048]{1,0:T(8,128)(2,1)S(1)} %shard_map.50), channel_id=1, source_target_pairs={{0,48},{8,56},{16,32},{24,40},{32,16},{40,24},{48,0},{56,8},{64,11... | collective-permute-start | bytes 393224 | tf_op jit(solution)/shard_map/ppermute | solution.py:287
  13.8 6.1 %collective-permute-start.3 = (bf16[32,2048]{1,0:T(8,128)(2,1)S(1)}, bf16[32,2048]{1,0:T(8,128)(2,1)S(1)}, u32[]{:S(2)}, u32[]{:S(2)}) collective-permute-start(bf16[32,2048]{1,0:T(8,128)(2,1)S(1)} %shard_map.51), channel_id=1, source_target_pairs={{0,16},{8,24},{16,0},{24,8},{32,48},{40,56},{48,32},{56,40},{64,80... | collective-permute-start | bytes 393224 | tf_op jit(solution)/shard_map/ppermute | solution.py:288
  19.9 7.5 %collective-permute-start.5 = (bf16[128,2048]{1,0:T(8,128)(2,1)S(1)}, bf16[128,2048]{1,0:T(8,128)(2,1)S(1)}, u32[]{:S(2)}, u32[]{:S(2)}) collective-permute-start(bf16[128,2048]{1,0:T(8,128)(2,1)S(1)} %constant_dynamic-update-slice_fusion.refs_1_), channel_id=1, source_target_pairs={{0,8},{8,0},{16,24},{24,16},{32,40},{40,32},{48,56},{56,48},{64,72... | collective-permute-start | bytes 1572872 | tf_op jit(solution)/shard_map/ppermute | solution.py:308
  19.9 7.5 %collective-permute-start.6 = (bf16[64,2048]{1,0:T(8,128)(2,1)S(1)}, bf16[64,2048]{1,0:T(8,128)(2,1)S(1)}, u32[]{:S(2)}, u32[]{:S(2)}) collective-permute-start(bf16[64,2048]{1,0:T(8,128)(2,1)S(1)} %constant_dynamic-update-slice_fusion.2.refs_2_), channel_id=1, source_target_pairs={{0,8},{8,0},{16,24},{24,16},{32,40},{40,32},{48,56},{56,48},{64,72... | collective-permute-start | bytes 786440 | tf_op jit(solution)/shard_map/ppermute | solution.py:308
  20.7 14.2 %collective-permute-start.9 = (bf16[32,2304]{1,0:T(8,128)(2,1)S(1)}, bf16[32,2304]{1,0:T(8,128)(2,1)S(1)}, u32[]{:S(2)}, u32[]{:S(2)}) collective-permute-start(bf16[32,2304]{1,0:T(8,128)(2,1)S(1)} %split.8), channel_id=1, source_target_pairs={{0,192},{8,200},{16,208},{24,216},{32,224},{40,232},{48,240},{56,2... | collective-permute-start | bytes 442376 | tf_op jit(solution)/shard_map/ppermute | solution.py:287
  26.4 8.5 %collective-permute-start.10 = (bf16[32,2304]{1,0:T(8,128)(2,1)S(1)}, bf16[32,2304]{1,0:T(8,128)(2,1)S(1)}, u32[]{:S(2)}, u32[]{:S(2)}) collective-permute-start(bf16[32,2304]{1,0:T(8,128)(2,1)S(1)} %split.9), channel_id=1, source_target_pairs={{0,64},{8,72},{16,80},{24,88},{32,96},{40,104},{48,112},{56,120},{... | collective-permute-start | bytes 442376 | tf_op jit(solution)/shard_map/ppermute | solution.py:288
  29.4 11.4 %collective-permute-start.11 = (f32[4,64,384]{2,1,0:T(8,128)S(1)}, f32[4,64,384]{2,1,0:T(8,128)S(1)}, u32[]{:S(2)}, u32[]{:S(2)}) collective-permute-start(f32[4,64,384]{2,1,0:T(8,128)S(1)} %get-tuple-element.32), channel_id=1, source_target_pairs={{0,2},{1,3},{2,0},{3,1},{4,6},{5,7},{6,4},{7,5},{8,10},{9,11},{10,... | collective-permute-start | bytes 1179656 | tf_op jit(solution)/shard_map/ppermute | solution.py:326
  31.0 11.7 %collective-permute-start.12 = (f32[4,64,384]{2,1,0:T(8,128)S(1)}, f32[4,64,384]{2,1,0:T(8,128)S(1)}, u32[]{:S(2)}, u32[]{:S(2)}) collective-permute-start(f32[4,64,384]{2,1,0:T(8,128)S(1)} %get-tuple-element.33), channel_id=1, source_target_pairs={{0,6},{1,7},{2,4},{3,5},{4,2},{5,3},{6,0},{7,1},{8,14},{9,15},{10,... | collective-permute-start | bytes 1179656 | tf_op jit(solution)/shard_map/ppermute | solution.py:326
  33.1 10.5 %collective-permute-start.13 = (f32[4,64,384]{2,1,0:T(8,128)S(1)}, f32[4,64,384]{2,1,0:T(8,128)S(1)}, u32[]{:S(2)}, u32[]{:S(2)}) collective-permute-start(f32[4,64,384]{2,1,0:T(8,128)S(1)} %get-tuple-element.34), channel_id=1, source_target_pairs={{0,1},{1,0},{2,3},{3,2},{4,5},{5,4},{6,7},{7,6},{8,9},{9,8},{10,11... | collective-permute-start | bytes 1179656 | tf_op jit(solution)/shard_map/ppermute | solution.py:326
  36.9 8.6 %collective-permute-start.14 = (f32[4,64,128]{2,1,0:T(8,128)S(1)}, f32[4,64,128]{2,1,0:T(8,128)S(1)}, u32[]{:S(2)}, u32[]{:S(2)}) collective-permute-start(f32[4,64,128]{2,1,0:T(8,128)S(1)} %get-tuple-element.36), channel_id=1, source_target_pairs={{0,2},{1,3},{2,0},{3,1},{4,6},{5,7},{6,4},{7,5},{8,10},{9,11},{10,... | collective-permute-start | bytes 393224 | tf_op jit(solution)/shard_map/ppermute | solution.py:329
  38.5 7.1 %collective-permute-start.15 = (f32[4,64,128]{2,1,0:T(8,128)S(1)}, f32[4,64,128]{2,1,0:T(8,128)S(1)}, u32[]{:S(2)}, u32[]{:S(2)}) collective-permute-start(f32[4,64,128]{2,1,0:T(8,128)S(1)} %get-tuple-element.37), channel_id=1, source_target_pairs={{0,6},{1,7},{2,4},{3,5},{4,2},{5,3},{6,0},{7,1},{8,14},{9,15},{10,... | collective-permute-start | bytes 393224 | tf_op jit(solution)/shard_map/ppermute | solution.py:329
  40.8 5.0 %collective-permute-start.16 = (f32[4,64,128]{2,1,0:T(8,128)S(1)}, f32[4,64,128]{2,1,0:T(8,128)S(1)}, u32[]{:S(2)}, u32[]{:S(2)}) collective-permute-start(f32[4,64,128]{2,1,0:T(8,128)S(1)} %get-tuple-element.38), channel_id=1, source_target_pairs={{0,1},{1,0},{2,3},{3,2},{4,5},{5,4},{6,7},{7,6},{8,9},{9,8},{10,11... | collective-permute-start | bytes 393224 | tf_op jit(solution)/shard_map/ppermute | solution.py:329
  45.8 6.5 %collective-permute-start.21 = (f32[2,64,512]{2,1,0:T(8,128)S(1)}, f32[2,64,512]{2,1,0:T(8,128)S(1)}, u32[]{:S(2)}, u32[]{:S(2)}) collective-permute-start(f32[2,64,512]{2,1,0:T(8,128)S(1)} %get-tuple-element.59), channel_id=1, source_target_pairs={{0,2},{1,3},{2,0},{3,1},{4,6},{5,7},{6,4},{7,5},{8,10},{9,11},{10,... | collective-permute-start | bytes 786440 | tf_op jit(solution)/shard_map/ppermute | solution.py:335
  47.3 7.7 %collective-permute-start.19 = (f32[2,64,512]{2,1,0:T(8,128)S(1)}, f32[2,64,512]{2,1,0:T(8,128)S(1)}, u32[]{:S(2)}, u32[]{:S(2)}) collective-permute-start(f32[2,64,512]{2,1,0:T(8,128)S(1)} %get-tuple-element.53), channel_id=1, source_target_pairs={{0,1},{1,0},{2,3},{3,2},{4,5},{5,4},{6,7},{7,6},{8,9},{9,8},{10,11... | collective-permute-start | bytes 786440 | tf_op jit(solution)/shard_map/ppermute | solution.py:335
  49.1 7.8 %collective-permute-start.17 = (f32[2,64,512]{2,1,0:T(8,128)S(1)}, f32[2,64,512]{2,1,0:T(8,128)S(1)}, u32[]{:S(2)}, u32[]{:S(2)}) collective-permute-start(f32[2,64,512]{2,1,0:T(8,128)S(1)} %get-tuple-element.47), channel_id=1, source_target_pairs={{0,6},{1,7},{2,4},{3,5},{4,2},{5,3},{6,0},{7,1},{8,14},{9,15},{10,... | collective-permute-start | bytes 786440 | tf_op jit(solution)/shard_map/ppermute | solution.py:335
  52.3 6.3 %collective-permute-start.22 = (f32[1,64,512]{2,1,0:T(8,128)S(1)}, f32[1,64,512]{2,1,0:T(8,128)S(1)}, u32[]{:S(2)}, u32[]{:S(2)}) collective-permute-start(f32[1,64,512]{2,1,0:T(8,128)S(1)} %slice_add_fusion), channel_id=1, source_target_pairs={{0,6},{1,7},{2,4},{3,5},{4,2},{5,3},{6,0},{7,1},{8,14},{9,15},{10,... | collective-permute-start | bytes 393224 | tf_op jit(solution)/shard_map/ppermute | solution.py:337
  55.0 5.1 %collective-permute-start.20 = (f32[1,64,512]{2,1,0:T(8,128)S(1)}, f32[1,64,512]{2,1,0:T(8,128)S(1)}, u32[]{:S(2)}, u32[]{:S(2)}) collective-permute-start(f32[1,64,512]{2,1,0:T(8,128)S(1)} %slice_add_fusion.1), channel_id=1, source_target_pairs={{0,2},{1,3},{2,0},{3,1},{4,6},{5,7},{6,4},{7,5},{8,10},{9,11},{10,... | collective-permute-start | bytes 393224 | tf_op jit(solution)/shard_map/ppermute | solution.py:337
  57.0 5.1 %collective-permute-start.18 = (f32[1,64,512]{2,1,0:T(8,128)S(1)}, f32[1,64,512]{2,1,0:T(8,128)S(1)}, u32[]{:S(2)}, u32[]{:S(2)}) collective-permute-start(f32[1,64,512]{2,1,0:T(8,128)S(1)} %slice_add_fusion.2), channel_id=1, source_target_pairs={{0,1},{1,0},{2,3},{3,2},{4,5},{5,4},{6,7},{7,6},{8,9},{9,8},{10,11... | collective-permute-start | bytes 393224 | tf_op jit(solution)/shard_map/ppermute | solution.py:337
  62.4 1.3 %collective-permute-start.23 = (f32[64,128]{1,0:T(8,128)S(1)}, f32[64,128]{1,0:T(8,128)S(1)}, u32[]{:S(2)}, u32[]{:S(2)}) collective-permute-start(f32[64,128]{1,0:T(8,128)S(1)} %shard_map.58), channel_id=1, source_target_pairs={{0,8},{8,0},{16,24},{24,16},{32,40},{40,32},{48,56},{56,48},{64,72... | collective-permute-start | bytes 98312 | tf_op jit(solution)/shard_map/ppermute | solution.py:294
  63.7 4.7 %collective-permute-start.24 = (f32[64,128]{1,0:T(8,128)S(1)}, f32[64,128]{1,0:T(8,128)S(1)}, u32[]{:S(2)}, u32[]{:S(2)}) collective-permute-start(f32[64,128]{1,0:T(8,128)S(1)} %add.35.refs_0_), channel_id=1, source_target_pairs={{0,16},{8,24},{16,0},{24,8},{32,48},{40,56},{48,32},{56,40},{64,80... | collective-permute-start | bytes 98312 | tf_op jit(solution)/shard_map/ppermute | solution.py:294
  64.2 5.4 %collective-permute-start.25 = (f32[64,128]{1,0:T(8,128)S(1)}, f32[64,128]{1,0:T(8,128)S(1)}, u32[]{:S(2)}, u32[]{:S(2)}) collective-permute-start(f32[64,128]{1,0:T(8,128)S(1)} %add.35.refs_0_), channel_id=1, source_target_pairs={{0,32},{8,40},{16,48},{24,56},{32,0},{40,8},{48,16},{56,24},{64,96... | collective-permute-start | bytes 98312 | tf_op jit(solution)/shard_map/ppermute | solution.py:294
  67.3 5.1 %collective-permute-start.26 = (f32[64,128]{1,0:T(8,128)S(1)}, f32[64,128]{1,0:T(8,128)S(1)}, u32[]{:S(2)}, u32[]{:S(2)}) collective-permute-start(f32[64,128]{1,0:T(8,128)S(1)} %add.35.refs_0_), channel_id=1, source_target_pairs={{0,48},{8,56},{16,32},{24,40},{32,16},{40,24},{48,0},{56,8},{64,11... | collective-permute-start | bytes 98312 | tf_op jit(solution)/shard_map/ppermute | solution.py:294
  72.8 4.8 %collective-permute-start.27 = (f32[136,128]{1,0:T(8,128)S(1)}, f32[136,128]{1,0:T(8,128)S(1)}, u32[]{:S(2)}, u32[]{:S(2)}) collective-permute-start(f32[136,128]{1,0:T(8,128)S(1)} %shard_map.59), channel_id=1, source_target_pairs={{0,2},{1,3},{2,0},{3,1},{4,6},{5,7},{6,4},{7,5},{8,10},{9,11},{10,... | collective-permute-start | bytes 208904 | tf_op jit(solution)/shard_map/ppermute | solution.py:294
  72.9 6.2 %collective-permute-start.28 = (f32[136,128]{1,0:T(8,128)S(1)}, f32[136,128]{1,0:T(8,128)S(1)}, u32[]{:S(2)}, u32[]{:S(2)}) collective-permute-start(f32[136,128]{1,0:T(8,128)S(1)} %shard_map.59), channel_id=1, source_target_pairs={{0,4},{1,5},{2,6},{3,7},{4,0},{5,1},{6,2},{7,3},{8,12},{9,13},{10,... | collective-permute-start | bytes 208904 | tf_op jit(solution)/shard_map/ppermute | solution.py:294
  76.0 5.5 %collective-permute-start.29 = (f32[136,128]{1,0:T(8,128)S(1)}, f32[136,128]{1,0:T(8,128)S(1)}, u32[]{:S(2)}, u32[]{:S(2)}) collective-permute-start(f32[136,128]{1,0:T(8,128)S(1)} %shard_map.59), channel_id=1, source_target_pairs={{0,6},{1,7},{2,4},{3,5},{4,2},{5,3},{6,0},{7,1},{8,14},{9,15},{10,... | collective-permute-start | bytes 208904 | tf_op jit(solution)/shard_map/ppermute | solution.py:294
  81.6 4.8 %collective-permute-start.30 = (f32[136,128]{1,0:T(8,128)S(1)}, f32[136,128]{1,0:T(8,128)S(1)}, u32[]{:S(2)}, u32[]{:S(2)}) collective-permute-start(f32[136,128]{1,0:T(8,128)S(1)} %select_select_fusion.1), channel_id=1, source_target_pairs={{0,1},{1,0},{2,3},{3,2},{4,5},{5,4},{6,7},{7,6},{8,9},{9,8},{10,11... | collective-permute-start | bytes 208904 | tf_op jit(solution)/shard_map/ppermute | solution.py:294
  86.5 4.9 %collective-permute-start.31 = (f32[72,128]{1,0:T(8,128)S(1)}, f32[72,128]{1,0:T(8,128)S(1)}, u32[]{:S(2)}, u32[]{:S(2)}) collective-permute-start(f32[72,128]{1,0:T(8,128)S(1)} %slice.23), channel_id=1, source_target_pairs={{0,64},{8,72},{16,80},{24,88},{32,96},{40,104},{48,112},{56,120},{... | collective-permute-start | bytes 110600 | tf_op jit(solution)/shard_map/ppermute | solution.py:294
  91.5 6.1 %collective-permute-start.32 = (f32[72,128]{1,0:T(8,128)S(1)}, f32[72,128]{1,0:T(8,128)S(1)}, u32[]{:S(2)}, u32[]{:S(2)}) collective-permute-start(f32[72,128]{1,0:T(8,128)S(1)} %slice_add_fusion.3.refs_0_), channel_id=1, source_target_pairs={{0,192},{8,200},{16,208},{24,216},{32,224},{40,232},{48,240},{56,2... | collective-permute-start | bytes 110600 | tf_op jit(solution)/shard_map/ppermute | solution.py:294

commit v4 on v3

--- a/solution.py
+++ b/solution.py
@@ -157,7 +157,7 @@
 
 def gram_body(*refs):
     out = refs[-1]
-    image = tree_sum([r[...] for r in refs[:-1]])
+    image = line_sum([r[...] for r in refs[:-1]])
     gram = lax.dot_general(
         image, image, (((0,), (0,)), ((), ())), precision=lax.Precision.HIGHEST, preferred_element_type=jnp.float32
     )
@@ -220,12 +220,14 @@
 
     left = [spread_row(left_tiles[0], i) for i in range(PANEL)]
     right = [spread_row(right_tiles[0], i) for i in range(PANEL)]
+    pairs = [(i, j) for i in range(PANEL) for j in range(i, PANEL)]
+    pivot = {(i, j): spread_lane(left[i], j) for i, j in pairs}
     for p in range(count):
         start, following = p * PANEL, (p + 1) * PANEL
-        pivot = {(i, j): spread_lane(left[i], start + j) for i in range(PANEL) for j in range(i, PANEL)}
         if p + 1 < count:
             next_left = [spread_row(left_tiles[p + 1], i) for i in range(PANEL)]
             next_right = [spread_row(right_tiles[p + 1], i) for i in range(PANEL)]
+            next_pivot = {(i, j): spread_lane(next_left[i], following + j) for i, j in pairs}
         for k in range(PANEL):
             inverse = lax.rsqrt(pivot[k, k])
             left[k] = left[k] * inverse
@@ -237,10 +239,12 @@
                 for j in range(i, PANEL):
                     pivot[i, j] = pivot[i, j] - upper[i] * upper[j]
             if p + 1 < count:
+                factors = [spread_lane(left[k], following + i) for i in range(PANEL)]
                 for i in range(PANEL):
-                    factor = spread_lane(left[k], following + i)
-                    next_left[i] = next_left[i] - factor * left[k]
-                    next_right[i] = next_right[i] - factor * right[k]
+                    next_left[i] = next_left[i] - factors[i] * left[k]
+                    next_right[i] = next_right[i] - factors[i] * right[k]
+                for i, j in pairs:
+                    next_pivot[i, j] = next_pivot[i, j] - factors[i] * factors[j]
         left_panel, right_panel = gather_rows(left), gather_rows(right)
         work[start:following, :size] = left_panel
         work[start:following, size:] = right_panel
@@ -254,7 +258,7 @@
                 left_tiles[t] = left_tiles[t] - update[span, :size]
                 right_tiles[t] = right_tiles[t] - update[span, size:]
         if p + 1 < count:
-            left, right = next_left, next_right
+            left, right, pivot = next_left, next_right, next_pivot
     upper = jnp.where(cols >= rows, work[:, :size], 0.0)
     triangle_ref[...] = upper.T
     basis_ref[...] = lax.dot_general(
@@ -292,6 +296,11 @@
 def spread(part, axis, shifts):
     perm = samp_perm if axis == "samp" else site_perm
     return [part] + [lax.ppermute(part, axis, perm(k)) for k in shifts]
+
+
+def line_sum(parts):
+    own, two, one, three = parts
+    return (own + one) + (two + three)
 
 
 def local(values, mask, factor):
@@ -339,13 +348,13 @@
     part = kernel_call(band_body, jax.ShapeDtypeStruct((height, columns), f32))(*terms, gathered, factor)
     part = tree_sum(spread(part, "samp", [1]))
     packed = columns // 2 + PANEL
-    message = kernel_call(gram_body, jax.ShapeDtypeStruct((packed + height, columns), f32))(*spread(part, "samp", [2, 4, 6]))
+    message = kernel_call(gram_body, jax.ShapeDtypeStruct((packed + height, columns), f32))(*spread(part, "samp", [4, 2, 6]))
     is_gram = lax.broadcasted_iota(jnp.int32, message.shape, 0) < packed
     apart = which[0]
-    came = spread(message, "site", [2, 4, 6])
+    came = spread(message, "site", [4, 2, 6])
     turn = apart >> 1
-    picked = jnp.where(turn < 2, jnp.where(turn == 0, came[0], came[1]), jnp.where(turn == 2, came[2], came[3]))
-    message = jnp.where(is_gram, tree_sum(came), picked)
+    picked = jnp.where(turn < 2, jnp.where(turn == 0, came[0], came[2]), jnp.where(turn == 2, came[1], came[3]))
+    message = jnp.where(is_gram, line_sum(came), picked)
     came = spread(message, "site", [1])
     message = jnp.where(is_gram, tree_sum(came), jnp.where((apart & 1) == 0, came[0], came[1]))
     gram, own_image = message[:packed], message[packed:]

time: 103 us -> 104 us (level)
  transfers between devices with their start and end apart: 33 -> 33, of which waited for: 18 -> 19; matrix products, arithmetic and copies ran while one was open for 0% -> 0% of each run, Pallas kernels for 6% -> 6%
where the time goes in v4:
time: 104 us
  starting transfers between devices  50.9 us (49%)
  waiting for transfers between devices  36.8 us (35%)
  Pallas kernels  13.5 us (13%)
  other arithmetic  1.49 us (1%)
    ppermute x10, waiting for transfers between devices, spread(): return [part] + [lax.ppermute(part, axis, perm(k)) for k in shifts]  21.6 us
    pallas_call x11, Pallas kernels, call(): pl.pallas_call(body, out_shape=out_shape, in_specs=in_specs, out_specs=ja...  13.5 us
    ppermute x10, starting transfers between devices, spread(): return [part] + [lax.ppermute(part, axis, perm(k)) for k in shifts]  12.4 us
    ppermute x2, starting transfers between devices, gather_line(): top = lax.ppermute(cut(one, 0), 'samp', samp_perm(other))  6.84 us
    ppermute x2, waiting for transfers between devices, gather_line(): top = lax.ppermute(cut(one, 0), 'samp', samp_perm(other))  5.89 us
    ppermute x2, starting transfers between devices, gather_line(): three = lax.ppermute(block, 'samp', samp_perm(other))  5.76 us
    ppermute x3, starting transfers between devices, local(): lax.ppermute(send_near[r], 'site', site_perm(ROUTES[r][0]))  5.54 us
    ppermute x3, starting transfers between devices, local(): lax.ppermute(folded[r][0], 'site', site_perm(ROUTES[r][1]))  5.22 us
  transfers between devices with their start and end apart: 33, of which 19 were waited for; matrix products, arithmetic and copies ran while one was open for 0% of the time, Pallas kernels for 6%

profile of v4, /device:TPU:32, one launch (start us, length us, event | category | flops | bytes accessed | tf_op | source)
XLA Modules:
  0.0 103.7 jit_solution(7151878932437917138)
XLA Ops:
  0.6 1.2 %compare_select_fusion.refs_0_.refs_6_ = bf16[64,2048]{1,0:T(8,128)(2,1)S(1)} fusion(bf16[64,2048]{1,0:T(8,128)(2,1)} %param.3, s32[64,2048]{1,0:T(8,128)} %param.4), kind=kLoop, calls=%fused_computation | loop fusion | flops 262144 | bytes 1048576 | tf_op jit(solution)/shard_map/jit(_where)/select_n | solution.py:310
  1.8 1.7 %collective-permute-start = (bf16[64,2048]{1,0:T(8,128)(2,1)S(1)}, bf16[64,2048]{1,0:T(8,128)(2,1)S(1)}, u32[]{:S(2)}, u32[]{:S(2)}) collective-permute-start(bf16[64,2048]{1,0:T(8,128)(2,1)S(1)} %compare_select_fusion.refs_0_.refs_6_), channel_id=1, source_target_pairs={{0,16},{8,24},{16,0},{24,8},{32,48},{40,56},{48,32},{56,40},{64,80... | collective-permute-start | bytes 786440 | tf_op jit(solution)/shard_map/ppermute | solution.py:289
  3.5 2.2 %collective-permute-start.1 = (bf16[64,2048]{1,0:T(8,128)(2,1)S(1)}, bf16[64,2048]{1,0:T(8,128)(2,1)S(1)}, u32[]{:S(2)}, u32[]{:S(2)}) collective-permute-start(bf16[64,2048]{1,0:T(8,128)(2,1)S(1)} %compare_select_fusion.refs_0_.refs_6_), channel_id=1, source_target_pairs={{0,48},{8,56},{16,32},{24,40},{32,16},{40,24},{48,0},{56,8},{64,11... | collective-permute-start | bytes 786440 | tf_op jit(solution)/shard_map/ppermute | solution.py:290
  5.7 3.4 %collective-permute-start.7 = (bf16[64,2304]{1,0:T(8,128)(2,1)S(1)}, bf16[64,2304]{1,0:T(8,128)(2,1)S(1)}, u32[]{:S(2)}, u32[]{:S(2)}) collective-permute-start(bf16[64,2304]{1,0:T(8,128)(2,1)S(1)} %pad_maximum_fusion), channel_id=1, source_target_pairs={{0,64},{8,72},{16,80},{24,88},{32,96},{40,104},{48,112},{56,120},{... | collective-permute-start | bytes 884744 | tf_op jit(solution)/shard_map/ppermute | solution.py:289
  9.1 3.6 %collective-permute-start.8 = (bf16[64,2304]{1,0:T(8,128)(2,1)S(1)}, bf16[64,2304]{1,0:T(8,128)(2,1)S(1)}, u32[]{:S(2)}, u32[]{:S(2)}) collective-permute-start(bf16[64,2304]{1,0:T(8,128)(2,1)S(1)} %pad_maximum_fusion), channel_id=1, source_target_pairs={{0,192},{8,200},{16,208},{24,216},{32,224},{40,232},{48,240},{56,2... | collective-permute-start | bytes 884744 | tf_op jit(solution)/shard_map/ppermute | solution.py:290
  12.7 1.1 %collective-permute-start.2 = (bf16[32,2048]{1,0:T(8,128)(2,1)S(1)}, bf16[32,2048]{1,0:T(8,128)(2,1)S(1)}, u32[]{:S(2)}, u32[]{:S(2)}) collective-permute-start(bf16[32,2048]{1,0:T(8,128)(2,1)S(1)} %shard_map.50), channel_id=1, source_target_pairs={{0,48},{8,56},{16,32},{24,40},{32,16},{40,24},{48,0},{56,8},{64,11... | collective-permute-start | bytes 393224 | tf_op jit(solution)/shard_map/ppermute | solution.py:291
  14.0 5.9 %collective-permute-done.2 = bf16[32,2048]{1,0:T(8,128)(2,1)S(1)} collective-permute-done((bf16[32,2048]{1,0:T(8,128)(2,1)S(1)}, bf16[32,2048]{1,0:T(8,128)(2,1)S(1)}, u32[]{:S(2)}, u32[]{:S(2)}) %collective-permute-start.2) | collective-permute-done | bytes 131104 | tf_op jit(solution)/shard_map/ppermute | solution.py:291
  19.9 0.6 collective-permute-start.6
  20.7 5.7 %collective-permute-start.9 = (bf16[32,2304]{1,0:T(8,128)(2,1)S(1)}, bf16[32,2304]{1,0:T(8,128)(2,1)S(1)}, u32[]{:S(2)}, u32[]{:S(2)}) collective-permute-start(bf16[32,2304]{1,0:T(8,128)(2,1)S(1)} %split.8), channel_id=1, source_target_pairs={{0,192},{8,200},{16,208},{24,216},{32,224},{40,232},{48,240},{56,2... | collective-permute-start | bytes 442376 | tf_op jit(solution)/shard_map/ppermute | solution.py:291
  26.4 1.0 collective-permute-start.10
  27.4 2.0 %shard_map.52 = (f32[4,64,384]{2,1,0:T(8,128)S(1)}, f32[4,64,384]{2,1,0:T(8,128)S(1)}, f32[4,64,384]{2,1,0:T(8,128)S(1)}) custom-call(s32[1]{0:T(128)} %bitcast.which, bf16[64,2048]{1,0:T(8,128)(2,1)S(1)} %compare_select_fusion.refs_0_.refs_6_, bf16[128,2048]{1,0:T(8,128)(2,1)S(1)} %constant_dynamic-update-slice_fusion.refs_1_, ...), custom_call_target="tpu_custom_call" | custom-call | flops 1000000 | bytes 100000 | tf_op jit(solution)/shard_map/pallas_call | solution.py:51
  29.4 1.6 %collective-permute-start.11 = (f32[4,64,384]{2,1,0:T(8,128)S(1)}, f32[4,64,384]{2,1,0:T(8,128)S(1)}, u32[]{:S(2)}, u32[]{:S(2)}) collective-permute-start(f32[4,64,384]{2,1,0:T(8,128)S(1)} %get-tuple-element.32), channel_id=1, source_target_pairs={{0,2},{1,3},{2,0},{3,1},{4,6},{5,7},{6,4},{7,5},{8,10},{9,11},{10,... | collective-permute-start | bytes 1179656 | tf_op jit(solution)/shard_map/ppermute | solution.py:335
  31.0 2.1 %collective-permute-start.12 = (f32[4,64,384]{2,1,0:T(8,128)S(1)}, f32[4,64,384]{2,1,0:T(8,128)S(1)}, u32[]{:S(2)}, u32[]{:S(2)}) collective-permute-start(f32[4,64,384]{2,1,0:T(8,128)S(1)} %get-tuple-element.33), channel_id=1, source_target_pairs={{0,6},{1,7},{2,4},{3,5},{4,2},{5,3},{6,0},{7,1},{8,14},{9,15},{10,... | collective-permute-start | bytes 1179656 | tf_op jit(solution)/shard_map/ppermute | solution.py:335
  33.1 1.9 %collective-permute-start.13 = (f32[4,64,384]{2,1,0:T(8,128)S(1)}, f32[4,64,384]{2,1,0:T(8,128)S(1)}, u32[]{:S(2)}, u32[]{:S(2)}) collective-permute-start(f32[4,64,384]{2,1,0:T(8,128)S(1)} %get-tuple-element.34), channel_id=1, source_target_pairs={{0,1},{1,0},{2,3},{3,2},{4,5},{5,4},{6,7},{7,6},{8,9},{9,8},{10,11... | collective-permute-start | bytes 1179656 | tf_op jit(solution)/shard_map/ppermute | solution.py:335
  35.0 2.0 %shard_map.53 = (f32[4,64,128]{2,1,0:T(8,128)S(1)}, f32[4,64,128]{2,1,0:T(8,128)S(1)}, f32[4,64,128]{2,1,0:T(8,128)S(1)}) custom-call(s32[1]{0:T(128)} %bitcast.which, bf16[64,2048]{1,0:T(8,128)(2,1)S(1)} %compare_select_fusion.refs_0_.refs_6_, bf16[128,2048]{1,0:T(8,128)(2,1)S(1)} %constant_dynamic-update-slice_fusion.refs_1_, ...), custom_call_target="tpu_custom_call" | custom-call | flops 10000000000 | bytes 100000 | tf_op jit(solution)/shard_map/pallas_call | solution.py:51
  36.9 1.5 %collective-permute-start.14 = (f32[4,64,128]{2,1,0:T(8,128)S(1)}, f32[4,64,128]{2,1,0:T(8,128)S(1)}, u32[]{:S(2)}, u32[]{:S(2)}) collective-permute-start(f32[4,64,128]{2,1,0:T(8,128)S(1)} %get-tuple-element.36), channel_id=1, source_target_pairs={{0,2},{1,3},{2,0},{3,1},{4,6},{5,7},{6,4},{7,5},{8,10},{9,11},{10,... | collective-permute-start | bytes 393224 | tf_op jit(solution)/shard_map/ppermute | solution.py:338
  38.5 2.3 %collective-permute-start.15 = (f32[4,64,128]{2,1,0:T(8,128)S(1)}, f32[4,64,128]{2,1,0:T(8,128)S(1)}, u32[]{:S(2)}, u32[]{:S(2)}) collective-permute-start(f32[4,64,128]{2,1,0:T(8,128)S(1)} %get-tuple-element.37), channel_id=1, source_target_pairs={{0,6},{1,7},{2,4},{3,5},{4,2},{5,3},{6,0},{7,1},{8,14},{9,15},{10,... | collective-permute-start | bytes 393224 | tf_op jit(solution)/shard_map/ppermute | solution.py:338
  40.8 1.4 %collective-permute-start.16 = (f32[4,64,128]{2,1,0:T(8,128)S(1)}, f32[4,64,128]{2,1,0:T(8,128)S(1)}, u32[]{:S(2)}, u32[]{:S(2)}) collective-permute-start(f32[4,64,128]{2,1,0:T(8,128)S(1)} %get-tuple-element.38), channel_id=1, source_target_pairs={{0,1},{1,0},{2,3},{3,2},{4,5},{5,4},{6,7},{7,6},{8,9},{9,8},{10,11... | collective-permute-start | bytes 393224 | tf_op jit(solution)/shard_map/ppermute | solution.py:338
  42.1 0.6 collective-permute-done.12.near
  42.7 0.8 collective-permute-done.13.near
  43.5 2.0 %shard_map.54 = (f32[4,64,512]{2,1,0:T(8,128)S(1)}, f32[4,64,512]{2,1,0:T(8,128)S(1)}, f32[4,64,512]{2,1,0:T(8,128)S(1)}, f32[192,128]{1,0:T(8,128)S(1)}) custom-call(s32[1]{0:T(128)} %bitcast.which, bf16[64,2048]{1,0:T(8,128)(2,1)S(1)} %compare_select_fusion.refs_0_.refs_6_, bf16[128,2048]{1,0:T(8,128)(2,1)S(1)} %constant_dynamic-update-slice_fusion.refs_1_, ...), custom_call_target="tpu_custom_call" | custom-call | flops 10000000000 | bytes 100000 | tf_op jit(solution)/shard_map/pallas_call | solution.py:51
  45.8 1.4 %collective-permute-start.21 = (f32[2,64,512]{2,1,0:T(8,128)S(1)}, f32[2,64,512]{2,1,0:T(8,128)S(1)}, u32[]{:S(2)}, u32[]{:S(2)}) collective-permute-start(f32[2,64,512]{2,1,0:T(8,128)S(1)} %get-tuple-element.59), channel_id=1, source_target_pairs={{0,2},{1,3},{2,0},{3,1},{4,6},{5,7},{6,4},{7,5},{8,10},{9,11},{10,... | collective-permute-start | bytes 786440 | tf_op jit(solution)/shard_map/ppermute | solution.py:344
  47.3 1.8 %collective-permute-start.19 = (f32[2,64,512]{2,1,0:T(8,128)S(1)}, f32[2,64,512]{2,1,0:T(8,128)S(1)}, u32[]{:S(2)}, u32[]{:S(2)}) collective-permute-start(f32[2,64,512]{2,1,0:T(8,128)S(1)} %get-tuple-element.53), channel_id=1, source_target_pairs={{0,1},{1,0},{2,3},{3,2},{4,5},{5,4},{6,7},{7,6},{8,9},{9,8},{10,11... | collective-permute-start | bytes 786440 | tf_op jit(solution)/shard_map/ppermute | solution.py:344
  49.1 2.0 %collective-permute-start.17 = (f32[2,64,512]{2,1,0:T(8,128)S(1)}, f32[2,64,512]{2,1,0:T(8,128)S(1)}, u32[]{:S(2)}, u32[]{:S(2)}) collective-permute-start(f32[2,64,512]{2,1,0:T(8,128)S(1)} %get-tuple-element.47), channel_id=1, source_target_pairs={{0,6},{1,7},{2,4},{3,5},{4,2},{5,3},{6,0},{7,1},{8,14},{9,15},{10,... | collective-permute-start | bytes 786440 | tf_op jit(solution)/shard_map/ppermute | solution.py:344
  51.1 1.1 %collective-permute-done.21.refs_7_ = f32[2,64,512]{2,1,0:T(8,128)S(1)} collective-permute-done((f32[2,64,512]{2,1,0:T(8,128)S(1)}, f32[2,64,512]{2,1,0:T(8,128)S(1)}, u32[]{:S(2)}, u32[]{:S(2)}) %collective-permute-start.21) | collective-permute-done | bytes 262176 | tf_op jit(solution)/shard_map/ppermute | solution.py:344
  52.3 2.7 %collective-permute-start.22 = (f32[1,64,512]{2,1,0:T(8,128)S(1)}, f32[1,64,512]{2,1,0:T(8,128)S(1)}, u32[]{:S(2)}, u32[]{:S(2)}) collective-permute-start(f32[1,64,512]{2,1,0:T(8,128)S(1)} %slice_add_fusion), channel_id=1, source_target_pairs={{0,6},{1,7},{2,4},{3,5},{4,2},{5,3},{6,0},{7,1},{8,14},{9,15},{10,... | collective-permute-start | bytes 393224 | tf_op jit(solution)/shard_map/ppermute | solution.py:346
  55.1 1.9 %collective-permute-done.17.refs_1_ = f32[2,64,512]{2,1,0:T(8,128)S(1)} collective-permute-done((f32[2,64,512]{2,1,0:T(8,128)S(1)}, f32[2,64,512]{2,1,0:T(8,128)S(1)}, u32[]{:S(2)}, u32[]{:S(2)}) %collective-permute-start.17) | collective-permute-done | bytes 262176 | tf_op jit(solution)/shard_map/ppermute | solution.py:344
  57.0 0.5 collective-permute-start.18
  57.5 1.0 collective-permute-done.22.refs_8_
  58.6 1.5 %collective-permute-done.20.refs_5_ = f32[1,64,512]{2,1,0:T(8,128)S(1)} collective-permute-done((f32[1,64,512]{2,1,0:T(8,128)S(1)}, f32[1,64,512]{2,1,0:T(8,128)S(1)}, u32[]{:S(2)}, u32[]{:S(2)}) %collective-permute-start.20) | collective-permute-done | bytes 131104 | tf_op jit(solution)/shard_map/ppermute | solution.py:346
  60.0 2.0 %collective-permute-done.18.refs_2_ = f32[1,64,512]{2,1,0:T(8,128)S(1)} collective-permute-done((f32[1,64,512]{2,1,0:T(8,128)S(1)}, f32[1,64,512]{2,1,0:T(8,128)S(1)}, u32[]{:S(2)}, u32[]{:S(2)}) %collective-permute-start.18) | collective-permute-done | bytes 131104 | tf_op jit(solution)/shard_map/ppermute | solution.py:346
  62.5 1.2 %collective-permute-done.23 = f32[64,128]{1,0:T(8,128)S(1)} collective-permute-done((f32[64,128]{1,0:T(8,128)S(1)}, f32[64,128]{1,0:T(8,128)S(1)}, u32[]{:S(2)}, u32[]{:S(2)}) %collective-permute-start.23) | collective-permute-done | bytes 32800 | tf_op jit(solution)/shard_map/ppermute | solution.py:298
  63.7 1.9 %collective-permute-start.24 = (f32[64,128]{1,0:T(8,128)S(1)}, f32[64,128]{1,0:T(8,128)S(1)}, u32[]{:S(2)}, u32[]{:S(2)}) collective-permute-start(f32[64,128]{1,0:T(8,128)S(1)} %add.35.refs_0_), channel_id=1, source_target_pairs={{0,32},{8,40},{16,48},{24,56},{32,0},{40,8},{48,16},{56,24},{64,96... | collective-permute-start | bytes 98312 | tf_op jit(solution)/shard_map/ppermute | solution.py:298
  65.6 1.0 %collective-permute-start.25 = (f32[64,128]{1,0:T(8,128)S(1)}, f32[64,128]{1,0:T(8,128)S(1)}, u32[]{:S(2)}, u32[]{:S(2)}) collective-permute-start(f32[64,128]{1,0:T(8,128)S(1)} %add.35.refs_0_), channel_id=1, source_target_pairs={{0,16},{8,24},{16,0},{24,8},{32,48},{40,56},{48,32},{56,40},{64,80... | collective-permute-start | bytes 98312 | tf_op jit(solution)/shard_map/ppermute | solution.py:298
  66.7 1.1 %collective-permute-start.26 = (f32[64,128]{1,0:T(8,128)S(1)}, f32[64,128]{1,0:T(8,128)S(1)}, u32[]{:S(2)}, u32[]{:S(2)}) collective-permute-start(f32[64,128]{1,0:T(8,128)S(1)} %add.35.refs_0_), channel_id=1, source_target_pairs={{0,48},{8,56},{16,32},{24,40},{32,16},{40,24},{48,0},{56,8},{64,11... | collective-permute-start | bytes 98312 | tf_op jit(solution)/shard_map/ppermute | solution.py:298
  67.8 1.6 %collective-permute-done.24.refs_1_ = f32[64,128]{1,0:T(8,128)S(1)} collective-permute-done((f32[64,128]{1,0:T(8,128)S(1)}, f32[64,128]{1,0:T(8,128)S(1)}, u32[]{:S(2)}, u32[]{:S(2)}) %collective-permute-start.24) | collective-permute-done | bytes 32800 | tf_op jit(solution)/shard_map/ppermute | solution.py:298
  69.6 2.3 %collective-permute-done.26.refs_3_ = f32[64,128]{1,0:T(8,128)S(1)} collective-permute-done((f32[64,128]{1,0:T(8,128)S(1)}, f32[64,128]{1,0:T(8,128)S(1)}, u32[]{:S(2)}, u32[]{:S(2)}) %collective-permute-start.26) | collective-permute-done | bytes 32800 | tf_op jit(solution)/shard_map/ppermute | solution.py:298
  72.3 3.1 %collective-permute-start.28 = (f32[136,128]{1,0:T(8,128)S(1)}, f32[136,128]{1,0:T(8,128)S(1)}, u32[]{:S(2)}, u32[]{:S(2)}) collective-permute-start(f32[136,128]{1,0:T(8,128)S(1)} %shard_map.59), channel_id=1, source_target_pairs={{0,4},{1,5},{2,6},{3,7},{4,0},{5,1},{6,2},{7,3},{8,12},{9,13},{10,... | collective-permute-start | bytes 208904 | tf_op jit(solution)/shard_map/ppermute | solution.py:298
  75.4 1.5 %collective-permute-start.29 = (f32[136,128]{1,0:T(8,128)S(1)}, f32[136,128]{1,0:T(8,128)S(1)}, u32[]{:S(2)}, u32[]{:S(2)}) collective-permute-start(f32[136,128]{1,0:T(8,128)S(1)} %shard_map.59), channel_id=1, source_target_pairs={{0,6},{1,7},{2,4},{3,5},{4,2},{5,3},{6,0},{7,1},{8,14},{9,15},{10,... | collective-permute-start | bytes 208904 | tf_op jit(solution)/shard_map/ppermute | solution.py:298
  76.9 1.6 %collective-permute-done.28 = f32[136,128]{1,0:T(8,128)S(1)} collective-permute-done((f32[136,128]{1,0:T(8,128)S(1)}, f32[136,128]{1,0:T(8,128)S(1)}, u32[]{:S(2)}, u32[]{:S(2)}) %collective-permute-start.28) | collective-permute-done | bytes 69664 | tf_op jit(solution)/shard_map/ppermute | solution.py:298
  78.5 2.4 %collective-permute-done.29 = f32[136,128]{1,0:T(8,128)S(1)} collective-permute-done((f32[136,128]{1,0:T(8,128)S(1)}, f32[136,128]{1,0:T(8,128)S(1)}, u32[]{:S(2)}, u32[]{:S(2)}) %collective-permute-start.29) | collective-permute-done | bytes 69664 | tf_op jit(solution)/shard_map/ppermute | solution.py:298
  81.0 1.4 %collective-permute-start.30 = (f32[136,128]{1,0:T(8,128)S(1)}, f32[136,128]{1,0:T(8,128)S(1)}, u32[]{:S(2)}, u32[]{:S(2)}) collective-permute-start(f32[136,128]{1,0:T(8,128)S(1)} %select_select_fusion.1), channel_id=1, source_target_pairs={{0,1},{1,0},{2,3},{3,2},{4,5},{5,4},{6,7},{7,6},{8,9},{9,8},{10,11... | collective-permute-start | bytes 208904 | tf_op jit(solution)/shard_map/ppermute | solution.py:298
  82.4 3.4 %collective-permute-done.30 = f32[136,128]{1,0:T(8,128)S(1)} collective-permute-done((f32[136,128]{1,0:T(8,128)S(1)}, f32[136,128]{1,0:T(8,128)S(1)}, u32[]{:S(2)}, u32[]{:S(2)}) %collective-permute-start.30) | collective-permute-done | bytes 69664 | tf_op jit(solution)/shard_map/ppermute | solution.py:298
  85.9 1.1 %collective-permute-start.31 = (f32[72,128]{1,0:T(8,128)S(1)}, f32[72,128]{1,0:T(8,128)S(1)}, u32[]{:S(2)}, u32[]{:S(2)}) collective-permute-start(f32[72,128]{1,0:T(8,128)S(1)} %slice.23), channel_id=1, source_target_pairs={{0,64},{8,72},{16,80},{24,88},{32,96},{40,104},{48,112},{56,120},{... | collective-permute-start | bytes 110600 | tf_op jit(solution)/shard_map/ppermute | solution.py:298
  87.0 3.9 %collective-permute-done.31 = f32[72,128]{1,0:T(8,128)S(1)} collective-permute-done((f32[72,128]{1,0:T(8,128)S(1)}, f32[72,128]{1,0:T(8,128)S(1)}, u32[]{:S(2)}, u32[]{:S(2)}) %collective-permute-start.31) | collective-permute-done | bytes 36896 | tf_op jit(solution)/shard_map/ppermute | solution.py:298
  90.9 0.9 collective-permute-start.32
  91.8 5.2 %collective-permute-done.32.refs_1_ = f32[72,128]{1,0:T(8,128)S(1)} collective-permute-done((f32[72,128]{1,0:T(8,128)S(1)}, f32[72,128]{1,0:T(8,128)S(1)}, u32[]{:S(2)}, u32[]{:S(2)}) %collective-permute-start.32) | collective-permute-done | bytes 36896 | tf_op jit(solution)/shard_map/ppermute | solution.py:298
  97.0 6.7 %shard_map.60 = (f32[64,128]{1,0:T(8,128)}, f32[128,128]{1,0:T(8,128)}) custom-call(f32[72,128]{1,0:T(8,128)S(1)} %slice_add_fusion.3.refs_0_, f32[72,128]{1,0:T(8,128)S(1)} %collective-permute-done.32.refs_1_, f32[64,128]{1,0:T(8,128)S(1)} %slice.24.refs_2_), custom_call_target="tpu_custom_call" | custom-call | tf_op jit(solution)/shard_map/pallas_call | solution.py:51
  (50 shorter events, 2.3 us)
Async XLA Ops:
  0.6 5.1 %copy-start = (f32[64,128]{1,0:T(8,128)S(1)}, f32[64,128]{1,0:T(8,128)}, u32[]{:S(2)}) copy-start(f32[64,128]{1,0:T(8,128)} %refs_10_.1) | copy-start | bytes 98308
  1.8 10.8 %collective-permute-start = (bf16[64,2048]{1,0:T(8,128)(2,1)S(1)}, bf16[64,2048]{1,0:T(8,128)(2,1)S(1)}, u32[]{:S(2)}, u32[]{:S(2)}) collective-permute-start(bf16[64,2048]{1,0:T(8,128)(2,1)S(1)} %compare_select_fusion.refs_0_.refs_6_), channel_id=1, source_target_pairs={{0,16},{8,24},{16,0},{24,8},{32,48},{40,56},{48,32},{56,40},{64,80... | collective-permute-start | bytes 786440 | tf_op jit(solution)/shard_map/ppermute | solution.py:289
  3.5 10.3 %collective-permute-start.1 = (bf16[64,2048]{1,0:T(8,128)(2,1)S(1)}, bf16[64,2048]{1,0:T(8,128)(2,1)S(1)}, u32[]{:S(2)}, u32[]{:S(2)}) collective-permute-start(bf16[64,2048]{1,0:T(8,128)(2,1)S(1)} %compare_select_fusion.refs_0_.refs_6_), channel_id=1, source_target_pairs={{0,48},{8,56},{16,32},{24,40},{32,16},{40,24},{48,0},{56,8},{64,11... | collective-permute-start | bytes 786440 | tf_op jit(solution)/shard_map/ppermute | solution.py:290
  5.7 15.0 %collective-permute-start.7 = (bf16[64,2304]{1,0:T(8,128)(2,1)S(1)}, bf16[64,2304]{1,0:T(8,128)(2,1)S(1)}, u32[]{:S(2)}, u32[]{:S(2)}) collective-permute-start(bf16[64,2304]{1,0:T(8,128)(2,1)S(1)} %pad_maximum_fusion), channel_id=1, source_target_pairs={{0,64},{8,72},{16,80},{24,88},{32,96},{40,104},{48,112},{56,120},{... | collective-permute-start | bytes 884744 | tf_op jit(solution)/shard_map/ppermute | solution.py:289
  9.1 17.3 %collective-permute-start.8 = (bf16[64,2304]{1,0:T(8,128)(2,1)S(1)}, bf16[64,2304]{1,0:T(8,128)(2,1)S(1)}, u32[]{:S(2)}, u32[]{:S(2)}) collective-permute-start(bf16[64,2304]{1,0:T(8,128)(2,1)S(1)} %pad_maximum_fusion), channel_id=1, source_target_pairs={{0,192},{8,200},{16,208},{24,216},{32,224},{40,232},{48,240},{56,2... | collective-permute-start | bytes 884744 | tf_op jit(solution)/shard_map/ppermute | solution.py:290
  12.7 14.8 %collective-permute-start.4 = (bf16[64,2048]{1,0:T(8,128)(2,1)S(1)}, bf16[64,2048]{1,0:T(8,128)(2,1)S(1)}, u32[]{:S(2)}, u32[]{:S(2)}) collective-permute-start(bf16[64,2048]{1,0:T(8,128)(2,1)S(1)} %compare_select_fusion.refs_0_.refs_6_), channel_id=1, source_target_pairs={{0,8},{8,0},{16,24},{24,16},{32,40},{40,32},{48,56},{56,48},{64,72... | collective-permute-start | bytes 786440 | tf_op jit(solution)/shard_map/ppermute | solution.py:317
  12.7 7.2 %collective-permute-start.2 = (bf16[32,2048]{1,0:T(8,128)(2,1)S(1)}, bf16[32,2048]{1,0:T(8,128)(2,1)S(1)}, u32[]{:S(2)}, u32[]{:S(2)}) collective-permute-start(bf16[32,2048]{1,0:T(8,128)(2,1)S(1)} %shard_map.50), channel_id=1, source_target_pairs={{0,48},{8,56},{16,32},{24,40},{32,16},{40,24},{48,0},{56,8},{64,11... | collective-permute-start | bytes 393224 | tf_op jit(solution)/shard_map/ppermute | solution.py:291
  13.8 6.1 %collective-permute-start.3 = (bf16[32,2048]{1,0:T(8,128)(2,1)S(1)}, bf16[32,2048]{1,0:T(8,128)(2,1)S(1)}, u32[]{:S(2)}, u32[]{:S(2)}) collective-permute-start(bf16[32,2048]{1,0:T(8,128)(2,1)S(1)} %shard_map.51), channel_id=1, source_target_pairs={{0,16},{8,24},{16,0},{24,8},{32,48},{40,56},{48,32},{56,40},{64,80... | collective-permute-start | bytes 393224 | tf_op jit(solution)/shard_map/ppermute | solution.py:292
  19.9 7.5 %collective-permute-start.5 = (bf16[128,2048]{1,0:T(8,128)(2,1)S(1)}, bf16[128,2048]{1,0:T(8,128)(2,1)S(1)}, u32[]{:S(2)}, u32[]{:S(2)}) collective-permute-start(bf16[128,2048]{1,0:T(8,128)(2,1)S(1)} %constant_dynamic-update-slice_fusion.refs_1_), channel_id=1, source_target_pairs={{0,8},{8,0},{16,24},{24,16},{32,40},{40,32},{48,56},{56,48},{64,72... | collective-permute-start | bytes 1572872 | tf_op jit(solution)/shard_map/ppermute | solution.py:317
  19.9 7.5 %collective-permute-start.6 = (bf16[64,2048]{1,0:T(8,128)(2,1)S(1)}, bf16[64,2048]{1,0:T(8,128)(2,1)S(1)}, u32[]{:S(2)}, u32[]{:S(2)}) collective-permute-start(bf16[64,2048]{1,0:T(8,128)(2,1)S(1)} %constant_dynamic-update-slice_fusion.2.refs_2_), channel_id=1, source_target_pairs={{0,8},{8,0},{16,24},{24,16},{32,40},{40,32},{48,56},{56,48},{64,72... | collective-permute-start | bytes 786440 | tf_op jit(solution)/shard_map/ppermute | solution.py:317
  20.7 14.2 %collective-permute-start.9 = (bf16[32,2304]{1,0:T(8,128)(2,1)S(1)}, bf16[32,2304]{1,0:T(8,128)(2,1)S(1)}, u32[]{:S(2)}, u32[]{:S(2)}) collective-permute-start(bf16[32,2304]{1,0:T(8,128)(2,1)S(1)} %split.8), channel_id=1, source_target_pairs={{0,192},{8,200},{16,208},{24,216},{32,224},{40,232},{48,240},{56,2... | collective-permute-start | bytes 442376 | tf_op jit(solution)/shard_map/ppermute | solution.py:291
  26.4 8.5 %collective-permute-start.10 = (bf16[32,2304]{1,0:T(8,128)(2,1)S(1)}, bf16[32,2304]{1,0:T(8,128)(2,1)S(1)}, u32[]{:S(2)}, u32[]{:S(2)}) collective-permute-start(bf16[32,2304]{1,0:T(8,128)(2,1)S(1)} %split.9), channel_id=1, source_target_pairs={{0,64},{8,72},{16,80},{24,88},{32,96},{40,104},{48,112},{56,120},{... | collective-permute-start | bytes 442376 | tf_op jit(solution)/shard_map/ppermute | solution.py:292
  29.4 11.4 %collective-permute-start.11 = (f32[4,64,384]{2,1,0:T(8,128)S(1)}, f32[4,64,384]{2,1,0:T(8,128)S(1)}, u32[]{:S(2)}, u32[]{:S(2)}) collective-permute-start(f32[4,64,384]{2,1,0:T(8,128)S(1)} %get-tuple-element.32), channel_id=1, source_target_pairs={{0,2},{1,3},{2,0},{3,1},{4,6},{5,7},{6,4},{7,5},{8,10},{9,11},{10,... | collective-permute-start | bytes 1179656 | tf_op jit(solution)/shard_map/ppermute | solution.py:335
  31.0 11.7 %collective-permute-start.12 = (f32[4,64,384]{2,1,0:T(8,128)S(1)}, f32[4,64,384]{2,1,0:T(8,128)S(1)}, u32[]{:S(2)}, u32[]{:S(2)}) collective-permute-start(f32[4,64,384]{2,1,0:T(8,128)S(1)} %get-tuple-element.33), channel_id=1, source_target_pairs={{0,6},{1,7},{2,4},{3,5},{4,2},{5,3},{6,0},{7,1},{8,14},{9,15},{10,... | collective-permute-start | bytes 1179656 | tf_op jit(solution)/shard_map/ppermute | solution.py:335
  33.1 10.5 %collective-permute-start.13 = (f32[4,64,384]{2,1,0:T(8,128)S(1)}, f32[4,64,384]{2,1,0:T(8,128)S(1)}, u32[]{:S(2)}, u32[]{:S(2)}) collective-permute-start(f32[4,64,384]{2,1,0:T(8,128)S(1)} %get-tuple-element.34), channel_id=1, source_target_pairs={{0,1},{1,0},{2,3},{3,2},{4,5},{5,4},{6,7},{7,6},{8,9},{9,8},{10,11... | collective-permute-start | bytes 1179656 | tf_op jit(solution)/shard_map/ppermute | solution.py:335
  36.9 8.6 %collective-permute-start.14 = (f32[4,64,128]{2,1,0:T(8,128)S(1)}, f32[4,64,128]{2,1,0:T(8,128)S(1)}, u32[]{:S(2)}, u32[]{:S(2)}) collective-permute-start(f32[4,64,128]{2,1,0:T(8,128)S(1)} %get-tuple-element.36), channel_id=1, source_target_pairs={{0,2},{1,3},{2,0},{3,1},{4,6},{5,7},{6,4},{7,5},{8,10},{9,11},{10,... | collective-permute-start | bytes 393224 | tf_op jit(solution)/shard_map/ppermute | solution.py:338
  38.5 7.1 %collective-permute-start.15 = (f32[4,64,128]{2,1,0:T(8,128)S(1)}, f32[4,64,128]{2,1,0:T(8,128)S(1)}, u32[]{:S(2)}, u32[]{:S(2)}) collective-permute-start(f32[4,64,128]{2,1,0:T(8,128)S(1)} %get-tuple-element.37), channel_id=1, source_target_pairs={{0,6},{1,7},{2,4},{3,5},{4,2},{5,3},{6,0},{7,1},{8,14},{9,15},{10,... | collective-permute-start | bytes 393224 | tf_op jit(solution)/shard_map/ppermute | solution.py:338
  40.8 5.0 %collective-permute-start.16 = (f32[4,64,128]{2,1,0:T(8,128)S(1)}, f32[4,64,128]{2,1,0:T(8,128)S(1)}, u32[]{:S(2)}, u32[]{:S(2)}) collective-permute-start(f32[4,64,128]{2,1,0:T(8,128)S(1)} %get-tuple-element.38), channel_id=1, source_target_pairs={{0,1},{1,0},{2,3},{3,2},{4,5},{5,4},{6,7},{7,6},{8,9},{9,8},{10,11... | collective-permute-start | bytes 393224 | tf_op jit(solution)/shard_map/ppermute | solution.py:338
  45.8 6.5 %collective-permute-start.21 = (f32[2,64,512]{2,1,0:T(8,128)S(1)}, f32[2,64,512]{2,1,0:T(8,128)S(1)}, u32[]{:S(2)}, u32[]{:S(2)}) collective-permute-start(f32[2,64,512]{2,1,0:T(8,128)S(1)} %get-tuple-element.59), channel_id=1, source_target_pairs={{0,2},{1,3},{2,0},{3,1},{4,6},{5,7},{6,4},{7,5},{8,10},{9,11},{10,... | collective-permute-start | bytes 786440 | tf_op jit(solution)/shard_map/ppermute | solution.py:344
  47.3 7.7 %collective-permute-start.19 = (f32[2,64,512]{2,1,0:T(8,128)S(1)}, f32[2,64,512]{2,1,0:T(8,128)S(1)}, u32[]{:S(2)}, u32[]{:S(2)}) collective-permute-start(f32[2,64,512]{2,1,0:T(8,128)S(1)} %get-tuple-element.53), channel_id=1, source_target_pairs={{0,1},{1,0},{2,3},{3,2},{4,5},{5,4},{6,7},{7,6},{8,9},{9,8},{10,11... | collective-permute-start | bytes 786440 | tf_op jit(solution)/shard_map/ppermute | solution.py:344
  49.1 7.8 %collective-permute-start.17 = (f32[2,64,512]{2,1,0:T(8,128)S(1)}, f32[2,64,512]{2,1,0:T(8,128)S(1)}, u32[]{:S(2)}, u32[]{:S(2)}) collective-permute-start(f32[2,64,512]{2,1,0:T(8,128)S(1)} %get-tuple-element.47), channel_id=1, source_target_pairs={{0,6},{1,7},{2,4},{3,5},{4,2},{5,3},{6,0},{7,1},{8,14},{9,15},{10,... | collective-permute-start | bytes 786440 | tf_op jit(solution)/shard_map/ppermute | solution.py:344
  52.3 6.3 %collective-permute-start.22 = (f32[1,64,512]{2,1,0:T(8,128)S(1)}, f32[1,64,512]{2,1,0:T(8,128)S(1)}, u32[]{:S(2)}, u32[]{:S(2)}) collective-permute-start(f32[1,64,512]{2,1,0:T(8,128)S(1)} %slice_add_fusion), channel_id=1, source_target_pairs={{0,6},{1,7},{2,4},{3,5},{4,2},{5,3},{6,0},{7,1},{8,14},{9,15},{10,... | collective-permute-start | bytes 393224 | tf_op jit(solution)/shard_map/ppermute | solution.py:346
  55.0 5.1 %collective-permute-start.20 = (f32[1,64,512]{2,1,0:T(8,128)S(1)}, f32[1,64,512]{2,1,0:T(8,128)S(1)}, u32[]{:S(2)}, u32[]{:S(2)}) collective-permute-start(f32[1,64,512]{2,1,0:T(8,128)S(1)} %slice_add_fusion.1), channel_id=1, source_target_pairs={{0,2},{1,3},{2,0},{3,1},{4,6},{5,7},{6,4},{7,5},{8,10},{9,11},{10,... | collective-permute-start | bytes 393224 | tf_op jit(solution)/shard_map/ppermute | solution.py:346
  57.0 5.1 %collective-permute-start.18 = (f32[1,64,512]{2,1,0:T(8,128)S(1)}, f32[1,64,512]{2,1,0:T(8,128)S(1)}, u32[]{:S(2)}, u32[]{:S(2)}) collective-permute-start(f32[1,64,512]{2,1,0:T(8,128)S(1)} %slice_add_fusion.2), channel_id=1, source_target_pairs={{0,1},{1,0},{2,3},{3,2},{4,5},{5,4},{6,7},{7,6},{8,9},{9,8},{10,11... | collective-permute-start | bytes 393224 | tf_op jit(solution)/shard_map/ppermute | solution.py:346
  62.4 1.3 %collective-permute-start.23 = (f32[64,128]{1,0:T(8,128)S(1)}, f32[64,128]{1,0:T(8,128)S(1)}, u32[]{:S(2)}, u32[]{:S(2)}) collective-permute-start(f32[64,128]{1,0:T(8,128)S(1)} %shard_map.58), channel_id=1, source_target_pairs={{0,8},{8,0},{16,24},{24,16},{32,40},{40,32},{48,56},{56,48},{64,72... | collective-permute-start | bytes 98312 | tf_op jit(solution)/shard_map/ppermute | solution.py:298
  63.7 5.7 %collective-permute-start.24 = (f32[64,128]{1,0:T(8,128)S(1)}, f32[64,128]{1,0:T(8,128)S(1)}, u32[]{:S(2)}, u32[]{:S(2)}) collective-permute-start(f32[64,128]{1,0:T(8,128)S(1)} %add.35.refs_0_), channel_id=1, source_target_pairs={{0,32},{8,40},{16,48},{24,56},{32,0},{40,8},{48,16},{56,24},{64,96... | collective-permute-start | bytes 98312 | tf_op jit(solution)/shard_map/ppermute | solution.py:298
  65.6 3.9 %collective-permute-start.25 = (f32[64,128]{1,0:T(8,128)S(1)}, f32[64,128]{1,0:T(8,128)S(1)}, u32[]{:S(2)}, u32[]{:S(2)}) collective-permute-start(f32[64,128]{1,0:T(8,128)S(1)} %add.35.refs_0_), channel_id=1, source_target_pairs={{0,16},{8,24},{16,0},{24,8},{32,48},{40,56},{48,32},{56,40},{64,80... | collective-permute-start | bytes 98312 | tf_op jit(solution)/shard_map/ppermute | solution.py:298
  66.7 5.1 %collective-permute-start.26 = (f32[64,128]{1,0:T(8,128)S(1)}, f32[64,128]{1,0:T(8,128)S(1)}, u32[]{:S(2)}, u32[]{:S(2)}) collective-permute-start(f32[64,128]{1,0:T(8,128)S(1)} %add.35.refs_0_), channel_id=1, source_target_pairs={{0,48},{8,56},{16,32},{24,40},{32,16},{40,24},{48,0},{56,8},{64,11... | collective-permute-start | bytes 98312 | tf_op jit(solution)/shard_map/ppermute | solution.py:298
  72.2 4.8 %collective-permute-start.27 = (f32[136,128]{1,0:T(8,128)S(1)}, f32[136,128]{1,0:T(8,128)S(1)}, u32[]{:S(2)}, u32[]{:S(2)}) collective-permute-start(f32[136,128]{1,0:T(8,128)S(1)} %shard_map.59), channel_id=1, source_target_pairs={{0,2},{1,3},{2,0},{3,1},{4,6},{5,7},{6,4},{7,5},{8,10},{9,11},{10,... | collective-permute-start | bytes 208904 | tf_op jit(solution)/shard_map/ppermute | solution.py:298
  72.3 6.2 %collective-permute-start.28 = (f32[136,128]{1,0:T(8,128)S(1)}, f32[136,128]{1,0:T(8,128)S(1)}, u32[]{:S(2)}, u32[]{:S(2)}) collective-permute-start(f32[136,128]{1,0:T(8,128)S(1)} %shard_map.59), channel_id=1, source_target_pairs={{0,4},{1,5},{2,6},{3,7},{4,0},{5,1},{6,2},{7,3},{8,12},{9,13},{10,... | collective-permute-start | bytes 208904 | tf_op jit(solution)/shard_map/ppermute | solution.py:298
  75.4 5.5 %collective-permute-start.29 = (f32[136,128]{1,0:T(8,128)S(1)}, f32[136,128]{1,0:T(8,128)S(1)}, u32[]{:S(2)}, u32[]{:S(2)}) collective-permute-start(f32[136,128]{1,0:T(8,128)S(1)} %shard_map.59), channel_id=1, source_target_pairs={{0,6},{1,7},{2,4},{3,5},{4,2},{5,3},{6,0},{7,1},{8,14},{9,15},{10,... | collective-permute-start | bytes 208904 | tf_op jit(solution)/shard_map/ppermute | solution.py:298
  81.0 4.8 %collective-permute-start.30 = (f32[136,128]{1,0:T(8,128)S(1)}, f32[136,128]{1,0:T(8,128)S(1)}, u32[]{:S(2)}, u32[]{:S(2)}) collective-permute-start(f32[136,128]{1,0:T(8,128)S(1)} %select_select_fusion.1), channel_id=1, source_target_pairs={{0,1},{1,0},{2,3},{3,2},{4,5},{5,4},{6,7},{7,6},{8,9},{9,8},{10,11... | collective-permute-start | bytes 208904 | tf_op jit(solution)/shard_map/ppermute | solution.py:298
  85.9 4.9 %collective-permute-start.31 = (f32[72,128]{1,0:T(8,128)S(1)}, f32[72,128]{1,0:T(8,128)S(1)}, u32[]{:S(2)}, u32[]{:S(2)}) collective-permute-start(f32[72,128]{1,0:T(8,128)S(1)} %slice.23), channel_id=1, source_target_pairs={{0,64},{8,72},{16,80},{24,88},{32,96},{40,104},{48,112},{56,120},{... | collective-permute-start | bytes 110600 | tf_op jit(solution)/shard_map/ppermute | solution.py:298
  90.9 6.1 %collective-permute-start.32 = (f32[72,128]{1,0:T(8,128)S(1)}, f32[72,128]{1,0:T(8,128)S(1)}, u32[]{:S(2)}, u32[]{:S(2)}) collective-permute-start(f32[72,128]{1,0:T(8,128)S(1)} %slice_add_fusion.3.refs_0_), channel_id=1, source_target_pairs={{0,192},{8,200},{16,208},{24,216},{32,224},{40,232},{48,240},{56,2... | collective-permute-start | bytes 110600 | tf_op jit(solution)/shard_map/ppermute | solution.py:298

commit v5 on v4

--- a/solution.py
+++ b/solution.py
@@ -189,22 +189,17 @@
 
 
 def factor_body(scale, *refs):
-    grams, (image_ref, basis_ref, triangle_ref, work) = refs[:2], refs[2:]
-    size = work.shape[0]
+    grams, (image_ref, basis_ref, triangle_ref, upper_ref, inverse_ref) = refs[:2], refs[2:]
+    size = upper_ref.shape[0]
     half = size // 2
     total = tree_sum([gram[...] for gram in grams]) * scale
     top, bottom = unpack_gram(total[:half], total[half : half + 1])
-    rows = lax.broadcasted_iota(jnp.int32, (size, size), 0)
-    cols = lax.broadcasted_iota(jnp.int32, (size, size), 1)
     shape = (PANEL, size)
     lane = lax.broadcasted_iota(jnp.int32, shape, 1)
     line = lax.broadcasted_iota(jnp.int32, shape, 0)
     count = size // PANEL
     per_half = count // 2
-    left_tiles = [
-        (top if t < per_half else bottom)[(t % per_half) * PANEL : (t % per_half + 1) * PANEL] for t in range(count)
-    ]
-    right_tiles = [jnp.where(lane == line + t * PANEL, 1.0, 0.0) for t in range(count)]
+    tiles = [(top if t < per_half else bottom)[(t % per_half) * PANEL : (t % per_half + 1) * PANEL] for t in range(count)]
 
     def spread_row(tile, i):
         return jnp.broadcast_to(tile[i : i + 1], shape)
@@ -212,57 +207,48 @@
     def spread_lane(row, at):
         return jnp.broadcast_to(row[:, at : at + 1], shape)
 
-    def gather_rows(lines):
-        tile = lines[0]
-        for i in range(1, PANEL):
-            tile = jnp.where(line == i, lines[i], tile)
-        return tile
-
-    left = [spread_row(left_tiles[0], i) for i in range(PANEL)]
-    right = [spread_row(right_tiles[0], i) for i in range(PANEL)]
-    pairs = [(i, j) for i in range(PANEL) for j in range(i, PANEL)]
-    pivot = {(i, j): spread_lane(left[i], j) for i, j in pairs}
+    rows = [spread_row(tiles[0], i) for i in range(PANEL)]
     for p in range(count):
         start, following = p * PANEL, (p + 1) * PANEL
+        in_panel = (lane >= start) & (lane < following)
+        pivot = {(i, j): spread_lane(rows[i], start + j) for i in range(PANEL) for j in range(i, PANEL)}
+        rows = [jnp.where(in_panel, jnp.where(lane == start + i, 1.0, 0.0), rows[i]) for i in range(PANEL)]
         if p + 1 < count:
-            next_left = [spread_row(left_tiles[p + 1], i) for i in range(PANEL)]
-            next_right = [spread_row(right_tiles[p + 1], i) for i in range(PANEL)]
-            next_pivot = {(i, j): spread_lane(next_left[i], following + j) for i, j in pairs}
+            cleared = jnp.where(in_panel, 0.0, tiles[p + 1])
+            next_rows = [spread_row(cleared, i) for i in range(PANEL)]
+        upper_tile = jnp.zeros(shape, jnp.float32)
         for k in range(PANEL):
             inverse = lax.rsqrt(pivot[k, k])
-            left[k] = left[k] * inverse
-            right[k] = right[k] * inverse
-            upper = {j: pivot[k, j] * inverse for j in range(k + 1, PANEL)}
+            rows[k] = rows[k] * inverse
+            upper = {j: pivot[k, j] * inverse for j in range(k, PANEL)}
             for i in range(k + 1, PANEL):
-                left[i] = left[i] - upper[i] * left[k]
-                right[i] = right[i] - upper[i] * right[k]
+                rows[i] = rows[i] - upper[i] * rows[k]
                 for j in range(i, PANEL):
                     pivot[i, j] = pivot[i, j] - upper[i] * upper[j]
             if p + 1 < count:
-                factors = [spread_lane(left[k], following + i) for i in range(PANEL)]
                 for i in range(PANEL):
-                    next_left[i] = next_left[i] - factors[i] * left[k]
-                    next_right[i] = next_right[i] - factors[i] * right[k]
-                for i, j in pairs:
-                    next_pivot[i, j] = next_pivot[i, j] - factors[i] * factors[j]
-        left_panel, right_panel = gather_rows(left), gather_rows(right)
-        work[start:following, :size] = left_panel
-        work[start:following, size:] = right_panel
+                    next_rows[i] = next_rows[i] - spread_lane(rows[k], following + i) * rows[k]
+            upper_line = jnp.where(lane >= following, rows[k], 0.0)
+            for j in range(k, PANEL):
+                upper_line = jnp.where(lane == start + j, upper[j], upper_line)
+            upper_tile = jnp.where(line == k, upper_line, upper_tile)
+        panel = rows[0]
+        for k in range(1, PANEL):
+            panel = jnp.where(line == k, rows[k], panel)
+        upper_ref[start:following] = upper_tile
+        inverse_ref[start:following] = jnp.where(lane < following, panel, 0.0)
         if p + 2 < count:
             update = lax.dot_general(
-                left_panel, jnp.concatenate([left_panel, right_panel], axis=1), (((0,), (0,)), ((), ())),
+                panel, panel, (((0,), (0,)), ((), ())),
                 precision=lax.Precision.HIGHEST, preferred_element_type=jnp.float32,
             )
             for t in range(p + 2, count):
-                span = slice(t * PANEL, (t + 1) * PANEL)
-                left_tiles[t] = left_tiles[t] - update[span, :size]
-                right_tiles[t] = right_tiles[t] - update[span, size:]
+                tiles[t] = jnp.where(in_panel, 0.0, tiles[t]) - update[t * PANEL : (t + 1) * PANEL]
         if p + 1 < count:
-            left, right, pivot = next_left, next_right, next_pivot
-    upper = jnp.where(cols >= rows, work[:, :size], 0.0)
-    triangle_ref[...] = upper.T
+            rows = next_rows
+    triangle_ref[...] = upper_ref[...].T
     basis_ref[...] = lax.dot_general(
-        image_ref[...], work[:, size:], (((1,), (1,)), ((), ())),
+        image_ref[...], inverse_ref[...], (((1,), (1,)), ((), ())),
         precision=lax.Precision.HIGHEST, preferred_element_type=jnp.float32,
     )
 
@@ -300,7 +286,7 @@
 
 def line_sum(parts):
     own, two, one, three = parts
-    return (own + one) + (two + three)
+    return (two + three) + (own + one)
 
 
 def local(values, mask, factor):
@@ -364,7 +350,7 @@
     basis, triangle = kernel_call(
         functools.partial(factor_body, scale),
         [jax.ShapeDtypeStruct((height, columns), f32), jax.ShapeDtypeStruct((columns, columns), f32)],
-        scratch=[pltpu.VMEM((columns, 2 * columns), f32)],
+        scratch=[pltpu.VMEM((columns, columns), f32)] * 2,
     )(*grams, own_image)
     return (basis, triangle)
 

time: 104 us -> 101 us (0.971)
  Pallas kernels: 13.5 us -> 12.2 us
  starting transfers between devices: 50.9 us -> 49.7 us
    pallas_call x11, Pallas kernels: 13.5 us -> 12.2 us  [call(): pl.pallas_call(body, out_shape=out_shape, in_specs=in_specs, out_specs=ja...]
    ppermute x10, starting transfers between devices: 12.4 us -> 11.1 us  [spread(): return [part] + [lax.ppermute(part, axis, perm(k)) for k in shifts]]
where the time goes in v5:
time: 101 us
  starting transfers between devices  49.7 us (49%)
  waiting for transfers between devices  36.4 us (36%)
  Pallas kernels  12.2 us (12%)
  other arithmetic  1.48 us (1%)
    ppermute x10, waiting for transfers between devices, spread(): return [part] + [lax.ppermute(part, axis, perm(k)) for k in shifts]  21.2 us
    pallas_call x11, Pallas kernels, call(): pl.pallas_call(body, out_shape=out_shape, in_specs=in_specs, out_specs=ja...  12.2 us
    ppermute x10, starting transfers between devices, spread(): return [part] + [lax.ppermute(part, axis, perm(k)) for k in shifts]  11.1 us
    ppermute x2, starting transfers between devices, gather_line(): top = lax.ppermute(cut(one, 0), 'samp', samp_perm(other))  6.84 us
    ppermute x2, waiting for transfers between devices, gather_line(): top = lax.ppermute(cut(one, 0), 'samp', samp_perm(other))  5.89 us
    ppermute x2, starting transfers between devices, gather_line(): three = lax.ppermute(block, 'samp', samp_perm(other))  5.76 us
    ppermute x3, starting transfers between devices, local(): lax.ppermute(send_near[r], 'site', site_perm(ROUTES[r][0]))  5.54 us
    ppermute x3, starting transfers between devices, local(): lax.ppermute(folded[r][0], 'site', site_perm(ROUTES[r][1]))  5.22 us
  transfers between devices with their start and end apart: 33, of which 19 were waited for; matrix products, arithmetic and copies ran while one was open for 0% of the time, Pallas kernels for 6%

profile of v5, /device:TPU:32, one launch (start us, length us, event | category | flops | bytes accessed | tf_op | source)
XLA Modules:
  0.0 100.7 jit_solution(8322136025120388219)
XLA Ops:
  0.6 1.2 %compare_select_fusion.refs_0_.refs_6_ = bf16[64,2048]{1,0:T(8,128)(2,1)S(1)} fusion(bf16[64,2048]{1,0:T(8,128)(2,1)} %param.3, s32[64,2048]{1,0:T(8,128)} %param.4), kind=kLoop, calls=%fused_computation | loop fusion | flops 262144 | bytes 1048576 | tf_op jit(solution)/shard_map/jit(_where)/select_n | solution.py:296
  1.8 1.7 %collective-permute-start = (bf16[64,2048]{1,0:T(8,128)(2,1)S(1)}, bf16[64,2048]{1,0:T(8,128)(2,1)S(1)}, u32[]{:S(2)}, u32[]{:S(2)}) collective-permute-start(bf16[64,2048]{1,0:T(8,128)(2,1)S(1)} %compare_select_fusion.refs_0_.refs_6_), channel_id=1, source_target_pairs={{0,16},{8,24},{16,0},{24,8},{32,48},{40,56},{48,32},{56,40},{64,80... | collective-permute-start | bytes 786440 | tf_op jit(solution)/shard_map/ppermute | solution.py:275
  3.5 2.2 %collective-permute-start.1 = (bf16[64,2048]{1,0:T(8,128)(2,1)S(1)}, bf16[64,2048]{1,0:T(8,128)(2,1)S(1)}, u32[]{:S(2)}, u32[]{:S(2)}) collective-permute-start(bf16[64,2048]{1,0:T(8,128)(2,1)S(1)} %compare_select_fusion.refs_0_.refs_6_), channel_id=1, source_target_pairs={{0,48},{8,56},{16,32},{24,40},{32,16},{40,24},{48,0},{56,8},{64,11... | collective-permute-start | bytes 786440 | tf_op jit(solution)/shard_map/ppermute | solution.py:276
  5.7 3.4 %collective-permute-start.7 = (bf16[64,2304]{1,0:T(8,128)(2,1)S(1)}, bf16[64,2304]{1,0:T(8,128)(2,1)S(1)}, u32[]{:S(2)}, u32[]{:S(2)}) collective-permute-start(bf16[64,2304]{1,0:T(8,128)(2,1)S(1)} %pad_maximum_fusion), channel_id=1, source_target_pairs={{0,64},{8,72},{16,80},{24,88},{32,96},{40,104},{48,112},{56,120},{... | collective-permute-start | bytes 884744 | tf_op jit(solution)/shard_map/ppermute | solution.py:275
  9.1 3.6 %collective-permute-start.8 = (bf16[64,2304]{1,0:T(8,128)(2,1)S(1)}, bf16[64,2304]{1,0:T(8,128)(2,1)S(1)}, u32[]{:S(2)}, u32[]{:S(2)}) collective-permute-start(bf16[64,2304]{1,0:T(8,128)(2,1)S(1)} %pad_maximum_fusion), channel_id=1, source_target_pairs={{0,192},{8,200},{16,208},{24,216},{32,224},{40,232},{48,240},{56,2... | collective-permute-start | bytes 884744 | tf_op jit(solution)/shard_map/ppermute | solution.py:276
  12.7 1.1 %collective-permute-start.2 = (bf16[32,2048]{1,0:T(8,128)(2,1)S(1)}, bf16[32,2048]{1,0:T(8,128)(2,1)S(1)}, u32[]{:S(2)}, u32[]{:S(2)}) collective-permute-start(bf16[32,2048]{1,0:T(8,128)(2,1)S(1)} %shard_map.50), channel_id=1, source_target_pairs={{0,48},{8,56},{16,32},{24,40},{32,16},{40,24},{48,0},{56,8},{64,11... | collective-permute-start | bytes 393224 | tf_op jit(solution)/shard_map/ppermute | solution.py:277
  14.0 5.9 %collective-permute-done.2 = bf16[32,2048]{1,0:T(8,128)(2,1)S(1)} collective-permute-done((bf16[32,2048]{1,0:T(8,128)(2,1)S(1)}, bf16[32,2048]{1,0:T(8,128)(2,1)S(1)}, u32[]{:S(2)}, u32[]{:S(2)}) %collective-permute-start.2) | collective-permute-done | bytes 131104 | tf_op jit(solution)/shard_map/ppermute | solution.py:277
  19.9 0.6 collective-permute-start.6
  20.7 5.7 %collective-permute-start.9 = (bf16[32,2304]{1,0:T(8,128)(2,1)S(1)}, bf16[32,2304]{1,0:T(8,128)(2,1)S(1)}, u32[]{:S(2)}, u32[]{:S(2)}) collective-permute-start(bf16[32,2304]{1,0:T(8,128)(2,1)S(1)} %split.8), channel_id=1, source_target_pairs={{0,192},{8,200},{16,208},{24,216},{32,224},{40,232},{48,240},{56,2... | collective-permute-start | bytes 442376 | tf_op jit(solution)/shard_map/ppermute | solution.py:277
  26.4 1.0 collective-permute-start.10
  27.4 2.0 %shard_map.52 = (f32[4,64,384]{2,1,0:T(8,128)S(1)}, f32[4,64,384]{2,1,0:T(8,128)S(1)}, f32[4,64,384]{2,1,0:T(8,128)S(1)}) custom-call(s32[1]{0:T(128)} %bitcast.which, bf16[64,2048]{1,0:T(8,128)(2,1)S(1)} %compare_select_fusion.refs_0_.refs_6_, bf16[128,2048]{1,0:T(8,128)(2,1)S(1)} %constant_dynamic-update-slice_fusion.refs_1_, ...), custom_call_target="tpu_custom_call" | custom-call | flops 1000000 | bytes 100000 | tf_op jit(solution)/shard_map/pallas_call | solution.py:51
  29.4 1.6 %collective-permute-start.11 = (f32[4,64,384]{2,1,0:T(8,128)S(1)}, f32[4,64,384]{2,1,0:T(8,128)S(1)}, u32[]{:S(2)}, u32[]{:S(2)}) collective-permute-start(f32[4,64,384]{2,1,0:T(8,128)S(1)} %get-tuple-element.32), channel_id=1, source_target_pairs={{0,2},{1,3},{2,0},{3,1},{4,6},{5,7},{6,4},{7,5},{8,10},{9,11},{10,... | collective-permute-start | bytes 1179656 | tf_op jit(solution)/shard_map/ppermute | solution.py:321
  31.0 2.1 %collective-permute-start.12 = (f32[4,64,384]{2,1,0:T(8,128)S(1)}, f32[4,64,384]{2,1,0:T(8,128)S(1)}, u32[]{:S(2)}, u32[]{:S(2)}) collective-permute-start(f32[4,64,384]{2,1,0:T(8,128)S(1)} %get-tuple-element.33), channel_id=1, source_target_pairs={{0,6},{1,7},{2,4},{3,5},{4,2},{5,3},{6,0},{7,1},{8,14},{9,15},{10,... | collective-permute-start | bytes 1179656 | tf_op jit(solution)/shard_map/ppermute | solution.py:321
  33.1 1.9 %collective-permute-start.13 = (f32[4,64,384]{2,1,0:T(8,128)S(1)}, f32[4,64,384]{2,1,0:T(8,128)S(1)}, u32[]{:S(2)}, u32[]{:S(2)}) collective-permute-start(f32[4,64,384]{2,1,0:T(8,128)S(1)} %get-tuple-element.34), channel_id=1, source_target_pairs={{0,1},{1,0},{2,3},{3,2},{4,5},{5,4},{6,7},{7,6},{8,9},{9,8},{10,11... | collective-permute-start | bytes 1179656 | tf_op jit(solution)/shard_map/ppermute | solution.py:321
  35.0 2.0 %shard_map.53 = (f32[4,64,128]{2,1,0:T(8,128)S(1)}, f32[4,64,128]{2,1,0:T(8,128)S(1)}, f32[4,64,128]{2,1,0:T(8,128)S(1)}) custom-call(s32[1]{0:T(128)} %bitcast.which, bf16[64,2048]{1,0:T(8,128)(2,1)S(1)} %compare_select_fusion.refs_0_.refs_6_, bf16[128,2048]{1,0:T(8,128)(2,1)S(1)} %constant_dynamic-update-slice_fusion.refs_1_, ...), custom_call_target="tpu_custom_call" | custom-call | flops 10000000000 | bytes 100000 | tf_op jit(solution)/shard_map/pallas_call | solution.py:51
  36.9 1.5 %collective-permute-start.14 = (f32[4,64,128]{2,1,0:T(8,128)S(1)}, f32[4,64,128]{2,1,0:T(8,128)S(1)}, u32[]{:S(2)}, u32[]{:S(2)}) collective-permute-start(f32[4,64,128]{2,1,0:T(8,128)S(1)} %get-tuple-element.36), channel_id=1, source_target_pairs={{0,2},{1,3},{2,0},{3,1},{4,6},{5,7},{6,4},{7,5},{8,10},{9,11},{10,... | collective-permute-start | bytes 393224 | tf_op jit(solution)/shard_map/ppermute | solution.py:324
  38.5 2.3 %collective-permute-start.15 = (f32[4,64,128]{2,1,0:T(8,128)S(1)}, f32[4,64,128]{2,1,0:T(8,128)S(1)}, u32[]{:S(2)}, u32[]{:S(2)}) collective-permute-start(f32[4,64,128]{2,1,0:T(8,128)S(1)} %get-tuple-element.37), channel_id=1, source_target_pairs={{0,6},{1,7},{2,4},{3,5},{4,2},{5,3},{6,0},{7,1},{8,14},{9,15},{10,... | collective-permute-start | bytes 393224 | tf_op jit(solution)/shard_map/ppermute | solution.py:324
  40.8 1.4 %collective-permute-start.16 = (f32[4,64,128]{2,1,0:T(8,128)S(1)}, f32[4,64,128]{2,1,0:T(8,128)S(1)}, u32[]{:S(2)}, u32[]{:S(2)}) collective-permute-start(f32[4,64,128]{2,1,0:T(8,128)S(1)} %get-tuple-element.38), channel_id=1, source_target_pairs={{0,1},{1,0},{2,3},{3,2},{4,5},{5,4},{6,7},{7,6},{8,9},{9,8},{10,11... | collective-permute-start | bytes 393224 | tf_op jit(solution)/shard_map/ppermute | solution.py:324
  42.1 0.6 collective-permute-done.12.near
  42.7 0.8 collective-permute-done.13.near
  43.5 2.0 %shard_map.54 = (f32[4,64,512]{2,1,0:T(8,128)S(1)}, f32[4,64,512]{2,1,0:T(8,128)S(1)}, f32[4,64,512]{2,1,0:T(8,128)S(1)}, f32[192,128]{1,0:T(8,128)S(1)}) custom-call(s32[1]{0:T(128)} %bitcast.which, bf16[64,2048]{1,0:T(8,128)(2,1)S(1)} %compare_select_fusion.refs_0_.refs_6_, bf16[128,2048]{1,0:T(8,128)(2,1)S(1)} %constant_dynamic-update-slice_fusion.refs_1_, ...), custom_call_target="tpu_custom_call" | custom-call | flops 10000000000 | bytes 100000 | tf_op jit(solution)/shard_map/pallas_call | solution.py:51
  45.8 1.4 %collective-permute-start.21 = (f32[2,64,512]{2,1,0:T(8,128)S(1)}, f32[2,64,512]{2,1,0:T(8,128)S(1)}, u32[]{:S(2)}, u32[]{:S(2)}) collective-permute-start(f32[2,64,512]{2,1,0:T(8,128)S(1)} %get-tuple-element.59), channel_id=1, source_target_pairs={{0,2},{1,3},{2,0},{3,1},{4,6},{5,7},{6,4},{7,5},{8,10},{9,11},{10,... | collective-permute-start | bytes 786440 | tf_op jit(solution)/shard_map/ppermute | solution.py:330
  47.3 1.8 %collective-permute-start.19 = (f32[2,64,512]{2,1,0:T(8,128)S(1)}, f32[2,64,512]{2,1,0:T(8,128)S(1)}, u32[]{:S(2)}, u32[]{:S(2)}) collective-permute-start(f32[2,64,512]{2,1,0:T(8,128)S(1)} %get-tuple-element.53), channel_id=1, source_target_pairs={{0,1},{1,0},{2,3},{3,2},{4,5},{5,4},{6,7},{7,6},{8,9},{9,8},{10,11... | collective-permute-start | bytes 786440 | tf_op jit(solution)/shard_map/ppermute | solution.py:330
  49.1 2.0 %collective-permute-start.17 = (f32[2,64,512]{2,1,0:T(8,128)S(1)}, f32[2,64,512]{2,1,0:T(8,128)S(1)}, u32[]{:S(2)}, u32[]{:S(2)}) collective-permute-start(f32[2,64,512]{2,1,0:T(8,128)S(1)} %get-tuple-element.47), channel_id=1, source_target_pairs={{0,6},{1,7},{2,4},{3,5},{4,2},{5,3},{6,0},{7,1},{8,14},{9,15},{10,... | collective-permute-start | bytes 786440 | tf_op jit(solution)/shard_map/ppermute | solution.py:330
  51.1 1.1 %collective-permute-done.21.refs_7_ = f32[2,64,512]{2,1,0:T(8,128)S(1)} collective-permute-done((f32[2,64,512]{2,1,0:T(8,128)S(1)}, f32[2,64,512]{2,1,0:T(8,128)S(1)}, u32[]{:S(2)}, u32[]{:S(2)}) %collective-permute-start.21) | collective-permute-done | bytes 262176 | tf_op jit(solution)/shard_map/ppermute | solution.py:330
  52.3 2.7 %collective-permute-start.22 = (f32[1,64,512]{2,1,0:T(8,128)S(1)}, f32[1,64,512]{2,1,0:T(8,128)S(1)}, u32[]{:S(2)}, u32[]{:S(2)}) collective-permute-start(f32[1,64,512]{2,1,0:T(8,128)S(1)} %slice_add_fusion), channel_id=1, source_target_pairs={{0,6},{1,7},{2,4},{3,5},{4,2},{5,3},{6,0},{7,1},{8,14},{9,15},{10,... | collective-permute-start | bytes 393224 | tf_op jit(solution)/shard_map/ppermute | solution.py:332
  55.1 1.9 %collective-permute-done.17.refs_1_ = f32[2,64,512]{2,1,0:T(8,128)S(1)} collective-permute-done((f32[2,64,512]{2,1,0:T(8,128)S(1)}, f32[2,64,512]{2,1,0:T(8,128)S(1)}, u32[]{:S(2)}, u32[]{:S(2)}) %collective-permute-start.17) | collective-permute-done | bytes 262176 | tf_op jit(solution)/shard_map/ppermute | solution.py:330
  57.5 1.0 %collective-permute-done.22.refs_8_ = f32[1,64,512]{2,1,0:T(8,128)S(1)} collective-permute-done((f32[1,64,512]{2,1,0:T(8,128)S(1)}, f32[1,64,512]{2,1,0:T(8,128)S(1)}, u32[]{:S(2)}, u32[]{:S(2)}) %collective-permute-start.22) | collective-permute-done | bytes 131104 | tf_op jit(solution)/shard_map/ppermute | solution.py:332
  58.6 1.5 %collective-permute-done.20.refs_5_ = f32[1,64,512]{2,1,0:T(8,128)S(1)} collective-permute-done((f32[1,64,512]{2,1,0:T(8,128)S(1)}, f32[1,64,512]{2,1,0:T(8,128)S(1)}, u32[]{:S(2)}, u32[]{:S(2)}) %collective-permute-start.20) | collective-permute-done | bytes 131104 | tf_op jit(solution)/shard_map/ppermute | solution.py:332
  60.0 2.0 %collective-permute-done.18.refs_2_ = f32[1,64,512]{2,1,0:T(8,128)S(1)} collective-permute-done((f32[1,64,512]{2,1,0:T(8,128)S(1)}, f32[1,64,512]{2,1,0:T(8,128)S(1)}, u32[]{:S(2)}, u32[]{:S(2)}) %collective-permute-start.18) | collective-permute-done | bytes 131104 | tf_op jit(solution)/shard_map/ppermute | solution.py:332
  62.5 1.2 %collective-permute-done.23 = f32[64,128]{1,0:T(8,128)S(1)} collective-permute-done((f32[64,128]{1,0:T(8,128)S(1)}, f32[64,128]{1,0:T(8,128)S(1)}, u32[]{:S(2)}, u32[]{:S(2)}) %collective-permute-start.23) | collective-permute-done | bytes 32800 | tf_op jit(solution)/shard_map/ppermute | solution.py:284
  63.7 1.9 %collective-permute-start.24 = (f32[64,128]{1,0:T(8,128)S(1)}, f32[64,128]{1,0:T(8,128)S(1)}, u32[]{:S(2)}, u32[]{:S(2)}) collective-permute-start(f32[64,128]{1,0:T(8,128)S(1)} %add.35.refs_0_), channel_id=1, source_target_pairs={{0,32},{8,40},{16,48},{24,56},{32,0},{40,8},{48,16},{56,24},{64,96... | collective-permute-start | bytes 98312 | tf_op jit(solution)/shard_map/ppermute | solution.py:284
  65.6 1.0 %collective-permute-start.25 = (f32[64,128]{1,0:T(8,128)S(1)}, f32[64,128]{1,0:T(8,128)S(1)}, u32[]{:S(2)}, u32[]{:S(2)}) collective-permute-start(f32[64,128]{1,0:T(8,128)S(1)} %add.35.refs_0_), channel_id=1, source_target_pairs={{0,16},{8,24},{16,0},{24,8},{32,48},{40,56},{48,32},{56,40},{64,80... | collective-permute-start | bytes 98312 | tf_op jit(solution)/shard_map/ppermute | solution.py:284
  66.7 1.1 %collective-permute-start.26 = (f32[64,128]{1,0:T(8,128)S(1)}, f32[64,128]{1,0:T(8,128)S(1)}, u32[]{:S(2)}, u32[]{:S(2)}) collective-permute-start(f32[64,128]{1,0:T(8,128)S(1)} %add.35.refs_0_), channel_id=1, source_target_pairs={{0,48},{8,56},{16,32},{24,40},{32,16},{40,24},{48,0},{56,8},{64,11... | collective-permute-start | bytes 98312 | tf_op jit(solution)/shard_map/ppermute | solution.py:284
  67.8 1.6 %collective-permute-done.24.refs_1_ = f32[64,128]{1,0:T(8,128)S(1)} collective-permute-done((f32[64,128]{1,0:T(8,128)S(1)}, f32[64,128]{1,0:T(8,128)S(1)}, u32[]{:S(2)}, u32[]{:S(2)}) %collective-permute-start.24) | collective-permute-done | bytes 32800 | tf_op jit(solution)/shard_map/ppermute | solution.py:284
  69.6 2.3 %collective-permute-done.26.refs_3_ = f32[64,128]{1,0:T(8,128)S(1)} collective-permute-done((f32[64,128]{1,0:T(8,128)S(1)}, f32[64,128]{1,0:T(8,128)S(1)}, u32[]{:S(2)}, u32[]{:S(2)}) %collective-permute-start.26) | collective-permute-done | bytes 32800 | tf_op jit(solution)/shard_map/ppermute | solution.py:284
  72.2 1.6 %collective-permute-start.27 = (f32[136,128]{1,0:T(8,128)S(1)}, f32[136,128]{1,0:T(8,128)S(1)}, u32[]{:S(2)}, u32[]{:S(2)}) collective-permute-start(f32[136,128]{1,0:T(8,128)S(1)} %shard_map.59), channel_id=1, source_target_pairs={{0,4},{1,5},{2,6},{3,7},{4,0},{5,1},{6,2},{7,3},{8,12},{9,13},{10,... | collective-permute-start | bytes 208904 | tf_op jit(solution)/shard_map/ppermute | solution.py:284
  73.8 1.2 %collective-permute-start.28 = (f32[136,128]{1,0:T(8,128)S(1)}, f32[136,128]{1,0:T(8,128)S(1)}, u32[]{:S(2)}, u32[]{:S(2)}) collective-permute-start(f32[136,128]{1,0:T(8,128)S(1)} %shard_map.59), channel_id=1, source_target_pairs={{0,6},{1,7},{2,4},{3,5},{4,2},{5,3},{6,0},{7,1},{8,14},{9,15},{10,... | collective-permute-start | bytes 208904 | tf_op jit(solution)/shard_map/ppermute | solution.py:284
  75.0 0.7 collective-permute-start.29
  75.7 2.7 %collective-permute-done.27 = f32[136,128]{1,0:T(8,128)S(1)} collective-permute-done((f32[136,128]{1,0:T(8,128)S(1)}, f32[136,128]{1,0:T(8,128)S(1)}, u32[]{:S(2)}, u32[]{:S(2)}) %collective-permute-start.27) | collective-permute-done | bytes 69664 | tf_op jit(solution)/shard_map/ppermute | solution.py:284
  78.4 0.9 collective-permute-done.28
  79.4 1.0 collective-permute-start.30
  80.4 3.8 %collective-permute-done.30 = f32[136,128]{1,0:T(8,128)S(1)} collective-permute-done((f32[136,128]{1,0:T(8,128)S(1)}, f32[136,128]{1,0:T(8,128)S(1)}, u32[]{:S(2)}, u32[]{:S(2)}) %collective-permute-start.30) | collective-permute-done | bytes 69664 | tf_op jit(solution)/shard_map/ppermute | solution.py:284
  84.3 1.5 %collective-permute-start.31 = (f32[72,128]{1,0:T(8,128)S(1)}, f32[72,128]{1,0:T(8,128)S(1)}, u32[]{:S(2)}, u32[]{:S(2)}) collective-permute-start(f32[72,128]{1,0:T(8,128)S(1)} %slice.23), channel_id=1, source_target_pairs={{0,64},{8,72},{16,80},{24,88},{32,96},{40,104},{48,112},{56,120},{... | collective-permute-start | bytes 110600 | tf_op jit(solution)/shard_map/ppermute | solution.py:284
  85.8 3.4 %collective-permute-done.31 = f32[72,128]{1,0:T(8,128)S(1)} collective-permute-done((f32[72,128]{1,0:T(8,128)S(1)}, f32[72,128]{1,0:T(8,128)S(1)}, u32[]{:S(2)}, u32[]{:S(2)}) %collective-permute-start.31) | collective-permute-done | bytes 36896 | tf_op jit(solution)/shard_map/ppermute | solution.py:284
  89.3 0.8 collective-permute-start.32
  90.1 5.2 %collective-permute-done.32.refs_1_ = f32[72,128]{1,0:T(8,128)S(1)} collective-permute-done((f32[72,128]{1,0:T(8,128)S(1)}, f32[72,128]{1,0:T(8,128)S(1)}, u32[]{:S(2)}, u32[]{:S(2)}) %collective-permute-start.32) | collective-permute-done | bytes 36896 | tf_op jit(solution)/shard_map/ppermute | solution.py:284
  95.3 5.4 %shard_map.60 = (f32[64,128]{1,0:T(8,128)}, f32[128,128]{1,0:T(8,128)}) custom-call(f32[72,128]{1,0:T(8,128)S(1)} %slice_add_fusion.3.refs_0_, f32[72,128]{1,0:T(8,128)S(1)} %collective-permute-done.32.refs_1_, f32[64,128]{1,0:T(8,128)S(1)} %slice.24.refs_2_), custom_call_target="tpu_custom_call" | custom-call | tf_op jit(solution)/shard_map/pallas_call | solution.py:51
  (50 shorter events, 2.7 us)
Async XLA Ops:
  0.6 5.1 %copy-start = (f32[64,128]{1,0:T(8,128)S(1)}, f32[64,128]{1,0:T(8,128)}, u32[]{:S(2)}) copy-start(f32[64,128]{1,0:T(8,128)} %refs_10_.1) | copy-start | bytes 98308
  1.8 10.8 %collective-permute-start = (bf16[64,2048]{1,0:T(8,128)(2,1)S(1)}, bf16[64,2048]{1,0:T(8,128)(2,1)S(1)}, u32[]{:S(2)}, u32[]{:S(2)}) collective-permute-start(bf16[64,2048]{1,0:T(8,128)(2,1)S(1)} %compare_select_fusion.refs_0_.refs_6_), channel_id=1, source_target_pairs={{0,16},{8,24},{16,0},{24,8},{32,48},{40,56},{48,32},{56,40},{64,80... | collective-permute-start | bytes 786440 | tf_op jit(solution)/shard_map/ppermute | solution.py:275
  3.5 10.3 %collective-permute-start.1 = (bf16[64,2048]{1,0:T(8,128)(2,1)S(1)}, bf16[64,2048]{1,0:T(8,128)(2,1)S(1)}, u32[]{:S(2)}, u32[]{:S(2)}) collective-permute-start(bf16[64,2048]{1,0:T(8,128)(2,1)S(1)} %compare_select_fusion.refs_0_.refs_6_), channel_id=1, source_target_pairs={{0,48},{8,56},{16,32},{24,40},{32,16},{40,24},{48,0},{56,8},{64,11... | collective-permute-start | bytes 786440 | tf_op jit(solution)/shard_map/ppermute | solution.py:276
  5.7 15.0 %collective-permute-start.7 = (bf16[64,2304]{1,0:T(8,128)(2,1)S(1)}, bf16[64,2304]{1,0:T(8,128)(2,1)S(1)}, u32[]{:S(2)}, u32[]{:S(2)}) collective-permute-start(bf16[64,2304]{1,0:T(8,128)(2,1)S(1)} %pad_maximum_fusion), channel_id=1, source_target_pairs={{0,64},{8,72},{16,80},{24,88},{32,96},{40,104},{48,112},{56,120},{... | collective-permute-start | bytes 884744 | tf_op jit(solution)/shard_map/ppermute | solution.py:275
  9.1 17.3 %collective-permute-start.8 = (bf16[64,2304]{1,0:T(8,128)(2,1)S(1)}, bf16[64,2304]{1,0:T(8,128)(2,1)S(1)}, u32[]{:S(2)}, u32[]{:S(2)}) collective-permute-start(bf16[64,2304]{1,0:T(8,128)(2,1)S(1)} %pad_maximum_fusion), channel_id=1, source_target_pairs={{0,192},{8,200},{16,208},{24,216},{32,224},{40,232},{48,240},{56,2... | collective-permute-start | bytes 884744 | tf_op jit(solution)/shard_map/ppermute | solution.py:276
  12.7 14.8 %collective-permute-start.4 = (bf16[64,2048]{1,0:T(8,128)(2,1)S(1)}, bf16[64,2048]{1,0:T(8,128)(2,1)S(1)}, u32[]{:S(2)}, u32[]{:S(2)}) collective-permute-start(bf16[64,2048]{1,0:T(8,128)(2,1)S(1)} %compare_select_fusion.refs_0_.refs_6_), channel_id=1, source_target_pairs={{0,8},{8,0},{16,24},{24,16},{32,40},{40,32},{48,56},{56,48},{64,72... | collective-permute-start | bytes 786440 | tf_op jit(solution)/shard_map/ppermute | solution.py:303
  12.7 7.2 %collective-permute-start.2 = (bf16[32,2048]{1,0:T(8,128)(2,1)S(1)}, bf16[32,2048]{1,0:T(8,128)(2,1)S(1)}, u32[]{:S(2)}, u32[]{:S(2)}) collective-permute-start(bf16[32,2048]{1,0:T(8,128)(2,1)S(1)} %shard_map.50), channel_id=1, source_target_pairs={{0,48},{8,56},{16,32},{24,40},{32,16},{40,24},{48,0},{56,8},{64,11... | collective-permute-start | bytes 393224 | tf_op jit(solution)/shard_map/ppermute | solution.py:277
  13.8 6.1 %collective-permute-start.3 = (bf16[32,2048]{1,0:T(8,128)(2,1)S(1)}, bf16[32,2048]{1,0:T(8,128)(2,1)S(1)}, u32[]{:S(2)}, u32[]{:S(2)}) collective-permute-start(bf16[32,2048]{1,0:T(8,128)(2,1)S(1)} %shard_map.51), channel_id=1, source_target_pairs={{0,16},{8,24},{16,0},{24,8},{32,48},{40,56},{48,32},{56,40},{64,80... | collective-permute-start | bytes 393224 | tf_op jit(solution)/shard_map/ppermute | solution.py:278
  19.9 7.5 %collective-permute-start.5 = (bf16[128,2048]{1,0:T(8,128)(2,1)S(1)}, bf16[128,2048]{1,0:T(8,128)(2,1)S(1)}, u32[]{:S(2)}, u32[]{:S(2)}) collective-permute-start(bf16[128,2048]{1,0:T(8,128)(2,1)S(1)} %constant_dynamic-update-slice_fusion.refs_1_), channel_id=1, source_target_pairs={{0,8},{8,0},{16,24},{24,16},{32,40},{40,32},{48,56},{56,48},{64,72... | collective-permute-start | bytes 1572872 | tf_op jit(solution)/shard_map/ppermute | solution.py:303
  19.9 7.5 %collective-permute-start.6 = (bf16[64,2048]{1,0:T(8,128)(2,1)S(1)}, bf16[64,2048]{1,0:T(8,128)(2,1)S(1)}, u32[]{:S(2)}, u32[]{:S(2)}) collective-permute-start(bf16[64,2048]{1,0:T(8,128)(2,1)S(1)} %constant_dynamic-update-slice_fusion.2.refs_2_), channel_id=1, source_target_pairs={{0,8},{8,0},{16,24},{24,16},{32,40},{40,32},{48,56},{56,48},{64,72... | collective-permute-start | bytes 786440 | tf_op jit(solution)/shard_map/ppermute | solution.py:303
  20.7 14.2 %collective-permute-start.9 = (bf16[32,2304]{1,0:T(8,128)(2,1)S(1)}, bf16[32,2304]{1,0:T(8,128)(2,1)S(1)}, u32[]{:S(2)}, u32[]{:S(2)}) collective-permute-start(bf16[32,2304]{1,0:T(8,128)(2,1)S(1)} %split.8), channel_id=1, source_target_pairs={{0,192},{8,200},{16,208},{24,216},{32,224},{40,232},{48,240},{56,2... | collective-permute-start | bytes 442376 | tf_op jit(solution)/shard_map/ppermute | solution.py:277
  26.4 8.5 %collective-permute-start.10 = (bf16[32,2304]{1,0:T(8,128)(2,1)S(1)}, bf16[32,2304]{1,0:T(8,128)(2,1)S(1)}, u32[]{:S(2)}, u32[]{:S(2)}) collective-permute-start(bf16[32,2304]{1,0:T(8,128)(2,1)S(1)} %split.9), channel_id=1, source_target_pairs={{0,64},{8,72},{16,80},{24,88},{32,96},{40,104},{48,112},{56,120},{... | collective-permute-start | bytes 442376 | tf_op jit(solution)/shard_map/ppermute | solution.py:278
  29.4 11.4 %collective-permute-start.11 = (f32[4,64,384]{2,1,0:T(8,128)S(1)}, f32[4,64,384]{2,1,0:T(8,128)S(1)}, u32[]{:S(2)}, u32[]{:S(2)}) collective-permute-start(f32[4,64,384]{2,1,0:T(8,128)S(1)} %get-tuple-element.32), channel_id=1, source_target_pairs={{0,2},{1,3},{2,0},{3,1},{4,6},{5,7},{6,4},{7,5},{8,10},{9,11},{10,... | collective-permute-start | bytes 1179656 | tf_op jit(solution)/shard_map/ppermute | solution.py:321
  31.0 11.7 %collective-permute-start.12 = (f32[4,64,384]{2,1,0:T(8,128)S(1)}, f32[4,64,384]{2,1,0:T(8,128)S(1)}, u32[]{:S(2)}, u32[]{:S(2)}) collective-permute-start(f32[4,64,384]{2,1,0:T(8,128)S(1)} %get-tuple-element.33), channel_id=1, source_target_pairs={{0,6},{1,7},{2,4},{3,5},{4,2},{5,3},{6,0},{7,1},{8,14},{9,15},{10,... | collective-permute-start | bytes 1179656 | tf_op jit(solution)/shard_map/ppermute | solution.py:321
  33.1 10.5 %collective-permute-start.13 = (f32[4,64,384]{2,1,0:T(8,128)S(1)}, f32[4,64,384]{2,1,0:T(8,128)S(1)}, u32[]{:S(2)}, u32[]{:S(2)}) collective-permute-start(f32[4,64,384]{2,1,0:T(8,128)S(1)} %get-tuple-element.34), channel_id=1, source_target_pairs={{0,1},{1,0},{2,3},{3,2},{4,5},{5,4},{6,7},{7,6},{8,9},{9,8},{10,11... | collective-permute-start | bytes 1179656 | tf_op jit(solution)/shard_map/ppermute | solution.py:321
  36.9 8.6 %collective-permute-start.14 = (f32[4,64,128]{2,1,0:T(8,128)S(1)}, f32[4,64,128]{2,1,0:T(8,128)S(1)}, u32[]{:S(2)}, u32[]{:S(2)}) collective-permute-start(f32[4,64,128]{2,1,0:T(8,128)S(1)} %get-tuple-element.36), channel_id=1, source_target_pairs={{0,2},{1,3},{2,0},{3,1},{4,6},{5,7},{6,4},{7,5},{8,10},{9,11},{10,... | collective-permute-start | bytes 393224 | tf_op jit(solution)/shard_map/ppermute | solution.py:324
  38.5 7.1 %collective-permute-start.15 = (f32[4,64,128]{2,1,0:T(8,128)S(1)}, f32[4,64,128]{2,1,0:T(8,128)S(1)}, u32[]{:S(2)}, u32[]{:S(2)}) collective-permute-start(f32[4,64,128]{2,1,0:T(8,128)S(1)} %get-tuple-element.37), channel_id=1, source_target_pairs={{0,6},{1,7},{2,4},{3,5},{4,2},{5,3},{6,0},{7,1},{8,14},{9,15},{10,... | collective-permute-start | bytes 393224 | tf_op jit(solution)/shard_map/ppermute | solution.py:324
  40.8 5.0 %collective-permute-start.16 = (f32[4,64,128]{2,1,0:T(8,128)S(1)}, f32[4,64,128]{2,1,0:T(8,128)S(1)}, u32[]{:S(2)}, u32[]{:S(2)}) collective-permute-start(f32[4,64,128]{2,1,0:T(8,128)S(1)} %get-tuple-element.38), channel_id=1, source_target_pairs={{0,1},{1,0},{2,3},{3,2},{4,5},{5,4},{6,7},{7,6},{8,9},{9,8},{10,11... | collective-permute-start | bytes 393224 | tf_op jit(solution)/shard_map/ppermute | solution.py:324
  45.8 6.5 %collective-permute-start.21 = (f32[2,64,512]{2,1,0:T(8,128)S(1)}, f32[2,64,512]{2,1,0:T(8,128)S(1)}, u32[]{:S(2)}, u32[]{:S(2)}) collective-permute-start(f32[2,64,512]{2,1,0:T(8,128)S(1)} %get-tuple-element.59), channel_id=1, source_target_pairs={{0,2},{1,3},{2,0},{3,1},{4,6},{5,7},{6,4},{7,5},{8,10},{9,11},{10,... | collective-permute-start | bytes 786440 | tf_op jit(solution)/shard_map/ppermute | solution.py:330
  47.3 7.7 %collective-permute-start.19 = (f32[2,64,512]{2,1,0:T(8,128)S(1)}, f32[2,64,512]{2,1,0:T(8,128)S(1)}, u32[]{:S(2)}, u32[]{:S(2)}) collective-permute-start(f32[2,64,512]{2,1,0:T(8,128)S(1)} %get-tuple-element.53), channel_id=1, source_target_pairs={{0,1},{1,0},{2,3},{3,2},{4,5},{5,4},{6,7},{7,6},{8,9},{9,8},{10,11... | collective-permute-start | bytes 786440 | tf_op jit(solution)/shard_map/ppermute | solution.py:330
  49.1 7.8 %collective-permute-start.17 = (f32[2,64,512]{2,1,0:T(8,128)S(1)}, f32[2,64,512]{2,1,0:T(8,128)S(1)}, u32[]{:S(2)}, u32[]{:S(2)}) collective-permute-start(f32[2,64,512]{2,1,0:T(8,128)S(1)} %get-tuple-element.47), channel_id=1, source_target_pairs={{0,6},{1,7},{2,4},{3,5},{4,2},{5,3},{6,0},{7,1},{8,14},{9,15},{10,... | collective-permute-start | bytes 786440 | tf_op jit(solution)/shard_map/ppermute | solution.py:330
  52.3 6.3 %collective-permute-start.22 = (f32[1,64,512]{2,1,0:T(8,128)S(1)}, f32[1,64,512]{2,1,0:T(8,128)S(1)}, u32[]{:S(2)}, u32[]{:S(2)}) collective-permute-start(f32[1,64,512]{2,1,0:T(8,128)S(1)} %slice_add_fusion), channel_id=1, source_target_pairs={{0,6},{1,7},{2,4},{3,5},{4,2},{5,3},{6,0},{7,1},{8,14},{9,15},{10,... | collective-permute-start | bytes 393224 | tf_op jit(solution)/shard_map/ppermute | solution.py:332
  55.0 5.1 %collective-permute-start.20 = (f32[1,64,512]{2,1,0:T(8,128)S(1)}, f32[1,64,512]{2,1,0:T(8,128)S(1)}, u32[]{:S(2)}, u32[]{:S(2)}) collective-permute-start(f32[1,64,512]{2,1,0:T(8,128)S(1)} %slice_add_fusion.1), channel_id=1, source_target_pairs={{0,2},{1,3},{2,0},{3,1},{4,6},{5,7},{6,4},{7,5},{8,10},{9,11},{10,... | collective-permute-start | bytes 393224 | tf_op jit(solution)/shard_map/ppermute | solution.py:332
  57.0 5.1 %collective-permute-start.18 = (f32[1,64,512]{2,1,0:T(8,128)S(1)}, f32[1,64,512]{2,1,0:T(8,128)S(1)}, u32[]{:S(2)}, u32[]{:S(2)}) collective-permute-start(f32[1,64,512]{2,1,0:T(8,128)S(1)} %slice_add_fusion.2), channel_id=1, source_target_pairs={{0,1},{1,0},{2,3},{3,2},{4,5},{5,4},{6,7},{7,6},{8,9},{9,8},{10,11... | collective-permute-start | bytes 393224 | tf_op jit(solution)/shard_map/ppermute | solution.py:332
  62.4 1.3 %collective-permute-start.23 = (f32[64,128]{1,0:T(8,128)S(1)}, f32[64,128]{1,0:T(8,128)S(1)}, u32[]{:S(2)}, u32[]{:S(2)}) collective-permute-start(f32[64,128]{1,0:T(8,128)S(1)} %shard_map.58), channel_id=1, source_target_pairs={{0,8},{8,0},{16,24},{24,16},{32,40},{40,32},{48,56},{56,48},{64,72... | collective-permute-start | bytes 98312 | tf_op jit(solution)/shard_map/ppermute | solution.py:284
  63.7 5.7 %collective-permute-start.24 = (f32[64,128]{1,0:T(8,128)S(1)}, f32[64,128]{1,0:T(8,128)S(1)}, u32[]{:S(2)}, u32[]{:S(2)}) collective-permute-start(f32[64,128]{1,0:T(8,128)S(1)} %add.35.refs_0_), channel_id=1, source_target_pairs={{0,32},{8,40},{16,48},{24,56},{32,0},{40,8},{48,16},{56,24},{64,96... | collective-permute-start | bytes 98312 | tf_op jit(solution)/shard_map/ppermute | solution.py:284
  65.6 3.9 %collective-permute-start.25 = (f32[64,128]{1,0:T(8,128)S(1)}, f32[64,128]{1,0:T(8,128)S(1)}, u32[]{:S(2)}, u32[]{:S(2)}) collective-permute-start(f32[64,128]{1,0:T(8,128)S(1)} %add.35.refs_0_), channel_id=1, source_target_pairs={{0,16},{8,24},{16,0},{24,8},{32,48},{40,56},{48,32},{56,40},{64,80... | collective-permute-start | bytes 98312 | tf_op jit(solution)/shard_map/ppermute | solution.py:284
  66.7 5.1 %collective-permute-start.26 = (f32[64,128]{1,0:T(8,128)S(1)}, f32[64,128]{1,0:T(8,128)S(1)}, u32[]{:S(2)}, u32[]{:S(2)}) collective-permute-start(f32[64,128]{1,0:T(8,128)S(1)} %add.35.refs_0_), channel_id=1, source_target_pairs={{0,48},{8,56},{16,32},{24,40},{32,16},{40,24},{48,0},{56,8},{64,11... | collective-permute-start | bytes 98312 | tf_op jit(solution)/shard_map/ppermute | solution.py:284
  72.2 6.3 %collective-permute-start.27 = (f32[136,128]{1,0:T(8,128)S(1)}, f32[136,128]{1,0:T(8,128)S(1)}, u32[]{:S(2)}, u32[]{:S(2)}) collective-permute-start(f32[136,128]{1,0:T(8,128)S(1)} %shard_map.59), channel_id=1, source_target_pairs={{0,4},{1,5},{2,6},{3,7},{4,0},{5,1},{6,2},{7,3},{8,12},{9,13},{10,... | collective-permute-start | bytes 208904 | tf_op jit(solution)/shard_map/ppermute | solution.py:284
  73.8 5.5 %collective-permute-start.28 = (f32[136,128]{1,0:T(8,128)S(1)}, f32[136,128]{1,0:T(8,128)S(1)}, u32[]{:S(2)}, u32[]{:S(2)}) collective-permute-start(f32[136,128]{1,0:T(8,128)S(1)} %shard_map.59), channel_id=1, source_target_pairs={{0,6},{1,7},{2,4},{3,5},{4,2},{5,3},{6,0},{7,1},{8,14},{9,15},{10,... | collective-permute-start | bytes 208904 | tf_op jit(solution)/shard_map/ppermute | solution.py:284
  75.0 4.3 %collective-permute-start.29 = (f32[136,128]{1,0:T(8,128)S(1)}, f32[136,128]{1,0:T(8,128)S(1)}, u32[]{:S(2)}, u32[]{:S(2)}) collective-permute-start(f32[136,128]{1,0:T(8,128)S(1)} %shard_map.59), channel_id=1, source_target_pairs={{0,2},{1,3},{2,0},{3,1},{4,6},{5,7},{6,4},{7,5},{8,10},{9,11},{10,... | collective-permute-start | bytes 208904 | tf_op jit(solution)/shard_map/ppermute | solution.py:284
  79.4 4.8 %collective-permute-start.30 = (f32[136,128]{1,0:T(8,128)S(1)}, f32[136,128]{1,0:T(8,128)S(1)}, u32[]{:S(2)}, u32[]{:S(2)}) collective-permute-start(f32[136,128]{1,0:T(8,128)S(1)} %select_select_fusion.1), channel_id=1, source_target_pairs={{0,1},{1,0},{2,3},{3,2},{4,5},{5,4},{6,7},{7,6},{8,9},{9,8},{10,11... | collective-permute-start | bytes 208904 | tf_op jit(solution)/shard_map/ppermute | solution.py:284
  84.3 4.9 %collective-permute-start.31 = (f32[72,128]{1,0:T(8,128)S(1)}, f32[72,128]{1,0:T(8,128)S(1)}, u32[]{:S(2)}, u32[]{:S(2)}) collective-permute-start(f32[72,128]{1,0:T(8,128)S(1)} %slice.23), channel_id=1, source_target_pairs={{0,64},{8,72},{16,80},{24,88},{32,96},{40,104},{48,112},{56,120},{... | collective-permute-start | bytes 110600 | tf_op jit(solution)/shard_map/ppermute | solution.py:284
  89.3 6.1 %collective-permute-start.32 = (f32[72,128]{1,0:T(8,128)S(1)}, f32[72,128]{1,0:T(8,128)S(1)}, u32[]{:S(2)}, u32[]{:S(2)}) collective-permute-start(f32[72,128]{1,0:T(8,128)S(1)} %slice_add_fusion.3.refs_0_), channel_id=1, source_target_pairs={{0,192},{8,200},{16,208},{24,216},{32,224},{40,232},{48,240},{56,2... | collective-permute-start | bytes 110600 | tf_op jit(solution)/shard_map/ppermute | solution.py:284

commit v6 on v5

--- a/solution.py
+++ b/solution.py
@@ -189,10 +189,10 @@
 
 
 def factor_body(scale, *refs):
-    grams, (image_ref, basis_ref, triangle_ref, upper_ref, inverse_ref) = refs[:2], refs[2:]
+    grams, (image_ref, basis_ref, triangle_ref, upper_ref, inverse_ref) = refs[:DEPTHS], refs[DEPTHS:]
     size = upper_ref.shape[0]
     half = size // 2
-    total = tree_sum([gram[...] for gram in grams]) * scale
+    total = line_sum([gram[...] for gram in grams]) * scale
     top, bottom = unpack_gram(total[:half], total[half : half + 1])
     shape = (PANEL, size)
     lane = lax.broadcasted_iota(jnp.int32, shape, 1)
@@ -344,8 +344,7 @@
     came = spread(message, "site", [1])
     message = jnp.where(is_gram, tree_sum(came), jnp.where((apart & 1) == 0, came[0], came[1]))
     gram, own_image = message[:packed], message[packed:]
-    gram = tree_sum(spread(gram, "samp", [BLOCKS]))
-    grams = spread(gram, "samp", [3 * BLOCKS])
+    grams = spread(gram, "samp", [2 * BLOCKS, BLOCKS, 3 * BLOCKS])
     scale = 1.0 / (height * DEPTHS * BLOCKS)
     basis, triangle = kernel_call(
         functools.partial(factor_body, scale),

time: 101 us -> 100 us (0.990)
  waiting for transfers between devices: 36.4 us -> 30.5 us
  starting transfers between devices: 49.7 us -> 53.9 us
    ppermute x10 -> x11, waiting for transfers between devices: 21.2 us -> 15.3 us  [spread(): return [part] + [lax.ppermute(part, axis, perm(k)) for k in shifts]]
    ppermute x10 -> x11, starting transfers between devices: 11.1 us -> 15.3 us  [spread(): return [part] + [lax.ppermute(part, axis, perm(k)) for k in shifts]]
  transfers between devices with their start and end apart: 33 -> 34, of which waited for: 19 -> 19; matrix products, arithmetic and copies ran while one was open for 0% -> 0% of each run, Pallas kernels for 6% -> 6%
where the time goes in v6:
time: 100 us; the launch traced here: 99 us
  starting transfers between devices  53.9 us (54%)
  waiting for transfers between devices  30.5 us (30%)
  Pallas kernels  12.2 us (12%)
  other arithmetic  1.48 us (1%)
    ppermute x11, starting transfers between devices, spread(): return [part] + [lax.ppermute(part, axis, perm(k)) for k in shifts]  15.3 us
    ppermute x11, waiting for transfers between devices, spread(): return [part] + [lax.ppermute(part, axis, perm(k)) for k in shifts]  15.3 us
    pallas_call x11, Pallas kernels, call(): pl.pallas_call(body, out_shape=out_shape, in_specs=in_specs, out_specs=ja...  12.2 us
    ppermute x2, starting transfers between devices, gather_line(): top = lax.ppermute(cut(one, 0), 'samp', samp_perm(other))  6.84 us
    ppermute x2, waiting for transfers between devices, gather_line(): top = lax.ppermute(cut(one, 0), 'samp', samp_perm(other))  5.89 us
    ppermute x2, starting transfers between devices, gather_line(): three = lax.ppermute(block, 'samp', samp_perm(other))  5.76 us
    ppermute x3, starting transfers between devices, local(): lax.ppermute(send_near[r], 'site', site_perm(ROUTES[r][0]))  5.54 us
    ppermute x3, starting transfers between devices, local(): lax.ppermute(folded[r][0], 'site', site_perm(ROUTES[r][1]))  5.22 us
  transfers between devices with their start and end apart: 34, of which 19 were waited for; matrix products, arithmetic and copies ran while one was open for 0% of the time, Pallas kernels for 6%

profile of v6, /device:TPU:32, one launch (start us, length us, event | category | flops | bytes accessed | tf_op | source)
XLA Modules:
  0.0 99.0 jit_solution(15267005109078790698)
XLA Ops:
  0.6 1.2 %compare_select_fusion.refs_0_.refs_6_ = bf16[64,2048]{1,0:T(8,128)(2,1)S(1)} fusion(bf16[64,2048]{1,0:T(8,128)(2,1)} %param.3, s32[64,2048]{1,0:T(8,128)} %param.4), kind=kLoop, calls=%fused_computation | loop fusion | flops 262144 | bytes 1048576 | tf_op jit(solution)/shard_map/jit(_where)/select_n | solution.py:296
  1.8 1.7 %collective-permute-start = (bf16[64,2048]{1,0:T(8,128)(2,1)S(1)}, bf16[64,2048]{1,0:T(8,128)(2,1)S(1)}, u32[]{:S(2)}, u32[]{:S(2)}) collective-permute-start(bf16[64,2048]{1,0:T(8,128)(2,1)S(1)} %compare_select_fusion.refs_0_.refs_6_), channel_id=1, source_target_pairs={{0,16},{8,24},{16,0},{24,8},{32,48},{40,56},{48,32},{56,40},{64,80... | collective-permute-start | bytes 786440 | tf_op jit(solution)/shard_map/ppermute | solution.py:275
  3.5 2.2 %collective-permute-start.1 = (bf16[64,2048]{1,0:T(8,128)(2,1)S(1)}, bf16[64,2048]{1,0:T(8,128)(2,1)S(1)}, u32[]{:S(2)}, u32[]{:S(2)}) collective-permute-start(bf16[64,2048]{1,0:T(8,128)(2,1)S(1)} %compare_select_fusion.refs_0_.refs_6_), channel_id=1, source_target_pairs={{0,48},{8,56},{16,32},{24,40},{32,16},{40,24},{48,0},{56,8},{64,11... | collective-permute-start | bytes 786440 | tf_op jit(solution)/shard_map/ppermute | solution.py:276
  5.7 3.4 %collective-permute-start.7 = (bf16[64,2304]{1,0:T(8,128)(2,1)S(1)}, bf16[64,2304]{1,0:T(8,128)(2,1)S(1)}, u32[]{:S(2)}, u32[]{:S(2)}) collective-permute-start(bf16[64,2304]{1,0:T(8,128)(2,1)S(1)} %pad_maximum_fusion), channel_id=1, source_target_pairs={{0,64},{8,72},{16,80},{24,88},{32,96},{40,104},{48,112},{56,120},{... | collective-permute-start | bytes 884744 | tf_op jit(solution)/shard_map/ppermute | solution.py:275
  9.1 3.6 %collective-permute-start.8 = (bf16[64,2304]{1,0:T(8,128)(2,1)S(1)}, bf16[64,2304]{1,0:T(8,128)(2,1)S(1)}, u32[]{:S(2)}, u32[]{:S(2)}) collective-permute-start(bf16[64,2304]{1,0:T(8,128)(2,1)S(1)} %pad_maximum_fusion), channel_id=1, source_target_pairs={{0,192},{8,200},{16,208},{24,216},{32,224},{40,232},{48,240},{56,2... | collective-permute-start | bytes 884744 | tf_op jit(solution)/shard_map/ppermute | solution.py:276
  12.7 1.1 %collective-permute-start.2 = (bf16[32,2048]{1,0:T(8,128)(2,1)S(1)}, bf16[32,2048]{1,0:T(8,128)(2,1)S(1)}, u32[]{:S(2)}, u32[]{:S(2)}) collective-permute-start(bf16[32,2048]{1,0:T(8,128)(2,1)S(1)} %shard_map.50), channel_id=1, source_target_pairs={{0,48},{8,56},{16,32},{24,40},{32,16},{40,24},{48,0},{56,8},{64,11... | collective-permute-start | bytes 393224 | tf_op jit(solution)/shard_map/ppermute | solution.py:277
  14.0 5.9 %collective-permute-done.2 = bf16[32,2048]{1,0:T(8,128)(2,1)S(1)} collective-permute-done((bf16[32,2048]{1,0:T(8,128)(2,1)S(1)}, bf16[32,2048]{1,0:T(8,128)(2,1)S(1)}, u32[]{:S(2)}, u32[]{:S(2)}) %collective-permute-start.2) | collective-permute-done | bytes 131104 | tf_op jit(solution)/shard_map/ppermute | solution.py:277
  19.9 0.6 collective-permute-start.6
  20.7 5.7 %collective-permute-start.9 = (bf16[32,2304]{1,0:T(8,128)(2,1)S(1)}, bf16[32,2304]{1,0:T(8,128)(2,1)S(1)}, u32[]{:S(2)}, u32[]{:S(2)}) collective-permute-start(bf16[32,2304]{1,0:T(8,128)(2,1)S(1)} %split.8), channel_id=1, source_target_pairs={{0,192},{8,200},{16,208},{24,216},{32,224},{40,232},{48,240},{56,2... | collective-permute-start | bytes 442376 | tf_op jit(solution)/shard_map/ppermute | solution.py:277
  26.4 1.0 %collective-permute-start.10 = (bf16[32,2304]{1,0:T(8,128)(2,1)S(1)}, bf16[32,2304]{1,0:T(8,128)(2,1)S(1)}, u32[]{:S(2)}, u32[]{:S(2)}) collective-permute-start(bf16[32,2304]{1,0:T(8,128)(2,1)S(1)} %split.9), channel_id=1, source_target_pairs={{0,64},{8,72},{16,80},{24,88},{32,96},{40,104},{48,112},{56,120},{... | collective-permute-start | bytes 442376 | tf_op jit(solution)/shard_map/ppermute | solution.py:278
  27.4 2.0 %shard_map.52 = (f32[4,64,384]{2,1,0:T(8,128)S(1)}, f32[4,64,384]{2,1,0:T(8,128)S(1)}, f32[4,64,384]{2,1,0:T(8,128)S(1)}) custom-call(s32[1]{0:T(128)} %bitcast.which, bf16[64,2048]{1,0:T(8,128)(2,1)S(1)} %compare_select_fusion.refs_0_.refs_6_, bf16[128,2048]{1,0:T(8,128)(2,1)S(1)} %constant_dynamic-update-slice_fusion.refs_1_, ...), custom_call_target="tpu_custom_call" | custom-call | flops 1000000 | bytes 100000 | tf_op jit(solution)/shard_map/pallas_call | solution.py:51
  29.4 1.6 %collective-permute-start.11 = (f32[4,64,384]{2,1,0:T(8,128)S(1)}, f32[4,64,384]{2,1,0:T(8,128)S(1)}, u32[]{:S(2)}, u32[]{:S(2)}) collective-permute-start(f32[4,64,384]{2,1,0:T(8,128)S(1)} %get-tuple-element.32), channel_id=1, source_target_pairs={{0,2},{1,3},{2,0},{3,1},{4,6},{5,7},{6,4},{7,5},{8,10},{9,11},{10,... | collective-permute-start | bytes 1179656 | tf_op jit(solution)/shard_map/ppermute | solution.py:321
  31.0 2.1 %collective-permute-start.12 = (f32[4,64,384]{2,1,0:T(8,128)S(1)}, f32[4,64,384]{2,1,0:T(8,128)S(1)}, u32[]{:S(2)}, u32[]{:S(2)}) collective-permute-start(f32[4,64,384]{2,1,0:T(8,128)S(1)} %get-tuple-element.33), channel_id=1, source_target_pairs={{0,6},{1,7},{2,4},{3,5},{4,2},{5,3},{6,0},{7,1},{8,14},{9,15},{10,... | collective-permute-start | bytes 1179656 | tf_op jit(solution)/shard_map/ppermute | solution.py:321
  33.1 1.9 %collective-permute-start.13 = (f32[4,64,384]{2,1,0:T(8,128)S(1)}, f32[4,64,384]{2,1,0:T(8,128)S(1)}, u32[]{:S(2)}, u32[]{:S(2)}) collective-permute-start(f32[4,64,384]{2,1,0:T(8,128)S(1)} %get-tuple-element.34), channel_id=1, source_target_pairs={{0,1},{1,0},{2,3},{3,2},{4,5},{5,4},{6,7},{7,6},{8,9},{9,8},{10,11... | collective-permute-start | bytes 1179656 | tf_op jit(solution)/shard_map/ppermute | solution.py:321
  35.0 2.0 %shard_map.53 = (f32[4,64,128]{2,1,0:T(8,128)S(1)}, f32[4,64,128]{2,1,0:T(8,128)S(1)}, f32[4,64,128]{2,1,0:T(8,128)S(1)}) custom-call(s32[1]{0:T(128)} %bitcast.which, bf16[64,2048]{1,0:T(8,128)(2,1)S(1)} %compare_select_fusion.refs_0_.refs_6_, bf16[128,2048]{1,0:T(8,128)(2,1)S(1)} %constant_dynamic-update-slice_fusion.refs_1_, ...), custom_call_target="tpu_custom_call" | custom-call | flops 10000000000 | bytes 100000 | tf_op jit(solution)/shard_map/pallas_call | solution.py:51
  36.9 1.5 %collective-permute-start.14 = (f32[4,64,128]{2,1,0:T(8,128)S(1)}, f32[4,64,128]{2,1,0:T(8,128)S(1)}, u32[]{:S(2)}, u32[]{:S(2)}) collective-permute-start(f32[4,64,128]{2,1,0:T(8,128)S(1)} %get-tuple-element.36), channel_id=1, source_target_pairs={{0,2},{1,3},{2,0},{3,1},{4,6},{5,7},{6,4},{7,5},{8,10},{9,11},{10,... | collective-permute-start | bytes 393224 | tf_op jit(solution)/shard_map/ppermute | solution.py:324
  38.5 2.3 %collective-permute-start.15 = (f32[4,64,128]{2,1,0:T(8,128)S(1)}, f32[4,64,128]{2,1,0:T(8,128)S(1)}, u32[]{:S(2)}, u32[]{:S(2)}) collective-permute-start(f32[4,64,128]{2,1,0:T(8,128)S(1)} %get-tuple-element.37), channel_id=1, source_target_pairs={{0,6},{1,7},{2,4},{3,5},{4,2},{5,3},{6,0},{7,1},{8,14},{9,15},{10,... | collective-permute-start | bytes 393224 | tf_op jit(solution)/shard_map/ppermute | solution.py:324
  40.8 1.4 %collective-permute-start.16 = (f32[4,64,128]{2,1,0:T(8,128)S(1)}, f32[4,64,128]{2,1,0:T(8,128)S(1)}, u32[]{:S(2)}, u32[]{:S(2)}) collective-permute-start(f32[4,64,128]{2,1,0:T(8,128)S(1)} %get-tuple-element.38), channel_id=1, source_target_pairs={{0,1},{1,0},{2,3},{3,2},{4,5},{5,4},{6,7},{7,6},{8,9},{9,8},{10,11... | collective-permute-start | bytes 393224 | tf_op jit(solution)/shard_map/ppermute | solution.py:324
  42.7 0.8 collective-permute-done.13.near
  43.5 2.0 %shard_map.54 = (f32[4,64,512]{2,1,0:T(8,128)S(1)}, f32[4,64,512]{2,1,0:T(8,128)S(1)}, f32[4,64,512]{2,1,0:T(8,128)S(1)}, f32[192,128]{1,0:T(8,128)S(1)}) custom-call(s32[1]{0:T(128)} %bitcast.which, bf16[64,2048]{1,0:T(8,128)(2,1)S(1)} %compare_select_fusion.refs_0_.refs_6_, bf16[128,2048]{1,0:T(8,128)(2,1)S(1)} %constant_dynamic-update-slice_fusion.refs_1_, ...), custom_call_target="tpu_custom_call" | custom-call | flops 10000000000 | bytes 100000 | tf_op jit(solution)/shard_map/pallas_call | solution.py:51
  45.8 1.4 %collective-permute-start.21 = (f32[2,64,512]{2,1,0:T(8,128)S(1)}, f32[2,64,512]{2,1,0:T(8,128)S(1)}, u32[]{:S(2)}, u32[]{:S(2)}) collective-permute-start(f32[2,64,512]{2,1,0:T(8,128)S(1)} %get-tuple-element.59), channel_id=1, source_target_pairs={{0,2},{1,3},{2,0},{3,1},{4,6},{5,7},{6,4},{7,5},{8,10},{9,11},{10,... | collective-permute-start | bytes 786440 | tf_op jit(solution)/shard_map/ppermute | solution.py:330
  47.3 1.8 %collective-permute-start.19 = (f32[2,64,512]{2,1,0:T(8,128)S(1)}, f32[2,64,512]{2,1,0:T(8,128)S(1)}, u32[]{:S(2)}, u32[]{:S(2)}) collective-permute-start(f32[2,64,512]{2,1,0:T(8,128)S(1)} %get-tuple-element.53), channel_id=1, source_target_pairs={{0,1},{1,0},{2,3},{3,2},{4,5},{5,4},{6,7},{7,6},{8,9},{9,8},{10,11... | collective-permute-start | bytes 786440 | tf_op jit(solution)/shard_map/ppermute | solution.py:330
  49.1 2.0 %collective-permute-start.17 = (f32[2,64,512]{2,1,0:T(8,128)S(1)}, f32[2,64,512]{2,1,0:T(8,128)S(1)}, u32[]{:S(2)}, u32[]{:S(2)}) collective-permute-start(f32[2,64,512]{2,1,0:T(8,128)S(1)} %get-tuple-element.47), channel_id=1, source_target_pairs={{0,6},{1,7},{2,4},{3,5},{4,2},{5,3},{6,0},{7,1},{8,14},{9,15},{10,... | collective-permute-start | bytes 786440 | tf_op jit(solution)/shard_map/ppermute | solution.py:330
  51.1 1.1 %collective-permute-done.21.refs_7_ = f32[2,64,512]{2,1,0:T(8,128)S(1)} collective-permute-done((f32[2,64,512]{2,1,0:T(8,128)S(1)}, f32[2,64,512]{2,1,0:T(8,128)S(1)}, u32[]{:S(2)}, u32[]{:S(2)}) %collective-permute-start.21) | collective-permute-done | bytes 262176 | tf_op jit(solution)/shard_map/ppermute | solution.py:330
  52.3 2.7 %collective-permute-start.22 = (f32[1,64,512]{2,1,0:T(8,128)S(1)}, f32[1,64,512]{2,1,0:T(8,128)S(1)}, u32[]{:S(2)}, u32[]{:S(2)}) collective-permute-start(f32[1,64,512]{2,1,0:T(8,128)S(1)} %slice_add_fusion), channel_id=1, source_target_pairs={{0,6},{1,7},{2,4},{3,5},{4,2},{5,3},{6,0},{7,1},{8,14},{9,15},{10,... | collective-permute-start | bytes 393224 | tf_op jit(solution)/shard_map/ppermute | solution.py:332
  55.1 1.9 %collective-permute-done.17.refs_1_ = f32[2,64,512]{2,1,0:T(8,128)S(1)} collective-permute-done((f32[2,64,512]{2,1,0:T(8,128)S(1)}, f32[2,64,512]{2,1,0:T(8,128)S(1)}, u32[]{:S(2)}, u32[]{:S(2)}) %collective-permute-start.17) | collective-permute-done | bytes 262176 | tf_op jit(solution)/shard_map/ppermute | solution.py:330
  57.5 1.0 %collective-permute-done.22.refs_8_ = f32[1,64,512]{2,1,0:T(8,128)S(1)} collective-permute-done((f32[1,64,512]{2,1,0:T(8,128)S(1)}, f32[1,64,512]{2,1,0:T(8,128)S(1)}, u32[]{:S(2)}, u32[]{:S(2)}) %collective-permute-start.22) | collective-permute-done | bytes 131104 | tf_op jit(solution)/shard_map/ppermute | solution.py:332
  58.6 1.5 %collective-permute-done.20.refs_5_ = f32[1,64,512]{2,1,0:T(8,128)S(1)} collective-permute-done((f32[1,64,512]{2,1,0:T(8,128)S(1)}, f32[1,64,512]{2,1,0:T(8,128)S(1)}, u32[]{:S(2)}, u32[]{:S(2)}) %collective-permute-start.20) | collective-permute-done | bytes 131104 | tf_op jit(solution)/shard_map/ppermute | solution.py:332
  60.0 2.0 %collective-permute-done.18.refs_2_ = f32[1,64,512]{2,1,0:T(8,128)S(1)} collective-permute-done((f32[1,64,512]{2,1,0:T(8,128)S(1)}, f32[1,64,512]{2,1,0:T(8,128)S(1)}, u32[]{:S(2)}, u32[]{:S(2)}) %collective-permute-start.18) | collective-permute-done | bytes 131104 | tf_op jit(solution)/shard_map/ppermute | solution.py:332
  62.5 1.2 %collective-permute-done.23 = f32[64,128]{1,0:T(8,128)S(1)} collective-permute-done((f32[64,128]{1,0:T(8,128)S(1)}, f32[64,128]{1,0:T(8,128)S(1)}, u32[]{:S(2)}, u32[]{:S(2)}) %collective-permute-start.23) | collective-permute-done | bytes 32800 | tf_op jit(solution)/shard_map/ppermute | solution.py:284
  63.7 1.9 %collective-permute-start.24 = (f32[64,128]{1,0:T(8,128)S(1)}, f32[64,128]{1,0:T(8,128)S(1)}, u32[]{:S(2)}, u32[]{:S(2)}) collective-permute-start(f32[64,128]{1,0:T(8,128)S(1)} %add.32.refs_0_), channel_id=1, source_target_pairs={{0,32},{8,40},{16,48},{24,56},{32,0},{40,8},{48,16},{56,24},{64,96... | collective-permute-start | bytes 98312 | tf_op jit(solution)/shard_map/ppermute | solution.py:284
  65.6 1.0 %collective-permute-start.25 = (f32[64,128]{1,0:T(8,128)S(1)}, f32[64,128]{1,0:T(8,128)S(1)}, u32[]{:S(2)}, u32[]{:S(2)}) collective-permute-start(f32[64,128]{1,0:T(8,128)S(1)} %add.32.refs_0_), channel_id=1, source_target_pairs={{0,16},{8,24},{16,0},{24,8},{32,48},{40,56},{48,32},{56,40},{64,80... | collective-permute-start | bytes 98312 | tf_op jit(solution)/shard_map/ppermute | solution.py:284
  66.7 1.1 %collective-permute-start.26 = (f32[64,128]{1,0:T(8,128)S(1)}, f32[64,128]{1,0:T(8,128)S(1)}, u32[]{:S(2)}, u32[]{:S(2)}) collective-permute-start(f32[64,128]{1,0:T(8,128)S(1)} %add.32.refs_0_), channel_id=1, source_target_pairs={{0,48},{8,56},{16,32},{24,40},{32,16},{40,24},{48,0},{56,8},{64,11... | collective-permute-start | bytes 98312 | tf_op jit(solution)/shard_map/ppermute | solution.py:284
  67.8 1.6 %collective-permute-done.24.refs_1_ = f32[64,128]{1,0:T(8,128)S(1)} collective-permute-done((f32[64,128]{1,0:T(8,128)S(1)}, f32[64,128]{1,0:T(8,128)S(1)}, u32[]{:S(2)}, u32[]{:S(2)}) %collective-permute-start.24) | collective-permute-done | bytes 32800 | tf_op jit(solution)/shard_map/ppermute | solution.py:284
  69.6 2.3 %collective-permute-done.26.refs_3_ = f32[64,128]{1,0:T(8,128)S(1)} collective-permute-done((f32[64,128]{1,0:T(8,128)S(1)}, f32[64,128]{1,0:T(8,128)S(1)}, u32[]{:S(2)}, u32[]{:S(2)}) %collective-permute-start.26) | collective-permute-done | bytes 32800 | tf_op jit(solution)/shard_map/ppermute | solution.py:284
  72.2 1.6 %collective-permute-start.27 = (f32[136,128]{1,0:T(8,128)S(1)}, f32[136,128]{1,0:T(8,128)S(1)}, u32[]{:S(2)}, u32[]{:S(2)}) collective-permute-start(f32[136,128]{1,0:T(8,128)S(1)} %shard_map.59), channel_id=1, source_target_pairs={{0,4},{1,5},{2,6},{3,7},{4,0},{5,1},{6,2},{7,3},{8,12},{9,13},{10,... | collective-permute-start | bytes 208904 | tf_op jit(solution)/shard_map/ppermute | solution.py:284
  73.8 1.2 %collective-permute-start.28 = (f32[136,128]{1,0:T(8,128)S(1)}, f32[136,128]{1,0:T(8,128)S(1)}, u32[]{:S(2)}, u32[]{:S(2)}) collective-permute-start(f32[136,128]{1,0:T(8,128)S(1)} %shard_map.59), channel_id=1, source_target_pairs={{0,6},{1,7},{2,4},{3,5},{4,2},{5,3},{6,0},{7,1},{8,14},{9,15},{10,... | collective-permute-start | bytes 208904 | tf_op jit(solution)/shard_map/ppermute | solution.py:284
  75.0 0.7 collective-permute-start.29
  75.7 2.7 %collective-permute-done.27 = f32[136,128]{1,0:T(8,128)S(1)} collective-permute-done((f32[136,128]{1,0:T(8,128)S(1)}, f32[136,128]{1,0:T(8,128)S(1)}, u32[]{:S(2)}, u32[]{:S(2)}) %collective-permute-start.27) | collective-permute-done | bytes 69664 | tf_op jit(solution)/shard_map/ppermute | solution.py:284
  78.4 0.9 collective-permute-done.28
  79.4 1.0 %collective-permute-start.30 = (f32[136,128]{1,0:T(8,128)S(1)}, f32[136,128]{1,0:T(8,128)S(1)}, u32[]{:S(2)}, u32[]{:S(2)}) collective-permute-start(f32[136,128]{1,0:T(8,128)S(1)} %select_select_fusion.1), channel_id=1, source_target_pairs={{0,1},{1,0},{2,3},{3,2},{4,5},{5,4},{6,7},{7,6},{8,9},{9,8},{10,11... | collective-permute-start | bytes 208904 | tf_op jit(solution)/shard_map/ppermute | solution.py:284
  80.4 3.4 %collective-permute-done.30 = f32[136,128]{1,0:T(8,128)S(1)} collective-permute-done((f32[136,128]{1,0:T(8,128)S(1)}, f32[136,128]{1,0:T(8,128)S(1)}, u32[]{:S(2)}, u32[]{:S(2)}) %collective-permute-start.30) | collective-permute-done | bytes 69664 | tf_op jit(solution)/shard_map/ppermute | solution.py:284
  83.9 2.5 %collective-permute-start.31 = (f32[72,128]{1,0:T(8,128)S(1)}, f32[72,128]{1,0:T(8,128)S(1)}, u32[]{:S(2)}, u32[]{:S(2)}) collective-permute-start(f32[72,128]{1,0:T(8,128)S(1)} %slice.23.refs_0_), channel_id=1, source_target_pairs={{0,128},{8,136},{16,144},{24,152},{32,160},{40,168},{48,176},{56,1... | collective-permute-start | bytes 110600 | tf_op jit(solution)/shard_map/ppermute | solution.py:284
  86.4 1.1 %collective-permute-start.32 = (f32[72,128]{1,0:T(8,128)S(1)}, f32[72,128]{1,0:T(8,128)S(1)}, u32[]{:S(2)}, u32[]{:S(2)}) collective-permute-start(f32[72,128]{1,0:T(8,128)S(1)} %slice.23.refs_0_), channel_id=1, source_target_pairs={{0,64},{8,72},{16,80},{24,88},{32,96},{40,104},{48,112},{56,120},{... | collective-permute-start | bytes 110600 | tf_op jit(solution)/shard_map/ppermute | solution.py:284
  87.5 3.0 %collective-permute-start.33 = (f32[72,128]{1,0:T(8,128)S(1)}, f32[72,128]{1,0:T(8,128)S(1)}, u32[]{:S(2)}, u32[]{:S(2)}) collective-permute-start(f32[72,128]{1,0:T(8,128)S(1)} %slice.23.refs_0_), channel_id=1, source_target_pairs={{0,192},{8,200},{16,208},{24,216},{32,224},{40,232},{48,240},{56,2... | collective-permute-start | bytes 110600 | tf_op jit(solution)/shard_map/ppermute | solution.py:284
  90.5 1.4 %collective-permute-done.31.refs_1_ = f32[72,128]{1,0:T(8,128)S(1)} collective-permute-done((f32[72,128]{1,0:T(8,128)S(1)}, f32[72,128]{1,0:T(8,128)S(1)}, u32[]{:S(2)}, u32[]{:S(2)}) %collective-permute-start.31) | collective-permute-done | bytes 36896 | tf_op jit(solution)/shard_map/ppermute | solution.py:284
  91.9 1.7 %collective-permute-done.33.refs_3_ = f32[72,128]{1,0:T(8,128)S(1)} collective-permute-done((f32[72,128]{1,0:T(8,128)S(1)}, f32[72,128]{1,0:T(8,128)S(1)}, u32[]{:S(2)}, u32[]{:S(2)}) %collective-permute-start.33) | collective-permute-done | bytes 36896 | tf_op jit(solution)/shard_map/ppermute | solution.py:284
  93.6 5.4 %shard_map.60 = (f32[64,128]{1,0:T(8,128)}, f32[128,128]{1,0:T(8,128)}) custom-call(f32[72,128]{1,0:T(8,128)S(1)} %slice.23.refs_0_, f32[72,128]{1,0:T(8,128)S(1)} %collective-permute-done.31.refs_1_, f32[72,128]{1,0:T(8,128)S(1)} %collective-permute-done.32.refs_2_, f32[72,128]{1,0:T(8,128)S(1)} %collective-permute-done.33.refs_3_, f32[64,128]{1,0:T(8,128)S(1)} %slice.24.refs_4_), custom_call_target="tpu_custom_call" | custom-call | tf_op jit(solution)/shard_map/pallas_call | solution.py:51
  (51 shorter events, 3.2 us)
Async XLA Ops:
  0.6 5.1 %copy-start = (f32[64,128]{1,0:T(8,128)S(1)}, f32[64,128]{1,0:T(8,128)}, u32[]{:S(2)}) copy-start(f32[64,128]{1,0:T(8,128)} %refs_10_.1) | copy-start | bytes 98308
  1.8 10.8 %collective-permute-start = (bf16[64,2048]{1,0:T(8,128)(2,1)S(1)}, bf16[64,2048]{1,0:T(8,128)(2,1)S(1)}, u32[]{:S(2)}, u32[]{:S(2)}) collective-permute-start(bf16[64,2048]{1,0:T(8,128)(2,1)S(1)} %compare_select_fusion.refs_0_.refs_6_), channel_id=1, source_target_pairs={{0,16},{8,24},{16,0},{24,8},{32,48},{40,56},{48,32},{56,40},{64,80... | collective-permute-start | bytes 786440 | tf_op jit(solution)/shard_map/ppermute | solution.py:275
  3.5 10.3 %collective-permute-start.1 = (bf16[64,2048]{1,0:T(8,128)(2,1)S(1)}, bf16[64,2048]{1,0:T(8,128)(2,1)S(1)}, u32[]{:S(2)}, u32[]{:S(2)}) collective-permute-start(bf16[64,2048]{1,0:T(8,128)(2,1)S(1)} %compare_select_fusion.refs_0_.refs_6_), channel_id=1, source_target_pairs={{0,48},{8,56},{16,32},{24,40},{32,16},{40,24},{48,0},{56,8},{64,11... | collective-permute-start | bytes 786440 | tf_op jit(solution)/shard_map/ppermute | solution.py:276
  5.7 15.0 %collective-permute-start.7 = (bf16[64,2304]{1,0:T(8,128)(2,1)S(1)}, bf16[64,2304]{1,0:T(8,128)(2,1)S(1)}, u32[]{:S(2)}, u32[]{:S(2)}) collective-permute-start(bf16[64,2304]{1,0:T(8,128)(2,1)S(1)} %pad_maximum_fusion), channel_id=1, source_target_pairs={{0,64},{8,72},{16,80},{24,88},{32,96},{40,104},{48,112},{56,120},{... | collective-permute-start | bytes 884744 | tf_op jit(solution)/shard_map/ppermute | solution.py:275
  9.1 17.3 %collective-permute-start.8 = (bf16[64,2304]{1,0:T(8,128)(2,1)S(1)}, bf16[64,2304]{1,0:T(8,128)(2,1)S(1)}, u32[]{:S(2)}, u32[]{:S(2)}) collective-permute-start(bf16[64,2304]{1,0:T(8,128)(2,1)S(1)} %pad_maximum_fusion), channel_id=1, source_target_pairs={{0,192},{8,200},{16,208},{24,216},{32,224},{40,232},{48,240},{56,2... | collective-permute-start | bytes 884744 | tf_op jit(solution)/shard_map/ppermute | solution.py:276
  12.7 14.8 %collective-permute-start.4 = (bf16[64,2048]{1,0:T(8,128)(2,1)S(1)}, bf16[64,2048]{1,0:T(8,128)(2,1)S(1)}, u32[]{:S(2)}, u32[]{:S(2)}) collective-permute-start(bf16[64,2048]{1,0:T(8,128)(2,1)S(1)} %compare_select_fusion.refs_0_.refs_6_), channel_id=1, source_target_pairs={{0,8},{8,0},{16,24},{24,16},{32,40},{40,32},{48,56},{56,48},{64,72... | collective-permute-start | bytes 786440 | tf_op jit(solution)/shard_map/ppermute | solution.py:303
  12.7 7.2 %collective-permute-start.2 = (bf16[32,2048]{1,0:T(8,128)(2,1)S(1)}, bf16[32,2048]{1,0:T(8,128)(2,1)S(1)}, u32[]{:S(2)}, u32[]{:S(2)}) collective-permute-start(bf16[32,2048]{1,0:T(8,128)(2,1)S(1)} %shard_map.50), channel_id=1, source_target_pairs={{0,48},{8,56},{16,32},{24,40},{32,16},{40,24},{48,0},{56,8},{64,11... | collective-permute-start | bytes 393224 | tf_op jit(solution)/shard_map/ppermute | solution.py:277
  13.8 6.1 %collective-permute-start.3 = (bf16[32,2048]{1,0:T(8,128)(2,1)S(1)}, bf16[32,2048]{1,0:T(8,128)(2,1)S(1)}, u32[]{:S(2)}, u32[]{:S(2)}) collective-permute-start(bf16[32,2048]{1,0:T(8,128)(2,1)S(1)} %shard_map.51), channel_id=1, source_target_pairs={{0,16},{8,24},{16,0},{24,8},{32,48},{40,56},{48,32},{56,40},{64,80... | collective-permute-start | bytes 393224 | tf_op jit(solution)/shard_map/ppermute | solution.py:278
  19.9 7.5 %collective-permute-start.5 = (bf16[128,2048]{1,0:T(8,128)(2,1)S(1)}, bf16[128,2048]{1,0:T(8,128)(2,1)S(1)}, u32[]{:S(2)}, u32[]{:S(2)}) collective-permute-start(bf16[128,2048]{1,0:T(8,128)(2,1)S(1)} %constant_dynamic-update-slice_fusion.refs_1_), channel_id=1, source_target_pairs={{0,8},{8,0},{16,24},{24,16},{32,40},{40,32},{48,56},{56,48},{64,72... | collective-permute-start | bytes 1572872 | tf_op jit(solution)/shard_map/ppermute | solution.py:303
  19.9 7.5 %collective-permute-start.6 = (bf16[64,2048]{1,0:T(8,128)(2,1)S(1)}, bf16[64,2048]{1,0:T(8,128)(2,1)S(1)}, u32[]{:S(2)}, u32[]{:S(2)}) collective-permute-start(bf16[64,2048]{1,0:T(8,128)(2,1)S(1)} %constant_dynamic-update-slice_fusion.2.refs_2_), channel_id=1, source_target_pairs={{0,8},{8,0},{16,24},{24,16},{32,40},{40,32},{48,56},{56,48},{64,72... | collective-permute-start | bytes 786440 | tf_op jit(solution)/shard_map/ppermute | solution.py:303
  20.7 14.2 %collective-permute-start.9 = (bf16[32,2304]{1,0:T(8,128)(2,1)S(1)}, bf16[32,2304]{1,0:T(8,128)(2,1)S(1)}, u32[]{:S(2)}, u32[]{:S(2)}) collective-permute-start(bf16[32,2304]{1,0:T(8,128)(2,1)S(1)} %split.8), channel_id=1, source_target_pairs={{0,192},{8,200},{16,208},{24,216},{32,224},{40,232},{48,240},{56,2... | collective-permute-start | bytes 442376 | tf_op jit(solution)/shard_map/ppermute | solution.py:277
  26.4 8.5 %collective-permute-start.10 = (bf16[32,2304]{1,0:T(8,128)(2,1)S(1)}, bf16[32,2304]{1,0:T(8,128)(2,1)S(1)}, u32[]{:S(2)}, u32[]{:S(2)}) collective-permute-start(bf16[32,2304]{1,0:T(8,128)(2,1)S(1)} %split.9), channel_id=1, source_target_pairs={{0,64},{8,72},{16,80},{24,88},{32,96},{40,104},{48,112},{56,120},{... | collective-permute-start | bytes 442376 | tf_op jit(solution)/shard_map/ppermute | solution.py:278
  29.4 11.4 %collective-permute-start.11 = (f32[4,64,384]{2,1,0:T(8,128)S(1)}, f32[4,64,384]{2,1,0:T(8,128)S(1)}, u32[]{:S(2)}, u32[]{:S(2)}) collective-permute-start(f32[4,64,384]{2,1,0:T(8,128)S(1)} %get-tuple-element.32), channel_id=1, source_target_pairs={{0,2},{1,3},{2,0},{3,1},{4,6},{5,7},{6,4},{7,5},{8,10},{9,11},{10,... | collective-permute-start | bytes 1179656 | tf_op jit(solution)/shard_map/ppermute | solution.py:321
  31.0 11.7 %collective-permute-start.12 = (f32[4,64,384]{2,1,0:T(8,128)S(1)}, f32[4,64,384]{2,1,0:T(8,128)S(1)}, u32[]{:S(2)}, u32[]{:S(2)}) collective-permute-start(f32[4,64,384]{2,1,0:T(8,128)S(1)} %get-tuple-element.33), channel_id=1, source_target_pairs={{0,6},{1,7},{2,4},{3,5},{4,2},{5,3},{6,0},{7,1},{8,14},{9,15},{10,... | collective-permute-start | bytes 1179656 | tf_op jit(solution)/shard_map/ppermute | solution.py:321
  33.1 10.5 %collective-permute-start.13 = (f32[4,64,384]{2,1,0:T(8,128)S(1)}, f32[4,64,384]{2,1,0:T(8,128)S(1)}, u32[]{:S(2)}, u32[]{:S(2)}) collective-permute-start(f32[4,64,384]{2,1,0:T(8,128)S(1)} %get-tuple-element.34), channel_id=1, source_target_pairs={{0,1},{1,0},{2,3},{3,2},{4,5},{5,4},{6,7},{7,6},{8,9},{9,8},{10,11... | collective-permute-start | bytes 1179656 | tf_op jit(solution)/shard_map/ppermute | solution.py:321
  36.9 8.6 %collective-permute-start.14 = (f32[4,64,128]{2,1,0:T(8,128)S(1)}, f32[4,64,128]{2,1,0:T(8,128)S(1)}, u32[]{:S(2)}, u32[]{:S(2)}) collective-permute-start(f32[4,64,128]{2,1,0:T(8,128)S(1)} %get-tuple-element.36), channel_id=1, source_target_pairs={{0,2},{1,3},{2,0},{3,1},{4,6},{5,7},{6,4},{7,5},{8,10},{9,11},{10,... | collective-permute-start | bytes 393224 | tf_op jit(solution)/shard_map/ppermute | solution.py:324
  38.5 7.1 %collective-permute-start.15 = (f32[4,64,128]{2,1,0:T(8,128)S(1)}, f32[4,64,128]{2,1,0:T(8,128)S(1)}, u32[]{:S(2)}, u32[]{:S(2)}) collective-permute-start(f32[4,64,128]{2,1,0:T(8,128)S(1)} %get-tuple-element.37), channel_id=1, source_target_pairs={{0,6},{1,7},{2,4},{3,5},{4,2},{5,3},{6,0},{7,1},{8,14},{9,15},{10,... | collective-permute-start | bytes 393224 | tf_op jit(solution)/shard_map/ppermute | solution.py:324
  40.8 5.0 %collective-permute-start.16 = (f32[4,64,128]{2,1,0:T(8,128)S(1)}, f32[4,64,128]{2,1,0:T(8,128)S(1)}, u32[]{:S(2)}, u32[]{:S(2)}) collective-permute-start(f32[4,64,128]{2,1,0:T(8,128)S(1)} %get-tuple-element.38), channel_id=1, source_target_pairs={{0,1},{1,0},{2,3},{3,2},{4,5},{5,4},{6,7},{7,6},{8,9},{9,8},{10,11... | collective-permute-start | bytes 393224 | tf_op jit(solution)/shard_map/ppermute | solution.py:324
  45.8 6.5 %collective-permute-start.21 = (f32[2,64,512]{2,1,0:T(8,128)S(1)}, f32[2,64,512]{2,1,0:T(8,128)S(1)}, u32[]{:S(2)}, u32[]{:S(2)}) collective-permute-start(f32[2,64,512]{2,1,0:T(8,128)S(1)} %get-tuple-element.59), channel_id=1, source_target_pairs={{0,2},{1,3},{2,0},{3,1},{4,6},{5,7},{6,4},{7,5},{8,10},{9,11},{10,... | collective-permute-start | bytes 786440 | tf_op jit(solution)/shard_map/ppermute | solution.py:330
  47.3 7.7 %collective-permute-start.19 = (f32[2,64,512]{2,1,0:T(8,128)S(1)}, f32[2,64,512]{2,1,0:T(8,128)S(1)}, u32[]{:S(2)}, u32[]{:S(2)}) collective-permute-start(f32[2,64,512]{2,1,0:T(8,128)S(1)} %get-tuple-element.53), channel_id=1, source_target_pairs={{0,1},{1,0},{2,3},{3,2},{4,5},{5,4},{6,7},{7,6},{8,9},{9,8},{10,11... | collective-permute-start | bytes 786440 | tf_op jit(solution)/shard_map/ppermute | solution.py:330
  49.1 7.8 %collective-permute-start.17 = (f32[2,64,512]{2,1,0:T(8,128)S(1)}, f32[2,64,512]{2,1,0:T(8,128)S(1)}, u32[]{:S(2)}, u32[]{:S(2)}) collective-permute-start(f32[2,64,512]{2,1,0:T(8,128)S(1)} %get-tuple-element.47), channel_id=1, source_target_pairs={{0,6},{1,7},{2,4},{3,5},{4,2},{5,3},{6,0},{7,1},{8,14},{9,15},{10,... | collective-permute-start | bytes 786440 | tf_op jit(solution)/shard_map/ppermute | solution.py:330
  52.3 6.3 %collective-permute-start.22 = (f32[1,64,512]{2,1,0:T(8,128)S(1)}, f32[1,64,512]{2,1,0:T(8,128)S(1)}, u32[]{:S(2)}, u32[]{:S(2)}) collective-permute-start(f32[1,64,512]{2,1,0:T(8,128)S(1)} %slice_add_fusion), channel_id=1, source_target_pairs={{0,6},{1,7},{2,4},{3,5},{4,2},{5,3},{6,0},{7,1},{8,14},{9,15},{10,... | collective-permute-start | bytes 393224 | tf_op jit(solution)/shard_map/ppermute | solution.py:332
  55.0 5.1 %collective-permute-start.20 = (f32[1,64,512]{2,1,0:T(8,128)S(1)}, f32[1,64,512]{2,1,0:T(8,128)S(1)}, u32[]{:S(2)}, u32[]{:S(2)}) collective-permute-start(f32[1,64,512]{2,1,0:T(8,128)S(1)} %slice_add_fusion.1), channel_id=1, source_target_pairs={{0,2},{1,3},{2,0},{3,1},{4,6},{5,7},{6,4},{7,5},{8,10},{9,11},{10,... | collective-permute-start | bytes 393224 | tf_op jit(solution)/shard_map/ppermute | solution.py:332
  57.0 5.1 %collective-permute-start.18 = (f32[1,64,512]{2,1,0:T(8,128)S(1)}, f32[1,64,512]{2,1,0:T(8,128)S(1)}, u32[]{:S(2)}, u32[]{:S(2)}) collective-permute-start(f32[1,64,512]{2,1,0:T(8,128)S(1)} %slice_add_fusion.2), channel_id=1, source_target_pairs={{0,1},{1,0},{2,3},{3,2},{4,5},{5,4},{6,7},{7,6},{8,9},{9,8},{10,11... | collective-permute-start | bytes 393224 | tf_op jit(solution)/shard_map/ppermute | solution.py:332
  62.4 1.3 %collective-permute-start.23 = (f32[64,128]{1,0:T(8,128)S(1)}, f32[64,128]{1,0:T(8,128)S(1)}, u32[]{:S(2)}, u32[]{:S(2)}) collective-permute-start(f32[64,128]{1,0:T(8,128)S(1)} %shard_map.58), channel_id=1, source_target_pairs={{0,8},{8,0},{16,24},{24,16},{32,40},{40,32},{48,56},{56,48},{64,72... | collective-permute-start | bytes 98312 | tf_op jit(solution)/shard_map/ppermute | solution.py:284
  63.7 5.7 %collective-permute-start.24 = (f32[64,128]{1,0:T(8,128)S(1)}, f32[64,128]{1,0:T(8,128)S(1)}, u32[]{:S(2)}, u32[]{:S(2)}) collective-permute-start(f32[64,128]{1,0:T(8,128)S(1)} %add.32.refs_0_), channel_id=1, source_target_pairs={{0,32},{8,40},{16,48},{24,56},{32,0},{40,8},{48,16},{56,24},{64,96... | collective-permute-start | bytes 98312 | tf_op jit(solution)/shard_map/ppermute | solution.py:284
  65.6 3.9 %collective-permute-start.25 = (f32[64,128]{1,0:T(8,128)S(1)}, f32[64,128]{1,0:T(8,128)S(1)}, u32[]{:S(2)}, u32[]{:S(2)}) collective-permute-start(f32[64,128]{1,0:T(8,128)S(1)} %add.32.refs_0_), channel_id=1, source_target_pairs={{0,16},{8,24},{16,0},{24,8},{32,48},{40,56},{48,32},{56,40},{64,80... | collective-permute-start | bytes 98312 | tf_op jit(solution)/shard_map/ppermute | solution.py:284
  66.7 5.1 %collective-permute-start.26 = (f32[64,128]{1,0:T(8,128)S(1)}, f32[64,128]{1,0:T(8,128)S(1)}, u32[]{:S(2)}, u32[]{:S(2)}) collective-permute-start(f32[64,128]{1,0:T(8,128)S(1)} %add.32.refs_0_), channel_id=1, source_target_pairs={{0,48},{8,56},{16,32},{24,40},{32,16},{40,24},{48,0},{56,8},{64,11... | collective-permute-start | bytes 98312 | tf_op jit(solution)/shard_map/ppermute | solution.py:284
  72.2 6.3 %collective-permute-start.27 = (f32[136,128]{1,0:T(8,128)S(1)}, f32[136,128]{1,0:T(8,128)S(1)}, u32[]{:S(2)}, u32[]{:S(2)}) collective-permute-start(f32[136,128]{1,0:T(8,128)S(1)} %shard_map.59), channel_id=1, source_target_pairs={{0,4},{1,5},{2,6},{3,7},{4,0},{5,1},{6,2},{7,3},{8,12},{9,13},{10,... | collective-permute-start | bytes 208904 | tf_op jit(solution)/shard_map/ppermute | solution.py:284
  73.8 5.5 %collective-permute-start.28 = (f32[136,128]{1,0:T(8,128)S(1)}, f32[136,128]{1,0:T(8,128)S(1)}, u32[]{:S(2)}, u32[]{:S(2)}) collective-permute-start(f32[136,128]{1,0:T(8,128)S(1)} %shard_map.59), channel_id=1, source_target_pairs={{0,6},{1,7},{2,4},{3,5},{4,2},{5,3},{6,0},{7,1},{8,14},{9,15},{10,... | collective-permute-start | bytes 208904 | tf_op jit(solution)/shard_map/ppermute | solution.py:284
  75.0 4.3 %collective-permute-start.29 = (f32[136,128]{1,0:T(8,128)S(1)}, f32[136,128]{1,0:T(8,128)S(1)}, u32[]{:S(2)}, u32[]{:S(2)}) collective-permute-start(f32[136,128]{1,0:T(8,128)S(1)} %shard_map.59), channel_id=1, source_target_pairs={{0,2},{1,3},{2,0},{3,1},{4,6},{5,7},{6,4},{7,5},{8,10},{9,11},{10,... | collective-permute-start | bytes 208904 | tf_op jit(solution)/shard_map/ppermute | solution.py:284
  79.4 4.4 %collective-permute-start.30 = (f32[136,128]{1,0:T(8,128)S(1)}, f32[136,128]{1,0:T(8,128)S(1)}, u32[]{:S(2)}, u32[]{:S(2)}) collective-permute-start(f32[136,128]{1,0:T(8,128)S(1)} %select_select_fusion.1), channel_id=1, source_target_pairs={{0,1},{1,0},{2,3},{3,2},{4,5},{5,4},{6,7},{7,6},{8,9},{9,8},{10,11... | collective-permute-start | bytes 208904 | tf_op jit(solution)/shard_map/ppermute | solution.py:284
  83.9 8.0 %collective-permute-start.31 = (f32[72,128]{1,0:T(8,128)S(1)}, f32[72,128]{1,0:T(8,128)S(1)}, u32[]{:S(2)}, u32[]{:S(2)}) collective-permute-start(f32[72,128]{1,0:T(8,128)S(1)} %slice.23.refs_0_), channel_id=1, source_target_pairs={{0,128},{8,136},{16,144},{24,152},{32,160},{40,168},{48,176},{56,1... | collective-permute-start | bytes 110600 | tf_op jit(solution)/shard_map/ppermute | solution.py:284
  86.4 5.4 %collective-permute-start.32 = (f32[72,128]{1,0:T(8,128)S(1)}, f32[72,128]{1,0:T(8,128)S(1)}, u32[]{:S(2)}, u32[]{:S(2)}) collective-permute-start(f32[72,128]{1,0:T(8,128)S(1)} %slice.23.refs_0_), channel_id=1, source_target_pairs={{0,64},{8,72},{16,80},{24,88},{32,96},{40,104},{48,112},{56,120},{... | collective-permute-start | bytes 110600 | tf_op jit(solution)/shard_map/ppermute | solution.py:284
  87.5 6.1 %collective-permute-start.33 = (f32[72,128]{1,0:T(8,128)S(1)}, f32[72,128]{1,0:T(8,128)S(1)}, u32[]{:S(2)}, u32[]{:S(2)}) collective-permute-start(f32[72,128]{1,0:T(8,128)S(1)} %slice.23.refs_0_), channel_id=1, source_target_pairs={{0,192},{8,200},{16,208},{24,216},{32,224},{40,232},{48,240},{56,2... | collective-permute-start | bytes 110600 | tf_op jit(solution)/shard_map/ppermute | solution.py:284

commit v7 on v6

--- a/solution.py
+++ b/solution.py
@@ -11,7 +11,7 @@
 BLOCKS = 8
 SITE_PARTS = 8
 PANEL = 8
-ROUTES = ((2, 6, 1), (6, 1, 2), (1, 2, 6))
+ROUTES = ((2, 6, 1), (1, 2, 6), (6, 1, 2))
 VMEM_LIMIT = 12 * 1024 * 1024
 PAIR_VMEM_LIMIT = 22 * 1024 * 1024
 

time: 100 us -> 101 us (1.010); the launches traced: 99 us -> 101 us
  waiting for transfers between devices: 30.5 us -> 33.5 us
    ppermute x3, waiting for transfers between devices: 1.4 us -> 2.55 us  [local(): lax.ppermute(send_near[r], 'site', site_perm(ROUTES[r][0]))]
where the time goes in v7:
time: 101 us
  starting transfers between devices  53 us (52%)
  waiting for transfers between devices  33.5 us (33%)
  Pallas kernels  12.2 us (12%)
  other arithmetic  1.48 us (1%)
    ppermute x11, waiting for transfers between devices, spread(): return [part] + [lax.ppermute(part, axis, perm(k)) for k in shifts]  16 us
    ppermute x11, starting transfers between devices, spread(): return [part] + [lax.ppermute(part, axis, perm(k)) for k in shifts]  14.6 us
    pallas_call x11, Pallas kernels, call(): pl.pallas_call(body, out_shape=out_shape, in_specs=in_specs, out_specs=ja...  12.2 us
    ppermute x2, starting transfers between devices, gather_line(): top = lax.ppermute(cut(one, 0), 'samp', samp_perm(other))  6.84 us
    ppermute x2, waiting for transfers between devices, gather_line(): top = lax.ppermute(cut(one, 0), 'samp', samp_perm(other))  5.89 us
    ppermute x2, starting transfers between devices, gather_line(): three = lax.ppermute(block, 'samp', samp_perm(other))  5.76 us
    ppermute x3, starting transfers between devices, local(): lax.ppermute(send_near[r], 'site', site_perm(ROUTES[r][0]))  5.54 us
    ppermute x2, starting transfers between devices, gather_line(): one = lax.ppermute(block, 'samp', samp_perm(near))  5.02 us
  transfers between devices with their start and end apart: 34, of which 19 were waited for; matrix products, arithmetic and copies ran while one was open for 0% of the time, Pallas kernels for 6%

profile of v7, /device:TPU:32, one launch (start us, length us, event | category | flops | bytes accessed | tf_op | source)
XLA Modules:
  0.0 101.1 jit_solution(7977431918693272102)
XLA Ops:
  0.6 1.2 %compare_select_fusion.refs_0_.refs_6_ = bf16[64,2048]{1,0:T(8,128)(2,1)S(1)} fusion(bf16[64,2048]{1,0:T(8,128)(2,1)} %param.3, s32[64,2048]{1,0:T(8,128)} %param.4), kind=kLoop, calls=%fused_computation | loop fusion | flops 262144 | bytes 1048576 | tf_op jit(solution)/shard_map/jit(_where)/select_n | solution.py:296
  1.8 1.7 %collective-permute-start = (bf16[64,2048]{1,0:T(8,128)(2,1)S(1)}, bf16[64,2048]{1,0:T(8,128)(2,1)S(1)}, u32[]{:S(2)}, u32[]{:S(2)}) collective-permute-start(bf16[64,2048]{1,0:T(8,128)(2,1)S(1)} %compare_select_fusion.refs_0_.refs_6_), channel_id=1, source_target_pairs={{0,16},{8,24},{16,0},{24,8},{32,48},{40,56},{48,32},{56,40},{64,80... | collective-permute-start | bytes 786440 | tf_op jit(solution)/shard_map/ppermute | solution.py:275
  3.5 2.2 %collective-permute-start.1 = (bf16[64,2048]{1,0:T(8,128)(2,1)S(1)}, bf16[64,2048]{1,0:T(8,128)(2,1)S(1)}, u32[]{:S(2)}, u32[]{:S(2)}) collective-permute-start(bf16[64,2048]{1,0:T(8,128)(2,1)S(1)} %compare_select_fusion.refs_0_.refs_6_), channel_id=1, source_target_pairs={{0,48},{8,56},{16,32},{24,40},{32,16},{40,24},{48,0},{56,8},{64,11... | collective-permute-start | bytes 786440 | tf_op jit(solution)/shard_map/ppermute | solution.py:276
  5.7 3.4 %collective-permute-start.7 = (bf16[64,2304]{1,0:T(8,128)(2,1)S(1)}, bf16[64,2304]{1,0:T(8,128)(2,1)S(1)}, u32[]{:S(2)}, u32[]{:S(2)}) collective-permute-start(bf16[64,2304]{1,0:T(8,128)(2,1)S(1)} %pad_maximum_fusion), channel_id=1, source_target_pairs={{0,64},{8,72},{16,80},{24,88},{32,96},{40,104},{48,112},{56,120},{... | collective-permute-start | bytes 884744 | tf_op jit(solution)/shard_map/ppermute | solution.py:275
  9.1 3.6 %collective-permute-start.8 = (bf16[64,2304]{1,0:T(8,128)(2,1)S(1)}, bf16[64,2304]{1,0:T(8,128)(2,1)S(1)}, u32[]{:S(2)}, u32[]{:S(2)}) collective-permute-start(bf16[64,2304]{1,0:T(8,128)(2,1)S(1)} %pad_maximum_fusion), channel_id=1, source_target_pairs={{0,192},{8,200},{16,208},{24,216},{32,224},{40,232},{48,240},{56,2... | collective-permute-start | bytes 884744 | tf_op jit(solution)/shard_map/ppermute | solution.py:276
  12.7 1.1 %collective-permute-start.2 = (bf16[32,2048]{1,0:T(8,128)(2,1)S(1)}, bf16[32,2048]{1,0:T(8,128)(2,1)S(1)}, u32[]{:S(2)}, u32[]{:S(2)}) collective-permute-start(bf16[32,2048]{1,0:T(8,128)(2,1)S(1)} %shard_map.50), channel_id=1, source_target_pairs={{0,48},{8,56},{16,32},{24,40},{32,16},{40,24},{48,0},{56,8},{64,11... | collective-permute-start | bytes 393224 | tf_op jit(solution)/shard_map/ppermute | solution.py:277
  14.0 5.9 %collective-permute-done.2 = bf16[32,2048]{1,0:T(8,128)(2,1)S(1)} collective-permute-done((bf16[32,2048]{1,0:T(8,128)(2,1)S(1)}, bf16[32,2048]{1,0:T(8,128)(2,1)S(1)}, u32[]{:S(2)}, u32[]{:S(2)}) %collective-permute-start.2) | collective-permute-done | bytes 131104 | tf_op jit(solution)/shard_map/ppermute | solution.py:277
  19.9 0.6 collective-permute-start.6
  20.7 5.7 %collective-permute-start.9 = (bf16[32,2304]{1,0:T(8,128)(2,1)S(1)}, bf16[32,2304]{1,0:T(8,128)(2,1)S(1)}, u32[]{:S(2)}, u32[]{:S(2)}) collective-permute-start(bf16[32,2304]{1,0:T(8,128)(2,1)S(1)} %split.8), channel_id=1, source_target_pairs={{0,192},{8,200},{16,208},{24,216},{32,224},{40,232},{48,240},{56,2... | collective-permute-start | bytes 442376 | tf_op jit(solution)/shard_map/ppermute | solution.py:277
  26.4 1.0 collective-permute-start.10
  27.4 2.0 %shard_map.52 = (f32[4,64,384]{2,1,0:T(8,128)S(1)}, f32[4,64,384]{2,1,0:T(8,128)S(1)}, f32[4,64,384]{2,1,0:T(8,128)S(1)}) custom-call(s32[1]{0:T(128)} %bitcast.which, bf16[64,2048]{1,0:T(8,128)(2,1)S(1)} %compare_select_fusion.refs_0_.refs_6_, bf16[128,2048]{1,0:T(8,128)(2,1)S(1)} %constant_dynamic-update-slice_fusion.refs_1_, ...), custom_call_target="tpu_custom_call" | custom-call | flops 1000000 | bytes 100000 | tf_op jit(solution)/shard_map/pallas_call | solution.py:51
  29.4 1.6 %collective-permute-start.11 = (f32[4,64,384]{2,1,0:T(8,128)S(1)}, f32[4,64,384]{2,1,0:T(8,128)S(1)}, u32[]{:S(2)}, u32[]{:S(2)}) collective-permute-start(f32[4,64,384]{2,1,0:T(8,128)S(1)} %get-tuple-element.32), channel_id=1, source_target_pairs={{0,2},{1,3},{2,0},{3,1},{4,6},{5,7},{6,4},{7,5},{8,10},{9,11},{10,... | collective-permute-start | bytes 1179656 | tf_op jit(solution)/shard_map/ppermute | solution.py:321
  31.0 1.9 %collective-permute-start.12 = (f32[4,64,384]{2,1,0:T(8,128)S(1)}, f32[4,64,384]{2,1,0:T(8,128)S(1)}, u32[]{:S(2)}, u32[]{:S(2)}) collective-permute-start(f32[4,64,384]{2,1,0:T(8,128)S(1)} %get-tuple-element.33), channel_id=1, source_target_pairs={{0,1},{1,0},{2,3},{3,2},{4,5},{5,4},{6,7},{7,6},{8,9},{9,8},{10,11... | collective-permute-start | bytes 1179656 | tf_op jit(solution)/shard_map/ppermute | solution.py:321
  32.9 2.1 %collective-permute-start.13 = (f32[4,64,384]{2,1,0:T(8,128)S(1)}, f32[4,64,384]{2,1,0:T(8,128)S(1)}, u32[]{:S(2)}, u32[]{:S(2)}) collective-permute-start(f32[4,64,384]{2,1,0:T(8,128)S(1)} %get-tuple-element.34), channel_id=1, source_target_pairs={{0,6},{1,7},{2,4},{3,5},{4,2},{5,3},{6,0},{7,1},{8,14},{9,15},{10,... | collective-permute-start | bytes 1179656 | tf_op jit(solution)/shard_map/ppermute | solution.py:321
  35.1 2.0 %shard_map.53 = (f32[4,64,128]{2,1,0:T(8,128)S(1)}, f32[4,64,128]{2,1,0:T(8,128)S(1)}, f32[4,64,128]{2,1,0:T(8,128)S(1)}) custom-call(s32[1]{0:T(128)} %bitcast.which, bf16[64,2048]{1,0:T(8,128)(2,1)S(1)} %compare_select_fusion.refs_0_.refs_6_, bf16[128,2048]{1,0:T(8,128)(2,1)S(1)} %constant_dynamic-update-slice_fusion.refs_1_, ...), custom_call_target="tpu_custom_call" | custom-call | flops 10000000000 | bytes 100000 | tf_op jit(solution)/shard_map/pallas_call | solution.py:51
  37.1 1.9 %collective-permute-start.14 = (f32[4,64,128]{2,1,0:T(8,128)S(1)}, f32[4,64,128]{2,1,0:T(8,128)S(1)}, u32[]{:S(2)}, u32[]{:S(2)}) collective-permute-start(f32[4,64,128]{2,1,0:T(8,128)S(1)} %get-tuple-element.36), channel_id=1, source_target_pairs={{0,2},{1,3},{2,0},{3,1},{4,6},{5,7},{6,4},{7,5},{8,10},{9,11},{10,... | collective-permute-start | bytes 393224 | tf_op jit(solution)/shard_map/ppermute | solution.py:324
  39.0 1.3 %collective-permute-done.11.near = f32[4,64,384]{2,1,0:T(8,128)S(1)} collective-permute-done((f32[4,64,384]{2,1,0:T(8,128)S(1)}, f32[4,64,384]{2,1,0:T(8,128)S(1)}, u32[]{:S(2)}, u32[]{:S(2)}) %collective-permute-start.11) | collective-permute-done | bytes 393248 | tf_op jit(solution)/shard_map/ppermute | solution.py:321
  40.3 2.8 %collective-permute-start.16 = (f32[4,64,128]{2,1,0:T(8,128)S(1)}, f32[4,64,128]{2,1,0:T(8,128)S(1)}, u32[]{:S(2)}, u32[]{:S(2)}) collective-permute-start(f32[4,64,128]{2,1,0:T(8,128)S(1)} %get-tuple-element.38), channel_id=1, source_target_pairs={{0,6},{1,7},{2,4},{3,5},{4,2},{5,3},{6,0},{7,1},{8,14},{9,15},{10,... | collective-permute-start | bytes 393224 | tf_op jit(solution)/shard_map/ppermute | solution.py:324
  43.3 1.0 collective-permute-done.13.near
  44.3 2.0 %shard_map.54 = (f32[4,64,512]{2,1,0:T(8,128)S(1)}, f32[4,64,512]{2,1,0:T(8,128)S(1)}, f32[4,64,512]{2,1,0:T(8,128)S(1)}, f32[192,128]{1,0:T(8,128)S(1)}) custom-call(s32[1]{0:T(128)} %bitcast.which, bf16[64,2048]{1,0:T(8,128)(2,1)S(1)} %compare_select_fusion.refs_0_.refs_6_, bf16[128,2048]{1,0:T(8,128)(2,1)S(1)} %constant_dynamic-update-slice_fusion.refs_1_, ...), custom_call_target="tpu_custom_call" | custom-call | flops 10000000000 | bytes 100000 | tf_op jit(solution)/shard_map/pallas_call | solution.py:51
  46.5 1.9 %collective-permute-start.21 = (f32[2,64,512]{2,1,0:T(8,128)S(1)}, f32[2,64,512]{2,1,0:T(8,128)S(1)}, u32[]{:S(2)}, u32[]{:S(2)}) collective-permute-start(f32[2,64,512]{2,1,0:T(8,128)S(1)} %get-tuple-element.59), channel_id=1, source_target_pairs={{0,1},{1,0},{2,3},{3,2},{4,5},{5,4},{6,7},{7,6},{8,9},{9,8},{10,11... | collective-permute-start | bytes 786440 | tf_op jit(solution)/shard_map/ppermute | solution.py:330
  48.5 0.4 collective-permute-start.19
  49.0 2.6 %collective-permute-start.17 = (f32[2,64,512]{2,1,0:T(8,128)S(1)}, f32[2,64,512]{2,1,0:T(8,128)S(1)}, u32[]{:S(2)}, u32[]{:S(2)}) collective-permute-start(f32[2,64,512]{2,1,0:T(8,128)S(1)} %get-tuple-element.47), channel_id=1, source_target_pairs={{0,6},{1,7},{2,4},{3,5},{4,2},{5,3},{6,0},{7,1},{8,14},{9,15},{10,... | collective-permute-start | bytes 786440 | tf_op jit(solution)/shard_map/ppermute | solution.py:330
  51.5 1.4 %collective-permute-done.21.refs_7_ = f32[2,64,512]{2,1,0:T(8,128)S(1)} collective-permute-done((f32[2,64,512]{2,1,0:T(8,128)S(1)}, f32[2,64,512]{2,1,0:T(8,128)S(1)}, u32[]{:S(2)}, u32[]{:S(2)}) %collective-permute-start.21) | collective-permute-done | bytes 262176 | tf_op jit(solution)/shard_map/ppermute | solution.py:330
  53.0 0.9 collective-permute-start.22
  53.9 2.5 %collective-permute-done.19.refs_4_ = f32[2,64,512]{2,1,0:T(8,128)S(1)} collective-permute-done((f32[2,64,512]{2,1,0:T(8,128)S(1)}, f32[2,64,512]{2,1,0:T(8,128)S(1)}, u32[]{:S(2)}, u32[]{:S(2)}) %collective-permute-start.19) | collective-permute-done | bytes 262176 | tf_op jit(solution)/shard_map/ppermute | solution.py:330
  56.4 2.6 %collective-permute-start.20 = (f32[1,64,512]{2,1,0:T(8,128)S(1)}, f32[1,64,512]{2,1,0:T(8,128)S(1)}, u32[]{:S(2)}, u32[]{:S(2)}) collective-permute-start(f32[1,64,512]{2,1,0:T(8,128)S(1)} %slice_add_fusion.1), channel_id=1, source_target_pairs={{0,6},{1,7},{2,4},{3,5},{4,2},{5,3},{6,0},{7,1},{8,14},{9,15},{10,... | collective-permute-start | bytes 393224 | tf_op jit(solution)/shard_map/ppermute | solution.py:332
  59.1 0.5 collective-permute-start.18
  59.5 3.1 %collective-permute-done.20.refs_5_ = f32[1,64,512]{2,1,0:T(8,128)S(1)} collective-permute-done((f32[1,64,512]{2,1,0:T(8,128)S(1)}, f32[1,64,512]{2,1,0:T(8,128)S(1)}, u32[]{:S(2)}, u32[]{:S(2)}) %collective-permute-start.20) | collective-permute-done | bytes 131104 | tf_op jit(solution)/shard_map/ppermute | solution.py:332
  62.7 1.5 %collective-permute-done.18.refs_2_ = f32[1,64,512]{2,1,0:T(8,128)S(1)} collective-permute-done((f32[1,64,512]{2,1,0:T(8,128)S(1)}, f32[1,64,512]{2,1,0:T(8,128)S(1)}, u32[]{:S(2)}, u32[]{:S(2)}) %collective-permute-start.18) | collective-permute-done | bytes 131104 | tf_op jit(solution)/shard_map/ppermute | solution.py:332
  64.6 1.2 %collective-permute-done.23 = f32[64,128]{1,0:T(8,128)S(1)} collective-permute-done((f32[64,128]{1,0:T(8,128)S(1)}, f32[64,128]{1,0:T(8,128)S(1)}, u32[]{:S(2)}, u32[]{:S(2)}) %collective-permute-start.23) | collective-permute-done | bytes 32800 | tf_op jit(solution)/shard_map/ppermute | solution.py:284
  65.8 1.2 %collective-permute-start.24 = (f32[64,128]{1,0:T(8,128)S(1)}, f32[64,128]{1,0:T(8,128)S(1)}, u32[]{:S(2)}, u32[]{:S(2)}) collective-permute-start(f32[64,128]{1,0:T(8,128)S(1)} %add.32.refs_0_), channel_id=1, source_target_pairs={{0,32},{8,40},{16,48},{24,56},{32,0},{40,8},{48,16},{56,24},{64,96... | collective-permute-start | bytes 98312 | tf_op jit(solution)/shard_map/ppermute | solution.py:284
  67.0 0.9 collective-permute-start.25
  67.9 2.0 %collective-permute-start.26 = (f32[64,128]{1,0:T(8,128)S(1)}, f32[64,128]{1,0:T(8,128)S(1)}, u32[]{:S(2)}, u32[]{:S(2)}) collective-permute-start(f32[64,128]{1,0:T(8,128)S(1)} %add.32.refs_0_), channel_id=1, source_target_pairs={{0,48},{8,56},{16,32},{24,40},{32,16},{40,24},{48,0},{56,8},{64,11... | collective-permute-start | bytes 98312 | tf_op jit(solution)/shard_map/ppermute | solution.py:284
  69.9 1.5 %collective-permute-done.24.refs_1_ = f32[64,128]{1,0:T(8,128)S(1)} collective-permute-done((f32[64,128]{1,0:T(8,128)S(1)}, f32[64,128]{1,0:T(8,128)S(1)}, u32[]{:S(2)}, u32[]{:S(2)}) %collective-permute-start.24) | collective-permute-done | bytes 32800 | tf_op jit(solution)/shard_map/ppermute | solution.py:284
  71.4 1.6 %collective-permute-done.26.refs_3_ = f32[64,128]{1,0:T(8,128)S(1)} collective-permute-done((f32[64,128]{1,0:T(8,128)S(1)}, f32[64,128]{1,0:T(8,128)S(1)}, u32[]{:S(2)}, u32[]{:S(2)}) %collective-permute-start.26) | collective-permute-done | bytes 32800 | tf_op jit(solution)/shard_map/ppermute | solution.py:284
  73.4 1.6 %collective-permute-start.27 = (f32[136,128]{1,0:T(8,128)S(1)}, f32[136,128]{1,0:T(8,128)S(1)}, u32[]{:S(2)}, u32[]{:S(2)}) collective-permute-start(f32[136,128]{1,0:T(8,128)S(1)} %shard_map.59), channel_id=1, source_target_pairs={{0,4},{1,5},{2,6},{3,7},{4,0},{5,1},{6,2},{7,3},{8,12},{9,13},{10,... | collective-permute-start | bytes 208904 | tf_op jit(solution)/shard_map/ppermute | solution.py:284
  75.0 0.6 collective-permute-start.28
  75.6 1.4 %collective-permute-start.29 = (f32[136,128]{1,0:T(8,128)S(1)}, f32[136,128]{1,0:T(8,128)S(1)}, u32[]{:S(2)}, u32[]{:S(2)}) collective-permute-start(f32[136,128]{1,0:T(8,128)S(1)} %shard_map.59), channel_id=1, source_target_pairs={{0,2},{1,3},{2,0},{3,1},{4,6},{5,7},{6,4},{7,5},{8,10},{9,11},{10,... | collective-permute-start | bytes 208904 | tf_op jit(solution)/shard_map/ppermute | solution.py:284
  77.0 2.6 %collective-permute-done.27 = f32[136,128]{1,0:T(8,128)S(1)} collective-permute-done((f32[136,128]{1,0:T(8,128)S(1)}, f32[136,128]{1,0:T(8,128)S(1)}, u32[]{:S(2)}, u32[]{:S(2)}) %collective-permute-start.27) | collective-permute-done | bytes 69664 | tf_op jit(solution)/shard_map/ppermute | solution.py:284
  79.6 0.9 collective-permute-done.28
  80.9 4.1 %collective-permute-done.30 = f32[136,128]{1,0:T(8,128)S(1)} collective-permute-done((f32[136,128]{1,0:T(8,128)S(1)}, f32[136,128]{1,0:T(8,128)S(1)}, u32[]{:S(2)}, u32[]{:S(2)}) %collective-permute-start.30) | collective-permute-done | bytes 69664 | tf_op jit(solution)/shard_map/ppermute | solution.py:284
  85.1 1.2 %collective-permute-start.31 = (f32[72,128]{1,0:T(8,128)S(1)}, f32[72,128]{1,0:T(8,128)S(1)}, u32[]{:S(2)}, u32[]{:S(2)}) collective-permute-start(f32[72,128]{1,0:T(8,128)S(1)} %slice.23.refs_0_), channel_id=1, source_target_pairs={{0,128},{8,136},{16,144},{24,152},{32,160},{40,168},{48,176},{56,1... | collective-permute-start | bytes 110600 | tf_op jit(solution)/shard_map/ppermute | solution.py:284
  86.3 3.0 %collective-permute-start.32 = (f32[72,128]{1,0:T(8,128)S(1)}, f32[72,128]{1,0:T(8,128)S(1)}, u32[]{:S(2)}, u32[]{:S(2)}) collective-permute-start(f32[72,128]{1,0:T(8,128)S(1)} %slice.23.refs_0_), channel_id=1, source_target_pairs={{0,64},{8,72},{16,80},{24,88},{32,96},{40,104},{48,112},{56,120},{... | collective-permute-start | bytes 110600 | tf_op jit(solution)/shard_map/ppermute | solution.py:284
  89.3 2.4 %collective-permute-start.33 = (f32[72,128]{1,0:T(8,128)S(1)}, f32[72,128]{1,0:T(8,128)S(1)}, u32[]{:S(2)}, u32[]{:S(2)}) collective-permute-start(f32[72,128]{1,0:T(8,128)S(1)} %slice.23.refs_0_), channel_id=1, source_target_pairs={{0,192},{8,200},{16,208},{24,216},{32,224},{40,232},{48,240},{56,2... | collective-permute-start | bytes 110600 | tf_op jit(solution)/shard_map/ppermute | solution.py:284
  91.7 1.8 %collective-permute-done.31.refs_1_ = f32[72,128]{1,0:T(8,128)S(1)} collective-permute-done((f32[72,128]{1,0:T(8,128)S(1)}, f32[72,128]{1,0:T(8,128)S(1)}, u32[]{:S(2)}, u32[]{:S(2)}) %collective-permute-start.31) | collective-permute-done | bytes 36896 | tf_op jit(solution)/shard_map/ppermute | solution.py:284
  93.5 2.3 %collective-permute-done.33.refs_3_ = f32[72,128]{1,0:T(8,128)S(1)} collective-permute-done((f32[72,128]{1,0:T(8,128)S(1)}, f32[72,128]{1,0:T(8,128)S(1)}, u32[]{:S(2)}, u32[]{:S(2)}) %collective-permute-start.33) | collective-permute-done | bytes 36896 | tf_op jit(solution)/shard_map/ppermute | solution.py:284
  95.7 5.4 %shard_map.60 = (f32[64,128]{1,0:T(8,128)}, f32[128,128]{1,0:T(8,128)}) custom-call(f32[72,128]{1,0:T(8,128)S(1)} %slice.23.refs_0_, f32[72,128]{1,0:T(8,128)S(1)} %collective-permute-done.31.refs_1_, f32[72,128]{1,0:T(8,128)S(1)} %collective-permute-done.32.refs_2_, f32[72,128]{1,0:T(8,128)S(1)} %collective-permute-done.33.refs_3_, f32[64,128]{1,0:T(8,128)S(1)} %slice.24.refs_4_), custom_call_target="tpu_custom_call" | custom-call | tf_op jit(solution)/shard_map/pallas_call | solution.py:51
  (51 shorter events, 2.5 us)
Async XLA Ops:
  0.6 5.1 %copy-start = (f32[64,128]{1,0:T(8,128)S(1)}, f32[64,128]{1,0:T(8,128)}, u32[]{:S(2)}) copy-start(f32[64,128]{1,0:T(8,128)} %refs_10_.1) | copy-start | bytes 98308
  1.8 10.8 %collective-permute-start = (bf16[64,2048]{1,0:T(8,128)(2,1)S(1)}, bf16[64,2048]{1,0:T(8,128)(2,1)S(1)}, u32[]{:S(2)}, u32[]{:S(2)}) collective-permute-start(bf16[64,2048]{1,0:T(8,128)(2,1)S(1)} %compare_select_fusion.refs_0_.refs_6_), channel_id=1, source_target_pairs={{0,16},{8,24},{16,0},{24,8},{32,48},{40,56},{48,32},{56,40},{64,80... | collective-permute-start | bytes 786440 | tf_op jit(solution)/shard_map/ppermute | solution.py:275
  3.5 10.3 %collective-permute-start.1 = (bf16[64,2048]{1,0:T(8,128)(2,1)S(1)}, bf16[64,2048]{1,0:T(8,128)(2,1)S(1)}, u32[]{:S(2)}, u32[]{:S(2)}) collective-permute-start(bf16[64,2048]{1,0:T(8,128)(2,1)S(1)} %compare_select_fusion.refs_0_.refs_6_), channel_id=1, source_target_pairs={{0,48},{8,56},{16,32},{24,40},{32,16},{40,24},{48,0},{56,8},{64,11... | collective-permute-start | bytes 786440 | tf_op jit(solution)/shard_map/ppermute | solution.py:276
  5.7 15.0 %collective-permute-start.7 = (bf16[64,2304]{1,0:T(8,128)(2,1)S(1)}, bf16[64,2304]{1,0:T(8,128)(2,1)S(1)}, u32[]{:S(2)}, u32[]{:S(2)}) collective-permute-start(bf16[64,2304]{1,0:T(8,128)(2,1)S(1)} %pad_maximum_fusion), channel_id=1, source_target_pairs={{0,64},{8,72},{16,80},{24,88},{32,96},{40,104},{48,112},{56,120},{... | collective-permute-start | bytes 884744 | tf_op jit(solution)/shard_map/ppermute | solution.py:275
  9.1 17.3 %collective-permute-start.8 = (bf16[64,2304]{1,0:T(8,128)(2,1)S(1)}, bf16[64,2304]{1,0:T(8,128)(2,1)S(1)}, u32[]{:S(2)}, u32[]{:S(2)}) collective-permute-start(bf16[64,2304]{1,0:T(8,128)(2,1)S(1)} %pad_maximum_fusion), channel_id=1, source_target_pairs={{0,192},{8,200},{16,208},{24,216},{32,224},{40,232},{48,240},{56,2... | collective-permute-start | bytes 884744 | tf_op jit(solution)/shard_map/ppermute | solution.py:276
  12.7 14.8 %collective-permute-start.4 = (bf16[64,2048]{1,0:T(8,128)(2,1)S(1)}, bf16[64,2048]{1,0:T(8,128)(2,1)S(1)}, u32[]{:S(2)}, u32[]{:S(2)}) collective-permute-start(bf16[64,2048]{1,0:T(8,128)(2,1)S(1)} %compare_select_fusion.refs_0_.refs_6_), channel_id=1, source_target_pairs={{0,8},{8,0},{16,24},{24,16},{32,40},{40,32},{48,56},{56,48},{64,72... | collective-permute-start | bytes 786440 | tf_op jit(solution)/shard_map/ppermute | solution.py:303
  12.7 7.2 %collective-permute-start.2 = (bf16[32,2048]{1,0:T(8,128)(2,1)S(1)}, bf16[32,2048]{1,0:T(8,128)(2,1)S(1)}, u32[]{:S(2)}, u32[]{:S(2)}) collective-permute-start(bf16[32,2048]{1,0:T(8,128)(2,1)S(1)} %shard_map.50), channel_id=1, source_target_pairs={{0,48},{8,56},{16,32},{24,40},{32,16},{40,24},{48,0},{56,8},{64,11... | collective-permute-start | bytes 393224 | tf_op jit(solution)/shard_map/ppermute | solution.py:277
  13.8 6.1 %collective-permute-start.3 = (bf16[32,2048]{1,0:T(8,128)(2,1)S(1)}, bf16[32,2048]{1,0:T(8,128)(2,1)S(1)}, u32[]{:S(2)}, u32[]{:S(2)}) collective-permute-start(bf16[32,2048]{1,0:T(8,128)(2,1)S(1)} %shard_map.51), channel_id=1, source_target_pairs={{0,16},{8,24},{16,0},{24,8},{32,48},{40,56},{48,32},{56,40},{64,80... | collective-permute-start | bytes 393224 | tf_op jit(solution)/shard_map/ppermute | solution.py:278
  19.9 7.5 %collective-permute-start.5 = (bf16[128,2048]{1,0:T(8,128)(2,1)S(1)}, bf16[128,2048]{1,0:T(8,128)(2,1)S(1)}, u32[]{:S(2)}, u32[]{:S(2)}) collective-permute-start(bf16[128,2048]{1,0:T(8,128)(2,1)S(1)} %constant_dynamic-update-slice_fusion.refs_1_), channel_id=1, source_target_pairs={{0,8},{8,0},{16,24},{24,16},{32,40},{40,32},{48,56},{56,48},{64,72... | collective-permute-start | bytes 1572872 | tf_op jit(solution)/shard_map/ppermute | solution.py:303
  19.9 7.5 %collective-permute-start.6 = (bf16[64,2048]{1,0:T(8,128)(2,1)S(1)}, bf16[64,2048]{1,0:T(8,128)(2,1)S(1)}, u32[]{:S(2)}, u32[]{:S(2)}) collective-permute-start(bf16[64,2048]{1,0:T(8,128)(2,1)S(1)} %constant_dynamic-update-slice_fusion.2.refs_2_), channel_id=1, source_target_pairs={{0,8},{8,0},{16,24},{24,16},{32,40},{40,32},{48,56},{56,48},{64,72... | collective-permute-start | bytes 786440 | tf_op jit(solution)/shard_map/ppermute | solution.py:303
  20.7 14.2 %collective-permute-start.9 = (bf16[32,2304]{1,0:T(8,128)(2,1)S(1)}, bf16[32,2304]{1,0:T(8,128)(2,1)S(1)}, u32[]{:S(2)}, u32[]{:S(2)}) collective-permute-start(bf16[32,2304]{1,0:T(8,128)(2,1)S(1)} %split.8), channel_id=1, source_target_pairs={{0,192},{8,200},{16,208},{24,216},{32,224},{40,232},{48,240},{56,2... | collective-permute-start | bytes 442376 | tf_op jit(solution)/shard_map/ppermute | solution.py:277
  26.4 8.7 %collective-permute-start.10 = (bf16[32,2304]{1,0:T(8,128)(2,1)S(1)}, bf16[32,2304]{1,0:T(8,128)(2,1)S(1)}, u32[]{:S(2)}, u32[]{:S(2)}) collective-permute-start(bf16[32,2304]{1,0:T(8,128)(2,1)S(1)} %split.9), channel_id=1, source_target_pairs={{0,64},{8,72},{16,80},{24,88},{32,96},{40,104},{48,112},{56,120},{... | collective-permute-start | bytes 442376 | tf_op jit(solution)/shard_map/ppermute | solution.py:278
  29.4 10.9 %collective-permute-start.11 = (f32[4,64,384]{2,1,0:T(8,128)S(1)}, f32[4,64,384]{2,1,0:T(8,128)S(1)}, u32[]{:S(2)}, u32[]{:S(2)}) collective-permute-start(f32[4,64,384]{2,1,0:T(8,128)S(1)} %get-tuple-element.32), channel_id=1, source_target_pairs={{0,2},{1,3},{2,0},{3,1},{4,6},{5,7},{6,4},{7,5},{8,10},{9,11},{10,... | collective-permute-start | bytes 1179656 | tf_op jit(solution)/shard_map/ppermute | solution.py:321
  31.0 12.3 %collective-permute-start.12 = (f32[4,64,384]{2,1,0:T(8,128)S(1)}, f32[4,64,384]{2,1,0:T(8,128)S(1)}, u32[]{:S(2)}, u32[]{:S(2)}) collective-permute-start(f32[4,64,384]{2,1,0:T(8,128)S(1)} %get-tuple-element.33), channel_id=1, source_target_pairs={{0,1},{1,0},{2,3},{3,2},{4,5},{5,4},{6,7},{7,6},{8,9},{9,8},{10,11... | collective-permute-start | bytes 1179656 | tf_op jit(solution)/shard_map/ppermute | solution.py:321
  32.9 11.4 %collective-permute-start.13 = (f32[4,64,384]{2,1,0:T(8,128)S(1)}, f32[4,64,384]{2,1,0:T(8,128)S(1)}, u32[]{:S(2)}, u32[]{:S(2)}) collective-permute-start(f32[4,64,384]{2,1,0:T(8,128)S(1)} %get-tuple-element.34), channel_id=1, source_target_pairs={{0,6},{1,7},{2,4},{3,5},{4,2},{5,3},{6,0},{7,1},{8,14},{9,15},{10,... | collective-permute-start | bytes 1179656 | tf_op jit(solution)/shard_map/ppermute | solution.py:321
  37.1 9.2 %collective-permute-start.14 = (f32[4,64,128]{2,1,0:T(8,128)S(1)}, f32[4,64,128]{2,1,0:T(8,128)S(1)}, u32[]{:S(2)}, u32[]{:S(2)}) collective-permute-start(f32[4,64,128]{2,1,0:T(8,128)S(1)} %get-tuple-element.36), channel_id=1, source_target_pairs={{0,2},{1,3},{2,0},{3,1},{4,6},{5,7},{6,4},{7,5},{8,10},{9,11},{10,... | collective-permute-start | bytes 393224 | tf_op jit(solution)/shard_map/ppermute | solution.py:324
  39.0 7.3 %collective-permute-start.15 = (f32[4,64,128]{2,1,0:T(8,128)S(1)}, f32[4,64,128]{2,1,0:T(8,128)S(1)}, u32[]{:S(2)}, u32[]{:S(2)}) collective-permute-start(f32[4,64,128]{2,1,0:T(8,128)S(1)} %get-tuple-element.37), channel_id=1, source_target_pairs={{0,1},{1,0},{2,3},{3,2},{4,5},{5,4},{6,7},{7,6},{8,9},{9,8},{10,11... | collective-permute-start | bytes 393224 | tf_op jit(solution)/shard_map/ppermute | solution.py:324
  40.3 6.2 %collective-permute-start.16 = (f32[4,64,128]{2,1,0:T(8,128)S(1)}, f32[4,64,128]{2,1,0:T(8,128)S(1)}, u32[]{:S(2)}, u32[]{:S(2)}) collective-permute-start(f32[4,64,128]{2,1,0:T(8,128)S(1)} %get-tuple-element.38), channel_id=1, source_target_pairs={{0,6},{1,7},{2,4},{3,5},{4,2},{5,3},{6,0},{7,1},{8,14},{9,15},{10,... | collective-permute-start | bytes 393224 | tf_op jit(solution)/shard_map/ppermute | solution.py:324
  46.5 6.5 %collective-permute-start.21 = (f32[2,64,512]{2,1,0:T(8,128)S(1)}, f32[2,64,512]{2,1,0:T(8,128)S(1)}, u32[]{:S(2)}, u32[]{:S(2)}) collective-permute-start(f32[2,64,512]{2,1,0:T(8,128)S(1)} %get-tuple-element.59), channel_id=1, source_target_pairs={{0,1},{1,0},{2,3},{3,2},{4,5},{5,4},{6,7},{7,6},{8,9},{9,8},{10,11... | collective-permute-start | bytes 786440 | tf_op jit(solution)/shard_map/ppermute | solution.py:330
  48.5 7.9 %collective-permute-start.19 = (f32[2,64,512]{2,1,0:T(8,128)S(1)}, f32[2,64,512]{2,1,0:T(8,128)S(1)}, u32[]{:S(2)}, u32[]{:S(2)}) collective-permute-start(f32[2,64,512]{2,1,0:T(8,128)S(1)} %get-tuple-element.53), channel_id=1, source_target_pairs={{0,2},{1,3},{2,0},{3,1},{4,6},{5,7},{6,4},{7,5},{8,10},{9,11},{10,... | collective-permute-start | bytes 786440 | tf_op jit(solution)/shard_map/ppermute | solution.py:330
  49.0 10.1 %collective-permute-start.17 = (f32[2,64,512]{2,1,0:T(8,128)S(1)}, f32[2,64,512]{2,1,0:T(8,128)S(1)}, u32[]{:S(2)}, u32[]{:S(2)}) collective-permute-start(f32[2,64,512]{2,1,0:T(8,128)S(1)} %get-tuple-element.47), channel_id=1, source_target_pairs={{0,6},{1,7},{2,4},{3,5},{4,2},{5,3},{6,0},{7,1},{8,14},{9,15},{10,... | collective-permute-start | bytes 786440 | tf_op jit(solution)/shard_map/ppermute | solution.py:330
  53.0 6.5 %collective-permute-start.22 = (f32[1,64,512]{2,1,0:T(8,128)S(1)}, f32[1,64,512]{2,1,0:T(8,128)S(1)}, u32[]{:S(2)}, u32[]{:S(2)}) collective-permute-start(f32[1,64,512]{2,1,0:T(8,128)S(1)} %slice_add_fusion), channel_id=1, source_target_pairs={{0,2},{1,3},{2,0},{3,1},{4,6},{5,7},{6,4},{7,5},{8,10},{9,11},{10,... | collective-permute-start | bytes 393224 | tf_op jit(solution)/shard_map/ppermute | solution.py:332
  56.4 6.3 %collective-permute-start.20 = (f32[1,64,512]{2,1,0:T(8,128)S(1)}, f32[1,64,512]{2,1,0:T(8,128)S(1)}, u32[]{:S(2)}, u32[]{:S(2)}) collective-permute-start(f32[1,64,512]{2,1,0:T(8,128)S(1)} %slice_add_fusion.1), channel_id=1, source_target_pairs={{0,6},{1,7},{2,4},{3,5},{4,2},{5,3},{6,0},{7,1},{8,14},{9,15},{10,... | collective-permute-start | bytes 393224 | tf_op jit(solution)/shard_map/ppermute | solution.py:332
  59.1 5.1 %collective-permute-start.18 = (f32[1,64,512]{2,1,0:T(8,128)S(1)}, f32[1,64,512]{2,1,0:T(8,128)S(1)}, u32[]{:S(2)}, u32[]{:S(2)}) collective-permute-start(f32[1,64,512]{2,1,0:T(8,128)S(1)} %slice_add_fusion.2), channel_id=1, source_target_pairs={{0,1},{1,0},{2,3},{3,2},{4,5},{5,4},{6,7},{7,6},{8,9},{9,8},{10,11... | collective-permute-start | bytes 393224 | tf_op jit(solution)/shard_map/ppermute | solution.py:332
  64.5 1.3 %collective-permute-start.23 = (f32[64,128]{1,0:T(8,128)S(1)}, f32[64,128]{1,0:T(8,128)S(1)}, u32[]{:S(2)}, u32[]{:S(2)}) collective-permute-start(f32[64,128]{1,0:T(8,128)S(1)} %shard_map.58), channel_id=1, source_target_pairs={{0,8},{8,0},{16,24},{24,16},{32,40},{40,32},{48,56},{56,48},{64,72... | collective-permute-start | bytes 98312 | tf_op jit(solution)/shard_map/ppermute | solution.py:284
  65.8 5.6 %collective-permute-start.24 = (f32[64,128]{1,0:T(8,128)S(1)}, f32[64,128]{1,0:T(8,128)S(1)}, u32[]{:S(2)}, u32[]{:S(2)}) collective-permute-start(f32[64,128]{1,0:T(8,128)S(1)} %add.32.refs_0_), channel_id=1, source_target_pairs={{0,32},{8,40},{16,48},{24,56},{32,0},{40,8},{48,16},{56,24},{64,96... | collective-permute-start | bytes 98312 | tf_op jit(solution)/shard_map/ppermute | solution.py:284
  67.0 4.4 %collective-permute-start.25 = (f32[64,128]{1,0:T(8,128)S(1)}, f32[64,128]{1,0:T(8,128)S(1)}, u32[]{:S(2)}, u32[]{:S(2)}) collective-permute-start(f32[64,128]{1,0:T(8,128)S(1)} %add.32.refs_0_), channel_id=1, source_target_pairs={{0,16},{8,24},{16,0},{24,8},{32,48},{40,56},{48,32},{56,40},{64,80... | collective-permute-start | bytes 98312 | tf_op jit(solution)/shard_map/ppermute | solution.py:284
  67.9 5.1 %collective-permute-start.26 = (f32[64,128]{1,0:T(8,128)S(1)}, f32[64,128]{1,0:T(8,128)S(1)}, u32[]{:S(2)}, u32[]{:S(2)}) collective-permute-start(f32[64,128]{1,0:T(8,128)S(1)} %add.32.refs_0_), channel_id=1, source_target_pairs={{0,48},{8,56},{16,32},{24,40},{32,16},{40,24},{48,0},{56,8},{64,11... | collective-permute-start | bytes 98312 | tf_op jit(solution)/shard_map/ppermute | solution.py:284
  73.4 6.2 %collective-permute-start.27 = (f32[136,128]{1,0:T(8,128)S(1)}, f32[136,128]{1,0:T(8,128)S(1)}, u32[]{:S(2)}, u32[]{:S(2)}) collective-permute-start(f32[136,128]{1,0:T(8,128)S(1)} %shard_map.59), channel_id=1, source_target_pairs={{0,4},{1,5},{2,6},{3,7},{4,0},{5,1},{6,2},{7,3},{8,12},{9,13},{10,... | collective-permute-start | bytes 208904 | tf_op jit(solution)/shard_map/ppermute | solution.py:284
  75.0 5.5 %collective-permute-start.28 = (f32[136,128]{1,0:T(8,128)S(1)}, f32[136,128]{1,0:T(8,128)S(1)}, u32[]{:S(2)}, u32[]{:S(2)}) collective-permute-start(f32[136,128]{1,0:T(8,128)S(1)} %shard_map.59), channel_id=1, source_target_pairs={{0,6},{1,7},{2,4},{3,5},{4,2},{5,3},{6,0},{7,1},{8,14},{9,15},{10,... | collective-permute-start | bytes 208904 | tf_op jit(solution)/shard_map/ppermute | solution.py:284
  75.6 4.9 %collective-permute-start.29 = (f32[136,128]{1,0:T(8,128)S(1)}, f32[136,128]{1,0:T(8,128)S(1)}, u32[]{:S(2)}, u32[]{:S(2)}) collective-permute-start(f32[136,128]{1,0:T(8,128)S(1)} %shard_map.59), channel_id=1, source_target_pairs={{0,2},{1,3},{2,0},{3,1},{4,6},{5,7},{6,4},{7,5},{8,10},{9,11},{10,... | collective-permute-start | bytes 208904 | tf_op jit(solution)/shard_map/ppermute | solution.py:284
  80.6 4.4 %collective-permute-start.30 = (f32[136,128]{1,0:T(8,128)S(1)}, f32[136,128]{1,0:T(8,128)S(1)}, u32[]{:S(2)}, u32[]{:S(2)}) collective-permute-start(f32[136,128]{1,0:T(8,128)S(1)} %select_select_fusion.1), channel_id=1, source_target_pairs={{0,1},{1,0},{2,3},{3,2},{4,5},{5,4},{6,7},{7,6},{8,9},{9,8},{10,11... | collective-permute-start | bytes 208904 | tf_op jit(solution)/shard_map/ppermute | solution.py:284
  85.1 8.3 %collective-permute-start.31 = (f32[72,128]{1,0:T(8,128)S(1)}, f32[72,128]{1,0:T(8,128)S(1)}, u32[]{:S(2)}, u32[]{:S(2)}) collective-permute-start(f32[72,128]{1,0:T(8,128)S(1)} %slice.23.refs_0_), channel_id=1, source_target_pairs={{0,128},{8,136},{16,144},{24,152},{32,160},{40,168},{48,176},{56,1... | collective-permute-start | bytes 110600 | tf_op jit(solution)/shard_map/ppermute | solution.py:284
  86.3 7.2 %collective-permute-start.32 = (f32[72,128]{1,0:T(8,128)S(1)}, f32[72,128]{1,0:T(8,128)S(1)}, u32[]{:S(2)}, u32[]{:S(2)}) collective-permute-start(f32[72,128]{1,0:T(8,128)S(1)} %slice.23.refs_0_), channel_id=1, source_target_pairs={{0,64},{8,72},{16,80},{24,88},{32,96},{40,104},{48,112},{56,120},{... | collective-permute-start | bytes 110600 | tf_op jit(solution)/shard_map/ppermute | solution.py:284
  89.3 6.5 %collective-permute-start.33 = (f32[72,128]{1,0:T(8,128)S(1)}, f32[72,128]{1,0:T(8,128)S(1)}, u32[]{:S(2)}, u32[]{:S(2)}) collective-permute-start(f32[72,128]{1,0:T(8,128)S(1)} %slice.23.refs_0_), channel_id=1, source_target_pairs={{0,192},{8,200},{16,208},{24,216},{32,224},{40,232},{48,240},{56,2... | collective-permute-start | bytes 110600 | tf_op jit(solution)/shard_map/ppermute | solution.py:284

commit v8 on v6

--- a/solution.py
+++ b/solution.py
@@ -157,7 +157,7 @@
 
 def gram_body(*refs):
     out = refs[-1]
-    image = line_sum([r[...] for r in refs[:-1]])
+    image = tree_sum([r[...] for r in refs[:-1]])
     gram = lax.dot_general(
         image, image, (((0,), (0,)), ((), ())), precision=lax.Precision.HIGHEST, preferred_element_type=jnp.float32
     )
@@ -332,9 +332,9 @@
     came3 = [lax.ppermute(send[r], "site", site_perm(ROUTES[r][2])) for r in range(3)]
     terms = [t for r in range(3) for t in (folded[r][2], came2[r], came3[r])]
     part = kernel_call(band_body, jax.ShapeDtypeStruct((height, columns), f32))(*terms, gathered, factor)
-    part = tree_sum(spread(part, "samp", [1]))
+    part = line_sum(spread(part, "samp", [4, 2, 6]))
     packed = columns // 2 + PANEL
-    message = kernel_call(gram_body, jax.ShapeDtypeStruct((packed + height, columns), f32))(*spread(part, "samp", [4, 2, 6]))
+    message = kernel_call(gram_body, jax.ShapeDtypeStruct((packed + height, columns), f32))(*spread(part, "samp", [1]))
     is_gram = lax.broadcasted_iota(jnp.int32, message.shape, 0) < packed
     apart = which[0]
     came = spread(message, "site", [4, 2, 6])

time: 100 us -> 100 us (level)
  transfers between devices with their start and end apart: 34 -> 34, of which waited for: 19 -> 20; matrix products, arithmetic and copies ran while one was open for 0% -> 0% of each run, Pallas kernels for 6% -> 6%
where the time goes in v8:
time: 100 us; the launch traced here: 99.6 us
  starting transfers between devices  53.6 us (54%)
  waiting for transfers between devices  31.4 us (31%)
  Pallas kernels  12.2 us (12%)
  other arithmetic  1.48 us (1%)
    ppermute x11, waiting for transfers between devices, spread(): return [part] + [lax.ppermute(part, axis, perm(k)) for k in shifts]  16.2 us
    ppermute x11, starting transfers between devices, spread(): return [part] + [lax.ppermute(part, axis, perm(k)) for k in shifts]  15 us
    pallas_call x11, Pallas kernels, call(): pl.pallas_call(body, out_shape=out_shape, in_specs=in_specs, out_specs=ja...  12.2 us
    ppermute x2, starting transfers between devices, gather_line(): top = lax.ppermute(cut(one, 0), 'samp', samp_perm(other))  6.84 us
    ppermute x2, waiting for transfers between devices, gather_line(): top = lax.ppermute(cut(one, 0), 'samp', samp_perm(other))  5.89 us
    ppermute x2, starting transfers between devices, gather_line(): three = lax.ppermute(block, 'samp', samp_perm(other))  5.76 us
    ppermute x3, starting transfers between devices, local(): lax.ppermute(send_near[r], 'site', site_perm(ROUTES[r][0]))  5.54 us
    ppermute x3, starting transfers between devices, local(): lax.ppermute(folded[r][0], 'site', site_perm(ROUTES[r][1]))  5.22 us
  transfers between devices with their start and end apart: 34, of which 20 were waited for; matrix products, arithmetic and copies ran while one was open for 0% of the time, Pallas kernels for 6%

profile of v8, /device:TPU:32, one launch (start us, length us, event | category | flops | bytes accessed | tf_op | source)
XLA Modules:
  0.0 99.6 jit_solution(9732027033534207828)
XLA Ops:
  0.6 1.2 %compare_select_fusion.refs_0_.refs_6_ = bf16[64,2048]{1,0:T(8,128)(2,1)S(1)} fusion(bf16[64,2048]{1,0:T(8,128)(2,1)} %param.3, s32[64,2048]{1,0:T(8,128)} %param.4), kind=kLoop, calls=%fused_computation | loop fusion | flops 262144 | bytes 1048576 | tf_op jit(solution)/shard_map/jit(_where)/select_n | solution.py:296
  1.8 1.7 %collective-permute-start = (bf16[64,2048]{1,0:T(8,128)(2,1)S(1)}, bf16[64,2048]{1,0:T(8,128)(2,1)S(1)}, u32[]{:S(2)}, u32[]{:S(2)}) collective-permute-start(bf16[64,2048]{1,0:T(8,128)(2,1)S(1)} %compare_select_fusion.refs_0_.refs_6_), channel_id=1, source_target_pairs={{0,16},{8,24},{16,0},{24,8},{32,48},{40,56},{48,32},{56,40},{64,80... | collective-permute-start | bytes 786440 | tf_op jit(solution)/shard_map/ppermute | solution.py:275
  3.5 2.2 %collective-permute-start.1 = (bf16[64,2048]{1,0:T(8,128)(2,1)S(1)}, bf16[64,2048]{1,0:T(8,128)(2,1)S(1)}, u32[]{:S(2)}, u32[]{:S(2)}) collective-permute-start(bf16[64,2048]{1,0:T(8,128)(2,1)S(1)} %compare_select_fusion.refs_0_.refs_6_), channel_id=1, source_target_pairs={{0,48},{8,56},{16,32},{24,40},{32,16},{40,24},{48,0},{56,8},{64,11... | collective-permute-start | bytes 786440 | tf_op jit(solution)/shard_map/ppermute | solution.py:276
  5.7 3.4 %collective-permute-start.7 = (bf16[64,2304]{1,0:T(8,128)(2,1)S(1)}, bf16[64,2304]{1,0:T(8,128)(2,1)S(1)}, u32[]{:S(2)}, u32[]{:S(2)}) collective-permute-start(bf16[64,2304]{1,0:T(8,128)(2,1)S(1)} %pad_maximum_fusion), channel_id=1, source_target_pairs={{0,64},{8,72},{16,80},{24,88},{32,96},{40,104},{48,112},{56,120},{... | collective-permute-start | bytes 884744 | tf_op jit(solution)/shard_map/ppermute | solution.py:275
  9.1 3.6 %collective-permute-start.8 = (bf16[64,2304]{1,0:T(8,128)(2,1)S(1)}, bf16[64,2304]{1,0:T(8,128)(2,1)S(1)}, u32[]{:S(2)}, u32[]{:S(2)}) collective-permute-start(bf16[64,2304]{1,0:T(8,128)(2,1)S(1)} %pad_maximum_fusion), channel_id=1, source_target_pairs={{0,192},{8,200},{16,208},{24,216},{32,224},{40,232},{48,240},{56,2... | collective-permute-start | bytes 884744 | tf_op jit(solution)/shard_map/ppermute | solution.py:276
  12.7 1.1 %collective-permute-start.2 = (bf16[32,2048]{1,0:T(8,128)(2,1)S(1)}, bf16[32,2048]{1,0:T(8,128)(2,1)S(1)}, u32[]{:S(2)}, u32[]{:S(2)}) collective-permute-start(bf16[32,2048]{1,0:T(8,128)(2,1)S(1)} %shard_map.50), channel_id=1, source_target_pairs={{0,48},{8,56},{16,32},{24,40},{32,16},{40,24},{48,0},{56,8},{64,11... | collective-permute-start | bytes 393224 | tf_op jit(solution)/shard_map/ppermute | solution.py:277
  14.0 5.9 %collective-permute-done.2 = bf16[32,2048]{1,0:T(8,128)(2,1)S(1)} collective-permute-done((bf16[32,2048]{1,0:T(8,128)(2,1)S(1)}, bf16[32,2048]{1,0:T(8,128)(2,1)S(1)}, u32[]{:S(2)}, u32[]{:S(2)}) %collective-permute-start.2) | collective-permute-done | bytes 131104 | tf_op jit(solution)/shard_map/ppermute | solution.py:277
  19.9 0.6 collective-permute-start.6
  20.7 5.7 %collective-permute-start.9 = (bf16[32,2304]{1,0:T(8,128)(2,1)S(1)}, bf16[32,2304]{1,0:T(8,128)(2,1)S(1)}, u32[]{:S(2)}, u32[]{:S(2)}) collective-permute-start(bf16[32,2304]{1,0:T(8,128)(2,1)S(1)} %split.8), channel_id=1, source_target_pairs={{0,192},{8,200},{16,208},{24,216},{32,224},{40,232},{48,240},{56,2... | collective-permute-start | bytes 442376 | tf_op jit(solution)/shard_map/ppermute | solution.py:277
  26.4 1.0 %collective-permute-start.10 = (bf16[32,2304]{1,0:T(8,128)(2,1)S(1)}, bf16[32,2304]{1,0:T(8,128)(2,1)S(1)}, u32[]{:S(2)}, u32[]{:S(2)}) collective-permute-start(bf16[32,2304]{1,0:T(8,128)(2,1)S(1)} %split.9), channel_id=1, source_target_pairs={{0,64},{8,72},{16,80},{24,88},{32,96},{40,104},{48,112},{56,120},{... | collective-permute-start | bytes 442376 | tf_op jit(solution)/shard_map/ppermute | solution.py:278
  27.4 2.0 %shard_map.52 = (f32[4,64,384]{2,1,0:T(8,128)S(1)}, f32[4,64,384]{2,1,0:T(8,128)S(1)}, f32[4,64,384]{2,1,0:T(8,128)S(1)}) custom-call(s32[1]{0:T(128)} %bitcast.which, bf16[64,2048]{1,0:T(8,128)(2,1)S(1)} %compare_select_fusion.refs_0_.refs_6_, bf16[128,2048]{1,0:T(8,128)(2,1)S(1)} %constant_dynamic-update-slice_fusion.refs_1_, ...), custom_call_target="tpu_custom_call" | custom-call | flops 1000000 | bytes 100000 | tf_op jit(solution)/shard_map/pallas_call | solution.py:51
  29.4 1.6 %collective-permute-start.11 = (f32[4,64,384]{2,1,0:T(8,128)S(1)}, f32[4,64,384]{2,1,0:T(8,128)S(1)}, u32[]{:S(2)}, u32[]{:S(2)}) collective-permute-start(f32[4,64,384]{2,1,0:T(8,128)S(1)} %get-tuple-element.32), channel_id=1, source_target_pairs={{0,2},{1,3},{2,0},{3,1},{4,6},{5,7},{6,4},{7,5},{8,10},{9,11},{10,... | collective-permute-start | bytes 1179656 | tf_op jit(solution)/shard_map/ppermute | solution.py:321
  31.0 2.1 %collective-permute-start.12 = (f32[4,64,384]{2,1,0:T(8,128)S(1)}, f32[4,64,384]{2,1,0:T(8,128)S(1)}, u32[]{:S(2)}, u32[]{:S(2)}) collective-permute-start(f32[4,64,384]{2,1,0:T(8,128)S(1)} %get-tuple-element.33), channel_id=1, source_target_pairs={{0,6},{1,7},{2,4},{3,5},{4,2},{5,3},{6,0},{7,1},{8,14},{9,15},{10,... | collective-permute-start | bytes 1179656 | tf_op jit(solution)/shard_map/ppermute | solution.py:321
  33.1 1.9 %collective-permute-start.13 = (f32[4,64,384]{2,1,0:T(8,128)S(1)}, f32[4,64,384]{2,1,0:T(8,128)S(1)}, u32[]{:S(2)}, u32[]{:S(2)}) collective-permute-start(f32[4,64,384]{2,1,0:T(8,128)S(1)} %get-tuple-element.34), channel_id=1, source_target_pairs={{0,1},{1,0},{2,3},{3,2},{4,5},{5,4},{6,7},{7,6},{8,9},{9,8},{10,11... | collective-permute-start | bytes 1179656 | tf_op jit(solution)/shard_map/ppermute | solution.py:321
  35.0 2.0 %shard_map.53 = (f32[4,64,128]{2,1,0:T(8,128)S(1)}, f32[4,64,128]{2,1,0:T(8,128)S(1)}, f32[4,64,128]{2,1,0:T(8,128)S(1)}) custom-call(s32[1]{0:T(128)} %bitcast.which, bf16[64,2048]{1,0:T(8,128)(2,1)S(1)} %compare_select_fusion.refs_0_.refs_6_, bf16[128,2048]{1,0:T(8,128)(2,1)S(1)} %constant_dynamic-update-slice_fusion.refs_1_, ...), custom_call_target="tpu_custom_call" | custom-call | flops 10000000000 | bytes 100000 | tf_op jit(solution)/shard_map/pallas_call | solution.py:51
  36.9 1.5 %collective-permute-start.14 = (f32[4,64,128]{2,1,0:T(8,128)S(1)}, f32[4,64,128]{2,1,0:T(8,128)S(1)}, u32[]{:S(2)}, u32[]{:S(2)}) collective-permute-start(f32[4,64,128]{2,1,0:T(8,128)S(1)} %get-tuple-element.36), channel_id=1, source_target_pairs={{0,2},{1,3},{2,0},{3,1},{4,6},{5,7},{6,4},{7,5},{8,10},{9,11},{10,... | collective-permute-start | bytes 393224 | tf_op jit(solution)/shard_map/ppermute | solution.py:324
  38.5 2.3 %collective-permute-start.15 = (f32[4,64,128]{2,1,0:T(8,128)S(1)}, f32[4,64,128]{2,1,0:T(8,128)S(1)}, u32[]{:S(2)}, u32[]{:S(2)}) collective-permute-start(f32[4,64,128]{2,1,0:T(8,128)S(1)} %get-tuple-element.37), channel_id=1, source_target_pairs={{0,6},{1,7},{2,4},{3,5},{4,2},{5,3},{6,0},{7,1},{8,14},{9,15},{10,... | collective-permute-start | bytes 393224 | tf_op jit(solution)/shard_map/ppermute | solution.py:324
  40.8 1.4 %collective-permute-start.16 = (f32[4,64,128]{2,1,0:T(8,128)S(1)}, f32[4,64,128]{2,1,0:T(8,128)S(1)}, u32[]{:S(2)}, u32[]{:S(2)}) collective-permute-start(f32[4,64,128]{2,1,0:T(8,128)S(1)} %get-tuple-element.38), channel_id=1, source_target_pairs={{0,1},{1,0},{2,3},{3,2},{4,5},{5,4},{6,7},{7,6},{8,9},{9,8},{10,11... | collective-permute-start | bytes 393224 | tf_op jit(solution)/shard_map/ppermute | solution.py:324
  42.1 0.6 collective-permute-done.12.near
  42.7 0.8 collective-permute-done.13.near
  43.5 2.0 %shard_map.54 = (f32[4,64,512]{2,1,0:T(8,128)S(1)}, f32[4,64,512]{2,1,0:T(8,128)S(1)}, f32[4,64,512]{2,1,0:T(8,128)S(1)}, f32[192,128]{1,0:T(8,128)S(1)}) custom-call(s32[1]{0:T(128)} %bitcast.which, bf16[64,2048]{1,0:T(8,128)(2,1)S(1)} %compare_select_fusion.refs_0_.refs_6_, bf16[128,2048]{1,0:T(8,128)(2,1)S(1)} %constant_dynamic-update-slice_fusion.refs_1_, ...), custom_call_target="tpu_custom_call" | custom-call | flops 10000000000 | bytes 100000 | tf_op jit(solution)/shard_map/pallas_call | solution.py:51
  45.8 1.4 %collective-permute-start.21 = (f32[2,64,512]{2,1,0:T(8,128)S(1)}, f32[2,64,512]{2,1,0:T(8,128)S(1)}, u32[]{:S(2)}, u32[]{:S(2)}) collective-permute-start(f32[2,64,512]{2,1,0:T(8,128)S(1)} %get-tuple-element.59), channel_id=1, source_target_pairs={{0,2},{1,3},{2,0},{3,1},{4,6},{5,7},{6,4},{7,5},{8,10},{9,11},{10,... | collective-permute-start | bytes 786440 | tf_op jit(solution)/shard_map/ppermute | solution.py:330
  47.3 1.8 %collective-permute-start.19 = (f32[2,64,512]{2,1,0:T(8,128)S(1)}, f32[2,64,512]{2,1,0:T(8,128)S(1)}, u32[]{:S(2)}, u32[]{:S(2)}) collective-permute-start(f32[2,64,512]{2,1,0:T(8,128)S(1)} %get-tuple-element.53), channel_id=1, source_target_pairs={{0,1},{1,0},{2,3},{3,2},{4,5},{5,4},{6,7},{7,6},{8,9},{9,8},{10,11... | collective-permute-start | bytes 786440 | tf_op jit(solution)/shard_map/ppermute | solution.py:330
  49.1 2.0 %collective-permute-start.17 = (f32[2,64,512]{2,1,0:T(8,128)S(1)}, f32[2,64,512]{2,1,0:T(8,128)S(1)}, u32[]{:S(2)}, u32[]{:S(2)}) collective-permute-start(f32[2,64,512]{2,1,0:T(8,128)S(1)} %get-tuple-element.47), channel_id=1, source_target_pairs={{0,6},{1,7},{2,4},{3,5},{4,2},{5,3},{6,0},{7,1},{8,14},{9,15},{10,... | collective-permute-start | bytes 786440 | tf_op jit(solution)/shard_map/ppermute | solution.py:330
  51.1 1.1 %collective-permute-done.21.refs_7_ = f32[2,64,512]{2,1,0:T(8,128)S(1)} collective-permute-done((f32[2,64,512]{2,1,0:T(8,128)S(1)}, f32[2,64,512]{2,1,0:T(8,128)S(1)}, u32[]{:S(2)}, u32[]{:S(2)}) %collective-permute-start.21) | collective-permute-done | bytes 262176 | tf_op jit(solution)/shard_map/ppermute | solution.py:330
  52.3 2.7 %collective-permute-start.22 = (f32[1,64,512]{2,1,0:T(8,128)S(1)}, f32[1,64,512]{2,1,0:T(8,128)S(1)}, u32[]{:S(2)}, u32[]{:S(2)}) collective-permute-start(f32[1,64,512]{2,1,0:T(8,128)S(1)} %slice_add_fusion), channel_id=1, source_target_pairs={{0,6},{1,7},{2,4},{3,5},{4,2},{5,3},{6,0},{7,1},{8,14},{9,15},{10,... | collective-permute-start | bytes 393224 | tf_op jit(solution)/shard_map/ppermute | solution.py:332
  55.1 1.9 %collective-permute-done.17.refs_1_ = f32[2,64,512]{2,1,0:T(8,128)S(1)} collective-permute-done((f32[2,64,512]{2,1,0:T(8,128)S(1)}, f32[2,64,512]{2,1,0:T(8,128)S(1)}, u32[]{:S(2)}, u32[]{:S(2)}) %collective-permute-start.17) | collective-permute-done | bytes 262176 | tf_op jit(solution)/shard_map/ppermute | solution.py:330
  57.5 1.0 %collective-permute-done.22.refs_8_ = f32[1,64,512]{2,1,0:T(8,128)S(1)} collective-permute-done((f32[1,64,512]{2,1,0:T(8,128)S(1)}, f32[1,64,512]{2,1,0:T(8,128)S(1)}, u32[]{:S(2)}, u32[]{:S(2)}) %collective-permute-start.22) | collective-permute-done | bytes 131104 | tf_op jit(solution)/shard_map/ppermute | solution.py:332
  58.6 1.5 %collective-permute-done.20.refs_5_ = f32[1,64,512]{2,1,0:T(8,128)S(1)} collective-permute-done((f32[1,64,512]{2,1,0:T(8,128)S(1)}, f32[1,64,512]{2,1,0:T(8,128)S(1)}, u32[]{:S(2)}, u32[]{:S(2)}) %collective-permute-start.20) | collective-permute-done | bytes 131104 | tf_op jit(solution)/shard_map/ppermute | solution.py:332
  60.0 2.0 %collective-permute-done.18.refs_2_ = f32[1,64,512]{2,1,0:T(8,128)S(1)} collective-permute-done((f32[1,64,512]{2,1,0:T(8,128)S(1)}, f32[1,64,512]{2,1,0:T(8,128)S(1)}, u32[]{:S(2)}, u32[]{:S(2)}) %collective-permute-start.18) | collective-permute-done | bytes 131104 | tf_op jit(solution)/shard_map/ppermute | solution.py:332
  62.4 2.0 %collective-permute-start.23 = (f32[64,128]{1,0:T(8,128)S(1)}, f32[64,128]{1,0:T(8,128)S(1)}, u32[]{:S(2)}, u32[]{:S(2)}) collective-permute-start(f32[64,128]{1,0:T(8,128)S(1)} %shard_map.58), channel_id=1, source_target_pairs={{0,32},{8,40},{16,48},{24,56},{32,0},{40,8},{48,16},{56,24},{64,96... | collective-permute-start | bytes 98312 | tf_op jit(solution)/shard_map/ppermute | solution.py:284
  64.4 1.3 %collective-permute-start.24 = (f32[64,128]{1,0:T(8,128)S(1)}, f32[64,128]{1,0:T(8,128)S(1)}, u32[]{:S(2)}, u32[]{:S(2)}) collective-permute-start(f32[64,128]{1,0:T(8,128)S(1)} %shard_map.58), channel_id=1, source_target_pairs={{0,48},{8,56},{16,32},{24,40},{32,16},{40,24},{48,0},{56,8},{64,11... | collective-permute-start | bytes 98312 | tf_op jit(solution)/shard_map/ppermute | solution.py:284
  66.0 1.9 %collective-permute-done.23 = f32[64,128]{1,0:T(8,128)S(1)} collective-permute-done((f32[64,128]{1,0:T(8,128)S(1)}, f32[64,128]{1,0:T(8,128)S(1)}, u32[]{:S(2)}, u32[]{:S(2)}) %collective-permute-start.23) | collective-permute-done | bytes 32800 | tf_op jit(solution)/shard_map/ppermute | solution.py:284
  67.9 1.6 %collective-permute-done.24 = f32[64,128]{1,0:T(8,128)S(1)} collective-permute-done((f32[64,128]{1,0:T(8,128)S(1)}, f32[64,128]{1,0:T(8,128)S(1)}, u32[]{:S(2)}, u32[]{:S(2)}) %collective-permute-start.24) | collective-permute-done | bytes 32800 | tf_op jit(solution)/shard_map/ppermute | solution.py:284
  69.7 1.2 %collective-permute-done.26.refs_1_ = f32[64,128]{1,0:T(8,128)S(1)} collective-permute-done((f32[64,128]{1,0:T(8,128)S(1)}, f32[64,128]{1,0:T(8,128)S(1)}, u32[]{:S(2)}, u32[]{:S(2)}) %collective-permute-start.26) | collective-permute-done | bytes 32800 | tf_op jit(solution)/shard_map/ppermute | solution.py:284
  71.3 2.6 %collective-permute-start.27 = (f32[136,128]{1,0:T(8,128)S(1)}, f32[136,128]{1,0:T(8,128)S(1)}, u32[]{:S(2)}, u32[]{:S(2)}) collective-permute-start(f32[136,128]{1,0:T(8,128)S(1)} %shard_map.59), channel_id=1, source_target_pairs={{0,4},{1,5},{2,6},{3,7},{4,0},{5,1},{6,2},{7,3},{8,12},{9,13},{10,... | collective-permute-start | bytes 208904 | tf_op jit(solution)/shard_map/ppermute | solution.py:284
  73.8 0.9 collective-permute-start.28
  75.2 2.0 %collective-permute-done.27 = f32[136,128]{1,0:T(8,128)S(1)} collective-permute-done((f32[136,128]{1,0:T(8,128)S(1)}, f32[136,128]{1,0:T(8,128)S(1)}, u32[]{:S(2)}, u32[]{:S(2)}) %collective-permute-start.27) | collective-permute-done | bytes 69664 | tf_op jit(solution)/shard_map/ppermute | solution.py:284
  77.2 2.2 %collective-permute-done.28 = f32[136,128]{1,0:T(8,128)S(1)} collective-permute-done((f32[136,128]{1,0:T(8,128)S(1)}, f32[136,128]{1,0:T(8,128)S(1)}, u32[]{:S(2)}, u32[]{:S(2)}) %collective-permute-start.28) | collective-permute-done | bytes 69664 | tf_op jit(solution)/shard_map/ppermute | solution.py:284
  79.4 0.9 collective-permute-start.30
  80.3 3.5 %collective-permute-done.30 = f32[136,128]{1,0:T(8,128)S(1)} collective-permute-done((f32[136,128]{1,0:T(8,128)S(1)}, f32[136,128]{1,0:T(8,128)S(1)}, u32[]{:S(2)}, u32[]{:S(2)}) %collective-permute-start.30) | collective-permute-done | bytes 69664 | tf_op jit(solution)/shard_map/ppermute | solution.py:284
  84.0 3.6 %collective-permute-start.31 = (f32[72,128]{1,0:T(8,128)S(1)}, f32[72,128]{1,0:T(8,128)S(1)}, u32[]{:S(2)}, u32[]{:S(2)}) collective-permute-start(f32[72,128]{1,0:T(8,128)S(1)} %slice.23.refs_0_), channel_id=1, source_target_pairs={{0,128},{8,136},{16,144},{24,152},{32,160},{40,168},{48,176},{56,1... | collective-permute-start | bytes 110600 | tf_op jit(solution)/shard_map/ppermute | solution.py:284
  87.5 0.7 collective-permute-start.32
  88.2 2.4 %collective-permute-start.33 = (f32[72,128]{1,0:T(8,128)S(1)}, f32[72,128]{1,0:T(8,128)S(1)}, u32[]{:S(2)}, u32[]{:S(2)}) collective-permute-start(f32[72,128]{1,0:T(8,128)S(1)} %slice.23.refs_0_), channel_id=1, source_target_pairs={{0,192},{8,200},{16,208},{24,216},{32,224},{40,232},{48,240},{56,2... | collective-permute-start | bytes 110600 | tf_op jit(solution)/shard_map/ppermute | solution.py:284
  90.5 1.4 %collective-permute-done.31.refs_1_ = f32[72,128]{1,0:T(8,128)S(1)} collective-permute-done((f32[72,128]{1,0:T(8,128)S(1)}, f32[72,128]{1,0:T(8,128)S(1)}, u32[]{:S(2)}, u32[]{:S(2)}) %collective-permute-start.31) | collective-permute-done | bytes 36896 | tf_op jit(solution)/shard_map/ppermute | solution.py:284
  91.9 0.8 collective-permute-done.32.refs_2_
  92.7 1.6 %collective-permute-done.33.refs_3_ = f32[72,128]{1,0:T(8,128)S(1)} collective-permute-done((f32[72,128]{1,0:T(8,128)S(1)}, f32[72,128]{1,0:T(8,128)S(1)}, u32[]{:S(2)}, u32[]{:S(2)}) %collective-permute-start.33) | collective-permute-done | bytes 36896 | tf_op jit(solution)/shard_map/ppermute | solution.py:284
  94.2 5.4 %shard_map.60 = (f32[64,128]{1,0:T(8,128)}, f32[128,128]{1,0:T(8,128)}) custom-call(f32[72,128]{1,0:T(8,128)S(1)} %slice.23.refs_0_, f32[72,128]{1,0:T(8,128)S(1)} %collective-permute-done.31.refs_1_, f32[72,128]{1,0:T(8,128)S(1)} %collective-permute-done.32.refs_2_, f32[72,128]{1,0:T(8,128)S(1)} %collective-permute-done.33.refs_3_, f32[64,128]{1,0:T(8,128)S(1)} %slice.24.refs_4_), custom_call_target="tpu_custom_call" | custom-call | tf_op jit(solution)/shard_map/pallas_call | solution.py:51
  (51 shorter events, 3.3 us)
Async XLA Ops:
  0.6 5.1 %copy-start = (f32[64,128]{1,0:T(8,128)S(1)}, f32[64,128]{1,0:T(8,128)}, u32[]{:S(2)}) copy-start(f32[64,128]{1,0:T(8,128)} %refs_10_.1) | copy-start | bytes 98308
  1.8 10.8 %collective-permute-start = (bf16[64,2048]{1,0:T(8,128)(2,1)S(1)}, bf16[64,2048]{1,0:T(8,128)(2,1)S(1)}, u32[]{:S(2)}, u32[]{:S(2)}) collective-permute-start(bf16[64,2048]{1,0:T(8,128)(2,1)S(1)} %compare_select_fusion.refs_0_.refs_6_), channel_id=1, source_target_pairs={{0,16},{8,24},{16,0},{24,8},{32,48},{40,56},{48,32},{56,40},{64,80... | collective-permute-start | bytes 786440 | tf_op jit(solution)/shard_map/ppermute | solution.py:275
  3.5 10.3 %collective-permute-start.1 = (bf16[64,2048]{1,0:T(8,128)(2,1)S(1)}, bf16[64,2048]{1,0:T(8,128)(2,1)S(1)}, u32[]{:S(2)}, u32[]{:S(2)}) collective-permute-start(bf16[64,2048]{1,0:T(8,128)(2,1)S(1)} %compare_select_fusion.refs_0_.refs_6_), channel_id=1, source_target_pairs={{0,48},{8,56},{16,32},{24,40},{32,16},{40,24},{48,0},{56,8},{64,11... | collective-permute-start | bytes 786440 | tf_op jit(solution)/shard_map/ppermute | solution.py:276
  5.7 15.0 %collective-permute-start.7 = (bf16[64,2304]{1,0:T(8,128)(2,1)S(1)}, bf16[64,2304]{1,0:T(8,128)(2,1)S(1)}, u32[]{:S(2)}, u32[]{:S(2)}) collective-permute-start(bf16[64,2304]{1,0:T(8,128)(2,1)S(1)} %pad_maximum_fusion), channel_id=1, source_target_pairs={{0,64},{8,72},{16,80},{24,88},{32,96},{40,104},{48,112},{56,120},{... | collective-permute-start | bytes 884744 | tf_op jit(solution)/shard_map/ppermute | solution.py:275
  9.1 17.3 %collective-permute-start.8 = (bf16[64,2304]{1,0:T(8,128)(2,1)S(1)}, bf16[64,2304]{1,0:T(8,128)(2,1)S(1)}, u32[]{:S(2)}, u32[]{:S(2)}) collective-permute-start(bf16[64,2304]{1,0:T(8,128)(2,1)S(1)} %pad_maximum_fusion), channel_id=1, source_target_pairs={{0,192},{8,200},{16,208},{24,216},{32,224},{40,232},{48,240},{56,2... | collective-permute-start | bytes 884744 | tf_op jit(solution)/shard_map/ppermute | solution.py:276
  12.7 14.8 %collective-permute-start.4 = (bf16[64,2048]{1,0:T(8,128)(2,1)S(1)}, bf16[64,2048]{1,0:T(8,128)(2,1)S(1)}, u32[]{:S(2)}, u32[]{:S(2)}) collective-permute-start(bf16[64,2048]{1,0:T(8,128)(2,1)S(1)} %compare_select_fusion.refs_0_.refs_6_), channel_id=1, source_target_pairs={{0,8},{8,0},{16,24},{24,16},{32,40},{40,32},{48,56},{56,48},{64,72... | collective-permute-start | bytes 786440 | tf_op jit(solution)/shard_map/ppermute | solution.py:303
  12.7 7.2 %collective-permute-start.2 = (bf16[32,2048]{1,0:T(8,128)(2,1)S(1)}, bf16[32,2048]{1,0:T(8,128)(2,1)S(1)}, u32[]{:S(2)}, u32[]{:S(2)}) collective-permute-start(bf16[32,2048]{1,0:T(8,128)(2,1)S(1)} %shard_map.50), channel_id=1, source_target_pairs={{0,48},{8,56},{16,32},{24,40},{32,16},{40,24},{48,0},{56,8},{64,11... | collective-permute-start | bytes 393224 | tf_op jit(solution)/shard_map/ppermute | solution.py:277
  13.8 6.1 %collective-permute-start.3 = (bf16[32,2048]{1,0:T(8,128)(2,1)S(1)}, bf16[32,2048]{1,0:T(8,128)(2,1)S(1)}, u32[]{:S(2)}, u32[]{:S(2)}) collective-permute-start(bf16[32,2048]{1,0:T(8,128)(2,1)S(1)} %shard_map.51), channel_id=1, source_target_pairs={{0,16},{8,24},{16,0},{24,8},{32,48},{40,56},{48,32},{56,40},{64,80... | collective-permute-start | bytes 393224 | tf_op jit(solution)/shard_map/ppermute | solution.py:278
  19.9 7.5 %collective-permute-start.5 = (bf16[128,2048]{1,0:T(8,128)(2,1)S(1)}, bf16[128,2048]{1,0:T(8,128)(2,1)S(1)}, u32[]{:S(2)}, u32[]{:S(2)}) collective-permute-start(bf16[128,2048]{1,0:T(8,128)(2,1)S(1)} %constant_dynamic-update-slice_fusion.refs_1_), channel_id=1, source_target_pairs={{0,8},{8,0},{16,24},{24,16},{32,40},{40,32},{48,56},{56,48},{64,72... | collective-permute-start | bytes 1572872 | tf_op jit(solution)/shard_map/ppermute | solution.py:303
  19.9 7.5 %collective-permute-start.6 = (bf16[64,2048]{1,0:T(8,128)(2,1)S(1)}, bf16[64,2048]{1,0:T(8,128)(2,1)S(1)}, u32[]{:S(2)}, u32[]{:S(2)}) collective-permute-start(bf16[64,2048]{1,0:T(8,128)(2,1)S(1)} %constant_dynamic-update-slice_fusion.2.refs_2_), channel_id=1, source_target_pairs={{0,8},{8,0},{16,24},{24,16},{32,40},{40,32},{48,56},{56,48},{64,72... | collective-permute-start | bytes 786440 | tf_op jit(solution)/shard_map/ppermute | solution.py:303
  20.7 14.2 %collective-permute-start.9 = (bf16[32,2304]{1,0:T(8,128)(2,1)S(1)}, bf16[32,2304]{1,0:T(8,128)(2,1)S(1)}, u32[]{:S(2)}, u32[]{:S(2)}) collective-permute-start(bf16[32,2304]{1,0:T(8,128)(2,1)S(1)} %split.8), channel_id=1, source_target_pairs={{0,192},{8,200},{16,208},{24,216},{32,224},{40,232},{48,240},{56,2... | collective-permute-start | bytes 442376 | tf_op jit(solution)/shard_map/ppermute | solution.py:277
  26.4 8.5 %collective-permute-start.10 = (bf16[32,2304]{1,0:T(8,128)(2,1)S(1)}, bf16[32,2304]{1,0:T(8,128)(2,1)S(1)}, u32[]{:S(2)}, u32[]{:S(2)}) collective-permute-start(bf16[32,2304]{1,0:T(8,128)(2,1)S(1)} %split.9), channel_id=1, source_target_pairs={{0,64},{8,72},{16,80},{24,88},{32,96},{40,104},{48,112},{56,120},{... | collective-permute-start | bytes 442376 | tf_op jit(solution)/shard_map/ppermute | solution.py:278
  29.4 11.4 %collective-permute-start.11 = (f32[4,64,384]{2,1,0:T(8,128)S(1)}, f32[4,64,384]{2,1,0:T(8,128)S(1)}, u32[]{:S(2)}, u32[]{:S(2)}) collective-permute-start(f32[4,64,384]{2,1,0:T(8,128)S(1)} %get-tuple-element.32), channel_id=1, source_target_pairs={{0,2},{1,3},{2,0},{3,1},{4,6},{5,7},{6,4},{7,5},{8,10},{9,11},{10,... | collective-permute-start | bytes 1179656 | tf_op jit(solution)/shard_map/ppermute | solution.py:321
  31.0 11.7 %collective-permute-start.12 = (f32[4,64,384]{2,1,0:T(8,128)S(1)}, f32[4,64,384]{2,1,0:T(8,128)S(1)}, u32[]{:S(2)}, u32[]{:S(2)}) collective-permute-start(f32[4,64,384]{2,1,0:T(8,128)S(1)} %get-tuple-element.33), channel_id=1, source_target_pairs={{0,6},{1,7},{2,4},{3,5},{4,2},{5,3},{6,0},{7,1},{8,14},{9,15},{10,... | collective-permute-start | bytes 1179656 | tf_op jit(solution)/shard_map/ppermute | solution.py:321
  33.1 10.5 %collective-permute-start.13 = (f32[4,64,384]{2,1,0:T(8,128)S(1)}, f32[4,64,384]{2,1,0:T(8,128)S(1)}, u32[]{:S(2)}, u32[]{:S(2)}) collective-permute-start(f32[4,64,384]{2,1,0:T(8,128)S(1)} %get-tuple-element.34), channel_id=1, source_target_pairs={{0,1},{1,0},{2,3},{3,2},{4,5},{5,4},{6,7},{7,6},{8,9},{9,8},{10,11... | collective-permute-start | bytes 1179656 | tf_op jit(solution)/shard_map/ppermute | solution.py:321
  36.9 8.6 %collective-permute-start.14 = (f32[4,64,128]{2,1,0:T(8,128)S(1)}, f32[4,64,128]{2,1,0:T(8,128)S(1)}, u32[]{:S(2)}, u32[]{:S(2)}) collective-permute-start(f32[4,64,128]{2,1,0:T(8,128)S(1)} %get-tuple-element.36), channel_id=1, source_target_pairs={{0,2},{1,3},{2,0},{3,1},{4,6},{5,7},{6,4},{7,5},{8,10},{9,11},{10,... | collective-permute-start | bytes 393224 | tf_op jit(solution)/shard_map/ppermute | solution.py:324
  38.5 7.1 %collective-permute-start.15 = (f32[4,64,128]{2,1,0:T(8,128)S(1)}, f32[4,64,128]{2,1,0:T(8,128)S(1)}, u32[]{:S(2)}, u32[]{:S(2)}) collective-permute-start(f32[4,64,128]{2,1,0:T(8,128)S(1)} %get-tuple-element.37), channel_id=1, source_target_pairs={{0,6},{1,7},{2,4},{3,5},{4,2},{5,3},{6,0},{7,1},{8,14},{9,15},{10,... | collective-permute-start | bytes 393224 | tf_op jit(solution)/shard_map/ppermute | solution.py:324
  40.8 5.0 %collective-permute-start.16 = (f32[4,64,128]{2,1,0:T(8,128)S(1)}, f32[4,64,128]{2,1,0:T(8,128)S(1)}, u32[]{:S(2)}, u32[]{:S(2)}) collective-permute-start(f32[4,64,128]{2,1,0:T(8,128)S(1)} %get-tuple-element.38), channel_id=1, source_target_pairs={{0,1},{1,0},{2,3},{3,2},{4,5},{5,4},{6,7},{7,6},{8,9},{9,8},{10,11... | collective-permute-start | bytes 393224 | tf_op jit(solution)/shard_map/ppermute | solution.py:324
  45.8 6.5 %collective-permute-start.21 = (f32[2,64,512]{2,1,0:T(8,128)S(1)}, f32[2,64,512]{2,1,0:T(8,128)S(1)}, u32[]{:S(2)}, u32[]{:S(2)}) collective-permute-start(f32[2,64,512]{2,1,0:T(8,128)S(1)} %get-tuple-element.59), channel_id=1, source_target_pairs={{0,2},{1,3},{2,0},{3,1},{4,6},{5,7},{6,4},{7,5},{8,10},{9,11},{10,... | collective-permute-start | bytes 786440 | tf_op jit(solution)/shard_map/ppermute | solution.py:330
  47.3 7.7 %collective-permute-start.19 = (f32[2,64,512]{2,1,0:T(8,128)S(1)}, f32[2,64,512]{2,1,0:T(8,128)S(1)}, u32[]{:S(2)}, u32[]{:S(2)}) collective-permute-start(f32[2,64,512]{2,1,0:T(8,128)S(1)} %get-tuple-element.53), channel_id=1, source_target_pairs={{0,1},{1,0},{2,3},{3,2},{4,5},{5,4},{6,7},{7,6},{8,9},{9,8},{10,11... | collective-permute-start | bytes 786440 | tf_op jit(solution)/shard_map/ppermute | solution.py:330
  49.1 7.8 %collective-permute-start.17 = (f32[2,64,512]{2,1,0:T(8,128)S(1)}, f32[2,64,512]{2,1,0:T(8,128)S(1)}, u32[]{:S(2)}, u32[]{:S(2)}) collective-permute-start(f32[2,64,512]{2,1,0:T(8,128)S(1)} %get-tuple-element.47), channel_id=1, source_target_pairs={{0,6},{1,7},{2,4},{3,5},{4,2},{5,3},{6,0},{7,1},{8,14},{9,15},{10,... | collective-permute-start | bytes 786440 | tf_op jit(solution)/shard_map/ppermute | solution.py:330
  52.3 6.3 %collective-permute-start.22 = (f32[1,64,512]{2,1,0:T(8,128)S(1)}, f32[1,64,512]{2,1,0:T(8,128)S(1)}, u32[]{:S(2)}, u32[]{:S(2)}) collective-permute-start(f32[1,64,512]{2,1,0:T(8,128)S(1)} %slice_add_fusion), channel_id=1, source_target_pairs={{0,6},{1,7},{2,4},{3,5},{4,2},{5,3},{6,0},{7,1},{8,14},{9,15},{10,... | collective-permute-start | bytes 393224 | tf_op jit(solution)/shard_map/ppermute | solution.py:332
  55.0 5.1 %collective-permute-start.20 = (f32[1,64,512]{2,1,0:T(8,128)S(1)}, f32[1,64,512]{2,1,0:T(8,128)S(1)}, u32[]{:S(2)}, u32[]{:S(2)}) collective-permute-start(f32[1,64,512]{2,1,0:T(8,128)S(1)} %slice_add_fusion.1), channel_id=1, source_target_pairs={{0,2},{1,3},{2,0},{3,1},{4,6},{5,7},{6,4},{7,5},{8,10},{9,11},{10,... | collective-permute-start | bytes 393224 | tf_op jit(solution)/shard_map/ppermute | solution.py:332
  57.0 5.1 %collective-permute-start.18 = (f32[1,64,512]{2,1,0:T(8,128)S(1)}, f32[1,64,512]{2,1,0:T(8,128)S(1)}, u32[]{:S(2)}, u32[]{:S(2)}) collective-permute-start(f32[1,64,512]{2,1,0:T(8,128)S(1)} %slice_add_fusion.2), channel_id=1, source_target_pairs={{0,1},{1,0},{2,3},{3,2},{4,5},{5,4},{6,7},{7,6},{8,9},{9,8},{10,11... | collective-permute-start | bytes 393224 | tf_op jit(solution)/shard_map/ppermute | solution.py:332
  62.4 5.5 %collective-permute-start.23 = (f32[64,128]{1,0:T(8,128)S(1)}, f32[64,128]{1,0:T(8,128)S(1)}, u32[]{:S(2)}, u32[]{:S(2)}) collective-permute-start(f32[64,128]{1,0:T(8,128)S(1)} %shard_map.58), channel_id=1, source_target_pairs={{0,32},{8,40},{16,48},{24,56},{32,0},{40,8},{48,16},{56,24},{64,96... | collective-permute-start | bytes 98312 | tf_op jit(solution)/shard_map/ppermute | solution.py:284
  64.4 5.1 %collective-permute-start.24 = (f32[64,128]{1,0:T(8,128)S(1)}, f32[64,128]{1,0:T(8,128)S(1)}, u32[]{:S(2)}, u32[]{:S(2)}) collective-permute-start(f32[64,128]{1,0:T(8,128)S(1)} %shard_map.58), channel_id=1, source_target_pairs={{0,48},{8,56},{16,32},{24,40},{32,16},{40,24},{48,0},{56,8},{64,11... | collective-permute-start | bytes 98312 | tf_op jit(solution)/shard_map/ppermute | solution.py:284
  65.7 3.9 %collective-permute-start.25 = (f32[64,128]{1,0:T(8,128)S(1)}, f32[64,128]{1,0:T(8,128)S(1)}, u32[]{:S(2)}, u32[]{:S(2)}) collective-permute-start(f32[64,128]{1,0:T(8,128)S(1)} %shard_map.58), channel_id=1, source_target_pairs={{0,16},{8,24},{16,0},{24,8},{32,48},{40,56},{48,32},{56,40},{64,80... | collective-permute-start | bytes 98312 | tf_op jit(solution)/shard_map/ppermute | solution.py:284
  69.6 1.3 %collective-permute-start.26 = (f32[64,128]{1,0:T(8,128)S(1)}, f32[64,128]{1,0:T(8,128)S(1)}, u32[]{:S(2)}, u32[]{:S(2)}) collective-permute-start(f32[64,128]{1,0:T(8,128)S(1)} %add_add_fusion.refs_0_), channel_id=1, source_target_pairs={{0,8},{8,0},{16,24},{24,16},{32,40},{40,32},{48,56},{56,48},{64,72... | collective-permute-start | bytes 98312 | tf_op jit(solution)/shard_map/ppermute | solution.py:284
  71.3 5.9 %collective-permute-start.27 = (f32[136,128]{1,0:T(8,128)S(1)}, f32[136,128]{1,0:T(8,128)S(1)}, u32[]{:S(2)}, u32[]{:S(2)}) collective-permute-start(f32[136,128]{1,0:T(8,128)S(1)} %shard_map.59), channel_id=1, source_target_pairs={{0,4},{1,5},{2,6},{3,7},{4,0},{5,1},{6,2},{7,3},{8,12},{9,13},{10,... | collective-permute-start | bytes 208904 | tf_op jit(solution)/shard_map/ppermute | solution.py:284
  73.8 5.5 %collective-permute-start.28 = (f32[136,128]{1,0:T(8,128)S(1)}, f32[136,128]{1,0:T(8,128)S(1)}, u32[]{:S(2)}, u32[]{:S(2)}) collective-permute-start(f32[136,128]{1,0:T(8,128)S(1)} %shard_map.59), channel_id=1, source_target_pairs={{0,6},{1,7},{2,4},{3,5},{4,2},{5,3},{6,0},{7,1},{8,14},{9,15},{10,... | collective-permute-start | bytes 208904 | tf_op jit(solution)/shard_map/ppermute | solution.py:284
  74.7 4.7 %collective-permute-start.29 = (f32[136,128]{1,0:T(8,128)S(1)}, f32[136,128]{1,0:T(8,128)S(1)}, u32[]{:S(2)}, u32[]{:S(2)}) collective-permute-start(f32[136,128]{1,0:T(8,128)S(1)} %shard_map.59), channel_id=1, source_target_pairs={{0,2},{1,3},{2,0},{3,1},{4,6},{5,7},{6,4},{7,5},{8,10},{9,11},{10,... | collective-permute-start | bytes 208904 | tf_op jit(solution)/shard_map/ppermute | solution.py:284
  79.4 4.4 %collective-permute-start.30 = (f32[136,128]{1,0:T(8,128)S(1)}, f32[136,128]{1,0:T(8,128)S(1)}, u32[]{:S(2)}, u32[]{:S(2)}) collective-permute-start(f32[136,128]{1,0:T(8,128)S(1)} %select_select_fusion.1), channel_id=1, source_target_pairs={{0,1},{1,0},{2,3},{3,2},{4,5},{5,4},{6,7},{7,6},{8,9},{9,8},{10,11... | collective-permute-start | bytes 208904 | tf_op jit(solution)/shard_map/ppermute | solution.py:284
  84.0 8.0 %collective-permute-start.31 = (f32[72,128]{1,0:T(8,128)S(1)}, f32[72,128]{1,0:T(8,128)S(1)}, u32[]{:S(2)}, u32[]{:S(2)}) collective-permute-start(f32[72,128]{1,0:T(8,128)S(1)} %slice.23.refs_0_), channel_id=1, source_target_pairs={{0,128},{8,136},{16,144},{24,152},{32,160},{40,168},{48,176},{56,1... | collective-permute-start | bytes 110600 | tf_op jit(solution)/shard_map/ppermute | solution.py:284
  87.5 5.2 %collective-permute-start.32 = (f32[72,128]{1,0:T(8,128)S(1)}, f32[72,128]{1,0:T(8,128)S(1)}, u32[]{:S(2)}, u32[]{:S(2)}) collective-permute-start(f32[72,128]{1,0:T(8,128)S(1)} %slice.23.refs_0_), channel_id=1, source_target_pairs={{0,64},{8,72},{16,80},{24,88},{32,96},{40,104},{48,112},{56,120},{... | collective-permute-start | bytes 110600 | tf_op jit(solution)/shard_map/ppermute | solution.py:284
  88.2 6.1 %collective-permute-start.33 = (f32[72,128]{1,0:T(8,128)S(1)}, f32[72,128]{1,0:T(8,128)S(1)}, u32[]{:S(2)}, u32[]{:S(2)}) collective-permute-start(f32[72,128]{1,0:T(8,128)S(1)} %slice.23.refs_0_), channel_id=1, source_target_pairs={{0,192},{8,200},{16,208},{24,216},{32,224},{40,232},{48,240},{56,2... | collective-permute-start | bytes 110600 | tf_op jit(solution)/shard_map/ppermute | solution.py:284
